TPU v7x, 128 devices: a whole 4x4x4 slice. The times are simulated.
128 devices in a mesh: section: 2 (over core), dp: 4 (over x), shard: 16 (over z, y).
Axes of the slice: x: 4, y: 4, z: 4, core: 2. Of those that a mesh axis runs over, the one named last changes fastest.
Arguments:
- tokens: bfloat16 [2, 64, 128, 1024], P(None, ('dp', 'shard')), may hold values from -6 to 6
- lengths: int32 [2, 64], P(None, ('dp', 'shard')), may hold values from 64 to 128, as said below
- cotangent: bfloat16 [2, 64, 128, 1024], P(None, ('dp', 'shard')), may hold values from -6 to 6
- w_qkv: bfloat16 [2, 1024, 3072], P('section', 'shard'), may hold values from -0.1875 to 0.1875
- bias_q: bfloat16 [2, 1024], P('section', 'shard'), may hold values from -3 to 3
- bias_v: bfloat16 [2, 1024], P('section', 'shard'), may hold values from -3 to 3
- w_out: bfloat16 [2, 1024, 1024], P('section', 'shard'), may hold values from -0.75 to 0.75
- bias_out: bfloat16 [2, 1024], P('section', 'shard'), may hold values from -3 to 3
- gain_attn: bfloat16 [2, 1024], P('section', 'shard'), may hold values from 0.25 to 1.75
- shift_attn: bfloat16 [2, 1024], P('section', 'shard'), may hold values from -3 to 3
- w_up: bfloat16 [2, 1024, 4096], P('section', 'shard'), may hold values from -0.1875 to 0.1875
- bias_up: bfloat16 [2, 4096], P('section', 'shard'), may hold values from -3 to 3
- w_down: bfloat16 [2, 4096, 1024], P('section', 'shard'), may hold values from -0.09375 to 0.09375
- bias_down: bfloat16 [2, 1024], P('section', 'shard'), may hold values from -3 to 3
- gain_mlp: bfloat16 [2, 1024], P('section', 'shard'), may hold values from 0.25 to 1.75
- shift_mlp: bfloat16 [2, 1024], P('section', 'shard'), may hold values from -3 to 3
Outputs:
- activations: bfloat16 [2, 2, 64, 128, 1024], P('section', None, ('dp', 'shard'))
- input_grads: bfloat16 [2, 2, 64, 128, 1024], P('section', None, ('dp', 'shard'))
- grad_w_qkv: float32 [2, 1024, 3072], P('section', 'shard')
- grad_bias_q: float32 [2, 1024], P('section', 'shard')
- grad_bias_v: float32 [2, 1024], P('section', 'shard')
- grad_w_out: float32 [2, 1024, 1024], P('section', 'shard')
- grad_bias_out: float32 [2, 1024], P('section', 'shard')
- grad_gain_attn: float32 [2, 1024], P('section', 'shard')
- grad_shift_attn: float32 [2, 1024], P('section', 'shard')
- grad_w_up: float32 [2, 1024, 4096], P('section', 'shard')
- grad_bias_up: float32 [2, 4096], P('section', 'shard')
- grad_w_down: float32 [2, 4096, 1024], P('section', 'shard')
- grad_bias_down: float32 [2, 1024], P('section', 'shard')
- grad_gain_mlp: float32 [2, 1024], P('section', 'shard')
- grad_shift_mlp: float32 [2, 1024], P('section', 'shard')
Inputs may be any that keep to these rules, and one draw needn't show every extreme that they name: `lengths`: the number of real tokens of each sequence; the first sequence of the first micro-batch is full.
All inputs are finite; a program needn't handle non-finite values.
Results may differ from a plain program's by a relative error of at most 0.023.
Values may be sent and summed in bfloat16 or wider, within the bound.
No kernel may reach another device: no remote copies, remote signals or barrier semaphores. Data moves between devices by JAX's collectives and lax.ppermute only.
A program may use at most 256 MiB of HBM per device.

v0:
```python
import jax
import jax.numpy as jnp
from jax import lax
from jax.sharding import PartitionSpec as P

HEAD_DIM = 64


EPSILON = 1e-06


def in_one_piece(arrays, axis, dim, along):
    columns = [a.reshape(*a.shape[:along], -1) for a in arrays]
    both = jnp.concatenate(columns, axis=along)
    whole, at, gathered = (lax.all_gather(both, axis, axis=dim, tiled=True), 0, [])
    for a, column in zip(arrays, columns):
        share = whole[..., at : at + column.shape[along]]
        gathered.append(share.reshape(*share.shape[:along], *a.shape[along:]))
        at += column.shape[along]
    return tuple(gathered)


def in_one_piece_2(arrays, axis, dim, along):
    both = jnp.concatenate(arrays, axis=along)
    whole, at, gathered = (lax.all_gather(both, axis, axis=dim, tiled=True), 0, [])
    for a in arrays:
        gathered.append(lax.slice_in_dim(whole, at, at + a.shape[along], axis=along))
        at += a.shape[along]
    return tuple(gathered)


def from_behind(block, axis, distance):
    devices = range(lax.axis_size(axis))
    route = [(i - distance, i) for i in devices if i - distance in devices]
    return lax.ppermute(block, axis, route)


def for_sending(value):
    return jax.tree.map(lambda a: a.astype(jnp.bfloat16) if a.dtype == jnp.float32 else a, value)


def norm_rows(values):
    centered = values - jnp.mean(values, axis=-1, keepdims=True)
    inverse = lax.rsqrt(jnp.mean(centered * centered, axis=-1, keepdims=True) + EPSILON)
    return (centered * inverse, inverse)


def norm_back(grad_norm, normed, inverse):
    return inverse * (
        grad_norm
        - jnp.mean(grad_norm, axis=-1, keepdims=True)
        - normed * jnp.mean(grad_norm * normed, axis=-1, keepdims=True)
    )


def transpose_dot(left_rows, right_rows):
    return lax.dot_general(
        left_rows, right_rows, (((0,), (0,)), ((), ())), preferred_element_type=jnp.float32
    )


def dot_transposed(left_rows, right_rows):
    return lax.dot_general(
        left_rows, right_rows, (((1,), (1,)), ((), ())), preferred_element_type=jnp.float32
    )


def split_heads(packed, part_number):
    model_width = packed.shape[1] // 3
    piece = packed[:, part_number * model_width : (part_number + 1) * model_width]
    return piece.reshape(piece.shape[0], model_width // HEAD_DIM, HEAD_DIM)


def masked_scores(packed, seq_length):
    scores = jnp.einsum(
        "qhd,khd->hqk",
        split_heads(packed, 0),
        split_heads(packed, 1),
        preferred_element_type=jnp.float32,
    ) * HEAD_DIM ** (-0.5)
    positions = lax.broadcasted_iota(jnp.int32, scores.shape, 2)
    return jnp.where(positions < seq_length, scores, -1000000000.0)


def layer_forward(inputs, weights, seq_length):
    (
        w_qkv,
        bias_q,
        bias_v,
        w_out,
        bias_out,
        gain_attn,
        shift_attn,
        w_up,
        bias_up,
        w_down,
        bias_down,
        gain_mlp,
        shift_mlp,
    ) = weights
    seq_rows = inputs.shape[0]
    bias_all = jnp.concatenate([bias_q, jnp.zeros_like(bias_q), bias_v]).astype(jnp.float32)
    packed = (jnp.dot(inputs, w_qkv, preferred_element_type=jnp.float32) + bias_all).astype(
        jnp.bfloat16
    )
    scores = masked_scores(packed, seq_length)
    row_max = jnp.max(scores, axis=-1, keepdims=True)
    exponent = jnp.exp(scores - row_max)
    row_total = jnp.sum(exponent, axis=-1, keepdims=True)
    soft_weights = exponent / row_total
    log_total = row_max + jnp.log(row_total)
    attended = jnp.einsum(
        "hqk,khd->qhd",
        soft_weights.astype(jnp.bfloat16),
        split_heads(packed, 2),
        preferred_element_type=jnp.float32,
    )
    attended = attended.reshape(seq_rows, -1).astype(jnp.bfloat16)
    branch = jnp.dot(attended, w_out, preferred_element_type=jnp.float32) + bias_out.astype(
        jnp.float32
    )
    normed_attn, inverse_attn = norm_rows(inputs.astype(jnp.float32) + branch)
    hidden = (normed_attn * gain_attn.astype(jnp.float32) + shift_attn.astype(jnp.float32)).astype(
        jnp.bfloat16
    )
    upward = jnp.dot(hidden, w_up, preferred_element_type=jnp.float32) + bias_up.astype(jnp.float32)
    activated = jax.nn.gelu(upward, approximate=False).astype(jnp.bfloat16)
    mixed = jnp.dot(activated, w_down, preferred_element_type=jnp.float32) + bias_down.astype(
        jnp.float32
    )
    normed_mlp, inverse_mlp = norm_rows(hidden.astype(jnp.float32) + mixed)
    result = normed_mlp * gain_mlp.astype(jnp.float32) + shift_mlp.astype(jnp.float32)
    kept = (
        inputs,
        packed,
        log_total,
        attended,
        normed_attn,
        inverse_attn,
        hidden,
        upward,
        activated,
        normed_mlp,
        inverse_mlp,
    )
    return (result, kept)


def layer_backward(grad_result, kept, weights, seq_length):
    (
        w_qkv,
        bias_q,
        bias_v,
        w_out,
        bias_out,
        gain_attn,
        shift_attn,
        w_up,
        bias_up,
        w_down,
        bias_down,
        gain_mlp,
        shift_mlp,
    ) = weights
    (
        inputs,
        packed,
        log_total,
        attended,
        normed_attn,
        inverse_attn,
        hidden,
        upward,
        activated,
        normed_mlp,
        inverse_mlp,
    ) = kept
    seq_rows = inputs.shape[0]
    scaling = HEAD_DIM ** (-0.5)
    grad_gain_mlp = jnp.sum(grad_result * normed_mlp, axis=0)
    grad_shift_mlp = jnp.sum(grad_result, axis=0)
    grad_resid_mlp = norm_back(grad_result * gain_mlp.astype(jnp.float32), normed_mlp, inverse_mlp)
    grad_mixed = grad_resid_mlp.astype(jnp.bfloat16)
    grad_bias_down = jnp.sum(grad_mixed.astype(jnp.float32), axis=0)
    grad_w_down = transpose_dot(activated, grad_mixed)
    grad_activated = dot_transposed(grad_mixed, w_down)
    unused, gelu_pull = jax.vjp(lambda point: jax.nn.gelu(point, approximate=False), upward)
    grad_upward = gelu_pull(grad_activated)[0].astype(jnp.bfloat16)
    grad_bias_up = jnp.sum(grad_upward.astype(jnp.float32), axis=0)
    grad_w_up = transpose_dot(hidden, grad_upward)
    grad_hidden = grad_resid_mlp + dot_transposed(grad_upward, w_up)
    grad_gain_attn = jnp.sum(grad_hidden * normed_attn, axis=0)
    grad_shift_attn = jnp.sum(grad_hidden, axis=0)
    grad_resid_attn = norm_back(
        grad_hidden * gain_attn.astype(jnp.float32), normed_attn, inverse_attn
    )
    grad_branch = grad_resid_attn.astype(jnp.bfloat16)
    grad_bias_out = jnp.sum(grad_branch.astype(jnp.float32), axis=0)
    grad_w_out = transpose_dot(attended, grad_branch)
    grad_attended = (
        dot_transposed(grad_branch, w_out).astype(jnp.bfloat16).reshape(seq_rows, -1, HEAD_DIM)
    )
    soft_weights = jnp.exp(masked_scores(packed, seq_length) - log_total)
    grad_values = jnp.einsum(
        "hqk,qhd->khd",
        soft_weights.astype(jnp.bfloat16),
        grad_attended,
        preferred_element_type=jnp.float32,
    )
    grad_soft = jnp.einsum(
        "qhd,khd->hqk", grad_attended, split_heads(packed, 2), preferred_element_type=jnp.float32
    )
    grad_scores = soft_weights * (
        grad_soft - jnp.sum(grad_soft * soft_weights, axis=-1, keepdims=True)
    )
    grad_scores = grad_scores.astype(jnp.bfloat16)
    grad_queries = (
        jnp.einsum(
            "hqk,khd->qhd", grad_scores, split_heads(packed, 1), preferred_element_type=jnp.float32
        )
        * scaling
    )
    grad_keys = (
        jnp.einsum(
            "hqk,qhd->khd", grad_scores, split_heads(packed, 0), preferred_element_type=jnp.float32
        )
        * scaling
    )
    grad_packed = jnp.concatenate(
        [
            grad_queries.reshape(seq_rows, -1),
            grad_keys.reshape(seq_rows, -1),
            grad_values.reshape(seq_rows, -1),
        ],
        axis=1,
    ).astype(jnp.bfloat16)
    grad_packed_wide = grad_packed.astype(jnp.float32)
    model_width = grad_packed.shape[1] // 3
    grad_bias_q = jnp.sum(grad_packed_wide[:, :model_width], axis=0)
    grad_bias_v = jnp.sum(grad_packed_wide[:, 2 * model_width :], axis=0)
    grad_w_qkv = transpose_dot(inputs, grad_packed)
    grad_inputs = grad_resid_attn + dot_transposed(grad_packed, w_qkv)
    return (
        grad_inputs,
        (
            grad_w_qkv,
            grad_bias_q,
            grad_bias_v,
            grad_w_out,
            grad_bias_out,
            grad_gain_attn,
            grad_shift_attn,
            grad_w_up,
            grad_bias_up,
            grad_w_down,
            grad_bias_down,
            grad_gain_mlp,
            grad_shift_mlp,
        ),
    )


def per_device(
    tokens,
    lengths,
    cotangent,
    w_qkv,
    bias_q,
    bias_v,
    w_out,
    bias_out,
    gain_attn,
    shift_attn,
    w_up,
    bias_up,
    w_down,
    bias_down,
    gain_mlp,
    shift_mlp,
):
    section_index = lax.axis_index("section")
    is_first = section_index == 0
    micro_count = tokens.shape[0]
    shards = (
        w_qkv,
        bias_q,
        bias_v,
        w_out,
        bias_out,
        gain_attn,
        shift_attn,
        w_up,
        bias_up,
        w_down,
        bias_down,
        gain_mlp,
        shift_mlp,
    )
    gathered = (
        *in_one_piece(
            (
                shards[0],
                shards[1],
                shards[2],
                shards[3],
                shards[4],
                shards[5],
                shards[6],
                shards[7],
            ),
            "shard",
            1,
            2,
        ),
        *in_one_piece((shards[8], shards[9]), "shard", 1, 2),
        *in_one_piece_2((shards[10], shards[11], shards[12]), "shard", 1, 0),
    )
    weights = tuple((member[0] for member in gathered))
    received = jnp.zeros(tokens.shape[2:], jnp.bfloat16)
    results = []
    kept_list = []
    for step_index in range(micro_count + 1):
        own_micro = min(step_index, micro_count - 1)
        layer_input = jnp.where(is_first, tokens[own_micro, 0], received)
        micro_index = jnp.where(is_first, own_micro, max(step_index - 1, 0))
        result, kept = layer_forward(layer_input, weights, lengths[micro_index, 0])
        result_low = result.astype(jnp.bfloat16)
        results.append(result_low)
        kept_list.append(kept)
        if step_index < micro_count:
            received = from_behind(result_low, "section", 1)
    activations = jnp.stack(
        [
            jnp.where(is_first, results[micro_slot], results[micro_slot + 1])
            for micro_slot in range(micro_count)
        ]
    )[None, :, None]
    kept_stack = jax.tree.map(lambda *members: jnp.stack(members), *kept_list)
    incoming = jnp.zeros(tokens.shape[2:], jnp.bfloat16)
    grad_list = []
    full_totals = tuple((jnp.zeros(member.shape, jnp.float32) for member in weights))
    for step_index in range(micro_count + 1):
        slot = jnp.where(is_first, max(step_index - 1, 0), min(step_index + 1, micro_count))
        micro_index = jnp.where(is_first, max(step_index - 1, 0), min(step_index, micro_count - 1))
        kept = jax.tree.map(lambda member: member[slot], kept_stack)
        grad_result = jnp.where(
            is_first, incoming, cotangent[min(step_index, micro_count - 1), 0]
        ).astype(jnp.float32)
        active = jnp.where(is_first, step_index >= 1, step_index < micro_count)
        grad_input, grads = layer_backward(grad_result, kept, weights, lengths[micro_index, 0])
        grad_low = grad_input.astype(jnp.bfloat16)
        grad_list.append(grad_low)
        grads = tuple((jnp.where(active, member, 0.0) for member in grads))
        if step_index < micro_count:
            incoming = from_behind(grad_low, "section", -1)
        full_totals = tuple((left + right for left, right in zip(full_totals, grads)))
    share_totals = jax.tree.map(
        lambda part: part.astype(jnp.float32),
        lax.psum_scatter(for_sending(full_totals), "shard", scatter_dimension=0, tiled=True),
    )
    summed = jax.tree.map(
        lambda part: part.astype(jnp.float32), lax.psum(for_sending(share_totals), "dp")
    )
    input_grads = jnp.stack(
        [
            jnp.where(is_first, grad_list[micro_slot + 1], grad_list[micro_slot])
            for micro_slot in range(micro_count)
        ]
    )[None, :, None]
    return (activations, input_grads) + tuple((member[None] for member in summed))


def solution(mesh):
    in_specs = (
        P(None, ("dp", "shard"), None, None),
        P(None, ("dp", "shard")),
        P(None, ("dp", "shard"), None, None),
        P("section", "shard", None),
        P("section", "shard"),
        P("section", "shard"),
        P("section", "shard", None),
        P("section", "shard"),
        P("section", "shard"),
        P("section", "shard"),
        P("section", "shard", None),
        P("section", "shard"),
        P("section", "shard", None),
        P("section", "shard"),
        P("section", "shard"),
        P("section", "shard"),
    )
    out_specs = (
        P("section", None, ("dp", "shard"), None, None),
        P("section", None, ("dp", "shard"), None, None),
        P("section", "shard", None),
        P("section", "shard"),
        P("section", "shard"),
        P("section", "shard", None),
        P("section", "shard"),
        P("section", "shard"),
        P("section", "shard"),
        P("section", "shard", None),
        P("section", "shard"),
        P("section", "shard", None),
        P("section", "shard"),
        P("section", "shard"),
        P("section", "shard"),
    )
    return jax.shard_map(
        per_device, mesh=mesh, in_specs=in_specs, out_specs=out_specs, check_vma=False
    )
```

profile of v0, /device:TPU:1, one launch (start us, length us, event | category | flops | bytes accessed | tf_op | source)
XLA Modules:
  0.0 796.6 jit_solution(9892007337004172787)
XLA Ops:
  17.4 21.3 %all-gather = bf16[16,64,3]{1,2,0:T(4,128)(2,1)S(1)} all-gather(bf16[1,64,3]{1,2,0:T(4,128)(2,1)S(1)} %maximum_bitcast_fusion.2), channel_id=1, replica_groups=mesh['section'=2,'dp'=4,'shard'=16] {'shard'}, dimensions={0}, use_global_device_ids=true | all-gather | bytes 6528 | tf_op jit(solution)/shard_map/all_gather | solution.py:25
  42.1 47.7 %all-gather.6.cloned.1.call-done = bf16[1,4096,1025]{2,1,0:T(8,128)(2,1)} async-done(((bf16[1,256,1025]{2,1,0:T(8,128)(2,1)}), bf16[1,4096,1025]{2,1,0:T(8,128)(2,1)}) %all-gather.6.cloned.1.call-update) | async-done | bytes 8396816 | tf_op jit(solution)/shard_map/all_gather | solution.py:15
  91.4 112.9 %all-gather.4.cloned.1.call-done = bf16[1,1024,8197]{2,1,0:T(8,128)(2,1)} async-done(((bf16[1,64,8197]{2,1,0:T(8,128)(2,1)}), bf16[1,1024,8197]{2,1,0:T(8,128)(2,1)}) %all-gather.4.cloned.1.call-update) | async-done | bytes 16787472 | tf_op jit(solution)/shard_map/all_gather | solution.py:15
  216.6 11.3 %fusion.17 = (bf16[128,4096]{1,0:T(8,128)(2,1)S(1)}, f32[128,4096]{1,0:T(8,128)}) fusion(f32[4096]{0:T(1024)S(1)} %convert_reduce_fusion, bf16[128,1024]{1,0:T(8,128)(2,1)S(1)} %get-tuple-element.155, bf16[1,1024,8197]{2,1,0:T(8,128)(2,1)} %all-gather.4.cloned.1.call-done), kind=kOutput, calls=%fused_computation.39 | convolution fusion | flops 1108344832 | bytes 11812864 | tf_op jit(solution)/shard_map/dot_general | solution.py:126
  235.5 3.9 fusion.1
  245.8 10.9 %fusion.20 = (bf16[128,4096]{1,0:T(8,128)(2,1)S(1)}, f32[128,4096]{1,0:T(8,128)}) fusion(f32[4096]{0:T(1024)S(1)} %convert_reduce_fusion, bf16[128,1024]{1,0:T(8,128)(2,1)S(1)} %get-tuple-element.157, bf16[1,1024,8197]{2,1,0:T(8,128)(2,1)} %all-gather.4.cloned.1.call-done), kind=kOutput, calls=%fused_computation.42 | convolution fusion | flops 1108344832 | bytes 11812864 | tf_op jit(solution)/shard_map/dot_general | solution.py:126
  264.2 3.9 fusion.2
  273.8 10.2 %fusion.23 = (bf16[128,4096]{1,0:T(8,128)(2,1)S(1)}, f32[128,4096]{1,0:T(8,128)S(1)}) fusion(f32[4096]{0:T(1024)S(1)} %convert_reduce_fusion, bf16[128,1024]{1,0:T(8,128)(2,1)S(1)} %get-tuple-element.159, bf16[1,1024,8197]{2,1,0:T(8,128)(2,1)} %all-gather.4.cloned.1.call-done), kind=kOutput, calls=%fused_computation.45 | convolution fusion | flops 1108344832 | bytes 11812864 | tf_op jit(solution)/shard_map/dot_general | solution.py:126
  291.5 13.9 %convert_reduce_fusion.3 = (f32[4096]{0:T(1024)}, bf16[128,4096]{1,0:T(8,128)(2,1)S(1)}) fusion(bf16[1,4096,1025]{2,1,0:T(8,128)(2,1)} %all-gather.6.cloned.1.call-done, f32[3,128,1024]{2,1,0:T(8,128)S(1)} %pad_maximum_fusion.3, s32[]{:T(128)S(6)} %select_n.321, f32[128]{0:T(128)S(1)} %broadcast_multiply_fusion.10, f32[128]{0:T(128)S(1)} %broadcast_multiply_fusion.11, ...), kind=kOutput, calls=%fused_computation.95 | convolution fusion | flops 1113583616 | bytes 12344320 | tf_op jit(solution)/shard_map/dot_general | solution.py:63
  305.4 4.5 fusion.202
  321.6 5.8 fusion.144
  336.7 4.0 fusion.217
  341.7 11.6 %convert_reduce_fusion.2 = (f32[4096]{0:T(1024)S(1)}, bf16[128,4096]{1,0:T(8,128)(2,1)S(1)}) fusion(bf16[1,4096,1025]{2,1,0:T(8,128)(2,1)} %all-gather.6.cloned.1.call-done, f32[128,1024]{1,0:T(8,128)S(1)} %get-tuple-element.120, f32[3,128,4096]{2,1,0:T(8,128)} %copy-done.2, s32[]{:T(128)S(6)} %select_n.320), kind=kOutput, calls=%fused_computation.94 | convolution fusion | flops 1112666112 | bytes 12075012 | tf_op jit(solution)/shard_map/dot_general | solution.py:63
  353.4 4.2 fusion.198
  366.4 5.2 fusion.143
  375.1 9.7 %convert_reduce_fusion.1 = (f32[4096]{0:T(1024)S(1)}, bf16[128,4096]{1,0:T(8,128)(2,1)S(1)}) fusion(bf16[1,4096,1025]{2,1,0:T(8,128)(2,1)S(1)} %bitcast.822, f32[128,1024]{1,0:T(8,128)S(1)} %get-tuple-element.122, f32[3,128,4096]{2,1,0:T(8,128)} %copy-done.2, s32[]{:T(128)S(6)} %select_n.327), kind=kOutput, calls=%fused_computation.93 | convolution fusion | flops 1112666112 | bytes 12075012 | tf_op jit(solution)/shard_map/dot_general | solution.py:63
  384.9 7.6 fusion.194
  405.9 7.4 fusion.222
  413.4 6.4 fusion.220
  428.9 13.3 %add_convert_fusion.2 = bf16[1024,3072]{1,0:T(8,128)(2,1)} fusion(f32[1024,3072]{1,0:T(8,128)} %fusion.220, f32[1024,3072]{1,0:T(8,128)} %fusion.222, pred[]{:T(512)S(6)} %eq.3, pred[]{:T(512)S(6)} %select_n.331, bf16[3,128,1024]{2,1,0:T(8,128)(2,1)} %copy-done.15, s32[]{:T(128)S(6)} %select_n.327, bf16[128,1024]{0,1:T(8,128)(2,1)S(1)} %bitcast.754, ...), kind=kOutput, calls=%fused_computation.2 | convolution fusion | flops 823394304 | bytes 32505862 | tf_op jit(solution)/shard_map/dot_general | solution.py:57
  444.3 8.1 %fusion.212 = f32[1024,4096]{1,0:T(8,128)} fusion(bf16[128,4096]{1,0:T(8,128)(2,1)S(1)} %copy-done.80, bf16[3,128,1024]{2,1,0:T(8,128)(2,1)S(1)} %pad_maximum_fusion.10, s32[]{:T(128)S(6)} %select_n.321), kind=kOutput, calls=%fused_computation.393 | convolution fusion | flops 1073741824 | bytes 18087940 | tf_op jit(solution)/shard_map/dot_general | solution.py:57
  452.4 8.1 %fusion.209 = f32[1024,4096]{1,0:T(8,128)} fusion(bf16[128,4096]{1,0:T(8,128)(2,1)S(1)} %copy-done.82, bf16[3,128,1024]{2,1,0:T(8,128)(2,1)S(1)} %pad_maximum_fusion.10, s32[]{:T(128)S(6)} %select_n.327), kind=kOutput, calls=%fused_computation.390 | convolution fusion | flops 1073741824 | bytes 18087940 | tf_op jit(solution)/shard_map/dot_general | solution.py:57
  460.5 9.9 %add_convert_fusion.1 = bf16[1024,4096]{1,0:T(8,128)(2,1)} fusion(f32[1024,4096]{1,0:T(8,128)} %fusion.209, f32[1024,4096]{1,0:T(8,128)} %fusion.212, bf16[128,4096]{1,0:T(8,128)(2,1)} %copy-done.57, pred[]{:T(512)S(6)} %eq.3, pred[]{:T(512)S(6)} %select_n.331, bf16[3,128,1024]{2,1,0:T(8,128)(2,1)S(1)} %pad_maximum_fusion.10, s32[]{:T(128)S(6)} %select_n.320), kind=kOutput, calls=%fused_computation.1 | convolution fusion | flops 1094713344 | bytes 43253768 | tf_op jit(solution)/shard_map/dot_general | solution.py:57
  473.5 8.2 %fusion.156 = f32[4096,1024]{1,0:T(8,128)} fusion(bf16[3,128,4096]{2,1,0:T(8,128)(2,1)S(1)} %pad_maximum_fusion.1, s32[]{:T(128)S(6)} %select_n.321, f32[3,128,1024]{2,1,0:T(8,128)S(1)} %pad_maximum_fusion.3, f32[128]{0:T(128)S(1)} %broadcast_multiply_fusion.10, f32[128]{0:T(128)S(1)} %broadcast_multiply_fusion.11, f32[1024]{0:T(1024)S(1)} %bitcast.806, ...), kind=kOutput, calls=%fused_computation.251 | convolution fusion | flops 1074790400 | bytes 18619392 | tf_op jit(solution)/shard_map/dot_general | solution.py:57
  481.7 8.1 %fusion.153 = f32[4096,1024]{1,0:T(8,128)} fusion(bf16[3,128,4096]{2,1,0:T(8,128)(2,1)S(1)} %pad_maximum_fusion.1, s32[]{:T(128)S(6)} %select_n.327, f32[128,1024]{1,0:T(8,128)S(1)} %copy-done.42), kind=kOutput, calls=%fused_computation.248 | convolution fusion | flops 1073872896 | bytes 18350084 | tf_op jit(solution)/shard_map/dot_general | solution.py:57
  489.8 10.9 %add_convert_fusion = bf16[4096,1024]{1,0:T(8,128)(2,1)} fusion(f32[4096,1024]{1,0:T(8,128)} %fusion.153, f32[4096,1024]{1,0:T(8,128)} %fusion.156, pred[]{:T(512)S(6)} %eq.3, pred[]{:T(512)S(6)} %select_n.331, bf16[3,128,4096]{2,1,0:T(8,128)(2,1)} %copy-done.1, s32[]{:T(128)S(6)} %select_n.320, f32[128,1024]{1,0:T(8,128)S(1)} %copy-done.40), kind=kOutput, calls=%fused_computation | convolution fusion | flops 1094844416 | bytes 43515912 | tf_op jit(solution)/shard_map/dot_general | solution.py:57
  507.3 58.7 %all-reduce.9 = (bf16[1024]{0:T(1024)(128)(2,1)S(1)}, bf16[1024]{0:T(1024)(128)(2,1)S(1)}, bf16[1024]{0:T(1024)(128)(2,1)S(1)}, bf16[1024]{0:T(1024)(128)(2,1)S(...) all-reduce(bf16[1024]{0:T(1024)(128)(2,1)S(1)} %add_convert_fusion., ...), channel_id=3, replica_groups=mesh['section'=2,'dp'=4,'shard'=16] {'shard'}, use_global_device_ids=true, to_apply=%region_38.39.clone | all-reduce | flops 12288 | bytes 49152
  566.1 74.5 %reduce-scatter.9.cloned.1.call-done = bf16[64,4096]{1,0:T(8,128)(2,1)} async-done(((bf16[1024,4096]{1,0:T(8,128)(2,1)}), bf16[64,4096]{1,0:T(8,128)(2,1)}) %reduce-scatter.9.cloned.1.call-update) | async-done | bytes 524304 | tf_op jit(solution)/shard_map/reduce_scatter | solution.py:359
  640.6 87.8 %reduce-scatter.11.cloned.1.call-done = bf16[256,1024]{1,0:T(8,128)(2,1)} async-done(((bf16[4096,1024]{1,0:T(8,128)(2,1)}), bf16[256,1024]{1,0:T(8,128)(2,1)}) %reduce-scatter.11.cloned.1.call-update) | async-done | bytes 524304 | tf_op jit(solution)/shard_map/reduce_scatter | solution.py:359
  729.0 8.5 %all-reduce.10 = (bf16[1,64]{1,0:T(2,128)(2,1)S(1)}, bf16[1,64]{1,0:T(2,128)(2,1)S(1)}, bf16[1,64]{1,0:T(2,128)(2,1)S(1)}, bf16[1,64]{1,0:T(2,128)(2,1)S(1)}, bf...) all-reduce(bf16[1,64]{1,0:T(2,128)(2,1)S(1)} %dynamic-slice_bitcast, ...), channel_id=1, replica_groups=mesh['section'=2,'dp'=4,'shard'=16] {'dp'}, use_global_device_ids=true, to_apply=%region_39.40 | all-reduce | flops 768 | bytes 3072 | tf_op jit(solution)/shard_map/psum | solution.py:362
  742.2 5.0 fusion.152
  748.1 34.3 %all-reduce.14.cloned.1.call-done = (bf16[1,64,3072]{2,1,0:T(8,128)(2,1)}, bf16[1,64,1024]{2,1,0:T(8,128)(2,1)}, bf16[1,64,4096]{2,1,0:T(8,128)(2,1)}, bf16[1,256,1024]{2,1,0:T(8,128)(2,1)}) async-done(((bf16[1,64,3072]{2,1,0:T(8,128)(2,1)}, bf16[1,64,1024]{2,1,0:T(8,128)(2,1)}, bf16[1,64,4096]{2,1,0:T(8,128)(2,1)}, bf16[1,256,1024]{2,1,0:T(8,128)(2,1)}), (bf16[1,64,3072]{2,1,0:T(8,128)(2,1)}, ...) | async-done | bytes 1572880 | tf_op jit(solution)/shard_map/psum | solution.py:362
  (478 shorter events, 140.5 us)
Async XLA Ops:
  7.2 82.6 %all-gather.6.cloned.1.call-start = ((), (), s32[]{:S(2)}) async-start(), calls=%async_computation.5 | async-start | bytes 10027008 | tf_op jit(solution)/shard_map/all_gather | solution.py:15
  10.2 28.5 %copy-start.93 = (s32[2,1]{0,1:T(1,128)S(1)}, s32[2,1]{0,1:T(1,128)}, u32[]{:S(2)}) copy-start(s32[2,1]{0,1:T(1,128)} %param.17) | copy-start | bytes 28
  10.2 31.1 %copy-start.56 = (bf16[2,1,128,1024]{3,2,1,0:T(8,128)(2,1)S(1)}, bf16[2,1,128,1024]{3,2,1,0:T(8,128)(2,1)}, u32[]{:S(2)}) copy-start(bf16[2,1,128,1024]{3,2,1,0:T(8,128)(2,1)} %param.16) | copy-start | bytes 1572868
  10.3 194.0 %all-gather.4.cloned.1.call-start = ((), (), s32[]{:S(2)}) async-start(), calls=%async_computation.4 | async-start | bytes 18104320 | tf_op jit(solution)/shard_map/all_gather | solution.py:15
  17.2 548.9 %reduce-scatter.7.cloned.1.call-start = ((), (), s32[]{:S(2)}) async-start(), calls=%async_computation.7 | async-start | bytes 2228224 | tf_op jit(solution)/shard_map/reduce_scatter | solution.py:359
  41.4 218.5 %copy-start.89 = (f32[1,1024]{1,0:T(1,128)}, f32[1,1024]{1,0:T(1,128)S(1)}, u32[]{:S(2)}) copy-start(f32[1,1024]{1,0:T(1,128)S(1)} %get-tuple-element.166) | copy-start | bytes 12292
  215.7 12.3 %slice-start.10 = ((s8[9437184]{0:T(1024)(128)(4,1)}), s8[4194304]{0:T(1024)(128)(4,1)S(1)}, s32[]{:S(2)}) async-start(s8[9437184]{0:T(1024)(128)(4,1)} %bitcast.815), calls=%async_computation.21 | async-start | bytes 8388608
  232.0 3.4 collective-permute-start
  241.7 15.0 %slice-start.13 = ((s8[9437184]{0:T(1024)(128)(4,1)}), s8[4194304]{0:T(1024)(128)(4,1)S(1)}, s32[]{:S(2)}) async-start(s8[9437184]{0:T(1024)(128)(4,1)} %bitcast.817), calls=%async_computation.24 | async-start | bytes 8388608
  260.8 3.4 collective-permute-start.1
  270.5 13.6 %slice-start.16 = ((s8[9437184]{0:T(1024)(128)(4,1)}), s8[4194304]{0:T(1024)(128)(4,1)S(1)}, s32[]{:S(2)}) async-start(s8[9437184]{0:T(1024)(128)(4,1)} %bitcast.819), calls=%async_computation.27 | async-start | bytes 8388608
  288.8 21.2 %copy-start.3 = (f32[3,128,1024]{2,1,0:T(8,128)}, f32[3,128,1024]{2,1,0:T(8,128)S(1)}, u32[]{:S(2)}) copy-start(f32[3,128,1024]{2,1,0:T(8,128)S(1)} %pad_maximum_fusion.4) | copy-start | bytes 4718596
  290.7 14.6 %slice-start = ((s8[17039360]{0:T(1024)(128)(4,1)}), s8[262144]{0:T(1024)(128)(4,1)S(1)}, s32[]{:S(2)}) async-start(s8[17039360]{0:T(1024)(128)(4,1)} %bitcast.760), calls=%async_computation.11 | async-start | bytes 524288
  291.4 13.9 %copy-start.2 = (f32[3,128,4096]{2,1,0:T(8,128)}, f32[3,128,4096]{2,1,0:T(8,128)S(1)}, u32[]{:S(2)}) copy-start(f32[3,128,4096]{2,1,0:T(8,128)S(1)} %pad_maximum_fusion) | copy-start | bytes 18874372
  291.4 13.9 %slice-start.1 = ((s8[17039360]{0:T(1024)(128)(4,1)}), s8[4194304]{0:T(1024)(128)(4,1)S(1)}, s32[]{:S(2)}) async-start(s8[17039360]{0:T(1024)(128)(4,1)} %bitcast.760), calls=%async_computation.12 | async-start | bytes 8388608
  291.5 13.9 %slice-start.2 = ((s8[17039360]{0:T(1024)(128)(4,1)}), s8[4194304]{0:T(1024)(128)(4,1)S(1)}, s32[]{:S(2)}) async-start(s8[17039360]{0:T(1024)(128)(4,1)} %bitcast.760), calls=%async_computation.13 | async-start | bytes 8388608
  291.5 13.9 %slice-start.3 = ((s8[17039360]{0:T(1024)(128)(4,1)}), s8[4194304]{0:T(1024)(128)(4,1)S(1)}, s32[]{:S(2)}) async-start(s8[17039360]{0:T(1024)(128)(4,1)} %bitcast.760), calls=%async_computation.14 | async-start | bytes 8388608
  291.5 13.9 %slice-start.4 = ((s8[17039360]{0:T(1024)(128)(4,1)}), s8[4194304]{0:T(1024)(128)(4,1)S(1)}, s32[]{:S(2)}) async-start(s8[17039360]{0:T(1024)(128)(4,1)} %bitcast.760), calls=%async_computation.15 | async-start | bytes 8388608
  327.4 13.7 %collective-permute-start.2 = (bf16[128,1024]{1,0:T(8,128)(2,1)}, bf16[128,1024]{1,0:T(8,128)(2,1)}, u32[]{:S(2)}, u32[]{:S(2)}) collective-permute-start(bf16[128,1024]{1,0:T(8,128)(2,1)} %fusion.144), channel_id=1, source_target_pairs={{64,0},{65,1},{66,2},{67,3},{68,4},{69,5},{70,6},{71,7},{72,8},{73... | collective-permute-start | bytes 786440 | tf_op jit(solution)/shard_map/ppermute | solution.py:35
  336.7 16.6 %slice-start.5 = ((s8[17039360]{0:T(1024)(128)(4,1)}), s8[4194304]{0:T(1024)(128)(4,1)S(1)}, s32[]{:S(2)}) async-start(s8[17039360]{0:T(1024)(128)(4,1)} %bitcast.762), calls=%async_computation.16 | async-start | bytes 8388608
  341.6 11.7 %copy-start.39 = (f32[128,1024]{1,0:T(8,128)}, f32[128,1024]{1,0:T(8,128)S(1)}, u32[]{:S(2)}) copy-start(f32[128,1024]{1,0:T(8,128)S(1)} %get-tuple-element.120) | copy-start | bytes 1572868
  341.6 11.7 %copy-start.4 = (f32[3,128,1024]{2,1,0:T(8,128)S(1)}, f32[3,128,1024]{2,1,0:T(8,128)}, u32[]{:S(2)}) copy-start(f32[3,128,1024]{2,1,0:T(8,128)} %copy-done.3) | copy-start | bytes 4718596
  341.7 11.7 %slice-start.6 = ((s8[17039360]{0:T(1024)(128)(4,1)}), s8[4194304]{0:T(1024)(128)(4,1)S(1)}, s32[]{:S(2)}) async-start(s8[17039360]{0:T(1024)(128)(4,1)} %bitcast.762), calls=%async_computation.17 | async-start | bytes 8388608
  341.7 11.7 %slice-start.7 = ((s8[17039360]{0:T(1024)(128)(4,1)}), s8[4194304]{0:T(1024)(128)(4,1)S(1)}, s32[]{:S(2)}) async-start(s8[17039360]{0:T(1024)(128)(4,1)} %bitcast.762), calls=%async_computation.18 | async-start | bytes 8388608
  341.7 11.7 %slice-start.8 = ((s8[17039360]{0:T(1024)(128)(4,1)}), s8[4194304]{0:T(1024)(128)(4,1)S(1)}, s32[]{:S(2)}) async-start(s8[17039360]{0:T(1024)(128)(4,1)} %bitcast.762), calls=%async_computation.19 | async-start | bytes 8388608
  341.7 11.7 %slice-start.9 = ((s8[17039360]{0:T(1024)(128)(4,1)}), s8[262144]{0:T(1024)(128)(4,1)S(1)}, s32[]{:S(2)}) async-start(s8[17039360]{0:T(1024)(128)(4,1)} %bitcast.762), calls=%async_computation.20 | async-start | bytes 524288
  371.6 2.8 collective-permute-start.3
  395.7 170.5 %reduce-scatter.5.cloned.1.call-start = ((), (), s32[]{:S(2)}) async-start(), calls=%async_computation.6 | async-start | bytes 6684672 | tf_op jit(solution)/shard_map/reduce_scatter | solution.py:359
  442.2 198.4 %reduce-scatter.9.cloned.1.call-start = ((), (), s32[]{:S(2)}) async-start(), calls=%async_computation.8 | async-start | bytes 8912896 | tf_op jit(solution)/shard_map/reduce_scatter | solution.py:359
  470.4 258.0 %reduce-scatter.11.cloned.1.call-start = ((), (), s32[]{:S(2)}) async-start(), calls=%async_computation.9 | async-start | bytes 8912896 | tf_op jit(solution)/shard_map/reduce_scatter | solution.py:359
  500.8 281.6 %all-reduce.14.cloned.1.call-start = ((), (), s32[]{:S(2)}) async-start(), calls=%async_computation.10 | async-start | bytes 3145728 | tf_op jit(solution)/shard_map/psum | solution.py:362
  506.7 235.6 %copy-start.45 = (f32[128,1024]{1,0:T(8,128)S(1)}, f32[128,1024]{1,0:T(8,128)}, u32[]{:S(2)}) copy-start(f32[128,1024]{1,0:T(8,128)} %copy-done.43) | copy-start | bytes 1572868
  (105 other events, 457.3 us)
Sparse Core Ops, SparseCore 0:
  10.7 79.0 all-gather.5
  91.9 112.3 all-gather.3
  395.8 72.2 reduce-scatter.6
  471.7 81.3 reduce-scatter.4
  556.7 83.8 reduce-scatter.8
  644.2 84.1 reduce-scatter.10
  731.2 51.2 all-reduce.13
where the time goes:
time: 807 us; the launch traced here: 797 us
  waiting for transfers between devices  360 us (45%)
  matrix products  234 us (29%)
  blocking collectives  88.6 us (11%)
  local copies, waits for them, and re-layouts  44.5 us (6%)
  other arithmetic  42.3 us (5%)
  between operations  18.2 us (2%)
  starting transfers between devices  8.38 us (1%)
    reduce_scatter x4, waiting for transfers between devices, per_device(): lax.psum_scatter(for_sending(full_totals), 'shard', scatter_dimension=0,...  162 us
    all_gather x2, waiting for transfers between devices, in_one_piece(): lax.all_gather(both, axis, axis=dim, tiled=True)  161 us
    dot_general x12, matrix products, transpose_dot(): lax.dot_general(left_rows, right_rows, (((0,), (0,)), ((), ())), preferre...  87.3 us
    dot_general x12, matrix products, dot_transposed(): lax.dot_general(left_rows, right_rows, (((1,), (1,)), ((), ())), preferre...  73.7 us
    unnamed x1, blocking collectives  58.7 us
    psum x1, waiting for transfers between devices, per_device(): lax.psum(for_sending(share_totals), 'dp')  34.3 us
    dot_general x3, matrix products, layer_forward(): jnp.dot(hidden, w_up, preferred_element_type=jnp.float32)  32.4 us
    all_gather x1, blocking collectives, in_one_piece_2(): lax.all_gather(both, axis, axis=dim, tiled=True)  21.3 us
  transfers between devices with their start and end apart: 11, of which 8 were waited for; matrix products, arithmetic and copies ran while one was open for 18% of the time, Pallas kernels for 0%

commit v1 on v0

v1 whole, which is shorter than its diff:
```python
import jax
import jax.numpy as jnp
from jax import lax
from jax.sharding import PartitionSpec as P


HEAD_DIM = 64
EPSILON = 1e-06
LANES = 128
BF = jnp.bfloat16
F32 = jnp.float32


def swap(value):
    return lax.ppermute(value, "section", [(0, 1), (1, 0)])


def pair_sum(part):
    low = part.astype(BF)
    other = swap(low)
    return low.astype(F32) + other.astype(F32)


def dot(left, right):
    return jnp.dot(left, right, preferred_element_type=F32)


def transpose_dot(left, right):
    return lax.dot_general(left, right, (((0,), (0,)), ((), ())), preferred_element_type=F32)


def dot_transposed(left, right):
    return lax.dot_general(left, right, (((1,), (1,)), ((), ())), preferred_element_type=F32)


def norm_rows(values):
    centered = values - jnp.mean(values, axis=-1, keepdims=True)
    inverse = lax.rsqrt(jnp.mean(centered * centered, axis=-1, keepdims=True) + EPSILON)
    return (centered * inverse, inverse)


def norm_back(grad_norm, normed, inverse):
    return inverse * (
        grad_norm
        - jnp.mean(grad_norm, axis=-1, keepdims=True)
        - normed * jnp.mean(grad_norm * normed, axis=-1, keepdims=True)
    )


def heads_of(packed, number, count):
    width = packed.shape[1] // 3
    piece = packed[:, number * width : (number + 1) * width]
    return piece.reshape(count, -1, width // HEAD_DIM, HEAD_DIM).transpose(0, 2, 1, 3)


def join_heads(parts):
    count, heads, rows, size = parts.shape
    return parts.transpose(0, 2, 1, 3).reshape(count * rows, heads * size)


def masked_scores(queries, keys, seq_lengths):
    scores = jnp.einsum("nhqd,nhkd->nhqk", queries, keys, preferred_element_type=F32)
    scores = scores * HEAD_DIM ** (-0.5)
    positions = lax.broadcasted_iota(jnp.int32, scores.shape, 3)
    return jnp.where(positions < seq_lengths[:, None, None, None], scores, -1000000000.0)


def layer_forward(inputs, weights, seq_lengths):
    count = seq_lengths.shape[0]
    packed = (dot(inputs, weights["qkv"]) + weights["bias_qkv"]).astype(BF)
    queries, keys, values = (heads_of(packed, n, count) for n in range(3))
    scores = masked_scores(queries, keys, seq_lengths)
    row_max = jnp.max(scores, axis=-1, keepdims=True)
    exponent = jnp.exp(scores - row_max)
    soft_weights = exponent / jnp.sum(exponent, axis=-1, keepdims=True)
    attended = jnp.einsum(
        "nhqk,nhkd->nhqd", soft_weights.astype(BF), values, preferred_element_type=F32
    )
    attended = join_heads(attended.astype(BF))
    branch = pair_sum(dot(attended, weights["out"])) + weights["bias_out"]
    normed_attn, inverse_attn = norm_rows(inputs.astype(F32) + branch)
    hidden = (normed_attn * weights["gain_attn"] + weights["shift_attn"]).astype(BF)
    upward = [dot(hidden, w) + b for w, b in zip(weights["up"], weights["bias_up"])]
    activated = [jax.nn.gelu(u, approximate=False).astype(BF) for u in upward]
    mixed = sum(dot(g, w) for g, w in zip(activated, weights["down"]))
    mixed = pair_sum(mixed) + weights["bias_down"]
    normed_mlp, inverse_mlp = norm_rows(hidden.astype(F32) + mixed)
    result = (normed_mlp * weights["gain_mlp"] + weights["shift_mlp"]).astype(BF)
    kept = dict(
        inputs=inputs,
        qkv=(queries, keys, values),
        soft_weights=soft_weights,
        attended=attended,
        normed_attn=normed_attn,
        inverse_attn=inverse_attn,
        hidden=hidden,
        upward=upward,
        activated=activated,
        normed_mlp=normed_mlp,
        inverse_mlp=inverse_mlp,
    )
    return (result, kept)


def layer_backward(grad_result, kept, weights):
    scaling = HEAD_DIM ** (-0.5)
    grad_result = grad_result.astype(F32)
    normed_mlp = kept["normed_mlp"]
    grad_gain_mlp = jnp.sum(grad_result * normed_mlp, axis=0)
    grad_shift_mlp = jnp.sum(grad_result, axis=0)
    grad_resid_mlp = norm_back(grad_result * weights["gain_mlp"], normed_mlp, kept["inverse_mlp"])
    grad_mixed = grad_resid_mlp.astype(BF)
    grad_bias_down = jnp.sum(grad_mixed.astype(F32), axis=0)
    grad_down = [transpose_dot(g, grad_mixed).astype(BF) for g in kept["activated"]]
    grad_upward = []
    for up, w in zip(kept["upward"], weights["down"]):
        pull = jax.vjp(lambda point: jax.nn.gelu(point, approximate=False), up)[1]
        grad_upward.append(pull(dot_transposed(grad_mixed, w))[0].astype(BF))
    grad_bias_up = [jnp.sum(u.astype(F32), axis=0) for u in grad_upward]
    grad_up = [transpose_dot(kept["hidden"], u).astype(BF) for u in grad_upward]
    passed = sum(dot_transposed(u, w) for u, w in zip(grad_upward, weights["up"]))
    grad_hidden = grad_resid_mlp + pair_sum(passed)
    normed_attn = kept["normed_attn"]
    grad_gain_attn = jnp.sum(grad_hidden * normed_attn, axis=0)
    grad_shift_attn = jnp.sum(grad_hidden, axis=0)
    grad_resid_attn = norm_back(
        grad_hidden * weights["gain_attn"], normed_attn, kept["inverse_attn"]
    )
    grad_branch = grad_resid_attn.astype(BF)
    grad_bias_out = jnp.sum(grad_branch.astype(F32), axis=0)
    grad_out = transpose_dot(kept["attended"], grad_branch).astype(BF)
    queries, keys, values = kept["qkv"]
    count = queries.shape[0]
    grad_attended = dot_transposed(grad_branch, weights["out"]).astype(BF)
    grad_attended = grad_attended.reshape(count, -1, queries.shape[1], HEAD_DIM)
    grad_attended = grad_attended.transpose(0, 2, 1, 3)
    soft_weights = kept["soft_weights"]
    grad_values = jnp.einsum(
        "nhqk,nhqd->nhkd", soft_weights.astype(BF), grad_attended, preferred_element_type=F32
    )
    grad_soft = jnp.einsum(
        "nhqd,nhkd->nhqk", grad_attended, values, preferred_element_type=F32
    )
    grad_scores = soft_weights * (
        grad_soft - jnp.sum(grad_soft * soft_weights, axis=-1, keepdims=True)
    )
    grad_scores = grad_scores.astype(BF)
    grad_queries = scaling * jnp.einsum(
        "nhqk,nhkd->nhqd", grad_scores, keys, preferred_element_type=F32
    )
    grad_keys = scaling * jnp.einsum(
        "nhqk,nhqd->nhkd", grad_scores, queries, preferred_element_type=F32
    )
    grad_packed = jnp.concatenate(
        [join_heads(g.astype(BF)) for g in (grad_queries, grad_keys, grad_values)], axis=1
    )
    columns = jnp.sum(grad_packed.astype(F32), axis=0)
    width = columns.shape[0] // 3
    grad_qkv = transpose_dot(kept["inputs"], grad_packed).astype(BF)
    grad_inputs = grad_resid_attn + pair_sum(dot_transposed(grad_packed, weights["qkv"]))
    grads = dict(
        qkv=grad_qkv,
        out=grad_out,
        up=grad_up,
        down=grad_down,
        bias_q=columns[:width],
        bias_v=columns[2 * width :],
        bias_up=grad_bias_up,
        whole=(
            grad_bias_out,
            grad_gain_attn,
            grad_shift_attn,
            grad_bias_down,
            grad_gain_mlp,
            grad_shift_mlp,
        ),
    )
    return (grad_inputs.astype(BF), grads)


def per_device(
    tokens,
    lengths,
    cotangent,
    w_qkv,
    bias_q,
    bias_v,
    w_out,
    bias_out,
    gain_attn,
    shift_attn,
    w_up,
    bias_up,
    w_down,
    bias_down,
    gain_mlp,
    shift_mlp,
):
    first = lax.axis_index("section") == 0
    shards = lax.axis_size("shard")
    rows = w_qkv.shape[1]
    model = w_qkv.shape[2] // 3
    ff = w_up.shape[2]
    half = model // 2
    unit = ff // shards // 2
    vector_count = 8 * rows + 2 * unit

    def choose(low, high):
        return jnp.where(first, low, high)

    def mine_of(low, high):
        return (choose(low, high), choose(high, low))

    def parts_of(part):
        qkv = w_qkv[0].reshape(rows, 3, 2, half)[:, :, part].reshape(rows, 3 * half)
        out = w_out[0][:, part * half : (part + 1) * half]
        up = w_up[0].reshape(rows, shards, 2, unit)[:, :, part].reshape(rows, shards * unit)
        down = w_down[0][part * unit : (part + 1) * unit].reshape(rows, -1)
        return jnp.concatenate([qkv, out, up, down], axis=1)

    vectors = jnp.concatenate(
        [
            v[0]
            for v in (
                bias_q,
                bias_v,
                bias_out,
                gain_attn,
                shift_attn,
                bias_down,
                gain_mlp,
                shift_mlp,
                bias_up,
            )
        ]
    )
    vectors = jnp.pad(vectors, (0, rows * LANES - vector_count)).reshape(rows, LANES)
    kept_part, sent_part = mine_of(parts_of(0), parts_of(1))
    own = jnp.concatenate([vectors, kept_part], axis=1)
    got = swap(jnp.concatenate([vectors, sent_part], axis=1))
    layers = mine_of(own, got)
    edges = (LANES + 3 * half, LANES + 4 * half, LANES + 4 * half + shards * unit)

    def gather(block):
        return lax.all_gather(block, "shard", axis=0, tiled=True)

    def gather_layer(block):
        attn = gather(block[:, : edges[1]])
        up = gather(block[:, edges[1] : edges[2]])
        down = gather(block[:, edges[2] :].reshape(unit, model))
        flat = attn[:, :LANES].reshape(shards, rows * LANES)[:, :vector_count].astype(F32)
        whole = [flat[:, n * rows : (n + 1) * rows].reshape(-1) for n in range(8)]
        bias_up_part = flat[:, 8 * rows :].reshape(shards, 2, unit)
        bias_up_part = choose(bias_up_part[:, 0], bias_up_part[:, 1]).reshape(-1)
        bias_q_part = choose(whole[0][:half], whole[0][half:])
        bias_v_part = choose(whole[1][:half], whole[1][half:])
        out = attn[:, edges[0] : edges[1]]
        held, handed = mine_of(out[:half], out[half:])
        arrived = swap(handed)
        return dict(
            qkv=attn[:, LANES : edges[0]],
            out=jnp.concatenate(mine_of(held, arrived), axis=1),
            up=[up],
            down=[down],
            bias_qkv=jnp.concatenate([bias_q_part, jnp.zeros_like(bias_q_part), bias_v_part]),
            bias_out=whole[2],
            gain_attn=whole[3],
            shift_attn=whole[4],
            bias_down=whole[5],
            gain_mlp=whole[6],
            shift_mlp=whole[7],
            bias_up=[bias_up_part],
        )

    weights = [gather_layer(block) for block in layers]

    def scatter(block):
        return lax.psum_scatter(block, "shard", scatter_dimension=0, tiled=True)

    def scatter_layer(grads):
        down = scatter(grads["down"][0])
        up = scatter(grads["up"][0])
        held, handed = mine_of(grads["out"][:, :half], grads["out"][:, half:])
        out = jnp.concatenate(mine_of(held, swap(handed)), axis=0)

        def widened(part):
            return jnp.concatenate([choose(part, 0.0), choose(0.0, part)])

        whole = [widened(grads["bias_q"]), widened(grads["bias_v"])]
        whole += [0.5 * v for v in grads["whole"]]
        part = grads["bias_up"][0].reshape(shards, unit)
        spread = jnp.concatenate([choose(part, 0.0), choose(0.0, part)], axis=1)
        flat = jnp.concatenate([v.reshape(shards, rows) for v in whole] + [spread], axis=1)
        flat = jnp.pad(flat.astype(BF), ((0, 0), (0, rows * LANES - vector_count)))
        flat = flat.reshape(shards * rows, LANES)
        attn = scatter(jnp.concatenate([flat, grads["qkv"], out], axis=1))
        return jnp.concatenate([attn, up, down.reshape(rows, -1)], axis=1)

    count = tokens.shape[0]
    seq_lengths = lengths[:, 0]
    middle, kept_first = layer_forward(tokens.reshape(-1, model), weights[0], seq_lengths)
    last, kept_second = layer_forward(middle, weights[1], seq_lengths)
    grad_middle, grads_second = layer_backward(cotangent.reshape(-1, model), kept_second, weights[1])
    summed_second = scatter_layer(grads_second)
    grad_first, grads_first = layer_backward(grad_middle, kept_first, weights[0])
    summed_first = scatter_layer(grads_first)
    summed_first, summed_second = lax.psum((summed_first, summed_second), "dp")

    held, handed = mine_of(summed_first, summed_second)
    low, high = mine_of(held, swap(handed))
    low, high = (low.astype(F32), high.astype(F32))

    def cut(block):
        flat = block[:, :LANES].reshape(-1)[:vector_count]
        qkv = block[:, LANES : edges[0]].reshape(rows, 3, half)
        up = block[:, edges[1] : edges[2]].reshape(rows, shards, unit)
        return (flat, qkv, block[:, edges[0] : edges[1]], up, block[:, edges[2] :].reshape(unit, -1))

    (flat_a, qkv_a, out_a, up_a, down_a), (flat_b, qkv_b, out_b, up_b, down_b) = (cut(low), cut(high))
    flat = flat_a + flat_b
    whole = [flat[n * rows : (n + 1) * rows] for n in range(8)]
    grads = (
        jnp.stack([qkv_a, qkv_b], axis=2).reshape(rows, -1),
        whole[0],
        whole[1],
        jnp.concatenate([out_a, out_b], axis=1),
        whole[2],
        whole[3],
        whole[4],
        jnp.stack([up_a, up_b], axis=2).reshape(rows, -1),
        flat[8 * rows :],
        jnp.concatenate([down_a, down_b], axis=0),
        whole[5],
        whole[6],
        whole[7],
    )
    shape = (1, count, 1, -1, model)
    activations = choose(middle, last).reshape(shape)
    input_grads = choose(grad_first, grad_middle).reshape(shape)
    return (activations, input_grads) + tuple(member[None] for member in grads)


def solution(mesh):
    rows = P(None, ("dp", "shard"), None, None)
    matrix = P("section", "shard", None)
    vector = P("section", "shard")
    weight_specs = (matrix, vector, vector, matrix, vector, vector, vector)
    weight_specs += (matrix, vector, matrix, vector, vector, vector)
    in_specs = (rows, P(None, ("dp", "shard")), rows) + weight_specs
    result = P("section", None, ("dp", "shard"), None, None)
    return jax.shard_map(
        per_device,
        mesh=mesh,
        in_specs=in_specs,
        out_specs=(result, result) + weight_specs,
        check_vma=False,
    )
```

time: 807 us -> 938 us (1.16)
  waiting for transfers between devices: 360 us -> 673 us
  matrix products: 234 us -> 92.8 us
  blocking collectives: 88.6 us -> 0 us
  local copies, waits for them, and re-layouts: 44.5 us -> 77.9 us
  other arithmetic: 42.3 us -> 58.5 us
    reduce_scatter x4 -> x6, waiting for transfers between devices: 162 us -> 360 us  [scatter(): return lax.psum_scatter(block, 'shard', scatter_dimension=0, tiled=True)]
    dot_general x57 -> x34, matrix products: 234 us -> 90.6 us  [the longest x8 34.2 us: dot(): return jnp.dot(left, right, preferred_element_type=F32)]
    all_gather x2 -> x6, waiting for transfers between devices: 161 us -> 257 us  [gather(): return lax.all_gather(block, 'shard', axis=0, tiled=True)]
    unnamed x1 -> x0, blocking collectives: 58.7 us -> none
    all_gather x1 -> x0, blocking collectives: 21.3 us -> none  [in_one_piece_2(): lax.all_gather(both, axis, axis=dim, tiled=True)]
    concatenate x1 -> x11, other arithmetic: 2.1 us -> 20.8 us  [the longest x2 15.7 us: scatter_layer(): attn = scatter(jnp.concatenate([flat, grads['qkv'], out], axis=1))]
    select_n x3 -> x18, other arithmetic: 0.8 us -> 15.4 us  [choose(): return jnp.where(first, low, high)]
    another operation x20 -> x16, other arithmetic: 14.1 us -> 0.36 us  [the longest x1 0.23 us: per_device(): jnp.stack([qkv_a, qkv_b], axis=2).reshape(rows, -1)]
  transfers between devices with their start and end apart: 11 -> 27, of which waited for: 8 -> 18; matrix products, arithmetic and copies ran while one was open for 18% -> 19% of each run, Pallas kernels for 0% -> 0%
where the time goes in v1:
time: 938 us; the launch traced here: 929 us
  waiting for transfers between devices  673 us (72%)
  matrix products  92.8 us (10%)
  local copies, waits for them, and re-layouts  77.9 us (8%)
  other arithmetic  58.5 us (6%)
  between operations  15.5 us (2%)
  starting transfers between devices  11.2 us (1%)
    reduce_scatter x6, waiting for transfers between devices, scatter(): return lax.psum_scatter(block, 'shard', scatter_dimension=0, tiled=True)  360 us
    all_gather x6, waiting for transfers between devices, gather(): return lax.all_gather(block, 'shard', axis=0, tiled=True)  257 us
    psum x1, waiting for transfers between devices, per_device(): summed_first, summed_second = lax.psum((summed_first, summed_second), 'dp')  46.6 us
    dot_general x8, matrix products, dot(): return jnp.dot(left, right, preferred_element_type=F32)  34.2 us
    dot_general x8, matrix products, dot_transposed(): lax.dot_general(left, right, (((1,), (1,)), ((), ())), preferred_element_...  27.7 us
    dot_general x8, matrix products, transpose_dot(): lax.dot_general(left, right, (((0,), (0,)), ((), ())), preferred_element_...  21.7 us
    unnamed x127, local copies, waits for them, and re-layouts  21.2 us
  transfers between devices with their start and end apart: 27, of which 18 were waited for; matrix products, arithmetic and copies ran while one was open for 19% of the time, Pallas kernels for 0%

profile of v1, /device:TPU:1, one launch (start us, length us, event | category | flops | bytes accessed | tf_op | source)
XLA Modules:
  0.0 928.7 jit_solution(498698377726235108)
XLA Ops:
  8.0 5.4 concatenate.85
  30.3 51.0 %all-gather.13.cloned.1.call-done = bf16[1024,2176]{1,0:T(8,128)(2,1)} async-done(((bf16[64,2176]{1,0:T(8,128)(2,1)}), bf16[1024,2176]{1,0:T(8,128)(2,1)}) %all-gather.13.cloned.1.call-update) | async-done | bytes 4456464 | tf_op jit(solution)/shard_map/all_gather | solution.py:245
  82.3 54.1 %all-gather.7.cloned.1.call-done = bf16[1024,2176]{1,0:T(8,128)(2,1)} async-done(((bf16[64,2176]{1,0:T(8,128)(2,1)}), bf16[1024,2176]{1,0:T(8,128)(2,1)}) %all-gather.7.cloned.1.call-update) | async-done | bytes 4456464 | tf_op jit(solution)/shard_map/all_gather | solution.py:245
  138.0 3.0 fusion.15
  154.3 36.2 %all-gather.9.cloned.1.call-done = bf16[1024,2048]{1,0:T(8,128)(2,1)} async-done(((bf16[64,2048]{1,0:T(8,128)(2,1)}), bf16[1024,2048]{1,0:T(8,128)(2,1)}) %all-gather.9.cloned.1.call-update) | async-done | bytes 4194320 | tf_op jit(solution)/shard_map/all_gather | solution.py:245
  190.5 8.9 multiply_convert_fusion.1
  199.4 44.9 %all-gather.11.cloned.1.call-done = bf16[2048,1024]{1,0:T(8,128)(2,1)} async-done(((bf16[128,1024]{1,0:T(8,128)(2,1)}), bf16[2048,1024]{1,0:T(8,128)(2,1)}) %all-gather.11.cloned.1.call-update) | async-done | bytes 4194320 | tf_op jit(solution)/shard_map/all_gather | solution.py:245
  244.3 4.2 convolution_convert_fusion.13
  253.9 3.0 fusion.12
  271.4 26.8 %all-gather.15.cloned.1.call-done = bf16[1024,2048]{1,0:T(8,128)(2,1)} async-done(((bf16[64,2048]{1,0:T(8,128)(2,1)}), bf16[1024,2048]{1,0:T(8,128)(2,1)}) %all-gather.15.cloned.1.call-update) | async-done | bytes 4194320 | tf_op jit(solution)/shard_map/all_gather | solution.py:245
  298.2 9.5 %multiply_convert_fusion = (bf16[256,2048]{1,0:T(8,128)(2,1)}, f32[256,2048]{1,0:T(8,128)}, f32[256,2048]{1,0:T(8,128)}) fusion(f32[2048]{0:T(1024)S(1)} %bitcast.300, bf16[1024,2048]{1,0:T(8,128)(2,1)} %all-gather.15.cloned.1.call-done, f32[256,1024]{1,0:T(8,128)S(1)} %get-tuple-element.128, f32[1024]{0:T(1024)S(1)} %add.251, f32[1024]{0:T(1024)S(1)} %mul.393, ...), kind=kOutput, calls=%fused_computation.32 | convolution fusion | flops 1109655552 | bytes 10504192 | tf_op jit(solution)/shard_map/dot_general | solution.py:25
  307.7 44.3 %all-gather.17.cloned.1.call-done = bf16[2048,1024]{1,0:T(8,128)(2,1)} async-done(((bf16[128,1024]{1,0:T(8,128)(2,1)}), bf16[2048,1024]{1,0:T(8,128)(2,1)}) %all-gather.17.cloned.1.call-update) | async-done | bytes 4194320 | tf_op jit(solution)/shard_map/all_gather | solution.py:245
  352.0 4.6 convolution_convert_fusion.12
  363.1 3.3 convolution_convert_fusion.2
  366.5 5.9 convert_reduce_fusion
  387.4 3.2 fusion.42
  396.0 3.4 convolution_convert_fusion.4
  399.4 4.7 convolution_convert_fusion.3
  411.1 2.8 convolution_convert_fusion
  417.6 3.7 pad_maximum_fusion
  422.6 5.4 convert_reduce_fusion.1
  428.9 3.4 convolution_convert_fusion.5
  432.4 4.6 convolution_convert_fusion.10
  463.0 11.9 %maximum_maximum_fusion = bf16[1024,2176]{0,1:T(8,128)(2,1)} fusion(bf16[512,512]{0,1:T(8,128)(2,1)S(1)} %get-tuple-element.148, bf16[512,512]{0,1:T(8,128)(2,1)S(1)} %get-tuple-element.147, bf16[1024,1536]{0,1:T(8,128)(2,1)S(1)} %fusion.2, bf16[1024,128]{0,1:T(8,128)(2,1)S(1)} %copy.271), kind=kLoop, calls=%fused_computation.2 | loop fusion | flops 17825792 | bytes 8912896 | tf_op jit(solution)/shard_map/concatenate | solution.py:296
  475.0 6.6 copy.301
  482.7 40.1 %reduce-scatter.15.cloned.1.call-done = bf16[128,1024]{1,0:T(8,128)(2,1)} async-done(((bf16[2048,1024]{1,0:T(8,128)(2,1)}), bf16[128,1024]{1,0:T(8,128)(2,1)}) %reduce-scatter.15.cloned.1.call-update) | async-done | bytes 262160 | tf_op jit(solution)/shard_map/reduce_scatter | solution.py:278
  523.9 79.3 %reduce-scatter.25.cloned.1.call-done = bf16[64,2048]{1,0:T(8,128)(2,1)} async-done(((bf16[1024,2048]{1,0:T(8,128)(2,1)}), bf16[64,2048]{1,0:T(8,128)(2,1)}) %reduce-scatter.25.cloned.1.call-update) | async-done | bytes 262160 | tf_op jit(solution)/shard_map/reduce_scatter | solution.py:278
  603.2 81.1 %reduce-scatter.23.cloned.1.call-done = bf16[64,2176]{1,0:T(8,128)(2,1)} async-done(((bf16[1024,2176]{1,0:T(8,128)(2,1)}), bf16[64,2176]{1,0:T(8,128)(2,1)}) %reduce-scatter.23.cloned.1.call-update) | async-done | bytes 278544 | tf_op jit(solution)/shard_map/reduce_scatter | solution.py:278
  686.3 78.8 %reduce-scatter.21.cloned.1.call-done = bf16[64,2048]{1,0:T(8,128)(2,1)} async-done(((bf16[1024,2048]{1,0:T(8,128)(2,1)}), bf16[64,2048]{1,0:T(8,128)(2,1)}) %reduce-scatter.21.cloned.1.call-update) | async-done | bytes 262160 | tf_op jit(solution)/shard_map/reduce_scatter | solution.py:278
  765.1 80.8 %reduce-scatter.19.cloned.1.call-done = bf16[64,2176]{1,0:T(8,128)(2,1)} async-done(((bf16[1024,2176]{1,0:T(8,128)(2,1)}), bf16[64,2176]{1,0:T(8,128)(2,1)}) %reduce-scatter.19.cloned.1.call-update) | async-done | bytes 278544 | tf_op jit(solution)/shard_map/reduce_scatter | solution.py:278
  847.9 3.7 fusion.39
  853.8 46.6 %all-reduce.6.cloned.1.call-done = (bf16[64,6272]{1,0:T(8,128)(2,1)}, bf16[64,6272]{1,0:T(8,128)(2,1)}) async-done(((bf16[64,6272]{1,0:T(8,128)(2,1)}, bf16[64,6272]{1,0:T(8,128)(2,1)}), (bf16[64,6272]{1,0:T(8,128)(2,1)}, bf16[64,6272]{1,0:T(8,128)(2,1)})) %all-reduce.6.cloned.1.call-update) | async-done | bytes 1605648 | tf_op jit(solution)/shard_map/psum | solution.py:307
  (403 shorter events, 147.9 us)
Async XLA Ops:
  7.2 10.5 %copy-start.39 = (bf16[1,64,4096]{2,1,0:T(8,128)(2,1)S(1)}, bf16[1,64,4096]{2,1,0:T(8,128)(2,1)}, u32[]{:S(2)}) copy-start(bf16[1,64,4096]{2,1,0:T(8,128)(2,1)} %param.26) | copy-start | bytes 1572868
  7.2 74.0 %all-gather.13.cloned.1.call-start = ((), (), s32[]{:S(2)}) async-start(), calls=%async_computation.9 | async-start | bytes 4734976 | tf_op jit(solution)/shard_map/all_gather | solution.py:245
  21.5 3.4 collective-permute-start
  26.0 110.5 %all-gather.7.cloned.1.call-start = ((), (), s32[]{:S(2)}) async-start(), calls=%async_computation.6 | async-start | bytes 4734976 | tf_op jit(solution)/shard_map/all_gather | solution.py:245
  26.8 163.7 %all-gather.9.cloned.1.call-start = ((), (), s32[]{:S(2)}) async-start(), calls=%async_computation.7 | async-start | bytes 4456448 | tf_op jit(solution)/shard_map/all_gather | solution.py:245
  27.6 216.7 %all-gather.11.cloned.1.call-start = ((), (), s32[]{:S(2)}) async-start(), calls=%async_computation.8 | async-start | bytes 4456448 | tf_op jit(solution)/shard_map/all_gather | solution.py:245
  28.5 109.5 %copy-start.23 = (bf16[2,1,128,1024]{3,2,1,0:T(8,128)(2,1)S(1)}, bf16[2,1,128,1024]{3,2,1,0:T(8,128)(2,1)}, u32[]{:S(2)}) copy-start(bf16[2,1,128,1024]{3,2,1,0:T(8,128)(2,1)} %param.16) | copy-start | bytes 1572868
  28.5 269.7 %all-gather.15.cloned.1.call-start = ((), (), s32[]{:S(2)}) async-start(), calls=%async_computation.10 | async-start | bytes 4456448 | tf_op jit(solution)/shard_map/all_gather | solution.py:245
  29.3 322.7 %all-gather.17.cloned.1.call-start = ((), (), s32[]{:S(2)}) async-start(), calls=%async_computation.11 | async-start | bytes 4456448 | tf_op jit(solution)/shard_map/all_gather | solution.py:245
  30.2 451.5 %reduce-scatter.17.cloned.1.call-start = ((), (), s32[]{:S(2)}) async-start(), calls=%async_computation.13 | async-start | bytes 4456448 | tf_op jit(solution)/shard_map/reduce_scatter | solution.py:278
  144.0 4.0 collective-permute-start.1
  150.5 2.2 collective-permute-start.2
  152.2 97.7 %collective-permute-start.4 = (bf16[512,512]{0,1:T(8,128)(2,1)}, bf16[512,512]{0,1:T(8,128)(2,1)}, u32[]{:S(2)}, u32[]{:S(2)}) collective-permute-start(bf16[512,512]{0,1:T(8,128)(2,1)} %broadcast_select_fusion.16), channel_id=1, source_target_pairs={{0,64},{64,0},{1,65},{65,1},{2,66},{66,2},{3,67},{67,3},{4,68},{68... | collective-permute-start | bytes 1572872 | tf_op jit(solution)/shard_map/ppermute | solution.py:15
  199.4 49.2 %copy-start.20 = (bf16[256,2048]{1,0:T(8,128)(2,1)}, bf16[256,2048]{1,0:T(8,128)(2,1)S(1)}, u32[]{:S(2)}) copy-start(bf16[256,2048]{1,0:T(8,128)(2,1)S(1)} %get-tuple-element.131) | copy-start | bytes 3145732
  248.6 3.4 collective-permute-start.3
  267.3 2.1 collective-permute-start.5
  356.6 2.7 collective-permute-start.6
  366.4 156.4 %reduce-scatter.15.cloned.1.call-start = ((), (), s32[]{:S(2)}) async-start(), calls=%async_computation.12 | async-start | bytes 4456448 | tf_op jit(solution)/shard_map/reduce_scatter | solution.py:278
  373.7 2.0 collective-permute-start.7
  390.6 2.5 collective-permute-start.8
  399.4 203.9 %reduce-scatter.25.cloned.1.call-start = ((), (), s32[]{:S(2)}) async-start(), calls=%async_computation.17 | async-start | bytes 4456448 | tf_op jit(solution)/shard_map/reduce_scatter | solution.py:278
  404.1 280.2 %reduce-scatter.23.cloned.1.call-start = ((), (), s32[]{:S(2)}) async-start(), calls=%async_computation.16 | async-start | bytes 4734976 | tf_op jit(solution)/shard_map/reduce_scatter | solution.py:278
  409.8 4.1 collective-permute-start.12
  421.4 343.7 %reduce-scatter.21.cloned.1.call-start = ((), (), s32[]{:S(2)}) async-start(), calls=%async_computation.15 | async-start | bytes 4456448 | tf_op jit(solution)/shard_map/reduce_scatter | solution.py:278
  432.3 413.5 %reduce-scatter.19.cloned.1.call-start = ((), (), s32[]{:S(2)}) async-start(), calls=%async_computation.14 | async-start | bytes 4734976 | tf_op jit(solution)/shard_map/reduce_scatter | solution.py:278
  437.0 2.4 collective-permute-start.9
  457.2 4.6 collective-permute-start.11
  481.6 418.8 %all-reduce.6.cloned.1.call-start = ((), (), s32[]{:S(2)}) async-start(), calls=%async_computation.18 | async-start | bytes 3211264 | tf_op jit(solution)/shard_map/psum | solution.py:307
  523.9 324.0 %copy-start.12 = (bf16[256,1536]{0,1:T(8,128)(2,1)S(1)}, bf16[256,1536]{0,1:T(8,128)(2,1)}, u32[]{:S(2)}) copy-start(bf16[256,1536]{0,1:T(8,128)(2,1)} %copy-done.11) | copy-start | bytes 2359300
  851.6 52.1 %copy-start.1 = (f32[256,1024]{1,0:T(8,128)S(1)}, f32[256,1024]{1,0:T(8,128)}, u32[]{:S(2)}) copy-start(f32[256,1024]{1,0:T(8,128)} %copy-done) | copy-start | bytes 3145732
  851.6 53.3 %collective-permute-start.10 = (bf16[256,1024]{1,0:T(8,128)(2,1)}, bf16[256,1024]{1,0:T(8,128)(2,1)}, u32[]{:S(2)}, u32[]{:S(2)}) collective-permute-start(bf16[256,1024]{1,0:T(8,128)(2,1)} %fusion.39), channel_id=1, source_target_pairs={{0,64},{64,0},{1,65},{65,1},{2,66},{66,2},{3,67},{67,3},{4,68},{68... | collective-permute-start | bytes 1572872 | tf_op jit(solution)/shard_map/ppermute | solution.py:15
  902.5 4.8 collective-permute-start.13
  (51 other events, 107.1 us)
Sparse Core Ops, SparseCore 0:
  26.1 55.0 all-gather.12
  83.9 52.5 all-gather.6
  139.2 51.2 all-gather.8
  193.1 51.2 all-gather.10
  246.9 51.2 all-gather.14
  300.7 51.2 all-gather.16
  366.6 75.4 reduce-scatter.16
  445.8 77.0 reduce-scatter.14
  526.2 77.0 reduce-scatter.24
  606.8 77.4 reduce-scatter.22
  688.0 76.9 reduce-scatter.20
  768.3 77.5 reduce-scatter.18
  848.8 51.5 all-reduce.5

commit v2 on v1

--- a/solution.py
+++ b/solution.py
@@ -7,6 +7,7 @@
 HEAD_DIM = 64
 EPSILON = 1e-06
 LANES = 128
+RING = 4
 BF = jnp.bfloat16
 F32 = jnp.float32
 
@@ -211,12 +212,81 @@
     def mine_of(low, high):
         return (choose(low, high), choose(high, low))
 
+    shard = lax.axis_index("shard")
+    place = {"x": lax.axis_index("dp"), "y": shard % RING, "z": shard // RING}
+    step = jnp.where(first, 1, -1)
+
+    def around(value, axis):
+        name = "dp" if axis == "x" else "shard"
+        size = lax.axis_size(name)
+        stride = RING if axis == "z" else 1
+        route = []
+        for core in range(2):
+            for at in range(size):
+                position = at // stride % RING
+                moved = (position + (1 if core == 0 else -1)) % RING
+                target = at + (moved - position) * stride
+                route.append((core * size + at, core * size + target))
+        return lax.ppermute(value, ("section", name), route)
+
+    def hop(value, axis, distance):
+        name = "dp" if axis == "x" else "shard"
+        stride = RING if axis == "z" else 1
+        route = []
+        for at in range(lax.axis_size(name)):
+            position = at // stride % RING
+            moved = (position + distance) % RING
+            route.append((at, at + (moved - position) * stride))
+        return lax.ppermute(value, name, route)
+
+    def put(whole, piece, at, dim):
+        start = [0] * whole.ndim
+        start[dim] = at
+        return lax.dynamic_update_slice(whole, jnp.expand_dims(piece, dim), start)
+
+    def ring_gather(block, axis, dim):
+        shape = block.shape[:dim] + (RING,) + block.shape[dim:]
+        whole = put(jnp.zeros(shape, block.dtype), block, place[axis], dim)
+        for n in range(1, RING):
+            block = around(block, axis)
+            whole = put(whole, block, (place[axis] - n * step) % RING, dim)
+        return whole
+
+    def direct_gather(block, axis, dim):
+        shape = block.shape[:dim] + (RING,) + block.shape[dim:]
+        whole = put(jnp.zeros(shape, block.dtype), block, place[axis], dim)
+        for n in range(1, RING):
+            whole = put(whole, hop(block, axis, n), (place[axis] - n) % RING, dim)
+        return whole
+
+    def chunk(value, at, dim):
+        return lax.dynamic_index_in_dim(value, at % RING, dim, keepdims=False).astype(F32)
+
+    def ring_scatter(value, axis, dim):
+        run = chunk(value, place[axis] - step, dim).astype(BF)
+        for n in range(2, RING + 1):
+            mine = chunk(value, place[axis] - n * step, dim)
+            run = (around(run, axis).astype(F32) + mine).astype(BF)
+        return run
+
+    def direct_scatter(value, axis, dim):
+        total = chunk(value, place[axis], dim)
+        for n in range(1, RING):
+            sent = chunk(value, place[axis] + n, dim).astype(BF)
+            total = total + hop(sent, axis, n).astype(F32)
+        return total.astype(BF)
+
+    def placed(width, pieces):
+        whole = jnp.zeros((pieces[0][1].shape[0], width), BF)
+        for at, piece in pieces:
+            whole = lax.dynamic_update_slice(whole, piece, (0, at))
+        return whole
+
     def parts_of(part):
         qkv = w_qkv[0].reshape(rows, 3, 2, half)[:, :, part].reshape(rows, 3 * half)
         out = w_out[0][:, part * half : (part + 1) * half]
         up = w_up[0].reshape(rows, shards, 2, unit)[:, :, part].reshape(rows, shards * unit)
-        down = w_down[0][part * unit : (part + 1) * unit].reshape(rows, -1)
-        return jnp.concatenate([qkv, out, up, down], axis=1)
+        return (qkv, out, up, w_down[0][part * unit : (part + 1) * unit])
 
     vectors = jnp.concatenate(
         [
@@ -235,30 +305,38 @@
         ]
     )
     vectors = jnp.pad(vectors, (0, rows * LANES - vector_count)).reshape(rows, LANES)
-    kept_part, sent_part = mine_of(parts_of(0), parts_of(1))
-    own = jnp.concatenate([vectors, kept_part], axis=1)
-    got = swap(jnp.concatenate([vectors, sent_part], axis=1))
-    layers = mine_of(own, got)
-    edges = (LANES + 3 * half, LANES + 4 * half, LANES + 4 * half + shards * unit)
-
-    def gather(block):
-        return lax.all_gather(block, "shard", axis=0, tiled=True)
-
-    def gather_layer(block):
-        attn = gather(block[:, : edges[1]])
-        up = gather(block[:, edges[1] : edges[2]])
-        down = gather(block[:, edges[2] :].reshape(unit, model))
+    split = [mine_of(low, high) for low, high in zip(parts_of(0), parts_of(1))]
+    kept_part = (vectors,) + tuple(low for low, high in split)
+    sent_part = (vectors,) + tuple(high for low, high in split)
+    got_part = tuple(swap(member) for member in sent_part)
+    blocks = [mine_of(own, got) for own, got in zip(kept_part, got_part)]
+    edges = (LANES, LANES + 3 * half, LANES + 4 * half, LANES + 4 * half + shards * unit)
+
+    def joined(layer, count):
+        return placed(edges[count - 1], list(zip((0,) + edges, [b[layer] for b in blocks[:count]])))
+
+    quarter = unit // RING
+    down = jnp.stack(blocks[4]).reshape(2, RING, quarter, model)
+    down = lax.dynamic_index_in_dim(down, place["x"], 1, keepdims=False)
+    down = ring_gather(ring_gather(down, "y", 1), "z", 1)
+    down = [ring_gather(down[layer], "x", 2).reshape(-1, model) for layer in range(2)]
+
+    first_whole = lax.all_gather(joined(0, 4), "shard", axis=0, tiled=True)
+    attn_whole = ring_gather(ring_gather(joined(1, 3), "y", 0), "z", 0).reshape(model, -1)
+    up_whole = ring_gather(ring_gather(blocks[3][1], "z", 0), "y", 1).reshape(model, -1)
+
+    def arranged(attn, up, down):
         flat = attn[:, :LANES].reshape(shards, rows * LANES)[:, :vector_count].astype(F32)
         whole = [flat[:, n * rows : (n + 1) * rows].reshape(-1) for n in range(8)]
         bias_up_part = flat[:, 8 * rows :].reshape(shards, 2, unit)
         bias_up_part = choose(bias_up_part[:, 0], bias_up_part[:, 1]).reshape(-1)
         bias_q_part = choose(whole[0][:half], whole[0][half:])
         bias_v_part = choose(whole[1][:half], whole[1][half:])
-        out = attn[:, edges[0] : edges[1]]
+        out = attn[:, edges[1] : edges[2]]
         held, handed = mine_of(out[:half], out[half:])
         arrived = swap(handed)
         return dict(
-            qkv=attn[:, LANES : edges[0]],
+            qkv=attn[:, LANES : edges[1]],
             out=jnp.concatenate(mine_of(held, arrived), axis=1),
             up=[up],
             down=[down],
@@ -272,14 +350,12 @@
             bias_up=[bias_up_part],
         )
 
-    weights = [gather_layer(block) for block in layers]
-
-    def scatter(block):
-        return lax.psum_scatter(block, "shard", scatter_dimension=0, tiled=True)
-
-    def scatter_layer(grads):
-        down = scatter(grads["down"][0])
-        up = scatter(grads["up"][0])
+    weights = [
+        arranged(first_whole[:, : edges[2]], first_whole[:, edges[2] :], down[0]),
+        arranged(attn_whole, up_whole, down[1]),
+    ]
+
+    def side_by_side(grads):
         held, handed = mine_of(grads["out"][:, :half], grads["out"][:, half:])
         out = jnp.concatenate(mine_of(held, swap(handed)), axis=0)
 
@@ -292,31 +368,49 @@
         spread = jnp.concatenate([choose(part, 0.0), choose(0.0, part)], axis=1)
         flat = jnp.concatenate([v.reshape(shards, rows) for v in whole] + [spread], axis=1)
         flat = jnp.pad(flat.astype(BF), ((0, 0), (0, rows * LANES - vector_count)))
-        flat = flat.reshape(shards * rows, LANES)
-        attn = scatter(jnp.concatenate([flat, grads["qkv"], out], axis=1))
-        return jnp.concatenate([attn, up, down.reshape(rows, -1)], axis=1)
+        return (flat.reshape(shards * rows, LANES), grads["qkv"], out, grads["up"][0])
+
+    def over_x(value):
+        return ring_scatter(value.reshape(RING * RING, RING, quarter, model), "x", 1)
 
     count = tokens.shape[0]
     seq_lengths = lengths[:, 0]
     middle, kept_first = layer_forward(tokens.reshape(-1, model), weights[0], seq_lengths)
     last, kept_second = layer_forward(middle, weights[1], seq_lengths)
     grad_middle, grads_second = layer_backward(cotangent.reshape(-1, model), kept_second, weights[1])
-    summed_second = scatter_layer(grads_second)
+    down_second = over_x(grads_second["down"][0])
+    pieces = list(zip((0,) + edges, side_by_side(grads_second)))
+    side_second = placed(edges[3], pieces)
+    grad_middle, side_second = lax.optimization_barrier((grad_middle, side_second))
+    side_second = lax.psum_scatter(side_second, "shard", scatter_dimension=0, tiled=True)
+    side_second = lax.psum(side_second, "dp")
+
     grad_first, grads_first = layer_backward(grad_middle, kept_first, weights[0])
-    summed_first = scatter_layer(grads_first)
-    summed_first, summed_second = lax.psum((summed_first, summed_second), "dp")
-
-    held, handed = mine_of(summed_first, summed_second)
-    low, high = mine_of(held, swap(handed))
-    low, high = (low.astype(F32), high.astype(F32))
+    down_first = over_x(grads_first["down"][0])
+    pieces = list(zip((0,) + edges, side_by_side(grads_first)))
+    up = pieces[3][1].reshape(RING, RING, rows, -1)
+    up = ring_scatter(ring_scatter(up, "y", 1), "z", 0)
+    attn = placed(edges[2], pieces[:3]).reshape(RING, RING, rows, -1)
+    attn = ring_scatter(ring_scatter(attn, "z", 0), "y", 0)
+    down = jnp.stack([down_first, down_second]).reshape(2, RING, RING, quarter, model)
+    down = direct_scatter(ring_scatter(down, "z", 1), "y", 1)
+    down = direct_gather(down, "x", 1).reshape(2, unit, model)
+    side_first = placed(edges[3], [(0, attn), (edges[2], up)]).reshape(RING, rows // RING, -1)
+    side_first = direct_scatter(side_first, "x", 0)
+    side_first = direct_gather(side_first, "x", 0).reshape(rows, -1)
+
+    summed_first, summed_second = ((side_first, down[0]), (side_second, down[1]))
+    mine, sent = zip(*(mine_of(a, b) for a, b in zip(summed_first, summed_second)))
+    both = [mine_of(a, swap(b)) for a, b in zip(mine, sent)]
+    (side_a, side_b), (down_a, down_b) = [[v.astype(F32) for v in pair] for pair in both]
 
     def cut(block):
         flat = block[:, :LANES].reshape(-1)[:vector_count]
-        qkv = block[:, LANES : edges[0]].reshape(rows, 3, half)
-        up = block[:, edges[1] : edges[2]].reshape(rows, shards, unit)
-        return (flat, qkv, block[:, edges[0] : edges[1]], up, block[:, edges[2] :].reshape(unit, -1))
-
-    (flat_a, qkv_a, out_a, up_a, down_a), (flat_b, qkv_b, out_b, up_b, down_b) = (cut(low), cut(high))
+        qkv = block[:, LANES : edges[1]].reshape(rows, 3, half)
+        up = block[:, edges[2] :].reshape(rows, shards, unit)
+        return (flat, qkv, block[:, edges[1] : edges[2]], up)
+
+    (flat_a, qkv_a, out_a, up_a), (flat_b, qkv_b, out_b, up_b) = (cut(side_a), cut(side_b))
     flat = flat_a + flat_b
     whole = [flat[n * rows : (n + 1) * rows] for n in range(8)]
     grads = (

time: 938 us -> 576 us (0.61)
  waiting for transfers between devices: 673 us -> 190 us
  starting transfers between devices: 11.2 us -> 140 us
    reduce_scatter x6 -> x1, waiting for transfers between devices: 360 us -> 0.02 us  [per_device(): lax.psum_scatter(side_second, 'shard', scatter_dimension=0, tiled=True)]
    all_gather x6 -> x1, waiting for transfers between devices: 257 us -> 0.01 us  [per_device(): first_whole = lax.all_gather(joined(0, 4), 'shard', axis=0, tiled=True)]
    ppermute x0 -> x57, waiting for transfers between devices: none -> 151 us  [the longest x45 131 us: around(): return lax.ppermute(value, ('section', name), route)]
    ppermute x0 -> x57, starting transfers between devices: none -> 112 us  [the longest x45 97.9 us: around(): return lax.ppermute(value, ('section', name), route)]
    concatenate x7 -> x1, other arithmetic: 20.8 us -> 0.01 us  [arranged(): jnp.concatenate([bias_q_part, jnp.zeros_like(bias_q_part), bias_v_part])]
    dynamic_update_slice x0 -> x40, local copies, waits for them, and re-layouts: none -> 17.1 us  [the longest x36 12.7 us: put(): return lax.dynamic_update_slice(whole, jnp.expand_dims(piece, dim), start)]
    ppermute x14 -> x19, starting transfers between devices: 10.7 us -> 26.8 us  [swap(): return lax.ppermute(value, 'section', [(0, 1), (1, 0)])]
    convert_element_type x3 -> x25, other arithmetic: 1.37 us -> 14.5 us  [the longest x21 11.7 us: ring_scatter(): run = (around(run, axis).astype(F32) + mine).astype(BF)]
  transfers between devices with their start and end apart: 27 -> 79, of which waited for: 18 -> 32; matrix products, arithmetic and copies ran while one was open for 19% -> 30% of each run, Pallas kernels for 0% -> 0%
where the time goes in v2:
time: 576 us; the launch traced here: 566 us
  waiting for transfers between devices  190 us (33%)
  starting transfers between devices  140 us (24%)
  matrix products  86.3 us (15%)
  local copies, waits for them, and re-layouts  82.2 us (14%)
  other arithmetic  51.7 us (9%)
  between operations  16.7 us (3%)
    ppermute x45, waiting for transfers between devices, around(): return lax.ppermute(value, ('section', name), route)  131 us
    ppermute x45, starting transfers between devices, around(): return lax.ppermute(value, ('section', name), route)  97.9 us
    psum x1, waiting for transfers between devices, per_device(): side_second = lax.psum(side_second, 'dp')  36.4 us
    dot_general x8, matrix products, dot(): return jnp.dot(left, right, preferred_element_type=F32)  30.6 us
    ppermute x19, starting transfers between devices, swap(): return lax.ppermute(value, 'section', [(0, 1), (1, 0)])  26.8 us
    dot_general x8, matrix products, dot_transposed(): lax.dot_general(left, right, (((1,), (1,)), ((), ())), preferred_element_...  24.2 us
    ppermute x12, waiting for transfers between devices, hop(): return lax.ppermute(value, name, route)  19.4 us
    dot_general x8, matrix products, transpose_dot(): lax.dot_general(left, right, (((0,), (0,)), ((), ())), preferred_element_...  17.7 us
  transfers between devices with their start and end apart: 79, of which 32 were waited for; matrix products, arithmetic and copies ran while one was open for 30% of the time, Pallas kernels for 0%

profile of v2, /device:TPU:1, one launch (start us, length us, event | category | flops | bytes accessed | tf_op | source)
XLA Modules:
  0.0 566.2 jit_solution(311593648725974005)
XLA Ops:
  7.9 5.4 concatenate.65
  27.4 3.8 collective-permute-start.25
  37.6 3.5 collective-permute-start.9
  41.2 4.6 collective-permute-start.26
  49.1 4.3 collective-permute-start.10
  60.4 6.9 %collective-permute-done.27 = bf16[64,2048]{1,0:T(8,128)(2,1)S(1)} collective-permute-done((bf16[64,2048]{1,0:T(8,128)(2,1)S(1)}, bf16[64,2048]{1,0:T(8,128)(2,1)S(1)}, u32[]{:S(2)}, u32[]{:S(2)}) %collective-permute-start.27) | collective-permute-done | bytes 262176 | tf_op jit(solution)/shard_map/ppermute | solution.py:230
  70.9 3.6 collective-permute-start.11
  75.2 39.5 %collective-permute-done.11 = bf16[2,4,32,1024]{3,2,1,0:T(8,128)(2,1)S(1)} collective-permute-done((bf16[2,4,32,1024]{3,2,1,0:T(8,128)(2,1)S(1)}, bf16[2,4,32,1024]{3,2,1,0:T(8,128)(2,1)S(1)}, u32[]{:S(2)}, u32[]{:S(2)}) %collective-permute-start.11) | collective-permute-done | bytes 524320 | tf_op jit(solution)/shard_map/ppermute | solution.py:230
  142.1 7.8 %collective-permute-done.13 = bf16[4,4,32,1024]{3,2,1,0:T(8,128)(2,1)S(1)} collective-permute-done((bf16[4,4,32,1024]{3,2,1,0:T(8,128)(2,1)S(1)}, bf16[4,4,32,1024]{3,2,1,0:T(8,128)(2,1)S(1)}, u32[]{:S(2)}, u32[]{:S(2)}) %collective-permute-start.13) | collective-permute-done | bytes 1048608 | tf_op jit(solution)/shard_map/ppermute | solution.py:230
  155.6 5.6 collective-permute-done.32
  164.4 8.0 %collective-permute-done.14 = bf16[4,4,32,1024]{3,2,1,0:T(8,128)(2,1)S(1)} collective-permute-done((bf16[4,4,32,1024]{3,2,1,0:T(8,128)(2,1)S(1)}, bf16[4,4,32,1024]{3,2,1,0:T(8,128)(2,1)S(1)}, u32[]{:S(2)}, u32[]{:S(2)}) %collective-permute-start.14) | collective-permute-done | bytes 1048608 | tf_op jit(solution)/shard_map/ppermute | solution.py:230
  181.5 3.7 collective-permute-start.23
  203.8 8.7 %multiply_convert_fusion.1 = (bf16[256,2048]{1,0:T(8,128)(2,1)S(1)}, f32[256,2048]{1,0:T(8,128)}, f32[256,2048]{1,0:T(8,128)}) fusion(f32[2048]{0:T(1024)S(1)} %bitcast.620, bf16[1024,4224]{1,0:T(8,128)(2,1)} %all-gather.2.cloned.1.call-done, f32[256,1024]{1,0:T(8,128)S(1)} %get-tuple-element.107, f32[1024]{0:T(1024)S(1)} %add.581, f32[1024]{0:T(1024)S(1)} %mul.420, ...), kind=kOutput, calls=%fused_computation.81 | convolution fusion | flops 1109655552 | bytes 10504192 | tf_op jit(solution)/shard_map/dot_general | solution.py:26
  212.5 3.8 convolution_convert_fusion.11
  239.6 7.3 %multiply_convert_fusion = (bf16[256,2048]{1,0:T(8,128)(2,1)S(1)}, f32[256,2048]{1,0:T(8,128)}, f32[256,2048]{1,0:T(8,128)}) fusion(f32[2048]{0:T(1024)S(1)} %bitcast.619, bf16[1024,2048]{1,0:T(8,128)(2,1)S(1)} %bitcast.582, f32[256,1024]{1,0:T(8,128)S(1)} %get-tuple-element.101, f32[1024]{0:T(1024)S(1)} %add.625, f32[1024]{0:T(1024)S(1)} %mul.438, ...), kind=kOutput, calls=%fused_computation.68 | convolution fusion | flops 1109655552 | bytes 10504192 | tf_op jit(solution)/shard_map/dot_general | solution.py:26
  246.8 3.9 convolution_convert_fusion.10
  260.8 4.4 convert_reduce_fusion.1
  293.5 4.0 dynamic_update_slice.205
  305.2 3.5 convert_dynamic-update-slice_fusion
  319.6 5.5 convert_reduce_fusion
  326.5 5.2 fusion.66
  360.1 6.9 %collective-permute-done.47 = bf16[4,64,2048]{2,1,0:T(8,128)(2,1)} collective-permute-done((bf16[4,64,2048]{2,1,0:T(8,128)(2,1)}, bf16[4,64,2048]{2,1,0:T(8,128)(2,1)}, u32[]{:S(2)}, u32[]{:S(2)}) %collective-permute-start.47) | collective-permute-done | bytes 1048608 | tf_op jit(solution)/shard_map/ppermute | solution.py:230
  389.6 8.0 %collective-permute-done.41 = bf16[4,64,2176]{2,1,0:T(8,128)(2,1)S(1)} collective-permute-done((bf16[4,64,2176]{2,1,0:T(8,128)(2,1)S(1)}, bf16[4,64,2176]{2,1,0:T(8,128)(2,1)S(1)}, u32[]{:S(2)}, u32[]{:S(2)}) %collective-permute-start.41) | collective-permute-done | bytes 1114144 | tf_op jit(solution)/shard_map/ppermute | solution.py:230
  397.9 3.8 collective-permute-start.42
  408.4 5.7 %collective-permute-done.42 = bf16[4,64,2176]{2,1,0:T(8,128)(2,1)S(1)} collective-permute-done((bf16[4,64,2176]{2,1,0:T(8,128)(2,1)S(1)}, bf16[4,64,2176]{2,1,0:T(8,128)(2,1)S(1)}, u32[]{:S(2)}, u32[]{:S(2)}) %collective-permute-start.42) | collective-permute-done | bytes 1114144 | tf_op jit(solution)/shard_map/ppermute | solution.py:230
  422.7 13.0 %collective-permute-done.66 = bf16[2,4,32,1024]{3,2,0,1:T(8,128)(2,1)S(1)} collective-permute-done((bf16[2,4,32,1024]{3,2,0,1:T(8,128)(2,1)S(1)}, bf16[2,4,32,1024]{3,2,0,1:T(8,128)(2,1)S(1)}, u32[]{:S(2)}, u32[]{:S(2)}) %collective-permute-start.66) | collective-permute-done | bytes 524320 | tf_op jit(solution)/shard_map/ppermute | solution.py:230
  445.4 3.5 collective-permute-start.68
  449.1 6.0 %collective-permute-done.68 = bf16[2,4,32,1024]{3,2,0,1:T(8,128)(2,1)S(1)} collective-permute-done((bf16[2,4,32,1024]{3,2,0,1:T(8,128)(2,1)S(1)}, bf16[2,4,32,1024]{3,2,0,1:T(8,128)(2,1)S(1)}, u32[]{:S(2)}, u32[]{:S(2)}) %collective-permute-start.68) | collective-permute-done | bytes 524320 | tf_op jit(solution)/shard_map/ppermute | solution.py:230
  483.9 13.0 %collective-permute-start.75 = (bf16[128,1024]{1,0:T(8,128)(2,1)}, bf16[128,1024]{1,0:T(8,128)(2,1)S(1)}, u32[]{:S(2)}, u32[]{:S(2)}) collective-permute-start(bf16[128,1024]{1,0:T(8,128)(2,1)} %bitcast.165), channel_id=1, source_target_pairs={{0,64},{64,0},{1,65},{65,1},{2,66},{66,2},{3,67},{67,3},{4,68},{68... | collective-permute-start | bytes 786440 | tf_op jit(solution)/shard_map/ppermute | solution.py:16
  499.9 3.9 collective-permute-done.57
  507.3 36.4 %all-reduce.9.cloned.1.call-done = bf16[64,4224]{1,0:T(8,128)(2,1)} async-done(((bf16[64,4224]{1,0:T(8,128)(2,1)}), bf16[64,4224]{1,0:T(8,128)(2,1)}) %all-reduce.9.cloned.1.call-update) | async-done | bytes 540688 | tf_op jit(solution)/shard_map/psum | solution.py:386
  543.8 3.9 collective-permute-start.59
  (596 shorter events, 302.5 us)
Async XLA Ops:
  7.2 178.0 %all-gather.2.cloned.1.call-start = ((), (), s32[]{:S(2)}) async-start(), calls=%async_computation.1 | async-start | bytes 9191424 | tf_op jit(solution)/shard_map/all_gather | solution.py:324
  22.4 481.5 %reduce-scatter.2.cloned.1.call-start = ((), (), s32[]{:S(2)}) async-start(), calls=%async_computation.2 | async-start | bytes 9191424 | tf_op jit(solution)/shard_map/reduce_scatter | solution.py:385
  34.3 19.4 %collective-permute-start.18 = (bf16[64,2176]{1,0:T(8,128)(2,1)S(1)}, bf16[64,2176]{1,0:T(8,128)(2,1)S(1)}, u32[]{:S(2)}, u32[]{:S(2)}) collective-permute-start(bf16[64,2176]{1,0:T(8,128)(2,1)S(1)} %collective-permute-done.17), channel_id=1, source_target_pairs={{0,1},{1,2},{2,3},{3,0},{4,5},{5,6},{6,7},{7,4},{8,9},{9,10},{10,1... | collective-permute-start | bytes 835592 | tf_op jit(solution)/shard_map/ppermute | solution.py:230
  49.1 21.8 %collective-permute-start.10 = (bf16[2,4,32,1024]{3,2,1,0:T(8,128)(2,1)S(1)}, bf16[2,4,32,1024]{3,2,1,0:T(8,128)(2,1)S(1)}, u32[]{:S(2)}, u32[]{:S(2)}) collective-permute-start(bf16[2,4,32,1024]{3,2,1,0:T(8,128)(2,1)S(1)} %bitcast_dynamic-update-slice_fusion.44), channel_id=1, source_target_pairs={{0,4},{1,5},{2,6},{3,7},{4,8},{5,9},{6,10},{7,11},{8,12},{9,13},{1... | collective-permute-start | bytes 1572872 | tf_op jit(solution)/shard_map/ppermute | solution.py:230
  60.1 60.9 %collective-permute-start.20 = (bf16[4,64,2176]{2,1,0:T(8,128)(2,1)S(1)}, bf16[4,64,2176]{2,1,0:T(8,128)(2,1)S(1)}, u32[]{:S(2)}, u32[]{:S(2)}) collective-permute-start(bf16[4,64,2176]{2,1,0:T(8,128)(2,1)S(1)} %bitcast_dynamic-update-slice_fusion.20), channel_id=1, source_target_pairs={{0,4},{1,5},{2,6},{3,7},{4,8},{5,9},{6,10},{7,11},{8,12},{9,13},{1... | collective-permute-start | bytes 3342344 | tf_op jit(solution)/shard_map/ppermute | solution.py:230
  67.4 50.7 %collective-permute-start.28 = (bf16[4,64,2048]{2,1,0:T(8,128)(2,1)S(1)}, bf16[4,64,2048]{2,1,0:T(8,128)(2,1)S(1)}, u32[]{:S(2)}, u32[]{:S(2)}) collective-permute-start(bf16[4,64,2048]{2,1,0:T(8,128)(2,1)S(1)} %bitcast_dynamic-update-slice_fusion.30), channel_id=1, source_target_pairs={{0,1},{1,2},{2,3},{3,0},{4,5},{5,6},{6,7},{7,4},{8,9},{9,10},{10,1... | collective-permute-start | bytes 3145736 | tf_op jit(solution)/shard_map/ppermute | solution.py:230
  70.9 43.8 %collective-permute-start.11 = (bf16[2,4,32,1024]{3,2,1,0:T(8,128)(2,1)S(1)}, bf16[2,4,32,1024]{3,2,1,0:T(8,128)(2,1)S(1)}, u32[]{:S(2)}, u32[]{:S(2)}) collective-permute-start(bf16[2,4,32,1024]{3,2,1,0:T(8,128)(2,1)S(1)} %collective-permute-done.10), channel_id=1, source_target_pairs={{0,4},{1,5},{2,6},{3,7},{4,8},{5,9},{6,10},{7,11},{8,12},{9,13},{1... | collective-permute-start | bytes 1572872 | tf_op jit(solution)/shard_map/ppermute | solution.py:230
  127.0 23.0 %collective-permute-start.13 = (bf16[4,4,32,1024]{3,2,1,0:T(8,128)(2,1)S(1)}, bf16[4,4,32,1024]{3,2,1,0:T(8,128)(2,1)S(1)}, u32[]{:S(2)}, u32[]{:S(2)}) collective-permute-start(bf16[4,4,32,1024]{3,2,1,0:T(8,128)(2,1)S(1)} %get-tuple-element.113), channel_id=1, source_target_pairs={{0,16},{16,32},{32,48},{48,0},{64,112},{80,64},{96,80},{112,96},{1... | collective-permute-start | bytes 3145736 | tf_op jit(solution)/shard_map/ppermute | solution.py:230
  134.8 20.6 %collective-permute-start.30 = (bf16[4,64,2048]{2,1,0:T(8,128)(2,1)S(1)}, bf16[4,64,2048]{2,1,0:T(8,128)(2,1)S(1)}, u32[]{:S(2)}, u32[]{:S(2)}) collective-permute-start(bf16[4,64,2048]{2,1,0:T(8,128)(2,1)S(1)} %collective-permute-done.29), channel_id=1, source_target_pairs={{0,1},{1,2},{2,3},{3,0},{4,5},{5,6},{6,7},{7,4},{8,9},{9,10},{10,1... | collective-permute-start | bytes 3145736 | tf_op jit(solution)/shard_map/ppermute | solution.py:230
  137.7 39.0 %collective-permute-start.22 = (bf16[4,64,2176]{2,1,0:T(8,128)(2,1)S(1)}, bf16[4,64,2176]{2,1,0:T(8,128)(2,1)S(1)}, u32[]{:S(2)}, u32[]{:S(2)}) collective-permute-start(bf16[4,64,2176]{2,1,0:T(8,128)(2,1)S(1)} %collective-permute-done.21), channel_id=1, source_target_pairs={{0,4},{1,5},{2,6},{3,7},{4,8},{5,9},{6,10},{7,11},{8,12},{9,13},{1... | collective-permute-start | bytes 3342344 | tf_op jit(solution)/shard_map/ppermute | solution.py:230
  141.0 20.2 %collective-permute-start.32 = (bf16[4,4,32,1024]{3,2,1,0:T(8,128)(2,1)S(1)}, bf16[4,4,32,1024]{3,2,1,0:T(8,128)(2,1)}, u32[]{:S(2)}, u32[]{:S(2)}) collective-permute-start(bf16[4,4,32,1024]{3,2,1,0:T(8,128)(2,1)S(1)} %collective-permute-done.31), channel_id=1, source_target_pairs={{0,16},{16,32},{32,48},{48,0},{64,112},{80,64},{96,80},{112,96},{1... | collective-permute-start | bytes 3145736 | tf_op jit(solution)/shard_map/ppermute | solution.py:230
  149.9 22.5 %collective-permute-start.14 = (bf16[4,4,32,1024]{3,2,1,0:T(8,128)(2,1)S(1)}, bf16[4,4,32,1024]{3,2,1,0:T(8,128)(2,1)S(1)}, u32[]{:S(2)}, u32[]{:S(2)}) collective-permute-start(bf16[4,4,32,1024]{3,2,1,0:T(8,128)(2,1)S(1)} %collective-permute-done.13), channel_id=1, source_target_pairs={{0,16},{16,32},{32,48},{48,0},{64,112},{80,64},{96,80},{112,96},{1... | collective-permute-start | bytes 3145736 | tf_op jit(solution)/shard_map/ppermute | solution.py:230
  161.2 73.7 %collective-permute-start.33 = (bf16[4,4,32,1024]{3,2,1,0:T(8,128)(2,1)}, bf16[4,4,32,1024]{3,2,1,0:T(8,128)(2,1)}, u32[]{:S(2)}, u32[]{:S(2)}) collective-permute-start(bf16[4,4,32,1024]{3,2,1,0:T(8,128)(2,1)} %collective-permute-done.32), channel_id=1, source_target_pairs={{0,16},{16,32},{32,48},{48,0},{64,112},{80,64},{96,80},{112,96},{1... | collective-permute-start | bytes 3145736 | tf_op jit(solution)/shard_map/ppermute | solution.py:230
  172.4 28.1 %collective-permute-start.15 = (bf16[4,4,32,1024]{3,2,1,0:T(8,128)(2,1)S(1)}, bf16[4,4,32,1024]{3,2,1,0:T(8,128)(2,1)S(1)}, u32[]{:S(2)}, u32[]{:S(2)}) collective-permute-start(bf16[4,4,32,1024]{3,2,1,0:T(8,128)(2,1)S(1)} %collective-permute-done.14), channel_id=1, source_target_pairs={{0,16},{16,32},{32,48},{48,0},{64,112},{80,64},{96,80},{112,96},{1... | collective-permute-start | bytes 3145736 | tf_op jit(solution)/shard_map/ppermute | solution.py:230
  181.5 37.9 %collective-permute-start.23 = (bf16[512,512]{1,0:T(8,128)(2,1)}, bf16[512,512]{1,0:T(8,128)(2,1)}, u32[]{:S(2)}, u32[]{:S(2)}) collective-permute-start(bf16[512,512]{1,0:T(8,128)(2,1)} %broadcast_select_fusion.10), channel_id=1, source_target_pairs={{0,64},{64,0},{1,65},{65,1},{2,66},{66,2},{3,67},{67,3},{4,68},{68... | collective-permute-start | bytes 1572872 | tf_op jit(solution)/shard_map/ppermute | solution.py:16
  270.1 30.3 %collective-permute-start.63 = (bf16[16,32,1024]{2,1,0:T(8,128)(2,1)}, bf16[16,32,1024]{2,1,0:T(8,128)(2,1)}, u32[]{:S(2)}, u32[]{:S(2)}) collective-permute-start(bf16[16,32,1024]{2,1,0:T(8,128)(2,1)} %dynamic-slice_bitcast_fusion.1), channel_id=1, source_target_pairs={{0,16},{16,32},{32,48},{48,0},{64,112},{80,64},{96,80},{112,96},{1... | collective-permute-start | bytes 3145736 | tf_op jit(solution)/shard_map/ppermute | solution.py:230
  291.1 17.7 %collective-permute-start.36 = (bf16[256,1024]{1,0:T(8,128)(2,1)}, bf16[256,1024]{1,0:T(8,128)(2,1)}, u32[]{:S(2)}, u32[]{:S(2)}) collective-permute-start(bf16[256,1024]{1,0:T(8,128)(2,1)} %fusion.63), channel_id=1, source_target_pairs={{0,64},{64,0},{1,65},{65,1},{2,66},{66,2},{3,67},{67,3},{4,68},{68... | collective-permute-start | bytes 1572872 | tf_op jit(solution)/shard_map/ppermute | solution.py:16
  303.3 74.4 %collective-permute-start.64 = (bf16[16,32,1024]{2,1,0:T(8,128)(2,1)}, bf16[16,32,1024]{2,1,0:T(8,128)(2,1)}, u32[]{:S(2)}, u32[]{:S(2)}) collective-permute-start(bf16[16,32,1024]{2,1,0:T(8,128)(2,1)} %fusion.34), channel_id=1, source_target_pairs={{0,16},{16,32},{32,48},{48,0},{64,112},{80,64},{96,80},{112,96},{1... | collective-permute-start | bytes 3145736 | tf_op jit(solution)/shard_map/ppermute | solution.py:230
  311.3 232.4 %all-reduce.9.cloned.1.call-start = ((), (), s32[]{:S(2)}) async-start(), calls=%async_computation.3 | async-start | bytes 1081344 | tf_op jit(solution)/shard_map/psum | solution.py:386
  332.9 34.1 %collective-permute-start.47 = (bf16[4,64,2048]{2,1,0:T(8,128)(2,1)}, bf16[4,64,2048]{2,1,0:T(8,128)(2,1)}, u32[]{:S(2)}, u32[]{:S(2)}) collective-permute-start(bf16[4,64,2048]{2,1,0:T(8,128)(2,1)} %dynamic-slice_bitcast_fusion.3), channel_id=1, source_target_pairs={{0,1},{1,2},{2,3},{3,0},{4,5},{5,6},{6,7},{7,4},{8,9},{9,10},{10,1... | collective-permute-start | bytes 3145736 | tf_op jit(solution)/shard_map/ppermute | solution.py:230
  334.0 35.3 %collective-permute-start.60 = (bf16[16,32,1024]{2,1,0:T(8,128)(2,1)}, bf16[16,32,1024]{2,1,0:T(8,128)(2,1)}, u32[]{:S(2)}, u32[]{:S(2)}) collective-permute-start(bf16[16,32,1024]{2,1,0:T(8,128)(2,1)} %dynamic-slice_bitcast_fusion.2), channel_id=1, source_target_pairs={{0,16},{16,32},{32,48},{48,0},{64,112},{80,64},{96,80},{112,96},{1... | collective-permute-start | bytes 3145736 | tf_op jit(solution)/shard_map/ppermute | solution.py:230
  374.1 23.5 %collective-permute-start.41 = (bf16[4,64,2176]{2,1,0:T(8,128)(2,1)S(1)}, bf16[4,64,2176]{2,1,0:T(8,128)(2,1)S(1)}, u32[]{:S(2)}, u32[]{:S(2)}) collective-permute-start(bf16[4,64,2176]{2,1,0:T(8,128)(2,1)S(1)} %dynamic-slice_bitcast_fusion), channel_id=1, source_target_pairs={{0,4},{1,5},{2,6},{3,7},{4,8},{5,9},{6,10},{7,11},{8,12},{9,13},{1... | collective-permute-start | bytes 3342344 | tf_op jit(solution)/shard_map/ppermute | solution.py:230
  379.3 22.4 %collective-permute-start.65 = (bf16[16,32,1024]{2,1,0:T(8,128)(2,1)S(1)}, bf16[16,32,1024]{2,1,0:T(8,128)(2,1)S(1)}, u32[]{:S(2)}, u32[]{:S(2)}) collective-permute-start(bf16[16,32,1024]{2,1,0:T(8,128)(2,1)S(1)} %fusion.33), channel_id=1, source_target_pairs={{0,16},{16,32},{32,48},{48,0},{64,112},{80,64},{96,80},{112,96},{1... | collective-permute-start | bytes 3145736 | tf_op jit(solution)/shard_map/ppermute | solution.py:230
  383.7 20.2 %collective-permute-start.49 = (bf16[4,64,2048]{2,1,0:T(8,128)(2,1)S(1)}, bf16[4,64,2048]{2,1,0:T(8,128)(2,1)S(1)}, u32[]{:S(2)}, u32[]{:S(2)}) collective-permute-start(bf16[4,64,2048]{2,1,0:T(8,128)(2,1)S(1)} %fusion.39), channel_id=1, source_target_pairs={{0,1},{1,2},{2,3},{3,0},{4,5},{5,6},{6,7},{7,4},{8,9},{9,10},{10,1... | collective-permute-start | bytes 3145736 | tf_op jit(solution)/shard_map/ppermute | solution.py:230
  386.6 21.5 %collective-permute-start.62 = (bf16[16,32,1024]{2,1,0:T(8,128)(2,1)S(1)}, bf16[16,32,1024]{2,1,0:T(8,128)(2,1)S(1)}, u32[]{:S(2)}, u32[]{:S(2)}) collective-permute-start(bf16[16,32,1024]{2,1,0:T(8,128)(2,1)S(1)} %fusion.36), channel_id=1, source_target_pairs={{0,16},{16,32},{32,48},{48,0},{64,112},{80,64},{96,80},{112,96},{1... | collective-permute-start | bytes 3145736 | tf_op jit(solution)/shard_map/ppermute | solution.py:230
  414.5 24.6 %collective-permute-start.43 = (bf16[4,64,2176]{2,1,0:T(8,128)(2,1)S(1)}, bf16[4,64,2176]{2,1,0:T(8,128)(2,1)S(1)}, u32[]{:S(2)}, u32[]{:S(2)}) collective-permute-start(bf16[4,64,2176]{2,1,0:T(8,128)(2,1)S(1)} %fusion.28), channel_id=1, source_target_pairs={{0,4},{1,5},{2,6},{3,7},{4,8},{5,9},{6,10},{7,11},{8,12},{9,13},{1... | collective-permute-start | bytes 3342344 | tf_op jit(solution)/shard_map/ppermute | solution.py:230
  417.7 18.0 %collective-permute-start.66 = (bf16[2,4,32,1024]{3,2,0,1:T(8,128)(2,1)S(1)}, bf16[2,4,32,1024]{3,2,0,1:T(8,128)(2,1)S(1)}, u32[]{:S(2)}, u32[]{:S(2)}) collective-permute-start(bf16[2,4,32,1024]{3,2,0,1:T(8,128)(2,1)S(1)} %fusion.103), channel_id=1, source_target_pairs={{0,4},{1,5},{2,6},{3,7},{4,8},{5,9},{6,10},{7,11},{8,12},{9,13},{1... | collective-permute-start | bytes 1572872 | tf_op jit(solution)/shard_map/ppermute | solution.py:230
  420.7 127.0 %collective-permute-start.39 = (bf16[256,1024]{1,0:T(8,128)(2,1)S(1)}, bf16[256,1024]{1,0:T(8,128)(2,1)}, u32[]{:S(2)}, u32[]{:S(2)}) collective-permute-start(bf16[256,1024]{1,0:T(8,128)(2,1)S(1)} %fusion.60), channel_id=1, source_target_pairs={{0,64},{64,0},{1,65},{65,1},{2,66},{66,2},{3,67},{67,3},{4,68},{68... | collective-permute-start | bytes 1572872 | tf_op jit(solution)/shard_map/ppermute | solution.py:16
  420.9 18.6 %collective-permute-start.51 = (bf16[64,2048]{1,0:T(8,128)(2,1)S(1)}, bf16[64,2048]{1,0:T(8,128)(2,1)S(1)}, u32[]{:S(2)}, u32[]{:S(2)}) collective-permute-start(bf16[64,2048]{1,0:T(8,128)(2,1)S(1)} %fusion.111), channel_id=1, source_target_pairs={{0,4},{1,5},{2,6},{3,7},{4,8},{5,9},{6,10},{7,11},{8,12},{9,13},{1... | collective-permute-start | bytes 786440 | tf_op jit(solution)/shard_map/ppermute | solution.py:230
  439.6 18.4 %collective-permute-start.52 = (bf16[64,2048]{1,0:T(8,128)(2,1)S(1)}, bf16[64,2048]{1,0:T(8,128)(2,1)S(1)}, u32[]{:S(2)}, u32[]{:S(2)}) collective-permute-start(bf16[64,2048]{1,0:T(8,128)(2,1)S(1)} %fusion.110), channel_id=1, source_target_pairs={{0,4},{1,5},{2,6},{3,7},{4,8},{5,9},{6,10},{7,11},{8,12},{9,13},{1... | collective-permute-start | bytes 786440 | tf_op jit(solution)/shard_map/ppermute | solution.py:230
  481.7 18.2 %collective-permute-start.56 = (bf16[16,4224]{1,0:T(8,128)(2,1)}, bf16[16,4224]{1,0:T(8,128)(2,1)S(1)}, u32[]{:S(2)}, u32[]{:S(2)}) collective-permute-start(bf16[16,4224]{1,0:T(8,128)(2,1)} %get-tuple-element.83), channel_id=1, source_target_pairs={{0,16},{16,32},{32,48},{48,0},{1,17},{17,33},{33,49},{49,1},{2,18}... | collective-permute-start | bytes 405512 | tf_op jit(solution)/shard_map/ppermute | solution.py:240
  483.9 65.9 %collective-permute-start.75 = (bf16[128,1024]{1,0:T(8,128)(2,1)}, bf16[128,1024]{1,0:T(8,128)(2,1)S(1)}, u32[]{:S(2)}, u32[]{:S(2)}) collective-permute-start(bf16[128,1024]{1,0:T(8,128)(2,1)} %bitcast.165), channel_id=1, source_target_pairs={{0,64},{64,0},{1,65},{65,1},{2,66},{66,2},{3,67},{67,3},{4,68},{68... | collective-permute-start | bytes 786440 | tf_op jit(solution)/shard_map/ppermute | solution.py:16
  (119 other events, 719.7 us)
Sparse Core Ops, SparseCore 0:
  22.5 93.4 all-gather.1
  311.4 88.7 reduce-scatter.1
  504.0 39.6 all-reduce.8

commit v3 on v2

--- a/solution.py
+++ b/solution.py
@@ -6,6 +6,7 @@
 
 HEAD_DIM = 64
 EPSILON = 1e-06
+TAU = 6.283185307179586
 LANES = 128
 RING = 4
 BF = jnp.bfloat16
@@ -82,7 +83,9 @@
     normed_attn, inverse_attn = norm_rows(inputs.astype(F32) + branch)
     hidden = (normed_attn * weights["gain_attn"] + weights["shift_attn"]).astype(BF)
     upward = [dot(hidden, w) + b for w, b in zip(weights["up"], weights["bias_up"])]
-    activated = [jax.nn.gelu(u, approximate=False).astype(BF) for u in upward]
+    share = [0.5 + 0.5 * lax.erf(u * 0.5**0.5) for u in upward]
+    activated = [(u * c).astype(BF) for u, c in zip(upward, share)]
+    slope = [c + u * jnp.exp(-0.5 * u * u) * TAU ** (-0.5) for u, c in zip(upward, share)]
     mixed = sum(dot(g, w) for g, w in zip(activated, weights["down"]))
     mixed = pair_sum(mixed) + weights["bias_down"]
     normed_mlp, inverse_mlp = norm_rows(hidden.astype(F32) + mixed)
@@ -95,7 +98,7 @@
         normed_attn=normed_attn,
         inverse_attn=inverse_attn,
         hidden=hidden,
-        upward=upward,
+        slope=slope,
         activated=activated,
         normed_mlp=normed_mlp,
         inverse_mlp=inverse_mlp,
@@ -113,10 +116,10 @@
     grad_mixed = grad_resid_mlp.astype(BF)
     grad_bias_down = jnp.sum(grad_mixed.astype(F32), axis=0)
     grad_down = [transpose_dot(g, grad_mixed).astype(BF) for g in kept["activated"]]
-    grad_upward = []
-    for up, w in zip(kept["upward"], weights["down"]):
-        pull = jax.vjp(lambda point: jax.nn.gelu(point, approximate=False), up)[1]
-        grad_upward.append(pull(dot_transposed(grad_mixed, w))[0].astype(BF))
+    grad_upward = [
+        (dot_transposed(grad_mixed, w) * c).astype(BF)
+        for c, w in zip(kept["slope"], weights["down"])
+    ]
     grad_bias_up = [jnp.sum(u.astype(F32), axis=0) for u in grad_upward]
     grad_up = [transpose_dot(kept["hidden"], u).astype(BF) for u in grad_upward]
     passed = sum(dot_transposed(u, w) for u, w in zip(grad_upward, weights["up"]))
@@ -214,9 +217,11 @@
 
     shard = lax.axis_index("shard")
     place = {"x": lax.axis_index("dp"), "y": shard % RING, "z": shard // RING}
-    step = jnp.where(first, 1, -1)
-
-    def around(value, axis):
+
+    near = {axis: at ^ choose(1, 3) for axis, at in place.items()}
+    far = {axis: at ^ choose(3, 1) for axis, at in place.items()}
+
+    def trade(value, axis, masks):
         name = "dp" if axis == "x" else "shard"
         size = lax.axis_size(name)
         stride = RING if axis == "z" else 1
@@ -224,57 +229,38 @@
         for core in range(2):
             for at in range(size):
                 position = at // stride % RING
-                moved = (position + (1 if core == 0 else -1)) % RING
-                target = at + (moved - position) * stride
+                target = at + ((position ^ masks[core]) - position) * stride
                 route.append((core * size + at, core * size + target))
         return lax.ppermute(value, ("section", name), route)
 
-    def hop(value, axis, distance):
-        name = "dp" if axis == "x" else "shard"
-        stride = RING if axis == "z" else 1
-        route = []
-        for at in range(lax.axis_size(name)):
-            position = at // stride % RING
-            moved = (position + distance) % RING
-            route.append((at, at + (moved - position) * stride))
-        return lax.ppermute(value, name, route)
+    def after(value, earlier):
+        return lax.optimization_barrier((value, earlier))[0]
 
     def put(whole, piece, at, dim):
         start = [0] * whole.ndim
         start[dim] = at
         return lax.dynamic_update_slice(whole, jnp.expand_dims(piece, dim), start)
 
-    def ring_gather(block, axis, dim):
-        shape = block.shape[:dim] + (RING,) + block.shape[dim:]
-        whole = put(jnp.zeros(shape, block.dtype), block, place[axis], dim)
-        for n in range(1, RING):
-            block = around(block, axis)
-            whole = put(whole, block, (place[axis] - n * step) % RING, dim)
-        return whole
-
-    def direct_gather(block, axis, dim):
-        shape = block.shape[:dim] + (RING,) + block.shape[dim:]
-        whole = put(jnp.zeros(shape, block.dtype), block, place[axis], dim)
-        for n in range(1, RING):
-            whole = put(whole, hop(block, axis, n), (place[axis] - n) % RING, dim)
-        return whole
-
-    def chunk(value, at, dim):
-        return lax.dynamic_index_in_dim(value, at % RING, dim, keepdims=False).astype(F32)
+    def ring_gather(block, axis, dim, between=None, behind=None):
+        beside = trade(block, axis, (1, 3))
+        both = jnp.stack([block, beside])
+        across = trade(both if between is None else after(both, between), axis, (3, 1))
+        across = across if behind is None else after(across, behind)
+        whole = jnp.zeros(block.shape[:dim] + (RING,) + block.shape[dim:], block.dtype)
+        whole = put(whole, block, place[axis], dim)
+        whole = put(whole, beside, near[axis], dim)
+        whole = put(whole, across[0], far[axis], dim)
+        return put(whole, across[1], place[axis] ^ 2, dim)
 
     def ring_scatter(value, axis, dim):
-        run = chunk(value, place[axis] - step, dim).astype(BF)
-        for n in range(2, RING + 1):
-            mine = chunk(value, place[axis] - n * step, dim)
-            run = (around(run, axis).astype(F32) + mine).astype(BF)
-        return run
-
-    def direct_scatter(value, axis, dim):
-        total = chunk(value, place[axis], dim)
-        for n in range(1, RING):
-            sent = chunk(value, place[axis] + n, dim).astype(BF)
-            total = total + hop(sent, axis, n).astype(F32)
-        return total.astype(BF)
+        def chunk(at):
+            return lax.dynamic_index_in_dim(value, at, dim, keepdims=False)
+
+        sent = jnp.stack([chunk(near[axis]), chunk(place[axis] ^ 2)])
+        beside = trade(sent, axis, (1, 3)).astype(F32)
+        sent = (chunk(far[axis]).astype(F32) + beside[1]).astype(BF)
+        across = trade(sent, axis, (3, 1)).astype(F32)
+        return (chunk(place[axis]).astype(F32) + beside[0] + across).astype(BF)
 
     def placed(width, pieces):
         whole = jnp.zeros((pieces[0][1].shape[0], width), BF)
@@ -316,14 +302,27 @@
         return placed(edges[count - 1], list(zip((0,) + edges, [b[layer] for b in blocks[:count]])))
 
     quarter = unit // RING
-    down = jnp.stack(blocks[4]).reshape(2, RING, quarter, model)
-    down = lax.dynamic_index_in_dim(down, place["x"], 1, keepdims=False)
-    down = ring_gather(ring_gather(down, "y", 1), "z", 1)
-    down = [ring_gather(down[layer], "x", 2).reshape(-1, model) for layer in range(2)]
-
-    first_whole = lax.all_gather(joined(0, 4), "shard", axis=0, tiled=True)
-    attn_whole = ring_gather(ring_gather(joined(1, 3), "y", 0), "z", 0).reshape(model, -1)
-    up_whole = ring_gather(ring_gather(blocks[3][1], "z", 0), "y", 1).reshape(model, -1)
+
+    def down_quarter(block, order):
+        mine = lax.dynamic_index_in_dim(
+            block.reshape(RING, quarter, model), place["x"], 0, keepdims=False
+        )
+        mine = ring_gather(mine, order[0], 0)
+        mine = ring_gather(mine, order[1], 0 if order[1] == "z" else 1)
+        return mine.reshape(shards, quarter, model)
+
+    attn_first = ring_gather(joined(0, 3), "y", 0)
+    up_first = ring_gather(blocks[3][0], "z", 0)
+    low_first = down_quarter(blocks[4][0], "yz")
+    attn_second = ring_gather(after(joined(1, 3), attn_first), "y", 0)
+    up_second = ring_gather(after(blocks[3][1], up_first), "z", 0)
+    low_second = down_quarter(after(blocks[4][1], low_first), "zy")
+    attn_first = ring_gather(attn_first, "z", 0)
+    up_first = ring_gather(up_first, "y", 1)
+    low_first = ring_gather(low_first, "x", 1)
+    attn_second = after(attn_second, attn_first)
+    up_second = after(up_second, up_first)
+    low_second = after(low_second, low_first)
 
     def arranged(attn, up, down):
         flat = attn[:, :LANES].reshape(shards, rows * LANES)[:, :vector_count].astype(F32)
@@ -350,10 +349,8 @@
             bias_up=[bias_up_part],
         )
 
-    weights = [
-        arranged(first_whole[:, : edges[2]], first_whole[:, edges[2] :], down[0]),
-        arranged(attn_whole, up_whole, down[1]),
-    ]
+    def flat_rows(*members):
+        return arranged(*(member.reshape(-1, member.shape[-1]) for member in members))
 
     def side_by_side(grads):
         held, handed = mine_of(grads["out"][:, :half], grads["out"][:, half:])
@@ -375,7 +372,13 @@
 
     count = tokens.shape[0]
     seq_lengths = lengths[:, 0]
+    weights = [flat_rows(attn_first, up_first, low_first)]
     middle, kept_first = layer_forward(tokens.reshape(-1, model), weights[0], seq_lengths)
+    points = (kept_first["attended"], kept_first["activated"][0])
+    attn_second = ring_gather(attn_second, "z", 0, *points)
+    up_second = ring_gather(up_second, "y", 1, *points)
+    low_second = ring_gather(low_second, "x", 1)
+    weights.append(flat_rows(attn_second, up_second, low_second))
     last, kept_second = layer_forward(middle, weights[1], seq_lengths)
     grad_middle, grads_second = layer_backward(cotangent.reshape(-1, model), kept_second, weights[1])
     down_second = over_x(grads_second["down"][0])
@@ -383,7 +386,6 @@
     side_second = placed(edges[3], pieces)
     grad_middle, side_second = lax.optimization_barrier((grad_middle, side_second))
     side_second = lax.psum_scatter(side_second, "shard", scatter_dimension=0, tiled=True)
-    side_second = lax.psum(side_second, "dp")
 
     grad_first, grads_first = layer_backward(grad_middle, kept_first, weights[0])
     down_first = over_x(grads_first["down"][0])
@@ -393,13 +395,13 @@
     attn = placed(edges[2], pieces[:3]).reshape(RING, RING, rows, -1)
     attn = ring_scatter(ring_scatter(attn, "z", 0), "y", 0)
     down = jnp.stack([down_first, down_second]).reshape(2, RING, RING, quarter, model)
-    down = direct_scatter(ring_scatter(down, "z", 1), "y", 1)
-    down = direct_gather(down, "x", 1).reshape(2, unit, model)
-    side_first = placed(edges[3], [(0, attn), (edges[2], up)]).reshape(RING, rows // RING, -1)
-    side_first = direct_scatter(side_first, "x", 0)
-    side_first = direct_gather(side_first, "x", 0).reshape(rows, -1)
-
-    summed_first, summed_second = ((side_first, down[0]), (side_second, down[1]))
+    down = ring_scatter(ring_scatter(down, "z", 1), "y", 1)
+    down = ring_gather(down, "x", 1).reshape(2, unit, model)
+    side_first = placed(edges[3], [(0, attn), (edges[2], up)])
+    side = jnp.stack([side_first, side_second]).reshape(2, RING, rows // RING, -1)
+    side = ring_gather(ring_scatter(side, "x", 1), "x", 1).reshape(2, rows, -1)
+
+    summed_first, summed_second = ((side[0], down[0]), (side[1], down[1]))
     mine, sent = zip(*(mine_of(a, b) for a, b in zip(summed_first, summed_second)))
     both = [mine_of(a, swap(b)) for a, b in zip(mine, sent)]
     (side_a, side_b), (down_a, down_b) = [[v.astype(F32) for v in pair] for pair in both]

time: 576 us -> 532 us (0.924)
  starting transfers between devices: 140 us -> 83.1 us
  matrix products: 86.3 us -> 67.6 us
  other arithmetic: 51.7 us -> 68.8 us
  local copies, waits for them, and re-layouts: 82.2 us -> 97.6 us
    ppermute x57 -> x50, starting transfers between devices: 112 us -> 57 us  [trade(): return lax.ppermute(value, ('section', name), route)]
    psum x1 -> x0, waiting for transfers between devices: 36.4 us -> none  [per_device(): side_second = lax.psum(side_second, 'dp')]
    ppermute x57 -> x50, waiting for transfers between devices: 151 us -> 185 us  [trade(): return lax.ppermute(value, ('section', name), route)]
    another operation x13 -> x39, other arithmetic: 0.06 us -> 13.8 us  [the longest x11 8.23 us: ring_scatter(): sent = jnp.stack([chunk(near[axis]), chunk(place[axis] ^ 2)])]
    dot_general x8, matrix products: 30.6 us -> 18.2 us  [dot(): return jnp.dot(left, right, preferred_element_type=F32)]
    unnamed x155 -> x203, local copies, waits for them, and re-layouts: 10.5 us -> 22.8 us
    dot_general x8, matrix products: 24.2 us -> 17.6 us  [dot_transposed(): lax.dot_general(left, right, (((1,), (1,)), ((), ())), preferred_element_...]
    convert_element_type x21 -> x25, other arithmetic: 11.7 us -> 17.9 us  [the longest x9 10.8 us: ring_scatter(): beside = trade(sent, axis, (1, 3)).astype(F32)]
  transfers between devices with their start and end apart: 79 -> 70, of which waited for: 32 -> 32; matrix products, arithmetic and copies ran while one was open for 30% -> 28% of each run, Pallas kernels for 0% -> 0%
where the time goes in v3:
time: 532 us; the launch traced here: 522 us
  waiting for transfers between devices  187 us (35%)
  local copies, waits for them, and re-layouts  97.6 us (18%)
  starting transfers between devices  83.1 us (16%)
  other arithmetic  68.8 us (13%)
  matrix products  67.6 us (13%)
  between operations  17.4 us (3%)
    ppermute x50, waiting for transfers between devices, trade(): return lax.ppermute(value, ('section', name), route)  185 us
    ppermute x50, starting transfers between devices, trade(): return lax.ppermute(value, ('section', name), route)  57 us
    ppermute x19, starting transfers between devices, swap(): return lax.ppermute(value, 'section', [(0, 1), (1, 0)])  26.1 us
    unnamed x203, local copies, waits for them, and re-layouts  22.8 us
    dot_general x8, matrix products, transpose_dot(): lax.dot_general(left, right, (((0,), (0,)), ((), ())), preferred_element_...  19.2 us
    dot_general x8, matrix products, dot(): return jnp.dot(left, right, preferred_element_type=F32)  18.2 us
    dot_general x8, matrix products, dot_transposed(): lax.dot_general(left, right, (((1,), (1,)), ((), ())), preferred_element_...  17.6 us
    dynamic_update_slice x61, local copies, waits for them, and re-layouts, put(): return lax.dynamic_update_slice(whole, jnp.expand_dims(piece, dim), start)  15.6 us
  transfers between devices with their start and end apart: 70, of which 32 were waited for; matrix products, arithmetic and copies ran while one was open for 28% of the time, Pallas kernels for 0%

profile of v3, /device:TPU:1, one launch (start us, length us, event | category | flops | bytes accessed | tf_op | source)
XLA Modules:
  0.0 521.8 jit_solution(276787879363104809)
XLA Ops:
  8.0 5.4 %concatenate.65 = bf16[768]{0:T(1024)(128)(2,1)S(1)} concatenate(bf16[64]{0:T(256)(128)(2,1)} %bitcast.797, bf16[64]{0:T(256)(128)(2,1)} %bitcast.798, bf16[64]{0:T(256)(128)(2,1)} %bitcast.799, bf16[64]{0:T(256)(128)(2,1)} %bitcast.800, bf16[64]{0:T(256)(128)(2,1)} %bitcast.801, bf16[64]{0:T(256)(128)(2,1)} %bitcast.802, bf16[64]{0:T(256)(128)(2,1)} %bitcast.803, ...), dimensions={0} | concatenate | bytes 3072 | tf_op jit(solution)/shard_map/concatenate | solution.py:277
  23.4 3.8 collective-permute-start.10
  27.8 3.9 collective-permute-done.15
  31.9 3.8 collective-permute-done.16
  36.6 5.8 %collective-permute-done.17 = bf16[4,32,1024]{2,1,0:T(8,128)(2,1)S(1)} collective-permute-done((bf16[4,32,1024]{2,1,0:T(8,128)(2,1)S(1)}, bf16[4,32,1024]{2,1,0:T(8,128)(2,1)S(1)}, u32[]{:S(2)}, u32[]{:S(2)}) %collective-permute-start.17) | collective-permute-done | bytes 262176 | tf_op jit(solution)/shard_map/ppermute | solution.py:234
  57.7 11.9 %collective-permute-done.28 = bf16[64,2048]{1,0:T(8,128)(2,1)S(1)} collective-permute-done((bf16[64,2048]{1,0:T(8,128)(2,1)S(1)}, bf16[64,2048]{1,0:T(8,128)(2,1)S(1)}, u32[]{:S(2)}, u32[]{:S(2)}) %collective-permute-start.28) | collective-permute-done | bytes 262176 | tf_op jit(solution)/shard_map/ppermute | solution.py:234
  75.5 7.8 %collective-permute-done.33 = bf16[2,32,1024]{2,1,0:T(8,128)(2,1)S(1)} collective-permute-done((bf16[2,32,1024]{2,1,0:T(8,128)(2,1)S(1)}, bf16[2,32,1024]{2,1,0:T(8,128)(2,1)S(1)}, u32[]{:S(2)}, u32[]{:S(2)}) %collective-permute-start.33) | collective-permute-done | bytes 131104 | tf_op jit(solution)/shard_map/ppermute | solution.py:234
  92.4 6.4 %collective-permute-done.23 = bf16[2,64,2176]{2,1,0:T(8,128)(2,1)S(1)} collective-permute-done((bf16[2,64,2176]{2,1,0:T(8,128)(2,1)S(1)}, bf16[2,64,2176]{2,1,0:T(8,128)(2,1)S(1)}, u32[]{:S(2)}, u32[]{:S(2)}) %collective-permute-start.23) | collective-permute-done | bytes 557088 | tf_op jit(solution)/shard_map/ppermute | solution.py:234
  99.7 4.6 collective-permute-done.35
  108.7 18.2 %collective-permute-done.13 = bf16[2,4,64,2048]{3,2,1,0:T(8,128)(2,1)S(1)} collective-permute-done((bf16[2,4,64,2048]{3,2,1,0:T(8,128)(2,1)S(1)}, bf16[2,4,64,2048]{3,2,1,0:T(8,128)(2,1)S(1)}, u32[]{:S(2)}, u32[]{:S(2)}) %collective-permute-start.13) | collective-permute-done | bytes 2097184 | tf_op jit(solution)/shard_map/ppermute | solution.py:234
  188.3 8.6 %collective-permute-done.31 = bf16[2,4,64,2048]{3,2,1,0:T(8,128)(2,1)S(1)} collective-permute-done((bf16[2,4,64,2048]{3,2,1,0:T(8,128)(2,1)S(1)}, bf16[2,4,64,2048]{3,2,1,0:T(8,128)(2,1)S(1)}, u32[]{:S(2)}, u32[]{:S(2)}) %collective-permute-start.31) | collective-permute-done | bytes 2097184 | tf_op jit(solution)/shard_map/ppermute | solution.py:234
  197.1 10.2 %collective-permute-done.37 = bf16[2,16,32,1024]{3,2,1,0:T(8,128)(2,1)S(1)} collective-permute-done((bf16[2,16,32,1024]{3,2,1,0:T(8,128)(2,1)S(1)}, bf16[2,16,32,1024]{3,2,1,0:T(8,128)(2,1)S(1)}, u32[]{:S(2)}, u32[]{:S(2)}) %collective-permute-start.37) | collective-permute-done | bytes 2097184 | tf_op jit(solution)/shard_map/ppermute | solution.py:234
  240.5 3.9 convolution_convert_fusion.11
  250.4 4.2 convert_reduce_fusion.1
  257.3 5.0 convolution_convert_fusion.2
  285.8 4.9 dynamic_update_slice.297
  296.0 3.5 convert_dynamic-update-slice_fusion
  309.9 3.5 convolution_convert_fusion.3
  348.5 3.3 convert_element_type.639
  354.3 28.0 %collective-permute-done.60 = bf16[2,16,32,1024]{3,2,1,0:T(8,128)(2,1)} collective-permute-done((bf16[2,16,32,1024]{3,2,1,0:T(8,128)(2,1)}, bf16[2,16,32,1024]{3,2,1,0:T(8,128)(2,1)}, u32[]{:S(2)}, u32[]{:S(2)}) %collective-permute-start.60) | collective-permute-done | bytes 2097184 | tf_op jit(solution)/shard_map/ppermute | solution.py:234
  388.4 10.4 %collective-permute-done.61 = bf16[16,32,1024]{2,1,0:T(8,128)(2,1)S(1)} collective-permute-done((bf16[16,32,1024]{2,1,0:T(8,128)(2,1)S(1)}, bf16[16,32,1024]{2,1,0:T(8,128)(2,1)S(1)}, u32[]{:S(2)}, u32[]{:S(2)}) %collective-permute-start.61) | collective-permute-done | bytes 1048608 | tf_op jit(solution)/shard_map/ppermute | solution.py:234
  402.5 8.1 %collective-permute-done.50 = bf16[4,64,2048]{2,1,0:T(8,128)(2,1)S(1)} collective-permute-done((bf16[4,64,2048]{2,1,0:T(8,128)(2,1)S(1)}, bf16[4,64,2048]{2,1,0:T(8,128)(2,1)S(1)}, u32[]{:S(2)}, u32[]{:S(2)}) %collective-permute-start.50) | collective-permute-done | bytes 1048608 | tf_op jit(solution)/shard_map/ppermute | solution.py:234
  418.3 10.3 %collective-permute-done.51 = bf16[2,64,2048]{2,1,0:T(8,128)(2,1)} collective-permute-done((bf16[2,64,2048]{2,1,0:T(8,128)(2,1)}, bf16[2,64,2048]{2,1,0:T(8,128)(2,1)}, u32[]{:S(2)}, u32[]{:S(2)}) %collective-permute-start.51) | collective-permute-done | bytes 524320 | tf_op jit(solution)/shard_map/ppermute | solution.py:234
  442.6 5.1 collective-permute-done.47
  450.7 4.7 collective-permute-done.48
  456.8 3.2 collective-permute-start.53
  463.2 4.2 collective-permute-start.43
  470.0 3.9 collective-permute-done.67
  473.9 3.2 collective-permute-done.54
  479.7 4.5 collective-permute-start.68
  486.1 9.5 %collective-permute-done.56 = bf16[2,2,16,4224]{3,2,1,0:T(8,128)(2,1)S(1)} collective-permute-done((bf16[2,2,16,4224]{3,2,1,0:T(8,128)(2,1)S(1)}, bf16[2,2,16,4224]{3,2,1,0:T(8,128)(2,1)S(1)}, u32[]{:S(2)}, u32[]{:S(2)}) %collective-permute-start.56) | collective-permute-done | bytes 540704 | tf_op jit(solution)/shard_map/ppermute | solution.py:234
  495.7 8.2 %collective-permute-start.57 = (bf16[64,4224]{1,0:T(8,128)(2,1)S(1)}, bf16[64,4224]{1,0:T(8,128)(2,1)S(1)}, u32[]{:S(2)}, u32[]{:S(2)}) collective-permute-start(bf16[64,4224]{1,0:T(8,128)(2,1)S(1)} %bitcast.773), channel_id=1, source_target_pairs={{0,64},{64,0},{1,65},{65,1},{2,66},{66,2},{3,67},{67,3},{4,68},{68... | collective-permute-start | bytes 1622024 | tf_op jit(solution)/shard_map/ppermute | solution.py:17
  (682 shorter events, 282.5 us)
Async XLA Ops:
  7.2 448.4 %reduce-scatter.2.cloned.1.call-start = ((), (), s32[]{:S(2)}) async-start(), calls=%async_computation.1 | async-start | bytes 9191424 | tf_op jit(solution)/shard_map/reduce_scatter | solution.py:388
  20.1 16.1 %collective-permute-start.3 = (bf16[64,2176]{1,0:T(8,128)(2,1)S(1)}, bf16[64,2176]{1,0:T(8,128)(2,1)S(1)}, u32[]{:S(2)}, u32[]{:S(2)}) collective-permute-start(bf16[64,2176]{1,0:T(8,128)(2,1)S(1)} %get-tuple-element.181), channel_id=1, source_target_pairs={{0,1},{1,0},{2,3},{3,2},{4,5},{5,4},{6,7},{7,6},{8,9},{9,8},{10,11... | collective-permute-start | bytes 835592 | tf_op jit(solution)/shard_map/ppermute | solution.py:234
  45.1 54.1 %collective-permute-start.5 = (bf16[4,64,2176]{2,1,0:T(8,128)(2,1)S(1)}, bf16[4,64,2176]{2,1,0:T(8,128)(2,1)S(1)}, u32[]{:S(2)}, u32[]{:S(2)}) collective-permute-start(bf16[4,64,2176]{2,1,0:T(8,128)(2,1)S(1)} %slice_dynamic-update-slice_fusion.6), channel_id=1, source_target_pairs={{0,4},{1,5},{2,6},{3,7},{4,0},{5,1},{6,2},{7,3},{8,12},{9,13},{10,... | collective-permute-start | bytes 3342344 | tf_op jit(solution)/shard_map/ppermute | solution.py:234
  47.6 26.3 %collective-permute-start.22 = (bf16[64,2176]{1,0:T(8,128)(2,1)S(1)}, bf16[64,2176]{1,0:T(8,128)(2,1)S(1)}, u32[]{:S(2)}, u32[]{:S(2)}) collective-permute-start(bf16[64,2176]{1,0:T(8,128)(2,1)S(1)} %get-tuple-element.27), channel_id=1, source_target_pairs={{0,1},{1,0},{2,3},{3,2},{4,5},{5,4},{6,7},{7,6},{8,9},{9,8},{10,11... | collective-permute-start | bytes 835592 | tf_op jit(solution)/shard_map/ppermute | solution.py:234
  49.2 49.6 %collective-permute-start.12 = (bf16[4,64,2048]{2,1,0:T(8,128)(2,1)S(1)}, bf16[4,64,2048]{2,1,0:T(8,128)(2,1)S(1)}, u32[]{:S(2)}, u32[]{:S(2)}) collective-permute-start(bf16[4,64,2048]{2,1,0:T(8,128)(2,1)S(1)} %slice_dynamic-update-slice_fusion.12), channel_id=1, source_target_pairs={{0,1},{1,0},{2,3},{3,2},{4,5},{5,4},{6,7},{7,6},{8,9},{9,8},{10,11... | collective-permute-start | bytes 3145736 | tf_op jit(solution)/shard_map/ppermute | solution.py:234
  51.3 18.3 %collective-permute-start.28 = (bf16[64,2048]{1,0:T(8,128)(2,1)S(1)}, bf16[64,2048]{1,0:T(8,128)(2,1)S(1)}, u32[]{:S(2)}, u32[]{:S(2)}) collective-permute-start(bf16[64,2048]{1,0:T(8,128)(2,1)S(1)} %bitcast_select_fusion.2), channel_id=1, source_target_pairs={{0,4},{1,5},{2,6},{3,7},{4,0},{5,1},{6,2},{7,3},{8,12},{9,13},{10,... | collective-permute-start | bytes 786440 | tf_op jit(solution)/shard_map/ppermute | solution.py:234
  54.4 51.4 %collective-permute-start.19 = (bf16[16,32,1024]{2,1,0:T(8,128)(2,1)S(1)}, bf16[16,32,1024]{2,1,0:T(8,128)(2,1)S(1)}, u32[]{:S(2)}, u32[]{:S(2)}) collective-permute-start(bf16[16,32,1024]{2,1,0:T(8,128)(2,1)S(1)} %bitcast.718), channel_id=1, source_target_pairs={{0,16},{16,0},{32,48},{48,32},{64,112},{80,96},{96,80},{112,64},{1... | collective-permute-start | bytes 3145736 | tf_op jit(solution)/shard_map/ppermute | solution.py:234
  73.9 17.0 %collective-permute-start.29 = (bf16[2,64,2048]{2,1,0:T(8,128)(2,1)S(1)}, bf16[2,64,2048]{2,1,0:T(8,128)(2,1)S(1)}, u32[]{:S(2)}, u32[]{:S(2)}) collective-permute-start(bf16[2,64,2048]{2,1,0:T(8,128)(2,1)S(1)} %pad_maximum_fusion.27), channel_id=1, source_target_pairs={{0,12},{1,13},{2,14},{3,15},{4,8},{5,9},{6,10},{7,11},{8,4},{9,5},... | collective-permute-start | bytes 1572872 | tf_op jit(solution)/shard_map/ppermute | solution.py:234
  99.0 27.9 %collective-permute-start.13 = (bf16[2,4,64,2048]{3,2,1,0:T(8,128)(2,1)S(1)}, bf16[2,4,64,2048]{3,2,1,0:T(8,128)(2,1)S(1)}, u32[]{:S(2)}, u32[]{:S(2)}) collective-permute-start(bf16[2,4,64,2048]{3,2,1,0:T(8,128)(2,1)S(1)} %pad_maximum_fusion.3), channel_id=1, source_target_pairs={{0,3},{1,2},{2,1},{3,0},{4,7},{5,6},{6,5},{7,4},{8,11},{9,10},{10,... | collective-permute-start | bytes 6291464 | tf_op jit(solution)/shard_map/ppermute | solution.py:234
  99.5 30.3 %collective-permute-start.6 = (bf16[2,4,64,2176]{3,2,1,0:T(8,128)(2,1)S(1)}, bf16[2,4,64,2176]{3,2,1,0:T(8,128)(2,1)S(1)}, u32[]{:S(2)}, u32[]{:S(2)}) collective-permute-start(bf16[2,4,64,2176]{3,2,1,0:T(8,128)(2,1)S(1)} %pad_maximum_fusion), channel_id=1, source_target_pairs={{0,12},{1,13},{2,14},{3,15},{4,8},{5,9},{6,10},{7,11},{8,4},{9,5},... | collective-permute-start | bytes 6684680 | tf_op jit(solution)/shard_map/ppermute | solution.py:234
  107.4 49.7 %collective-permute-start.20 = (bf16[2,16,32,1024]{3,2,1,0:T(8,128)(2,1)}, bf16[2,16,32,1024]{3,2,1,0:T(8,128)(2,1)}, u32[]{:S(2)}, u32[]{:S(2)}) collective-permute-start(bf16[2,16,32,1024]{3,2,1,0:T(8,128)(2,1)} %pad_maximum_fusion.4), channel_id=1, source_target_pairs={{0,48},{16,32},{32,16},{48,0},{64,80},{80,64},{96,112},{112,96},{1... | collective-permute-start | bytes 6291464 | tf_op jit(solution)/shard_map/ppermute | solution.py:234
  127.2 43.4 %collective-permute-start.30 = (bf16[4,64,2048]{2,1,0:T(8,128)(2,1)S(1)}, bf16[4,64,2048]{2,1,0:T(8,128)(2,1)S(1)}, u32[]{:S(2)}, u32[]{:S(2)}) collective-permute-start(bf16[4,64,2048]{2,1,0:T(8,128)(2,1)S(1)} %slice_dynamic-update-slice_fusion.8), channel_id=1, source_target_pairs={{0,1},{1,0},{2,3},{3,2},{4,5},{5,4},{6,7},{7,6},{8,9},{9,8},{10,11... | collective-permute-start | bytes 3145736 | tf_op jit(solution)/shard_map/ppermute | solution.py:234
  135.5 47.7 %collective-permute-start.24 = (bf16[4,64,2176]{2,1,0:T(8,128)(2,1)S(1)}, bf16[4,64,2176]{2,1,0:T(8,128)(2,1)}, u32[]{:S(2)}, u32[]{:S(2)}) collective-permute-start(bf16[4,64,2176]{2,1,0:T(8,128)(2,1)S(1)} %slice_dynamic-update-slice_fusion.4), channel_id=1, source_target_pairs={{0,4},{1,5},{2,6},{3,7},{4,0},{5,1},{6,2},{7,3},{8,12},{9,13},{10,... | collective-permute-start | bytes 3342344 | tf_op jit(solution)/shard_map/ppermute | solution.py:234
  153.2 15.4 %collective-permute-start.7 = (bf16[512,512]{1,0:T(8,128)(2,1)}, bf16[512,512]{1,0:T(8,128)(2,1)}, u32[]{:S(2)}, u32[]{:S(2)}) collective-permute-start(bf16[512,512]{1,0:T(8,128)(2,1)} %broadcast_select_fusion.16), channel_id=1, source_target_pairs={{0,64},{64,0},{1,65},{65,1},{2,66},{66,2},{3,67},{67,3},{4,68},{68... | collective-permute-start | bytes 1572872 | tf_op jit(solution)/shard_map/ppermute | solution.py:17
  161.2 19.4 %collective-permute-start.36 = (bf16[16,32,1024]{2,1,0:T(8,128)(2,1)}, bf16[16,32,1024]{2,1,0:T(8,128)(2,1)S(1)}, u32[]{:S(2)}, u32[]{:S(2)}) collective-permute-start(bf16[16,32,1024]{2,1,0:T(8,128)(2,1)} %bitcast.90), channel_id=1, source_target_pairs={{0,16},{16,0},{32,48},{48,32},{64,112},{80,96},{96,80},{112,64},{1... | collective-permute-start | bytes 3145736 | tf_op jit(solution)/shard_map/ppermute | solution.py:234
  171.2 25.7 %collective-permute-start.31 = (bf16[2,4,64,2048]{3,2,1,0:T(8,128)(2,1)S(1)}, bf16[2,4,64,2048]{3,2,1,0:T(8,128)(2,1)S(1)}, u32[]{:S(2)}, u32[]{:S(2)}) collective-permute-start(bf16[2,4,64,2048]{3,2,1,0:T(8,128)(2,1)S(1)} %pad_maximum_fusion.5), channel_id=1, source_target_pairs={{0,3},{1,2},{2,1},{3,0},{4,7},{5,6},{6,5},{7,4},{8,11},{9,10},{10,... | collective-permute-start | bytes 6291464 | tf_op jit(solution)/shard_map/ppermute | solution.py:234
  182.0 25.3 %collective-permute-start.37 = (bf16[2,16,32,1024]{3,2,1,0:T(8,128)(2,1)S(1)}, bf16[2,16,32,1024]{3,2,1,0:T(8,128)(2,1)S(1)}, u32[]{:S(2)}, u32[]{:S(2)}) collective-permute-start(bf16[2,16,32,1024]{3,2,1,0:T(8,128)(2,1)S(1)} %pad_maximum_fusion.6), channel_id=1, source_target_pairs={{0,48},{16,32},{32,16},{48,0},{64,80},{80,64},{96,112},{112,96},{1... | collective-permute-start | bytes 6291464 | tf_op jit(solution)/shard_map/ppermute | solution.py:234
  184.7 26.7 %collective-permute-start.25 = (bf16[2,4,64,2176]{3,2,1,0:T(8,128)(2,1)S(1)}, bf16[2,4,64,2176]{3,2,1,0:T(8,128)(2,1)S(1)}, u32[]{:S(2)}, u32[]{:S(2)}) collective-permute-start(bf16[2,4,64,2176]{3,2,1,0:T(8,128)(2,1)S(1)} %pad_maximum_fusion.1), channel_id=1, source_target_pairs={{0,12},{1,13},{2,14},{3,15},{4,8},{5,9},{6,10},{7,11},{8,4},{9,5},... | collective-permute-start | bytes 6684680 | tf_op jit(solution)/shard_map/ppermute | solution.py:234
  214.7 16.2 %collective-permute-start.26 = (bf16[512,512]{1,0:T(8,128)(2,1)}, bf16[512,512]{1,0:T(8,128)(2,1)}, u32[]{:S(2)}, u32[]{:S(2)}) collective-permute-start(bf16[512,512]{1,0:T(8,128)(2,1)} %broadcast_select_fusion.12), channel_id=1, source_target_pairs={{0,64},{64,0},{1,65},{65,1},{2,66},{66,2},{3,67},{67,3},{4,68},{68... | collective-permute-start | bytes 1572872 | tf_op jit(solution)/shard_map/ppermute | solution.py:17
  279.6 19.8 %collective-permute-start.40 = (bf16[256,1024]{1,0:T(8,128)(2,1)}, bf16[256,1024]{1,0:T(8,128)(2,1)}, u32[]{:S(2)}, u32[]{:S(2)}) collective-permute-start(bf16[256,1024]{1,0:T(8,128)(2,1)} %fusion.61), channel_id=1, source_target_pairs={{0,64},{64,0},{1,65},{65,1},{2,66},{66,2},{3,67},{67,3},{4,68},{68... | collective-permute-start | bytes 1572872 | tf_op jit(solution)/shard_map/ppermute | solution.py:17
  315.5 69.3 %collective-permute-start.49 = (bf16[2,4,64,2048]{3,2,1,0:T(8,128)(2,1)}, bf16[2,4,64,2048]{3,2,1,0:T(8,128)(2,1)}, u32[]{:S(2)}, u32[]{:S(2)}) collective-permute-start(bf16[2,4,64,2048]{3,2,1,0:T(8,128)(2,1)} %pad_maximum_fusion.7), channel_id=1, source_target_pairs={{0,1},{1,0},{2,3},{3,2},{4,5},{5,4},{6,7},{7,6},{8,9},{9,8},{10,11... | collective-permute-start | bytes 6291464 | tf_op jit(solution)/shard_map/ppermute | solution.py:234
  321.8 26.7 %collective-permute-start.58 = (bf16[2,16,32,1024]{3,2,1,0:T(8,128)(2,1)}, bf16[2,16,32,1024]{3,2,1,0:T(8,128)(2,1)}, u32[]{:S(2)}, u32[]{:S(2)}) collective-permute-start(bf16[2,16,32,1024]{3,2,1,0:T(8,128)(2,1)} %pad_maximum_fusion.8), channel_id=1, source_target_pairs={{0,16},{16,0},{32,48},{48,32},{64,112},{80,96},{96,80},{112,64},{1... | collective-permute-start | bytes 6291464 | tf_op jit(solution)/shard_map/ppermute | solution.py:234
  325.3 57.0 %collective-permute-start.60 = (bf16[2,16,32,1024]{3,2,1,0:T(8,128)(2,1)}, bf16[2,16,32,1024]{3,2,1,0:T(8,128)(2,1)}, u32[]{:S(2)}, u32[]{:S(2)}) collective-permute-start(bf16[2,16,32,1024]{3,2,1,0:T(8,128)(2,1)} %pad_maximum_fusion.9), channel_id=1, source_target_pairs={{0,16},{16,0},{32,48},{48,32},{64,112},{80,96},{96,80},{112,64},{1... | collective-permute-start | bytes 6291464 | tf_op jit(solution)/shard_map/ppermute | solution.py:234
  352.2 35.7 %collective-permute-start.59 = (bf16[16,32,1024]{2,1,0:T(8,128)(2,1)S(1)}, bf16[16,32,1024]{2,1,0:T(8,128)(2,1)S(1)}, u32[]{:S(2)}, u32[]{:S(2)}) collective-permute-start(bf16[16,32,1024]{2,1,0:T(8,128)(2,1)S(1)} %fusion.40), channel_id=1, source_target_pairs={{0,48},{16,32},{32,16},{48,0},{64,80},{80,64},{96,112},{112,96},{1... | collective-permute-start | bytes 3145736 | tf_op jit(solution)/shard_map/ppermute | solution.py:234
  352.5 58.6 %collective-permute-start.45 = (bf16[2,4,64,2176]{3,2,1,0:T(8,128)(2,1)S(1)}, bf16[2,4,64,2176]{3,2,1,0:T(8,128)(2,1)S(1)}, u32[]{:S(2)}, u32[]{:S(2)}) collective-permute-start(bf16[2,4,64,2176]{3,2,1,0:T(8,128)(2,1)S(1)} %pad_maximum_fusion.2), channel_id=1, source_target_pairs={{0,4},{1,5},{2,6},{3,7},{4,0},{5,1},{6,2},{7,3},{8,12},{9,13},{10,... | collective-permute-start | bytes 6684680 | tf_op jit(solution)/shard_map/ppermute | solution.py:234
  384.7 14.1 %collective-permute-start.61 = (bf16[16,32,1024]{2,1,0:T(8,128)(2,1)S(1)}, bf16[16,32,1024]{2,1,0:T(8,128)(2,1)S(1)}, u32[]{:S(2)}, u32[]{:S(2)}) collective-permute-start(bf16[16,32,1024]{2,1,0:T(8,128)(2,1)S(1)} %fusion.35), channel_id=1, source_target_pairs={{0,48},{16,32},{32,16},{48,0},{64,80},{80,64},{96,112},{112,96},{1... | collective-permute-start | bytes 3145736 | tf_op jit(solution)/shard_map/ppermute | solution.py:234
  387.8 22.8 %collective-permute-start.50 = (bf16[4,64,2048]{2,1,0:T(8,128)(2,1)S(1)}, bf16[4,64,2048]{2,1,0:T(8,128)(2,1)S(1)}, u32[]{:S(2)}, u32[]{:S(2)}) collective-permute-start(bf16[4,64,2048]{2,1,0:T(8,128)(2,1)S(1)} %fusion.45), channel_id=1, source_target_pairs={{0,3},{1,2},{2,1},{3,0},{4,7},{5,6},{6,5},{7,4},{8,11},{9,10},{10,... | collective-permute-start | bytes 3145736 | tf_op jit(solution)/shard_map/ppermute | solution.py:234
  400.7 29.1 %collective-permute-start.62 = (bf16[2,2,4,32,1024]{4,3,1,2,0:T(8,128)(2,1)}, bf16[2,2,4,32,1024]{4,3,1,2,0:T(8,128)(2,1)}, u32[]{:S(2)}, u32[]{:S(2)}) collective-permute-start(bf16[2,2,4,32,1024]{4,3,1,2,0:T(8,128)(2,1)} %pad_maximum_fusion.14), channel_id=1, source_target_pairs={{0,4},{1,5},{2,6},{3,7},{4,0},{5,1},{6,2},{7,3},{8,12},{9,13},{10,... | collective-permute-start | bytes 3145736 | tf_op jit(solution)/shard_map/ppermute | solution.py:234
  414.0 21.6 %collective-permute-start.46 = (bf16[4,64,2176]{2,1,0:T(8,128)(2,1)}, bf16[4,64,2176]{2,1,0:T(8,128)(2,1)}, u32[]{:S(2)}, u32[]{:S(2)}) collective-permute-start(bf16[4,64,2176]{2,1,0:T(8,128)(2,1)} %fusion.76), channel_id=1, source_target_pairs={{0,12},{1,13},{2,14},{3,15},{4,8},{5,9},{6,10},{7,11},{8,4},{9,5},... | collective-permute-start | bytes 3342344 | tf_op jit(solution)/shard_map/ppermute | solution.py:234
  414.9 13.8 %collective-permute-start.51 = (bf16[2,64,2048]{2,1,0:T(8,128)(2,1)}, bf16[2,64,2048]{2,1,0:T(8,128)(2,1)}, u32[]{:S(2)}, u32[]{:S(2)}) collective-permute-start(bf16[2,64,2048]{2,1,0:T(8,128)(2,1)} %pad_maximum_fusion.29), channel_id=1, source_target_pairs={{0,4},{1,5},{2,6},{3,7},{4,0},{5,1},{6,2},{7,3},{8,12},{9,13},{10,... | collective-permute-start | bytes 1572872 | tf_op jit(solution)/shard_map/ppermute | solution.py:234
  463.2 40.8 %collective-permute-start.43 = (bf16[256,1024]{1,0:T(8,128)(2,1)S(1)}, bf16[256,1024]{1,0:T(8,128)(2,1)S(1)}, u32[]{:S(2)}, u32[]{:S(2)}) collective-permute-start(bf16[256,1024]{1,0:T(8,128)(2,1)S(1)} %fusion.58), channel_id=1, source_target_pairs={{0,64},{64,0},{1,65},{65,1},{2,66},{66,2},{3,67},{67,3},{4,68},{68... | collective-permute-start | bytes 1572872 | tf_op jit(solution)/shard_map/ppermute | solution.py:17
  479.7 25.4 %collective-permute-start.68 = (bf16[128,1024]{1,0:T(8,128)(2,1)S(1)}, bf16[128,1024]{1,0:T(8,128)(2,1)S(1)}, u32[]{:S(2)}, u32[]{:S(2)}) collective-permute-start(bf16[128,1024]{1,0:T(8,128)(2,1)S(1)} %bitcast.791), channel_id=1, source_target_pairs={{0,64},{64,0},{1,65},{65,1},{2,66},{66,2},{3,67},{67,3},{4,68},{68... | collective-permute-start | bytes 786440 | tf_op jit(solution)/shard_map/ppermute | solution.py:17
  (135 other events, 731.4 us)
Sparse Core Ops, SparseCore 0:
  317.2 92.7 reduce-scatter.1

commit v4 on v3

v4 whole, which is shorter than its diff:
```python
import jax
import jax.numpy as jnp
from jax import lax
from jax.sharding import PartitionSpec as P


HEAD_DIM = 64
EPSILON = 1e-06
TAU = 6.283185307179586
LANES = 128
RING = 4
BF = jnp.bfloat16
F32 = jnp.float32


def swap(value):
    return lax.ppermute(value, "section", [(0, 1), (1, 0)])


def pair_sum(part):
    low = part.astype(BF)
    other = swap(low)
    return low.astype(F32) + other.astype(F32)


def dot(left, right):
    return jnp.dot(left, right, preferred_element_type=F32)


def transpose_dot(left, right):
    return lax.dot_general(left, right, (((0,), (0,)), ((), ())), preferred_element_type=F32)


def dot_transposed(left, right):
    return lax.dot_general(left, right, (((1,), (1,)), ((), ())), preferred_element_type=F32)


def norm_rows(values):
    centered = values - jnp.mean(values, axis=-1, keepdims=True)
    inverse = lax.rsqrt(jnp.mean(centered * centered, axis=-1, keepdims=True) + EPSILON)
    return (centered * inverse, inverse)


def norm_back(grad_norm, normed, inverse):
    return inverse * (
        grad_norm
        - jnp.mean(grad_norm, axis=-1, keepdims=True)
        - normed * jnp.mean(grad_norm * normed, axis=-1, keepdims=True)
    )


def heads_of(packed, number, count):
    width = packed.shape[1] // 3
    piece = packed[:, number * width : (number + 1) * width]
    return piece.reshape(count, -1, width // HEAD_DIM, HEAD_DIM).transpose(0, 2, 1, 3)


def join_heads(parts):
    count, heads, rows, size = parts.shape
    return parts.transpose(0, 2, 1, 3).reshape(count * rows, heads * size)


def masked_scores(queries, keys, seq_lengths):
    scores = jnp.einsum("nhqd,nhkd->nhqk", queries, keys, preferred_element_type=F32)
    scores = scores * HEAD_DIM ** (-0.5)
    positions = lax.broadcasted_iota(jnp.int32, scores.shape, 3)
    return jnp.where(positions < seq_lengths[:, None, None, None], scores, -1000000000.0)


def forward_attention(inputs, weights, seq_lengths):
    count = seq_lengths.shape[0]
    packed = (dot(inputs, weights["qkv"]) + weights["bias_qkv"]).astype(BF)
    queries, keys, values = (heads_of(packed, n, count) for n in range(3))
    scores = masked_scores(queries, keys, seq_lengths)
    row_max = jnp.max(scores, axis=-1, keepdims=True)
    exponent = jnp.exp(scores - row_max)
    soft_weights = exponent / jnp.sum(exponent, axis=-1, keepdims=True)
    attended = jnp.einsum(
        "nhqk,nhkd->nhqd", soft_weights.astype(BF), values, preferred_element_type=F32
    )
    attended = join_heads(attended.astype(BF))
    return (attended, dict(inputs=inputs, qkv=(queries, keys, values), soft_weights=soft_weights))


def forward_hidden(attended, kept, weights):
    branch = pair_sum(dot(attended, weights["out"])) + weights["bias_out"]
    normed, inverse = norm_rows(kept["inputs"].astype(F32) + branch)
    hidden = (normed * weights["gain_attn"] + weights["shift_attn"]).astype(BF)
    upward = dot(hidden, weights["up"]) + weights["bias_up"]
    share = 0.5 + 0.5 * lax.erf(upward * 0.5**0.5)
    activated = (upward * share).astype(BF)
    slope = share + upward * jnp.exp(-0.5 * upward * upward) * TAU ** (-0.5)
    kept.update(attended=attended, normed_attn=normed, inverse_attn=inverse)
    kept.update(hidden=hidden, slope=slope)
    return activated


def forward_output(activated, kept, weights):
    mixed = pair_sum(dot(activated, weights["down"])) + weights["bias_down"]
    normed, inverse = norm_rows(kept["hidden"].astype(F32) + mixed)
    kept.update(activated=activated, normed_mlp=normed, inverse_mlp=inverse)
    return (normed * weights["gain_mlp"] + weights["shift_mlp"]).astype(BF)


def backward_mlp(grad_result, kept, weights):
    grad_result = grad_result.astype(F32)
    normed = kept["normed_mlp"]
    grad_gain = jnp.sum(grad_result * normed, axis=0)
    grad_shift = jnp.sum(grad_result, axis=0)
    grad_resid = norm_back(grad_result * weights["gain_mlp"], normed, kept["inverse_mlp"])
    grad_mixed = grad_resid.astype(BF)
    grad_upward = (dot_transposed(grad_mixed, weights["down"]) * kept["slope"]).astype(BF)
    passed = dot_transposed(grad_upward, weights["up"])
    grads = dict(
        down=transpose_dot(kept["activated"], grad_mixed).astype(BF),
        up=transpose_dot(kept["hidden"], grad_upward).astype(BF),
        bias_up=jnp.sum(grad_upward.astype(F32), axis=0),
        bias_down=jnp.sum(grad_mixed.astype(F32), axis=0),
        gain_mlp=grad_gain,
        shift_mlp=grad_shift,
    )
    return (grad_resid + pair_sum(passed), grads)


def backward_attention(grad_hidden, grads, kept, weights):
    scaling = HEAD_DIM ** (-0.5)
    normed = kept["normed_attn"]
    grad_resid = norm_back(grad_hidden * weights["gain_attn"], normed, kept["inverse_attn"])
    grad_branch = grad_resid.astype(BF)
    grads.update(
        gain_attn=jnp.sum(grad_hidden * normed, axis=0),
        shift_attn=jnp.sum(grad_hidden, axis=0),
        bias_out=jnp.sum(grad_branch.astype(F32), axis=0),
        out=transpose_dot(kept["attended"], grad_branch).astype(BF),
    )
    queries, keys, values = kept["qkv"]
    count = queries.shape[0]
    grad_attended = dot_transposed(grad_branch, weights["out"]).astype(BF)
    grad_attended = grad_attended.reshape(count, -1, queries.shape[1], HEAD_DIM)
    grad_attended = grad_attended.transpose(0, 2, 1, 3)
    soft_weights = kept["soft_weights"]
    grad_values = jnp.einsum(
        "nhqk,nhqd->nhkd", soft_weights.astype(BF), grad_attended, preferred_element_type=F32
    )
    grad_soft = jnp.einsum(
        "nhqd,nhkd->nhqk", grad_attended, values, preferred_element_type=F32
    )
    grad_scores = soft_weights * (
        grad_soft - jnp.sum(grad_soft * soft_weights, axis=-1, keepdims=True)
    )
    grad_scores = grad_scores.astype(BF)
    grad_queries = scaling * jnp.einsum(
        "nhqk,nhkd->nhqd", grad_scores, keys, preferred_element_type=F32
    )
    grad_keys = scaling * jnp.einsum(
        "nhqk,nhqd->nhkd", grad_scores, queries, preferred_element_type=F32
    )
    grad_packed = jnp.concatenate(
        [join_heads(g.astype(BF)) for g in (grad_queries, grad_keys, grad_values)], axis=1
    )
    return (grad_resid, grad_packed)


def backward_inputs(grad_resid, grad_packed, grads, kept, weights):
    columns = jnp.sum(grad_packed.astype(F32), axis=0)
    width = columns.shape[0] // 3
    grads.update(
        bias_q=columns[:width],
        bias_v=columns[2 * width :],
        qkv=transpose_dot(kept["inputs"], grad_packed).astype(BF),
    )
    passed = dot_transposed(grad_packed, weights["qkv"])
    return (grad_resid + pair_sum(passed)).astype(BF)


def per_device(
    tokens,
    lengths,
    cotangent,
    w_qkv,
    bias_q,
    bias_v,
    w_out,
    bias_out,
    gain_attn,
    shift_attn,
    w_up,
    bias_up,
    w_down,
    bias_down,
    gain_mlp,
    shift_mlp,
):
    first = lax.axis_index("section") == 0
    shards = lax.axis_size("shard")
    rows = w_qkv.shape[1]
    model = w_qkv.shape[2] // 3
    ff = w_up.shape[2]
    half = model // 2
    unit = ff // shards // 2
    vector_count = 8 * rows + 2 * unit

    def choose(low, high):
        return jnp.where(first, low, high)

    def mine_of(low, high):
        return (choose(low, high), choose(high, low))

    shard = lax.axis_index("shard")
    place = {"x": lax.axis_index("dp"), "y": shard % RING, "z": shard // RING}

    near = {axis: at ^ choose(1, 3) for axis, at in place.items()}
    far = {axis: at ^ choose(3, 1) for axis, at in place.items()}

    def trade(value, axis, masks):
        name = "dp" if axis == "x" else "shard"
        size = lax.axis_size(name)
        stride = RING if axis == "z" else 1
        route = []
        for core in range(2):
            for at in range(size):
                position = at // stride % RING
                target = at + ((position ^ masks[core]) - position) * stride
                route.append((core * size + at, core * size + target))
        return lax.ppermute(value, ("section", name), route)

    def after(value, earlier):
        return lax.optimization_barrier((value, earlier))[0]

    def put(whole, piece, at, dim):
        start = [0] * whole.ndim
        start[dim] = at
        return lax.dynamic_update_slice(whole, jnp.expand_dims(piece, dim), start)

    def gather_one(block, axis):
        return trade(block, axis, (1, 3))

    def gather_two(block, beside, axis):
        return trade(jnp.stack([block, beside]), axis, (3, 1))

    def gather_end(block, beside, across, axis, dim):
        whole = jnp.zeros(block.shape[:dim] + (RING,) + block.shape[dim:], block.dtype)
        whole = put(whole, block, place[axis], dim)
        whole = put(whole, beside, near[axis], dim)
        whole = put(whole, across[0], far[axis], dim)
        return put(whole, across[1], place[axis] ^ 2, dim)

    def chunk(value, at, dim):
        return lax.dynamic_index_in_dim(value, at, dim, keepdims=False)

    def scatter_one(value, axis, dim):
        sent = [chunk(value, near[axis], dim), chunk(value, place[axis] ^ 2, dim)]
        return trade(jnp.stack(sent), axis, (1, 3))

    def scatter_two(value, beside, axis, dim):
        sent = chunk(value, far[axis], dim).astype(F32) + beside[1].astype(F32)
        return trade(sent.astype(BF), axis, (3, 1))

    def scatter_end(value, beside, across, axis, dim):
        kept = chunk(value, place[axis], dim).astype(F32) + beside[0].astype(F32)
        return (kept + across.astype(F32)).astype(BF)

    def together(*values):
        return lax.optimization_barrier(values)

    def placed(width, pieces):
        whole = jnp.zeros((pieces[0][1].shape[0], width), BF)
        for at, piece in pieces:
            whole = lax.dynamic_update_slice(whole, piece, (0, at))
        return whole

    def parts_of(part):
        qkv = w_qkv[0].reshape(rows, 3, 2, half)[:, :, part].reshape(rows, 3 * half)
        out = w_out[0][:, part * half : (part + 1) * half]
        up = w_up[0].reshape(rows, shards, 2, unit)[:, :, part].reshape(rows, shards * unit)
        return (qkv, out, up, w_down[0][part * unit : (part + 1) * unit])

    vectors = jnp.concatenate(
        [
            v[0]
            for v in (
                bias_q,
                bias_v,
                bias_out,
                gain_attn,
                shift_attn,
                bias_down,
                gain_mlp,
                shift_mlp,
                bias_up,
            )
        ]
    )
    vectors = jnp.pad(vectors, (0, rows * LANES - vector_count)).reshape(rows, LANES)
    split = [mine_of(low, high) for low, high in zip(parts_of(0), parts_of(1))]
    kept_part = (vectors,) + tuple(low for low, high in split)
    sent_part = (vectors,) + tuple(high for low, high in split)
    got_part = tuple(swap(member) for member in sent_part)
    blocks = [mine_of(own, got) for own, got in zip(kept_part, got_part)]
    edges = (LANES, LANES + 3 * half, LANES + 4 * half, LANES + 4 * half + shards * unit)

    def joined(layer, count):
        return placed(edges[count - 1], list(zip((0,) + edges, [b[layer] for b in blocks[:count]])))

    quarter = unit // RING

    def quarter_of(block):
        return chunk(block.reshape(RING, quarter, model), place["x"], 0)

    a0, b0, c0 = (joined(0, 3), blocks[3][0], quarter_of(blocks[4][0]))
    a1, b1, c1 = (joined(1, 3), blocks[3][1], quarter_of(blocks[4][1]))
    an, bn, cn = together(gather_one(a0, "y"), gather_one(b0, "z"), gather_one(c0, "y"))
    af, bf, cf = together(
        gather_two(a0, an, "y"), gather_two(b0, bn, "z"), gather_two(c0, cn, "y")
    )
    a0 = gather_end(a0, an, af, "y", 0)
    b0 = gather_end(b0, bn, bf, "z", 0)
    c0 = gather_end(c0, cn, cf, "y", 0)
    an0, bn0, cn0 = together(gather_one(a0, "z"), gather_one(b0, "y"), gather_one(c0, "z"))
    af0, bf0, cf0 = (
        gather_two(a0, an0, "z"),
        gather_two(b0, bn0, "y"),
        gather_two(c0, cn0, "z"),
    )
    a1, b1, c1 = (after(a1, an0), after(b1, an0), after(c1, an0))
    an, bn, cn = together(gather_one(a1, "y"), gather_one(b1, "z"), gather_one(c1, "z"))
    af, bf, cf = together(
        gather_two(a1, an, "y"), gather_two(b1, bn, "z"), gather_two(c1, cn, "z")
    )
    c1 = gather_end(c1, cn, cf, "z", 0)
    cn1 = gather_one(c1, "y")
    cf1 = gather_two(c1, cn1, "y")
    a1 = gather_end(a1, an, af, "y", 0)
    b1 = gather_end(b1, bn, bf, "z", 0)
    af0, bf0, cf0, cf1 = together(af0, bf0, cf0, cf1)
    a0 = gather_end(a0, an0, af0, "z", 0)
    b0 = gather_end(b0, bn0, bf0, "y", 1)
    c0 = gather_end(c0, cn0, cf0, "z", 0).reshape(shards, quarter, model)
    c1 = gather_end(c1, cn1, cf1, "y", 1).reshape(shards, quarter, model)
    a1, b1 = (after(a1, af0), after(b1, bf0))

    def arranged(attn, up):
        attn, up = (attn.reshape(model, -1), up.reshape(model, -1))
        flat = attn[:, :LANES].reshape(shards, rows * LANES)[:, :vector_count].astype(F32)
        whole = [flat[:, n * rows : (n + 1) * rows].reshape(-1) for n in range(8)]
        bias_up_part = flat[:, 8 * rows :].reshape(shards, 2, unit)
        bias_up_part = choose(bias_up_part[:, 0], bias_up_part[:, 1]).reshape(-1)
        bias_q_part = choose(whole[0][:half], whole[0][half:])
        bias_v_part = choose(whole[1][:half], whole[1][half:])
        out = attn[:, edges[1] : edges[2]]
        held, handed = mine_of(out[:half], out[half:])
        arrived = swap(handed)
        return dict(
            qkv=attn[:, LANES : edges[1]],
            out=jnp.concatenate(mine_of(held, arrived), axis=1),
            up=up,
            bias_qkv=jnp.concatenate([bias_q_part, jnp.zeros_like(bias_q_part), bias_v_part]),
            bias_out=whole[2],
            gain_attn=whole[3],
            shift_attn=whole[4],
            bias_down=whole[5],
            gain_mlp=whole[6],
            shift_mlp=whole[7],
            bias_up=bias_up_part,
        )

    def side_by_side(grads):
        held, handed = mine_of(grads["out"][:, :half], grads["out"][:, half:])
        out = jnp.concatenate(mine_of(held, swap(handed)), axis=0)

        def widened(part):
            return jnp.concatenate([choose(part, 0.0), choose(0.0, part)])

        whole = [widened(grads["bias_q"]), widened(grads["bias_v"])]
        names = ("bias_out", "gain_attn", "shift_attn", "bias_down", "gain_mlp", "shift_mlp")
        whole += [0.5 * grads[name] for name in names]
        part = grads["bias_up"].reshape(shards, unit)
        spread = jnp.concatenate([choose(part, 0.0), choose(0.0, part)], axis=1)
        flat = jnp.concatenate([v.reshape(shards, rows) for v in whole] + [spread], axis=1)
        flat = jnp.pad(flat.astype(BF), ((0, 0), (0, rows * LANES - vector_count)))
        pieces = (flat.reshape(shards * rows, LANES), grads["qkv"], out)
        return placed(edges[2], list(zip((0,) + edges, pieces))).reshape(RING, RING, rows, -1)

    count = tokens.shape[0]
    seq_lengths = lengths[:, 0]

    first_weights = arranged(a0, b0)
    an, bn, cn = (gather_one(a1, "z"), gather_one(b1, "y"), gather_one(c0, "x"))
    attended, kept0 = forward_attention(tokens.reshape(-1, model), first_weights, seq_lengths)
    an, bn, cn, attended = together(an, bn, cn, attended)
    af, bf, cf = (gather_two(a1, an, "z"), gather_two(b1, bn, "y"), gather_two(c0, cn, "x"))
    activated = forward_hidden(attended, kept0, first_weights)
    af, bf, cf, activated = together(af, bf, cf, activated)
    first_weights["down"] = gather_end(c0, cn, cf, "x", 1).reshape(-1, model)
    cn = gather_one(after(c1, cf), "x")
    middle = forward_output(activated, kept0, first_weights)
    cn, middle = together(cn, middle)
    cf = gather_two(c1, cn, "x")
    second_weights = arranged(
        gather_end(a1, an, af, "z", 0), gather_end(b1, bn, bf, "y", 1)
    )
    attended, kept1 = forward_attention(middle, second_weights, seq_lengths)
    activated = forward_hidden(attended, kept1, second_weights)
    cf, activated = together(cf, activated)
    second_weights["down"] = gather_end(c1, cn, cf, "x", 1).reshape(-1, model)
    last = forward_output(activated, kept1, second_weights)

    def down_of(grads):
        return grads["down"].reshape(shards, RING, quarter, model)

    def up_of(grads):
        return grads["up"].reshape(RING, RING, rows, -1)

    grad_hidden, grads1 = backward_mlp(cotangent.reshape(-1, model), kept1, second_weights)
    c1, b1 = (down_of(grads1), up_of(grads1))
    cn, bn = (scatter_one(c1, "x", 1), scatter_one(b1, "y", 1))
    grad_resid, grad_packed = backward_attention(grad_hidden, grads1, kept1, second_weights)
    cn, bn, grad_packed = together(cn, bn, grad_packed)
    cf, bf = (scatter_two(c1, cn, "x", 1), scatter_two(b1, bn, "y", 1))
    grad_middle = backward_inputs(grad_resid, grad_packed, grads1, kept1, second_weights)
    a1 = side_by_side(grads1)
    a1, cf, bf, grad_middle = together(a1, cf, bf, grad_middle)
    c1, b1 = (scatter_end(c1, cn, cf, "x", 1), scatter_end(b1, bn, bf, "y", 1))
    an1 = scatter_one(a1, "z", 0)

    grad_hidden, grads0 = backward_mlp(grad_middle, kept0, first_weights)
    c0, b0 = (down_of(grads0), up_of(grads0))
    cn, bn = (scatter_one(c0, "x", 1), scatter_one(b0, "y", 1))
    an1, grad_hidden = together(an1, grad_hidden)
    af1 = scatter_two(a1, an1, "z", 0)
    grad_resid, grad_packed = backward_attention(grad_hidden, grads0, kept0, first_weights)
    af1, cn, bn, grad_packed = together(af1, cn, bn, grad_packed)
    a1 = scatter_end(a1, an1, af1, "z", 0)
    cf, bf = (scatter_two(c0, cn, "x", 1), scatter_two(b0, bn, "y", 1))
    grad_first = backward_inputs(grad_resid, grad_packed, grads0, kept0, first_weights)
    a0 = side_by_side(grads0)
    a0, cf, bf = together(a0, cf, bf)
    c0, b0 = (scatter_end(c0, cn, cf, "x", 1), scatter_end(b0, bn, bf, "y", 1))

    b = jnp.stack([b0, b1]).reshape(2, RING, RING, rows // RING, -1)
    c = jnp.stack([c0, c1]).reshape(2, RING, RING, quarter, model)
    an, bn, cn, dn = together(
        scatter_one(a0, "z", 0), scatter_one(b, "x", 2), scatter_one(c, "y", 2), scatter_one(a1, "y", 0)
    )
    af, bf, cf, df = together(
        scatter_two(a0, an, "z", 0),
        scatter_two(b, bn, "x", 2),
        scatter_two(c, cn, "y", 2),
        scatter_two(a1, dn, "y", 0),
    )
    a0 = scatter_end(a0, an, af, "z", 0)
    a1 = scatter_end(a1, dn, df, "y", 0).reshape(RING, rows // RING, -1)
    b, c = (scatter_end(b, bn, bf, "x", 2), scatter_end(c, cn, cf, "y", 2))
    an, bn, cn, dn = together(
        scatter_one(a0, "y", 0), scatter_one(b, "z", 1), scatter_one(c, "z", 1), scatter_one(a1, "x", 0)
    )
    af, bf, cf, df = together(
        scatter_two(a0, an, "y", 0),
        scatter_two(b, bn, "z", 1),
        scatter_two(c, cn, "z", 1),
        scatter_two(a1, dn, "x", 0),
    )
    a0 = scatter_end(a0, an, af, "y", 0).reshape(RING, rows // RING, -1)
    a1 = scatter_end(a1, dn, df, "x", 0)
    b, c = (scatter_end(b, bn, bf, "z", 1), scatter_end(c, cn, cf, "z", 1))
    c = c.reshape(2, rows // RING, -1)
    bc = jnp.concatenate([b, c], axis=2)
    an, bn = together(scatter_one(a0, "x", 0), gather_one(bc, "x"))
    af, bf = together(scatter_two(a0, an, "x", 0), gather_two(bc, bn, "x"))
    a = jnp.stack([scatter_end(a0, an, af, "x", 0), a1])
    bc = gather_end(bc, bn, bf, "x", 1)
    b = bc[..., : b.shape[2]].reshape(2, rows, -1)
    c = bc[..., b.shape[2] :].reshape(2, unit, model)
    an = gather_one(a, "x")
    af = gather_two(a, an, "x")
    a = gather_end(a, an, af, "x", 1).reshape(2, rows, -1)

    summed_first, summed_second = ((a[0], b[0], c[0]), (a[1], b[1], c[1]))
    mine, sent = zip(*(mine_of(a, b) for a, b in zip(summed_first, summed_second)))
    both = [mine_of(a, swap(b)) for a, b in zip(mine, sent)]
    both = [[v.astype(F32) for v in pair] for pair in both]
    (side_a, side_b), (up_a, up_b), (down_a, down_b) = both

    def cut(block):
        flat = block[:, :LANES].reshape(-1)[:vector_count]
        return (flat, block[:, LANES : edges[1]].reshape(rows, 3, half), block[:, edges[1] :])

    (flat_a, qkv_a, out_a), (flat_b, qkv_b, out_b) = (cut(side_a), cut(side_b))
    up_a, up_b = (up_a.reshape(rows, shards, unit), up_b.reshape(rows, shards, unit))
    flat = flat_a + flat_b
    whole = [flat[n * rows : (n + 1) * rows] for n in range(8)]
    grads = (
        jnp.stack([qkv_a, qkv_b], axis=2).reshape(rows, -1),
        whole[0],
        whole[1],
        jnp.concatenate([out_a, out_b], axis=1),
        whole[2],
        whole[3],
        whole[4],
        jnp.stack([up_a, up_b], axis=2).reshape(rows, -1),
        flat[8 * rows :],
        jnp.concatenate([down_a, down_b], axis=0),
        whole[5],
        whole[6],
        whole[7],
    )
    shape = (1, count, 1, -1, model)
    activations = choose(middle, last).reshape(shape)
    input_grads = choose(grad_first, grad_middle).reshape(shape)
    return (activations, input_grads) + tuple(member[None] for member in grads)


def solution(mesh):
    rows = P(None, ("dp", "shard"), None, None)
    matrix = P("section", "shard", None)
    vector = P("section", "shard")
    weight_specs = (matrix, vector, vector, matrix, vector, vector, vector)
    weight_specs += (matrix, vector, matrix, vector, vector, vector)
    in_specs = (rows, P(None, ("dp", "shard")), rows) + weight_specs
    result = P("section", None, ("dp", "shard"), None, None)
    return jax.shard_map(
        per_device,
        mesh=mesh,
        in_specs=in_specs,
        out_specs=(result, result) + weight_specs,
        check_vma=False,
    )
```

time: 532 us -> 563 us (1.058)
  starting transfers between devices: 83.1 us -> 106 us
  other arithmetic: 68.8 us -> 90.9 us
  between operations: 17.4 us -> 4.06 us
  local copies, waits for them, and re-layouts: 97.6 us -> 110 us
  matrix products: 67.6 us -> 58.6 us
    ppermute x19 -> x20, starting transfers between devices: 26.1 us -> 46.7 us  [swap(): return lax.ppermute(value, 'section', [(0, 1), (1, 0)])]
    convert_element_type x29 -> x31, other arithmetic: 21.7 us -> 40.2 us  [the longest x12 21 us: scatter_end(): return (kept + across.astype(F32)).astype(BF)]
    dynamic_update_slice x61, local copies, waits for them, and re-layouts: 15.6 us -> 29.5 us  [put(): return lax.dynamic_update_slice(whole, jnp.expand_dims(piece, dim), start)]
    select_n x26 -> x27, other arithmetic: 14.6 us -> 19.4 us  [choose(): return jnp.where(first, low, high)]
    ppermute x50 -> x60, waiting for transfers between devices: 185 us -> 182 us  [trade(): return lax.ppermute(value, ('section', name), route)]
    unnamed x203 -> x262, local copies, waits for them, and re-layouts: 22.8 us -> 25.8 us
    ppermute x50 -> x60, starting transfers between devices: 57 us -> 59.7 us  [trade(): return lax.ppermute(value, ('section', name), route)]
    another operation x40 -> x50, other arithmetic: 14.8 us -> 16.9 us  [the longest x18 8.79 us: gather_two(): return trade(jnp.stack([block, beside]), axis, (3, 1))]
  transfers between devices with their start and end apart: 70 -> 80, of which waited for: 32 -> 43; matrix products, arithmetic and copies ran while one was open for 28% -> 28% of each run, Pallas kernels for 0% -> 0%
where the time goes in v4:
time: 563 us; the launch traced here: 553 us
  waiting for transfers between devices  183 us (33%)
  local copies, waits for them, and re-layouts  110 us (20%)
  starting transfers between devices  106 us (19%)
  other arithmetic  90.9 us (16%)
  matrix products  58.6 us (10%)
    ppermute x60, waiting for transfers between devices, trade(): return lax.ppermute(value, ('section', name), route)  182 us
    ppermute x60, starting transfers between devices, trade(): return lax.ppermute(value, ('section', name), route)  59.7 us
    ppermute x20, starting transfers between devices, swap(): return lax.ppermute(value, 'section', [(0, 1), (1, 0)])  46.7 us
    dynamic_update_slice x61, local copies, waits for them, and re-layouts, put(): return lax.dynamic_update_slice(whole, jnp.expand_dims(piece, dim), start)  29.5 us
    unnamed x262, local copies, waits for them, and re-layouts  25.8 us
    convert_element_type x12, other arithmetic, scatter_end(): return (kept + across.astype(F32)).astype(BF)  21 us
    select_n x27, other arithmetic, choose(): return jnp.where(first, low, high)  19.4 us
    convert_element_type x14, other arithmetic, scatter_two(): return trade(sent.astype(BF), axis, (3, 1))  16.8 us
  transfers between devices with their start and end apart: 80, of which 43 were waited for; matrix products, arithmetic and copies ran while one was open for 28% of the time, Pallas kernels for 0%

profile of v4, /device:TPU:1, one launch (start us, length us, event | category | flops | bytes accessed | tf_op | source)
XLA Modules:
  0.0 552.7 jit_solution(17425687743739103685)
XLA Ops:
  1.3 5.4 concatenate.67
  18.9 3.8 collective-permute-start.6
  22.9 3.5 collective-permute-done.6
  30.7 4.4 collective-permute-done.9
  45.6 8.8 %collective-permute-done.12 = bf16[4,64,2048]{2,1,0:T(8,128)(2,1)S(1)} collective-permute-done((bf16[4,64,2048]{2,1,0:T(8,128)(2,1)S(1)}, bf16[4,64,2048]{2,1,0:T(8,128)(2,1)S(1)}, u32[]{:S(2)}, u32[]{:S(2)}) %collective-permute-start.12) | collective-permute-done | bytes 1048608 | tf_op jit(solution)/shard_map/ppermute | solution.py:225
  54.4 3.5 collective-permute-done.11
  70.4 4.8 collective-permute-done.19
  75.2 5.6 %collective-permute-done.18 = bf16[2,64,2048]{2,1,0:T(8,128)(2,1)S(1)} collective-permute-done((bf16[2,64,2048]{2,1,0:T(8,128)(2,1)S(1)}, bf16[2,64,2048]{2,1,0:T(8,128)(2,1)S(1)}, u32[]{:S(2)}, u32[]{:S(2)}) %collective-permute-start.18) | collective-permute-done | bytes 524320 | tf_op jit(solution)/shard_map/ppermute | solution.py:225
  80.8 17.1 %collective-permute-done.17 = bf16[2,64,2176]{2,1,0:T(8,128)(2,1)S(1)} collective-permute-done((bf16[2,64,2176]{2,1,0:T(8,128)(2,1)S(1)}, bf16[2,64,2176]{2,1,0:T(8,128)(2,1)S(1)}, u32[]{:S(2)}, u32[]{:S(2)}) %collective-permute-start.17) | collective-permute-done | bytes 557088 | tf_op jit(solution)/shard_map/ppermute | solution.py:225
  98.9 5.9 %collective-permute-done.20 = bf16[4,32,1024]{2,1,0:T(8,128)(2,1)S(1)} collective-permute-done((bf16[4,32,1024]{2,1,0:T(8,128)(2,1)S(1)}, bf16[4,32,1024]{2,1,0:T(8,128)(2,1)S(1)}, u32[]{:S(2)}, u32[]{:S(2)}) %collective-permute-start.20) | collective-permute-done | bytes 262176 | tf_op jit(solution)/shard_map/ppermute | solution.py:225
  105.9 7.4 %collective-permute-done.24 = bf16[2,4,32,1024]{3,2,1,0:T(8,128)(2,1)S(1)} collective-permute-done((bf16[2,4,32,1024]{3,2,1,0:T(8,128)(2,1)S(1)}, bf16[2,4,32,1024]{3,2,1,0:T(8,128)(2,1)S(1)}, u32[]{:S(2)}, u32[]{:S(2)}) %collective-permute-start.24) | collective-permute-done | bytes 524320 | tf_op jit(solution)/shard_map/ppermute | solution.py:225
  168.9 9.7 %collective-permute-done.30 = bf16[2,16,32,1024]{3,2,1,0:T(8,128)(2,1)S(1)} collective-permute-done((bf16[2,16,32,1024]{3,2,1,0:T(8,128)(2,1)S(1)}, bf16[2,16,32,1024]{3,2,1,0:T(8,128)(2,1)S(1)}, u32[]{:S(2)}, u32[]{:S(2)}) %collective-permute-start.30) | collective-permute-done | bytes 2097184 | tf_op jit(solution)/shard_map/ppermute | solution.py:225
  180.9 5.0 collective-permute-done.28
  193.3 4.7 collective-permute-start.34
  207.4 5.7 %collective-permute-done.33 = bf16[16,32,1024]{2,1,0:T(8,128)(2,1)} collective-permute-done((bf16[16,32,1024]{2,1,0:T(8,128)(2,1)S(1)}, bf16[16,32,1024]{2,1,0:T(8,128)(2,1)}, u32[]{:S(2)}, u32[]{:S(2)}) %collective-permute-start.33) | collective-permute-done | bytes 1048608 | tf_op jit(solution)/shard_map/ppermute | solution.py:225
  235.5 5.8 %collective-permute-done.37 = bf16[2,16,32,1024]{3,2,1,0:T(8,128)(2,1)} collective-permute-done((bf16[2,16,32,1024]{3,2,1,0:T(8,128)(2,1)}, bf16[2,16,32,1024]{3,2,1,0:T(8,128)(2,1)}, u32[]{:S(2)}, u32[]{:S(2)}) %collective-permute-start.37) | collective-permute-done | bytes 2097184 | tf_op jit(solution)/shard_map/ppermute | solution.py:225
  258.0 3.5 convolution_convert_fusion.4
  294.9 4.3 collective-permute-done.39
  299.3 3.7 fusion.56
  325.0 3.4 convolution_convert_fusion.3
  333.8 3.8 collective-permute-start.47
  358.3 13.2 %collective-permute-done.46 = bf16[2,4,64,2176]{3,2,1,0:T(8,128)(2,1)S(1)} collective-permute-done((bf16[2,4,64,2176]{3,2,1,0:T(8,128)(2,1)S(1)}, bf16[2,4,64,2176]{3,2,1,0:T(8,128)(2,1)S(1)}, u32[]{:S(2)}, u32[]{:S(2)}) %collective-permute-start.46) | collective-permute-done | bytes 2228256 | tf_op jit(solution)/shard_map/ppermute | solution.py:225
  394.3 5.2 collective-permute-done.48
  407.3 3.6 fusion.23
  411.0 7.4 %collective-permute-done.54 = bf16[4,64,2048]{2,1,0:T(8,128)(2,1)S(1)} collective-permute-done((bf16[4,64,2048]{2,1,0:T(8,128)(2,1)S(1)}, bf16[4,64,2048]{2,1,0:T(8,128)(2,1)S(1)}, u32[]{:S(2)}, u32[]{:S(2)}) %collective-permute-start.54) | collective-permute-done | bytes 1048608 | tf_op jit(solution)/shard_map/ppermute | solution.py:225
  432.2 16.1 %collective-permute-done.58 = bf16[2,64,2176]{2,1,0:T(8,128)(2,1)S(1)} collective-permute-done((bf16[2,64,2176]{2,1,0:T(8,128)(2,1)S(1)}, bf16[2,64,2176]{2,1,0:T(8,128)(2,1)S(1)}, u32[]{:S(2)}, u32[]{:S(2)}) %collective-permute-start.58) | collective-permute-done | bytes 557088 | tf_op jit(solution)/shard_map/ppermute | solution.py:225
  456.3 5.9 %collective-permute-done.62 = bf16[64,2176]{1,0:T(8,128)(2,1)S(1)} collective-permute-done((bf16[64,2176]{1,0:T(8,128)(2,1)}, bf16[64,2176]{1,0:T(8,128)(2,1)S(1)}, u32[]{:S(2)}, u32[]{:S(2)}) %collective-permute-start.62) | collective-permute-done | bytes 278560 | tf_op jit(solution)/shard_map/ppermute | solution.py:225
  462.9 4.8 collective-permute-done.59
  480.3 5.0 collective-permute-start.51
  508.2 9.9 %collective-permute-done.74 = bf16[2,2,16,4096]{3,2,1,0:T(8,128)(2,1)S(1)} collective-permute-done((bf16[2,2,16,4096]{3,2,1,0:T(8,128)(2,1)S(1)}, bf16[2,2,16,4096]{3,2,1,0:T(8,128)(2,1)S(1)}, u32[]{:S(2)}, u32[]{:S(2)}) %collective-permute-start.74) | collective-permute-done | bytes 524320 | tf_op jit(solution)/shard_map/ppermute | solution.py:225
  520.5 11.5 %collective-permute-start.79 = (bf16[128,1024]{1,0:T(8,128)(2,1)S(1)}, bf16[128,1024]{1,0:T(8,128)(2,1)S(1)}, u32[]{:S(2)}, u32[]{:S(2)}) collective-permute-start(bf16[128,1024]{1,0:T(8,128)(2,1)S(1)} %select_n.745), channel_id=1, source_target_pairs={{0,64},{64,0},{1,65},{65,1},{2,66},{66,2},{3,67},{67,3},{4,68},{68... | collective-permute-start | bytes 786440 | tf_op jit(solution)/shard_map/ppermute | solution.py:17
  539.1 6.8 %collective-permute-start.77 = (bf16[64,2176]{1,0:T(8,128)(2,1)S(1)}, bf16[64,2176]{1,0:T(8,128)(2,1)S(1)}, u32[]{:S(2)}, u32[]{:S(2)}) collective-permute-start(bf16[64,2176]{1,0:T(8,128)(2,1)S(1)} %bitcast.784), channel_id=1, source_target_pairs={{0,64},{64,0},{1,65},{65,1},{2,66},{66,2},{3,67},{67,3},{4,68},{68... | collective-permute-start | bytes 835592 | tf_op jit(solution)/shard_map/ppermute | solution.py:17
  (784 shorter events, 339.3 us)
Async XLA Ops:
  39.5 14.9 %collective-permute-start.12 = (bf16[4,64,2048]{2,1,0:T(8,128)(2,1)S(1)}, bf16[4,64,2048]{2,1,0:T(8,128)(2,1)S(1)}, u32[]{:S(2)}, u32[]{:S(2)}) collective-permute-start(bf16[4,64,2048]{2,1,0:T(8,128)(2,1)S(1)} %slice_dynamic-update-slice_fusion.12), channel_id=1, source_target_pairs={{0,1},{1,0},{2,3},{3,2},{4,5},{5,4},{6,7},{7,6},{8,9},{9,8},{10,11... | collective-permute-start | bytes 3145736 | tf_op jit(solution)/shard_map/ppermute | solution.py:225
  42.3 15.6 %collective-permute-start.11 = (bf16[4,64,2176]{2,1,0:T(8,128)(2,1)S(1)}, bf16[4,64,2176]{2,1,0:T(8,128)(2,1)S(1)}, u32[]{:S(2)}, u32[]{:S(2)}) collective-permute-start(bf16[4,64,2176]{2,1,0:T(8,128)(2,1)S(1)} %slice_dynamic-update-slice_fusion.6), channel_id=1, source_target_pairs={{0,4},{1,5},{2,6},{3,7},{4,0},{5,1},{6,2},{7,3},{8,12},{9,13},{10,... | collective-permute-start | bytes 3342344 | tf_op jit(solution)/shard_map/ppermute | solution.py:225
  63.5 42.4 %collective-permute-start.23 = (bf16[2,4,32,1024]{3,2,1,0:T(8,128)(2,1)S(1)}, bf16[2,4,32,1024]{3,2,1,0:T(8,128)(2,1)S(1)}, u32[]{:S(2)}, u32[]{:S(2)}) collective-permute-start(bf16[2,4,32,1024]{3,2,1,0:T(8,128)(2,1)S(1)} %pad_maximum_fusion.29), channel_id=1, source_target_pairs={{0,12},{1,13},{2,14},{3,15},{4,8},{5,9},{6,10},{7,11},{8,4},{9,5},... | collective-permute-start | bytes 1572872 | tf_op jit(solution)/shard_map/ppermute | solution.py:225
  63.8 49.5 %collective-permute-start.22 = (bf16[2,4,64,2048]{3,2,1,0:T(8,128)(2,1)S(1)}, bf16[2,4,64,2048]{3,2,1,0:T(8,128)(2,1)S(1)}, u32[]{:S(2)}, u32[]{:S(2)}) collective-permute-start(bf16[2,4,64,2048]{3,2,1,0:T(8,128)(2,1)S(1)} %pad_maximum_fusion.4), channel_id=1, source_target_pairs={{0,3},{1,2},{2,1},{3,0},{4,7},{5,6},{6,5},{7,4},{8,11},{9,10},{10,... | collective-permute-start | bytes 6291464 | tf_op jit(solution)/shard_map/ppermute | solution.py:225
  68.9 29.1 %collective-permute-start.17 = (bf16[2,64,2176]{2,1,0:T(8,128)(2,1)S(1)}, bf16[2,64,2176]{2,1,0:T(8,128)(2,1)S(1)}, u32[]{:S(2)}, u32[]{:S(2)}) collective-permute-start(bf16[2,64,2176]{2,1,0:T(8,128)(2,1)S(1)} %pad_maximum_fusion.24), channel_id=1, source_target_pairs={{0,3},{1,2},{2,1},{3,0},{4,7},{5,6},{6,5},{7,4},{8,11},{9,10},{10,... | collective-permute-start | bytes 1671176 | tf_op jit(solution)/shard_map/ppermute | solution.py:225
  75.2 38.9 %collective-permute-start.21 = (bf16[2,4,64,2176]{3,2,1,0:T(8,128)(2,1)S(1)}, bf16[2,4,64,2176]{3,2,1,0:T(8,128)(2,1)S(1)}, u32[]{:S(2)}, u32[]{:S(2)}) collective-permute-start(bf16[2,4,64,2176]{3,2,1,0:T(8,128)(2,1)S(1)} %pad_maximum_fusion), channel_id=1, source_target_pairs={{0,12},{1,13},{2,14},{3,15},{4,8},{5,9},{6,10},{7,11},{8,4},{9,5},... | collective-permute-start | bytes 6684680 | tf_op jit(solution)/shard_map/ppermute | solution.py:225
  121.4 29.6 %collective-permute-start.26 = (bf16[4,64,2048]{2,1,0:T(8,128)(2,1)}, bf16[4,64,2048]{2,1,0:T(8,128)(2,1)}, u32[]{:S(2)}, u32[]{:S(2)}) collective-permute-start(bf16[4,64,2048]{2,1,0:T(8,128)(2,1)} %slice_dynamic-update-slice_fusion.10), channel_id=1, source_target_pairs={{0,1},{1,0},{2,3},{3,2},{4,5},{5,4},{6,7},{7,6},{8,9},{9,8},{10,11... | collective-permute-start | bytes 3145736 | tf_op jit(solution)/shard_map/ppermute | solution.py:225
  121.4 29.6 %collective-permute-start.27 = (bf16[16,32,1024]{2,1,0:T(8,128)(2,1)}, bf16[16,32,1024]{2,1,0:T(8,128)(2,1)}, u32[]{:S(2)}, u32[]{:S(2)}) collective-permute-start(bf16[16,32,1024]{2,1,0:T(8,128)(2,1)} %bitcast.45), channel_id=1, source_target_pairs={{0,16},{16,0},{32,48},{48,32},{64,112},{80,96},{96,80},{112,64},{1... | collective-permute-start | bytes 3145736 | tf_op jit(solution)/shard_map/ppermute | solution.py:225
  123.9 27.1 %collective-permute-start.25 = (bf16[4,64,2176]{2,1,0:T(8,128)(2,1)S(1)}, bf16[4,64,2176]{2,1,0:T(8,128)(2,1)}, u32[]{:S(2)}, u32[]{:S(2)}) collective-permute-start(bf16[4,64,2176]{2,1,0:T(8,128)(2,1)S(1)} %slice_dynamic-update-slice_fusion.4), channel_id=1, source_target_pairs={{0,4},{1,5},{2,6},{3,7},{4,0},{5,1},{6,2},{7,3},{8,12},{9,13},{10,... | collective-permute-start | bytes 3342344 | tf_op jit(solution)/shard_map/ppermute | solution.py:225
  127.6 21.9 %collective-permute-start.31 = (bf16[512,512]{1,0:T(8,128)(2,1)}, bf16[512,512]{1,0:T(8,128)(2,1)}, u32[]{:S(2)}, u32[]{:S(2)}) collective-permute-start(bf16[512,512]{1,0:T(8,128)(2,1)} %broadcast_select_fusion.14), channel_id=1, source_target_pairs={{0,64},{64,0},{1,65},{65,1},{2,66},{66,2},{3,67},{67,3},{4,68},{68... | collective-permute-start | bytes 1572872 | tf_op jit(solution)/shard_map/ppermute | solution.py:17
  153.3 25.3 %collective-permute-start.30 = (bf16[2,16,32,1024]{3,2,1,0:T(8,128)(2,1)S(1)}, bf16[2,16,32,1024]{3,2,1,0:T(8,128)(2,1)S(1)}, u32[]{:S(2)}, u32[]{:S(2)}) collective-permute-start(bf16[2,16,32,1024]{3,2,1,0:T(8,128)(2,1)S(1)} %pad_maximum_fusion.6), channel_id=1, source_target_pairs={{0,48},{16,32},{32,16},{48,0},{64,80},{80,64},{96,112},{112,96},{1... | collective-permute-start | bytes 6291464 | tf_op jit(solution)/shard_map/ppermute | solution.py:225
  155.4 25.5 %collective-permute-start.29 = (bf16[2,4,64,2048]{3,2,1,0:T(8,128)(2,1)S(1)}, bf16[2,4,64,2048]{3,2,1,0:T(8,128)(2,1)S(1)}, u32[]{:S(2)}, u32[]{:S(2)}) collective-permute-start(bf16[2,4,64,2048]{3,2,1,0:T(8,128)(2,1)S(1)} %pad_maximum_fusion.5), channel_id=1, source_target_pairs={{0,3},{1,2},{2,1},{3,0},{4,7},{5,6},{6,5},{7,4},{8,11},{9,10},{10,... | collective-permute-start | bytes 6291464 | tf_op jit(solution)/shard_map/ppermute | solution.py:225
  158.9 27.1 %collective-permute-start.28 = (bf16[2,4,64,2176]{3,2,1,0:T(8,128)(2,1)S(1)}, bf16[2,4,64,2176]{3,2,1,0:T(8,128)(2,1)S(1)}, u32[]{:S(2)}, u32[]{:S(2)}) collective-permute-start(bf16[2,4,64,2176]{3,2,1,0:T(8,128)(2,1)S(1)} %pad_maximum_fusion.1), channel_id=1, source_target_pairs={{0,12},{1,13},{2,14},{3,15},{4,8},{5,9},{6,10},{7,11},{8,4},{9,5},... | collective-permute-start | bytes 6684680 | tf_op jit(solution)/shard_map/ppermute | solution.py:225
  198.1 15.0 %collective-permute-start.33 = (bf16[16,32,1024]{2,1,0:T(8,128)(2,1)S(1)}, bf16[16,32,1024]{2,1,0:T(8,128)(2,1)}, u32[]{:S(2)}, u32[]{:S(2)}) collective-permute-start(bf16[16,32,1024]{2,1,0:T(8,128)(2,1)S(1)} %bitcast.712), channel_id=1, source_target_pairs={{0,16},{16,0},{32,48},{48,32},{64,112},{80,96},{96,80},{112,64},{1... | collective-permute-start | bytes 3145736 | tf_op jit(solution)/shard_map/ppermute | solution.py:225
  215.8 25.5 %collective-permute-start.37 = (bf16[2,16,32,1024]{3,2,1,0:T(8,128)(2,1)}, bf16[2,16,32,1024]{3,2,1,0:T(8,128)(2,1)}, u32[]{:S(2)}, u32[]{:S(2)}) collective-permute-start(bf16[2,16,32,1024]{3,2,1,0:T(8,128)(2,1)} %pad_maximum_fusion.7), channel_id=1, source_target_pairs={{0,48},{16,32},{32,16},{48,0},{64,80},{80,64},{96,112},{112,96},{1... | collective-permute-start | bytes 6291464 | tf_op jit(solution)/shard_map/ppermute | solution.py:225
  268.5 26.4 %collective-permute-start.40 = (bf16[2,4,64,2048]{3,2,1,0:T(8,128)(2,1)}, bf16[2,4,64,2048]{3,2,1,0:T(8,128)(2,1)}, u32[]{:S(2)}, u32[]{:S(2)}) collective-permute-start(bf16[2,4,64,2048]{3,2,1,0:T(8,128)(2,1)} %pad_maximum_fusion.9), channel_id=1, source_target_pairs={{0,1},{1,0},{2,3},{3,2},{4,5},{5,4},{6,7},{7,6},{8,9},{9,8},{10,11... | collective-permute-start | bytes 6291464 | tf_op jit(solution)/shard_map/ppermute | solution.py:225
  272.7 26.6 %collective-permute-start.39 = (bf16[2,16,32,1024]{3,2,1,0:T(8,128)(2,1)}, bf16[2,16,32,1024]{3,2,1,0:T(8,128)(2,1)}, u32[]{:S(2)}, u32[]{:S(2)}) collective-permute-start(bf16[2,16,32,1024]{3,2,1,0:T(8,128)(2,1)} %pad_maximum_fusion.8), channel_id=1, source_target_pairs={{0,16},{16,0},{32,48},{48,32},{64,112},{80,96},{96,80},{112,64},{1... | collective-permute-start | bytes 6291464 | tf_op jit(solution)/shard_map/ppermute | solution.py:225
  309.2 14.3 %collective-permute-start.44 = (bf16[4,64,2048]{2,1,0:T(8,128)(2,1)}, bf16[4,64,2048]{2,1,0:T(8,128)(2,1)S(1)}, u32[]{:S(2)}, u32[]{:S(2)}) collective-permute-start(bf16[4,64,2048]{2,1,0:T(8,128)(2,1)} %fusion.42), channel_id=1, source_target_pairs={{0,3},{1,2},{2,1},{3,0},{4,7},{5,6},{6,5},{7,4},{8,11},{9,10},{10,... | collective-permute-start | bytes 3145736 | tf_op jit(solution)/shard_map/ppermute | solution.py:225
  309.2 14.3 %collective-permute-start.43 = (bf16[16,32,1024]{2,1,0:T(8,128)(2,1)}, bf16[16,32,1024]{2,1,0:T(8,128)(2,1)}, u32[]{:S(2)}, u32[]{:S(2)}) collective-permute-start(bf16[16,32,1024]{2,1,0:T(8,128)(2,1)} %fusion.43), channel_id=1, source_target_pairs={{0,48},{16,32},{32,16},{48,0},{64,80},{80,64},{96,112},{112,96},{1... | collective-permute-start | bytes 3145736 | tf_op jit(solution)/shard_map/ppermute | solution.py:225
  333.8 24.3 %collective-permute-start.47 = (bf16[256,1024]{1,0:T(8,128)(2,1)}, bf16[256,1024]{1,0:T(8,128)(2,1)S(1)}, u32[]{:S(2)}, u32[]{:S(2)}) collective-permute-start(bf16[256,1024]{1,0:T(8,128)(2,1)} %convolution_convert_fusion.10), channel_id=1, source_target_pairs={{0,64},{64,0},{1,65},{65,1},{2,66},{66,2},{3,67},{67,3},{4,68},{68... | collective-permute-start | bytes 1572872 | tf_op jit(solution)/shard_map/ppermute | solution.py:17
  340.8 53.5 %collective-permute-start.49 = (bf16[2,16,32,1024]{3,2,1,0:T(8,128)(2,1)}, bf16[2,16,32,1024]{3,2,1,0:T(8,128)(2,1)}, u32[]{:S(2)}, u32[]{:S(2)}) collective-permute-start(bf16[2,16,32,1024]{3,2,1,0:T(8,128)(2,1)} %pad_maximum_fusion.10), channel_id=1, source_target_pairs={{0,16},{16,0},{32,48},{48,32},{64,112},{80,96},{96,80},{112,64},{1... | collective-permute-start | bytes 6291464 | tf_op jit(solution)/shard_map/ppermute | solution.py:225
  343.6 27.9 %collective-permute-start.46 = (bf16[2,4,64,2176]{3,2,1,0:T(8,128)(2,1)S(1)}, bf16[2,4,64,2176]{3,2,1,0:T(8,128)(2,1)S(1)}, u32[]{:S(2)}, u32[]{:S(2)}) collective-permute-start(bf16[2,4,64,2176]{3,2,1,0:T(8,128)(2,1)S(1)} %pad_maximum_fusion.2), channel_id=1, source_target_pairs={{0,4},{1,5},{2,6},{3,7},{4,0},{5,1},{6,2},{7,3},{8,12},{9,13},{10,... | collective-permute-start | bytes 6684680 | tf_op jit(solution)/shard_map/ppermute | solution.py:225
  351.7 42.7 %collective-permute-start.50 = (bf16[2,4,64,2048]{3,2,1,0:T(8,128)(2,1)}, bf16[2,4,64,2048]{3,2,1,0:T(8,128)(2,1)}, u32[]{:S(2)}, u32[]{:S(2)}) collective-permute-start(bf16[2,4,64,2048]{3,2,1,0:T(8,128)(2,1)} %pad_maximum_fusion.11), channel_id=1, source_target_pairs={{0,1},{1,0},{2,3},{3,2},{4,5},{5,4},{6,7},{7,6},{8,9},{9,8},{10,11... | collective-permute-start | bytes 6291464 | tf_op jit(solution)/shard_map/ppermute | solution.py:225
  384.5 15.0 %collective-permute-start.48 = (bf16[4,64,2176]{2,1,0:T(8,128)(2,1)}, bf16[4,64,2176]{2,1,0:T(8,128)(2,1)}, u32[]{:S(2)}, u32[]{:S(2)}) collective-permute-start(bf16[4,64,2176]{2,1,0:T(8,128)(2,1)} %fusion.71), channel_id=1, source_target_pairs={{0,12},{1,13},{2,14},{3,15},{4,8},{5,9},{6,10},{7,11},{8,4},{9,5},... | collective-permute-start | bytes 3342344 | tf_op jit(solution)/shard_map/ppermute | solution.py:225
  404.3 14.0 %collective-permute-start.54 = (bf16[4,64,2048]{2,1,0:T(8,128)(2,1)S(1)}, bf16[4,64,2048]{2,1,0:T(8,128)(2,1)S(1)}, u32[]{:S(2)}, u32[]{:S(2)}) collective-permute-start(bf16[4,64,2048]{2,1,0:T(8,128)(2,1)S(1)} %fusion.40), channel_id=1, source_target_pairs={{0,3},{1,2},{2,1},{3,0},{4,7},{5,6},{6,5},{7,4},{8,11},{9,10},{10,... | collective-permute-start | bytes 3145736 | tf_op jit(solution)/shard_map/ppermute | solution.py:225
  404.4 14.0 %collective-permute-start.53 = (bf16[16,32,1024]{2,1,0:T(8,128)(2,1)S(1)}, bf16[16,32,1024]{2,1,0:T(8,128)(2,1)S(1)}, u32[]{:S(2)}, u32[]{:S(2)}) collective-permute-start(bf16[16,32,1024]{2,1,0:T(8,128)(2,1)S(1)} %fusion.41), channel_id=1, source_target_pairs={{0,48},{16,32},{32,16},{48,0},{64,80},{80,64},{96,112},{112,96},{1... | collective-permute-start | bytes 3145736 | tf_op jit(solution)/shard_map/ppermute | solution.py:225
  421.0 27.8 %collective-permute-start.55 = (bf16[2,4,64,2176]{3,2,1,0:T(8,128)(2,1)S(1)}, bf16[2,4,64,2176]{3,2,1,0:T(8,128)(2,1)S(1)}, u32[]{:S(2)}, u32[]{:S(2)}) collective-permute-start(bf16[2,4,64,2176]{3,2,1,0:T(8,128)(2,1)S(1)} %pad_maximum_fusion.3), channel_id=1, source_target_pairs={{0,4},{1,5},{2,6},{3,7},{4,0},{5,1},{6,2},{7,3},{8,12},{9,13},{10,... | collective-permute-start | bytes 6684680 | tf_op jit(solution)/shard_map/ppermute | solution.py:225
  427.4 20.9 %collective-permute-start.57 = (bf16[2,2,4,32,1024]{4,3,2,1,0:T(8,128)(2,1)S(1)}, bf16[2,2,4,32,1024]{4,3,2,1,0:T(8,128)(2,1)S(1)}, u32[]{:S(2)}, u32[]{:S(2)}) collective-permute-start(bf16[2,2,4,32,1024]{4,3,2,1,0:T(8,128)(2,1)S(1)} %pad_maximum_fusion.15), channel_id=1, source_target_pairs={{0,1},{1,0},{2,3},{3,2},{4,5},{5,4},{6,7},{7,6},{8,9},{9,8},{10,11... | collective-permute-start | bytes 3145736 | tf_op jit(solution)/shard_map/ppermute | solution.py:225
  428.0 20.4 %collective-permute-start.56 = (bf16[2,2,4,16,2048]{4,3,1,2,0:T(8,128)(2,1)S(1)}, bf16[2,2,4,16,2048]{4,3,1,2,0:T(8,128)(2,1)S(1)}, u32[]{:S(2)}, u32[]{:S(2)}) collective-permute-start(bf16[2,2,4,16,2048]{4,3,1,2,0:T(8,128)(2,1)S(1)} %pad_maximum_fusion.14), channel_id=1, source_target_pairs={{0,16},{16,0},{32,48},{48,32},{64,112},{80,96},{96,80},{112,64},{1... | collective-permute-start | bytes 3145736 | tf_op jit(solution)/shard_map/ppermute | solution.py:225
  429.8 18.5 %collective-permute-start.58 = (bf16[2,64,2176]{2,1,0:T(8,128)(2,1)S(1)}, bf16[2,64,2176]{2,1,0:T(8,128)(2,1)S(1)}, u32[]{:S(2)}, u32[]{:S(2)}) collective-permute-start(bf16[2,64,2176]{2,1,0:T(8,128)(2,1)S(1)} %pad_maximum_fusion.25), channel_id=1, source_target_pairs={{0,1},{1,0},{2,3},{3,2},{4,5},{5,4},{6,7},{7,6},{8,9},{9,8},{10,11... | collective-permute-start | bytes 1671176 | tf_op jit(solution)/shard_map/ppermute | solution.py:225
  452.7 15.0 %collective-permute-start.59 = (bf16[4,64,2176]{2,1,0:T(8,128)(2,1)}, bf16[4,64,2176]{2,1,0:T(8,128)(2,1)}, u32[]{:S(2)}, u32[]{:S(2)}) collective-permute-start(bf16[4,64,2176]{2,1,0:T(8,128)(2,1)} %fusion.72), channel_id=1, source_target_pairs={{0,12},{1,13},{2,14},{3,15},{4,8},{5,9},{6,10},{7,11},{8,4},{9,5},... | collective-permute-start | bytes 3342344 | tf_op jit(solution)/shard_map/ppermute | solution.py:225
  520.5 25.5 %collective-permute-start.79 = (bf16[128,1024]{1,0:T(8,128)(2,1)S(1)}, bf16[128,1024]{1,0:T(8,128)(2,1)S(1)}, u32[]{:S(2)}, u32[]{:S(2)}) collective-permute-start(bf16[128,1024]{1,0:T(8,128)(2,1)S(1)} %select_n.745), channel_id=1, source_target_pairs={{0,64},{64,0},{1,65},{65,1},{2,66},{66,2},{3,67},{67,3},{4,68},{68... | collective-permute-start | bytes 786440 | tf_op jit(solution)/shard_map/ppermute | solution.py:17
  (172 other events, 938.9 us)

commit v5 on v4

--- a/solution.py
+++ b/solution.py
@@ -198,7 +198,6 @@
     ff = w_up.shape[2]
     half = model // 2
     unit = ff // shards // 2
-    vector_count = 8 * rows + 2 * unit
 
     def choose(low, high):
         return jnp.where(first, low, high)
@@ -227,6 +226,10 @@
     def after(value, earlier):
         return lax.optimization_barrier((value, earlier))[0]
 
+    def hop(value, distance):
+        route = [(at, (at + distance) % RING) for at in range(RING)]
+        return lax.ppermute(value, "dp", route)
+
     def put(whole, piece, at, dim):
         start = [0] * whole.ndim
         start[dim] = at
@@ -275,23 +278,26 @@
         up = w_up[0].reshape(rows, shards, 2, unit)[:, :, part].reshape(rows, shards * unit)
         return (qkv, out, up, w_down[0][part * unit : (part + 1) * unit])
 
-    vectors = jnp.concatenate(
-        [
-            v[0]
-            for v in (
-                bias_q,
-                bias_v,
-                bias_out,
-                gain_attn,
-                shift_attn,
-                bias_down,
-                gain_mlp,
-                shift_mlp,
-                bias_up,
-            )
-        ]
-    )
-    vectors = jnp.pad(vectors, (0, rows * LANES - vector_count)).reshape(rows, LANES)
+    lines = [
+        v.reshape(-1, rows)
+        for v in (
+            bias_q,
+            bias_v,
+            bias_out,
+            gain_attn,
+            shift_attn,
+            bias_down,
+            gain_mlp,
+            shift_mlp,
+            bias_up,
+        )
+    ]
+    vectors, at = (jnp.zeros((rows, LANES), BF), 0)
+    for line in lines:
+        height = line.shape[0]
+        vectors += jnp.pad(line, ((at, rows - at - height), (0, LANES - rows)))
+        at += height
+    vector_rows = at
     split = [mine_of(low, high) for low, high in zip(parts_of(0), parts_of(1))]
     kept_part = (vectors,) + tuple(low for low, high in split)
     sent_part = (vectors,) + tuple(high for low, high in split)
@@ -299,51 +305,31 @@
     blocks = [mine_of(own, got) for own, got in zip(kept_part, got_part)]
     edges = (LANES, LANES + 3 * half, LANES + 4 * half, LANES + 4 * half + shards * unit)
 
-    def joined(layer, count):
-        return placed(edges[count - 1], list(zip((0,) + edges, [b[layer] for b in blocks[:count]])))
+    side = []
+    for layer in range(2):
+        side += [(layer * edges[3] + at, b[layer]) for at, b in zip((0,) + edges, blocks[:4])]
+    side = placed(2 * edges[3], side)
 
     quarter = unit // RING
 
     def quarter_of(block):
         return chunk(block.reshape(RING, quarter, model), place["x"], 0)
 
-    a0, b0, c0 = (joined(0, 3), blocks[3][0], quarter_of(blocks[4][0]))
-    a1, b1, c1 = (joined(1, 3), blocks[3][1], quarter_of(blocks[4][1]))
-    an, bn, cn = together(gather_one(a0, "y"), gather_one(b0, "z"), gather_one(c0, "y"))
-    af, bf, cf = together(
-        gather_two(a0, an, "y"), gather_two(b0, bn, "z"), gather_two(c0, cn, "y")
-    )
-    a0 = gather_end(a0, an, af, "y", 0)
-    b0 = gather_end(b0, bn, bf, "z", 0)
-    c0 = gather_end(c0, cn, cf, "y", 0)
-    an0, bn0, cn0 = together(gather_one(a0, "z"), gather_one(b0, "y"), gather_one(c0, "z"))
-    af0, bf0, cf0 = (
-        gather_two(a0, an0, "z"),
-        gather_two(b0, bn0, "y"),
-        gather_two(c0, cn0, "z"),
-    )
-    a1, b1, c1 = (after(a1, an0), after(b1, an0), after(c1, an0))
-    an, bn, cn = together(gather_one(a1, "y"), gather_one(b1, "z"), gather_one(c1, "z"))
-    af, bf, cf = together(
-        gather_two(a1, an, "y"), gather_two(b1, bn, "z"), gather_two(c1, cn, "z")
-    )
-    c1 = gather_end(c1, cn, cf, "z", 0)
-    cn1 = gather_one(c1, "y")
-    cf1 = gather_two(c1, cn1, "y")
-    a1 = gather_end(a1, an, af, "y", 0)
-    b1 = gather_end(b1, bn, bf, "z", 0)
-    af0, bf0, cf0, cf1 = together(af0, bf0, cf0, cf1)
-    a0 = gather_end(a0, an0, af0, "z", 0)
-    b0 = gather_end(b0, bn0, bf0, "y", 1)
-    c0 = gather_end(c0, cn0, cf0, "z", 0).reshape(shards, quarter, model)
-    c1 = gather_end(c1, cn1, cf1, "y", 1).reshape(shards, quarter, model)
-    a1, b1 = (after(a1, af0), after(b1, bf0))
-
-    def arranged(attn, up):
-        attn, up = (attn.reshape(model, -1), up.reshape(model, -1))
-        flat = attn[:, :LANES].reshape(shards, rows * LANES)[:, :vector_count].astype(F32)
-        whole = [flat[:, n * rows : (n + 1) * rows].reshape(-1) for n in range(8)]
-        bias_up_part = flat[:, 8 * rows :].reshape(shards, 2, unit)
+    c = jnp.stack([quarter_of(block) for block in blocks[4]])
+    cn = gather_one(c, "y")
+    c = gather_end(c, cn, gather_two(c, cn, "y"), "y", 1)
+    cn = gather_one(c, "z")
+    c = gather_end(c, cn, gather_two(c, cn, "z"), "z", 1).reshape(2, shards, quarter, model)
+    cn = gather_one(c, "x")
+    c = gather_end(c, cn, gather_two(c, cn, "x"), "x", 2).reshape(2, -1, model)
+
+    side = lax.all_gather(side, "shard", axis=0, tiled=True)
+    sides = [side[:, layer * edges[3] : (layer + 1) * edges[3]] for layer in range(2)]
+
+    def arranged(attn, down):
+        flat = attn[:, :LANES].reshape(shards, rows, LANES)[:, :vector_rows, :rows].astype(F32)
+        whole = [flat[:, n].reshape(-1) for n in range(8)]
+        bias_up_part = flat[:, 8:].reshape(shards, 2, unit)
         bias_up_part = choose(bias_up_part[:, 0], bias_up_part[:, 1]).reshape(-1)
         bias_q_part = choose(whole[0][:half], whole[0][half:])
         bias_v_part = choose(whole[1][:half], whole[1][half:])
@@ -353,7 +339,8 @@
         return dict(
             qkv=attn[:, LANES : edges[1]],
             out=jnp.concatenate(mine_of(held, arrived), axis=1),
-            up=up,
+            up=attn[:, edges[2] :],
+            down=down,
             bias_qkv=jnp.concatenate([bias_q_part, jnp.zeros_like(bias_q_part), bias_v_part]),
             bias_out=whole[2],
             gain_attn=whole[3],
@@ -376,119 +363,97 @@
         whole += [0.5 * grads[name] for name in names]
         part = grads["bias_up"].reshape(shards, unit)
         spread = jnp.concatenate([choose(part, 0.0), choose(0.0, part)], axis=1)
-        flat = jnp.concatenate([v.reshape(shards, rows) for v in whole] + [spread], axis=1)
-        flat = jnp.pad(flat.astype(BF), ((0, 0), (0, rows * LANES - vector_count)))
-        pieces = (flat.reshape(shards * rows, LANES), grads["qkv"], out)
-        return placed(edges[2], list(zip((0,) + edges, pieces))).reshape(RING, RING, rows, -1)
+        flat = [v.reshape(shards, 1, rows) for v in whole] + [spread.reshape(shards, -1, rows)]
+        flat = jnp.concatenate(flat, axis=1).astype(BF)
+        flat = jnp.pad(flat, ((0, 0), (0, rows - vector_rows), (0, LANES - rows)))
+        return (flat.reshape(shards * rows, LANES), grads["qkv"], out)
 
     count = tokens.shape[0]
     seq_lengths = lengths[:, 0]
 
-    first_weights = arranged(a0, b0)
-    an, bn, cn = (gather_one(a1, "z"), gather_one(b1, "y"), gather_one(c0, "x"))
+    first_weights = arranged(sides[0], c[0])
     attended, kept0 = forward_attention(tokens.reshape(-1, model), first_weights, seq_lengths)
-    an, bn, cn, attended = together(an, bn, cn, attended)
-    af, bf, cf = (gather_two(a1, an, "z"), gather_two(b1, bn, "y"), gather_two(c0, cn, "x"))
     activated = forward_hidden(attended, kept0, first_weights)
-    af, bf, cf, activated = together(af, bf, cf, activated)
-    first_weights["down"] = gather_end(c0, cn, cf, "x", 1).reshape(-1, model)
-    cn = gather_one(after(c1, cf), "x")
     middle = forward_output(activated, kept0, first_weights)
-    cn, middle = together(cn, middle)
-    cf = gather_two(c1, cn, "x")
-    second_weights = arranged(
-        gather_end(a1, an, af, "z", 0), gather_end(b1, bn, bf, "y", 1)
-    )
+    second_weights = arranged(sides[1], c[1])
     attended, kept1 = forward_attention(middle, second_weights, seq_lengths)
     activated = forward_hidden(attended, kept1, second_weights)
-    cf, activated = together(cf, activated)
-    second_weights["down"] = gather_end(c1, cn, cf, "x", 1).reshape(-1, model)
     last = forward_output(activated, kept1, second_weights)
 
     def down_of(grads):
         return grads["down"].reshape(shards, RING, quarter, model)
 
-    def up_of(grads):
-        return grads["up"].reshape(RING, RING, rows, -1)
-
     grad_hidden, grads1 = backward_mlp(cotangent.reshape(-1, model), kept1, second_weights)
-    c1, b1 = (down_of(grads1), up_of(grads1))
-    cn, bn = (scatter_one(c1, "x", 1), scatter_one(b1, "y", 1))
+    c1 = down_of(grads1)
+    cn = scatter_one(c1, "x", 1)
     grad_resid, grad_packed = backward_attention(grad_hidden, grads1, kept1, second_weights)
+    cn, grad_packed = together(cn, grad_packed)
+    cf = scatter_two(c1, cn, "x", 1)
+    grad_middle = backward_inputs(grad_resid, grad_packed, grads1, kept1, second_weights)
+    pieces = side_by_side(grads1) + (grads1["up"],)
+    side1 = placed(edges[3], list(zip((0,) + edges, pieces)))
+    side1, cf, grad_middle = together(side1, cf, grad_middle)
+    side1 = lax.psum_scatter(side1, "shard", scatter_dimension=0, tiled=True)
+    c1 = scatter_end(c1, cn, cf, "x", 1)
+
+    grad_hidden, grads0 = backward_mlp(grad_middle, kept0, first_weights)
+    c0, b0 = (down_of(grads0), grads0["up"].reshape(RING, RING, rows, -1))
+    cn, bn = (scatter_one(c0, "x", 1), scatter_one(b0, "y", 1))
+    grad_resid, grad_packed = backward_attention(grad_hidden, grads0, kept0, first_weights)
     cn, bn, grad_packed = together(cn, bn, grad_packed)
-    cf, bf = (scatter_two(c1, cn, "x", 1), scatter_two(b1, bn, "y", 1))
-    grad_middle = backward_inputs(grad_resid, grad_packed, grads1, kept1, second_weights)
-    a1 = side_by_side(grads1)
-    a1, cf, bf, grad_middle = together(a1, cf, bf, grad_middle)
-    c1, b1 = (scatter_end(c1, cn, cf, "x", 1), scatter_end(b1, bn, bf, "y", 1))
-    an1 = scatter_one(a1, "z", 0)
-
-    grad_hidden, grads0 = backward_mlp(grad_middle, kept0, first_weights)
-    c0, b0 = (down_of(grads0), up_of(grads0))
-    cn, bn = (scatter_one(c0, "x", 1), scatter_one(b0, "y", 1))
-    an1, grad_hidden = together(an1, grad_hidden)
-    af1 = scatter_two(a1, an1, "z", 0)
-    grad_resid, grad_packed = backward_attention(grad_hidden, grads0, kept0, first_weights)
-    af1, cn, bn, grad_packed = together(af1, cn, bn, grad_packed)
-    a1 = scatter_end(a1, an1, af1, "z", 0)
     cf, bf = (scatter_two(c0, cn, "x", 1), scatter_two(b0, bn, "y", 1))
     grad_first = backward_inputs(grad_resid, grad_packed, grads0, kept0, first_weights)
-    a0 = side_by_side(grads0)
+    a0 = placed(edges[2], list(zip((0,) + edges, side_by_side(grads0))))
+    a0 = a0.reshape(RING, RING, rows, -1)
     a0, cf, bf = together(a0, cf, bf)
     c0, b0 = (scatter_end(c0, cn, cf, "x", 1), scatter_end(b0, bn, bf, "y", 1))
 
-    b = jnp.stack([b0, b1]).reshape(2, RING, RING, rows // RING, -1)
+    b = b0.reshape(RING, RING, rows // RING, -1)
     c = jnp.stack([c0, c1]).reshape(2, RING, RING, quarter, model)
+    an, bn, cn = together(scatter_one(a0, "z", 0), scatter_one(b, "x", 1), scatter_one(c, "y", 2))
+    af, bf, cf, side1 = together(
+        scatter_two(a0, an, "z", 0), scatter_two(b, bn, "x", 1), scatter_two(c, cn, "y", 2), side1
+    )
+    side1 = side1.reshape(RING, rows // RING, -1)
+    a0 = scatter_end(a0, an, af, "z", 0)
+    b, c = (scatter_end(b, bn, bf, "x", 1), scatter_end(c, cn, cf, "y", 2))
     an, bn, cn, dn = together(
-        scatter_one(a0, "z", 0), scatter_one(b, "x", 2), scatter_one(c, "y", 2), scatter_one(a1, "y", 0)
-    )
-    af, bf, cf, df = together(
-        scatter_two(a0, an, "z", 0),
-        scatter_two(b, bn, "x", 2),
-        scatter_two(c, cn, "y", 2),
-        scatter_two(a1, dn, "y", 0),
-    )
-    a0 = scatter_end(a0, an, af, "z", 0)
-    a1 = scatter_end(a1, dn, df, "y", 0).reshape(RING, rows // RING, -1)
-    b, c = (scatter_end(b, bn, bf, "x", 2), scatter_end(c, cn, cf, "y", 2))
-    an, bn, cn, dn = together(
-        scatter_one(a0, "y", 0), scatter_one(b, "z", 1), scatter_one(c, "z", 1), scatter_one(a1, "x", 0)
+        scatter_one(a0, "y", 0), scatter_one(b, "z", 0), scatter_one(c, "z", 1), scatter_one(side1, "x", 0)
     )
     af, bf, cf, df = together(
         scatter_two(a0, an, "y", 0),
-        scatter_two(b, bn, "z", 1),
+        scatter_two(b, bn, "z", 0),
         scatter_two(c, cn, "z", 1),
-        scatter_two(a1, dn, "x", 0),
-    )
-    a0 = scatter_end(a0, an, af, "y", 0).reshape(RING, rows // RING, -1)
-    a1 = scatter_end(a1, dn, df, "x", 0)
-    b, c = (scatter_end(b, bn, bf, "z", 1), scatter_end(c, cn, cf, "z", 1))
-    c = c.reshape(2, rows // RING, -1)
-    bc = jnp.concatenate([b, c], axis=2)
-    an, bn = together(scatter_one(a0, "x", 0), gather_one(bc, "x"))
-    af, bf = together(scatter_two(a0, an, "x", 0), gather_two(bc, bn, "x"))
-    a = jnp.stack([scatter_end(a0, an, af, "x", 0), a1])
-    bc = gather_end(bc, bn, bf, "x", 1)
-    b = bc[..., : b.shape[2]].reshape(2, rows, -1)
-    c = bc[..., b.shape[2] :].reshape(2, unit, model)
-    an = gather_one(a, "x")
-    af = gather_two(a, an, "x")
-    a = gather_end(a, an, af, "x", 1).reshape(2, rows, -1)
-
-    summed_first, summed_second = ((a[0], b[0], c[0]), (a[1], b[1], c[1]))
+        scatter_two(side1, dn, "x", 0),
+    )
+    a0 = scatter_end(a0, an, af, "y", 0)
+    b, c = (scatter_end(b, bn, bf, "z", 0), scatter_end(c, cn, cf, "z", 1))
+    side1 = scatter_end(side1, dn, df, "x", 0)
+    wide = b.shape[1]
+    bc = jnp.concatenate([b, c[0].reshape(b.shape), c[1].reshape(b.shape), side1], axis=1)
+    bn = gather_one(bc, "x")
+    others = [hop(a0, n) for n in range(1, RING)]
+    bn, others = together(bn, others)
+    a0 = a0.astype(F32) + sum(other.astype(F32) for other in others)
+    bc = gather_end(bc, bn, gather_two(bc, bn, "x"), "x", 0).reshape(rows, -1)
+    b0, side1 = (bc[:, :wide], bc[:, 3 * wide :])
+    c0, c1 = (bc[:, n * wide : (n + 1) * wide].reshape(unit, model) for n in (1, 2))
+
+    summed_first = (a0.astype(BF), b0, c0)
+    summed_second = (side1[:, : edges[2]], side1[:, edges[2] :], c1)
     mine, sent = zip(*(mine_of(a, b) for a, b in zip(summed_first, summed_second)))
     both = [mine_of(a, swap(b)) for a, b in zip(mine, sent)]
     both = [[v.astype(F32) for v in pair] for pair in both]
     (side_a, side_b), (up_a, up_b), (down_a, down_b) = both
 
     def cut(block):
-        flat = block[:, :LANES].reshape(-1)[:vector_count]
+        flat = block[:vector_rows, :rows]
         return (flat, block[:, LANES : edges[1]].reshape(rows, 3, half), block[:, edges[1] :])
 
     (flat_a, qkv_a, out_a), (flat_b, qkv_b, out_b) = (cut(side_a), cut(side_b))
     up_a, up_b = (up_a.reshape(rows, shards, unit), up_b.reshape(rows, shards, unit))
     flat = flat_a + flat_b
-    whole = [flat[n * rows : (n + 1) * rows] for n in range(8)]
+    whole = [flat[n] for n in range(8)]
     grads = (
         jnp.stack([qkv_a, qkv_b], axis=2).reshape(rows, -1),
         whole[0],
@@ -498,7 +463,7 @@
         whole[3],
         whole[4],
         jnp.stack([up_a, up_b], axis=2).reshape(rows, -1),
-        flat[8 * rows :],
+        flat[8:].reshape(-1),
         jnp.concatenate([down_a, down_b], axis=0),
         whole[5],
         whole[6],

time: 563 us -> 559 us (level)
  waiting for transfers between devices: 183 us -> 218 us
  starting transfers between devices: 106 us -> 80.2 us
  local copies, waits for them, and re-layouts: 110 us -> 84.5 us
  between operations: 4.06 us -> 16.8 us
  other arithmetic: 90.9 us -> 82.2 us
  matrix products: 58.6 us -> 66.6 us
    ppermute x60 -> x28, waiting for transfers between devices: 182 us -> 205 us  [trade(): return lax.ppermute(value, ('section', name), route)]
    ppermute x60 -> x28, starting transfers between devices: 59.7 us -> 39.9 us  [trade(): return lax.ppermute(value, ('section', name), route)]
    dynamic_update_slice x61 -> x14, local copies, waits for them, and re-layouts: 29.5 us -> 12 us  [put(): return lax.dynamic_update_slice(whole, jnp.expand_dims(piece, dim), start)]
    ppermute x20, starting transfers between devices: 46.7 us -> 36.8 us  [swap(): return lax.ppermute(value, 'section', [(0, 1), (1, 0)])]
    another operation x15 -> x3, local copies, waits for them, and re-layouts: 7.92 us -> 0.06 us  [the longest x1 0.03 us: per_device(): c[1].reshape(b.shape)]
    convert_element_type x12 -> x10, other arithmetic: 21 us -> 13.2 us  [scatter_end(): return (kept + across.astype(F32)).astype(BF)]
    dot_general x8, matrix products: 15.4 us -> 23.1 us  [dot_transposed(): lax.dot_general(left, right, (((1,), (1,)), ((), ())), preferred_element_...]
    unnamed x262 -> x259, local copies, waits for them, and re-layouts: 25.8 us -> 18.4 us
  transfers between devices with their start and end apart: 80 -> 53, of which waited for: 43 -> 27; matrix products, arithmetic and copies ran while one was open for 28% -> 29% of each run, Pallas kernels for 0% -> 0%
where the time goes in v5:
time: 559 us; the launch traced here: 549 us
  waiting for transfers between devices  218 us (39%)
  local copies, waits for them, and re-layouts  84.5 us (15%)
  other arithmetic  82.2 us (15%)
  starting transfers between devices  80.2 us (14%)
  matrix products  66.6 us (12%)
  between operations  16.8 us (3%)
    ppermute x28, waiting for transfers between devices, trade(): return lax.ppermute(value, ('section', name), route)  205 us
    ppermute x28, starting transfers between devices, trade(): return lax.ppermute(value, ('section', name), route)  39.9 us
    ppermute x20, starting transfers between devices, swap(): return lax.ppermute(value, 'section', [(0, 1), (1, 0)])  36.8 us
    dot_general x8, matrix products, dot_transposed(): lax.dot_general(left, right, (((1,), (1,)), ((), ())), preferred_element_...  23.1 us
    dot_general x8, matrix products, dot(): return jnp.dot(left, right, preferred_element_type=F32)  19.9 us
    unnamed x259, local copies, waits for them, and re-layouts  18.4 us
    select_n x21, other arithmetic, choose(): return jnp.where(first, low, high)  18.1 us
    dot_general x8, matrix products, transpose_dot(): lax.dot_general(left, right, (((0,), (0,)), ((), ())), preferred_element_...  14.7 us
  transfers between devices with their start and end apart: 53, of which 27 were waited for; matrix products, arithmetic and copies ran while one was open for 29% of the time, Pallas kernels for 0%

profile of v5, /device:TPU:1, one launch (start us, length us, event | category | flops | bytes accessed | tf_op | source)
XLA Modules:
  0.0 548.5 jit_solution(16226711828703209622)
XLA Ops:
  25.2 5.1 collective-permute-done.8
  30.3 3.8 collective-permute-start.9
  34.1 18.0 %collective-permute-done.9 = bf16[2,4,32,1024]{3,2,1,0:T(8,128)(2,1)S(1)} collective-permute-done((bf16[2,4,32,1024]{3,2,1,0:T(8,128)(2,1)S(1)}, bf16[2,4,32,1024]{3,2,1,0:T(8,128)(2,1)S(1)}, u32[]{:S(2)}, u32[]{:S(2)}) %collective-permute-start.9) | collective-permute-done | bytes 524320 | tf_op jit(solution)/shard_map/ppermute | solution.py:224
  53.6 14.7 %collective-permute-done.10 = bf16[2,2,4,32,1024]{4,3,2,1,0:T(8,128)(2,1)} collective-permute-done((bf16[2,2,4,32,1024]{4,3,2,1,0:T(8,128)(2,1)}, bf16[2,2,4,32,1024]{4,3,2,1,0:T(8,128)(2,1)}, u32[]{:S(2)}, u32[]{:S(2)}) %collective-permute-start.10) | collective-permute-done | bytes 1048608 | tf_op jit(solution)/shard_map/ppermute | solution.py:224
  73.1 24.1 %collective-permute-done.11 = bf16[2,16,32,1024]{3,2,1,0:T(8,128)(2,1)S(1)} collective-permute-done((bf16[2,16,32,1024]{3,2,1,0:T(8,128)(2,1)S(1)}, bf16[2,16,32,1024]{3,2,1,0:T(8,128)(2,1)S(1)}, u32[]{:S(2)}, u32[]{:S(2)}) %collective-permute-start.11) | collective-permute-done | bytes 2097184 | tf_op jit(solution)/shard_map/ppermute | solution.py:224
  99.9 4.4 broadcast_in_dim.93
  108.1 45.9 %collective-permute-done.12 = bf16[2,2,16,32,1024]{4,3,2,1,0:T(8,128)(2,1)} collective-permute-done((bf16[2,2,16,32,1024]{4,3,2,1,0:T(8,128)(2,1)}, bf16[2,2,16,32,1024]{4,3,2,1,0:T(8,128)(2,1)}, u32[]{:S(2)}, u32[]{:S(2)}) %collective-permute-start.12) | collective-permute-done | bytes 4194336 | tf_op jit(solution)/shard_map/ppermute | solution.py:224
  154.0 3.2 fusion.46
  157.2 3.2 fusion.45
  162.8 14.3 %collective-permute-start.14 = (bf16[512,512]{1,0:T(8,128)(2,1)S(1)}, bf16[512,512]{1,0:T(8,128)(2,1)S(1)}, u32[]{:S(2)}, u32[]{:S(2)}) collective-permute-start(bf16[512,512]{1,0:T(8,128)(2,1)S(1)} %broadcast_select_fusion.10), channel_id=1, source_target_pairs={{0,64},{64,0},{1,65},{65,1},{2,66},{66,2},{3,67},{67,3},{4,68},{68... | collective-permute-start | bytes 1572872 | tf_op jit(solution)/shard_map/ppermute | solution.py:17
  189.0 6.4 %fusion.218 = (bf16[1,16,4,32,1024]{4,3,2,1,0:T(8,128)(2,1)}, bf16[1,16,4,32,1024]{4,3,2,1,0:T(8,128)(2,1)}) fusion(bf16[2,16,4,32,1024]{4,3,2,1,0:T(8,128)(2,1)} %fusion.45), kind=kLoop, calls=%fused_computation.478 | loop fusion | bytes 16777216 | tf_op jit(solution)/shard_map/slice | solution.py:378
  197.2 5.2 multiply_convert_fusion.1
  227.5 5.2 multiply_convert_fusion
  249.7 4.6 fusion.74
  281.6 4.0 dynamic_update_slice.113
  285.6 3.0 fusion.55
  288.6 3.7 fusion.68
  299.1 3.5 convert_dynamic-update-slice_fusion
  308.3 3.7 convert_reduce_fusion
  312.1 4.4 fusion.71
  328.0 6.8 %collective-permute-start.24 = (bf16[2,4,64,2048]{3,2,1,0:T(8,128)(2,1)}, bf16[2,4,64,2048]{3,2,1,0:T(8,128)(2,1)}, u32[]{:S(2)}, u32[]{:S(2)}) collective-permute-start(bf16[2,4,64,2048]{3,2,1,0:T(8,128)(2,1)} %pad_maximum_fusion.4), channel_id=1, source_target_pairs={{0,1},{1,0},{2,3},{3,2},{4,5},{5,4},{6,7},{7,6},{8,9},{9,8},{10,11... | collective-permute-start | bytes 6291464 | tf_op jit(solution)/shard_map/ppermute | solution.py:224
  351.4 32.5 %collective-permute-done.24 = bf16[2,4,64,2048]{3,2,1,0:T(8,128)(2,1)} collective-permute-done((bf16[2,4,64,2048]{3,2,1,0:T(8,128)(2,1)}, bf16[2,4,64,2048]{3,2,1,0:T(8,128)(2,1)}, u32[]{:S(2)}, u32[]{:S(2)}) %collective-permute-start.24) | collective-permute-done | bytes 2097184 | tf_op jit(solution)/shard_map/ppermute | solution.py:224
  387.0 3.3 fusion.53
  393.7 7.4 %collective-permute-done.27 = bf16[16,32,1024]{2,1,0:T(8,128)(2,1)} collective-permute-done((bf16[16,32,1024]{2,1,0:T(8,128)(2,1)}, bf16[16,32,1024]{2,1,0:T(8,128)(2,1)}, u32[]{:S(2)}, u32[]{:S(2)}) %collective-permute-start.27) | collective-permute-done | bytes 1048608 | tf_op jit(solution)/shard_map/ppermute | solution.py:224
  401.1 9.4 %collective-permute-done.28 = bf16[4,64,2048]{2,1,0:T(8,128)(2,1)} collective-permute-done((bf16[4,64,2048]{2,1,0:T(8,128)(2,1)}, bf16[4,64,2048]{2,1,0:T(8,128)(2,1)}, u32[]{:S(2)}, u32[]{:S(2)}) %collective-permute-start.28) | collective-permute-done | bytes 1048608 | tf_op jit(solution)/shard_map/ppermute | solution.py:224
  425.6 7.3 %collective-permute-done.30 = bf16[2,4,16,2048]{3,2,1,0:T(8,128)(2,1)S(1)} collective-permute-done((bf16[2,4,16,2048]{3,2,1,0:T(8,128)(2,1)S(1)}, bf16[2,4,16,2048]{3,2,1,0:T(8,128)(2,1)S(1)}, u32[]{:S(2)}, u32[]{:S(2)}) %collective-permute-start.30) | collective-permute-done | bytes 524320 | tf_op jit(solution)/shard_map/ppermute | solution.py:224
  434.1 4.4 collective-permute-done.29
  450.2 4.8 collective-permute-done.32
  484.5 6.1 %collective-permute-done.44 = bf16[64,2176]{1,0:T(8,128)(2,1)} collective-permute-done((bf16[64,2176]{1,0:T(8,128)(2,1)S(1)}, bf16[64,2176]{1,0:T(8,128)(2,1)}, u32[]{:S(2)}, u32[]{:S(2)}) %collective-permute-start.44) | collective-permute-done | bytes 278560 | tf_op jit(solution)/shard_map/ppermute | solution.py:231
  490.6 3.4 collective-permute-done.43
  494.4 16.8 %collective-permute-done.47 = bf16[2,16,10368]{2,1,0:T(8,128)(2,1)S(1)} collective-permute-done((bf16[2,16,10368]{2,1,0:T(8,128)(2,1)S(1)}, bf16[2,16,10368]{2,1,0:T(8,128)(2,1)S(1)}, u32[]{:S(2)}, u32[]{:S(2)}) %collective-permute-start.47) | collective-permute-done | bytes 663584 | tf_op jit(solution)/shard_map/ppermute | solution.py:224
  511.3 13.2 %collective-permute-start.49 = (bf16[64,2048]{1,0:T(8,128)(2,1)S(1)}, bf16[64,2048]{1,0:T(8,128)(2,1)S(1)}, u32[]{:S(2)}, u32[]{:S(2)}) collective-permute-start(bf16[64,2048]{1,0:T(8,128)(2,1)S(1)} %broadcast_select_fusion.25), channel_id=1, source_target_pairs={{0,64},{64,0},{1,65},{65,1},{2,66},{66,2},{3,67},{67,3},{4,68},{68... | collective-permute-start | bytes 786440 | tf_op jit(solution)/shard_map/ppermute | solution.py:17
  (645 shorter events, 236.0 us)
Async XLA Ops:
  7.2 153.2 %all-gather.2.cloned.1.call-start = ((), (), s32[]{:S(2)}) async-start(), calls=%async_computation.1 | async-start | bytes 18382848 | tf_op jit(solution)/shard_map/all_gather | solution.py:326
  17.6 437.4 %reduce-scatter.2.cloned.1.call-start = ((), (), s32[]{:S(2)}) async-start(), calls=%async_computation.2 | async-start | bytes 9191424 | tf_op jit(solution)/shard_map/reduce_scatter | solution.py:396
  30.3 21.8 %collective-permute-start.9 = (bf16[2,4,32,1024]{3,2,1,0:T(8,128)(2,1)S(1)}, bf16[2,4,32,1024]{3,2,1,0:T(8,128)(2,1)S(1)}, u32[]{:S(2)}, u32[]{:S(2)}) collective-permute-start(bf16[2,4,32,1024]{3,2,1,0:T(8,128)(2,1)S(1)} %fusion.165), channel_id=1, source_target_pairs={{0,4},{1,5},{2,6},{3,7},{4,0},{5,1},{6,2},{7,3},{8,12},{9,13},{10,... | collective-permute-start | bytes 1572872 | tf_op jit(solution)/shard_map/ppermute | solution.py:224
  53.2 15.1 %collective-permute-start.10 = (bf16[2,2,4,32,1024]{4,3,2,1,0:T(8,128)(2,1)}, bf16[2,2,4,32,1024]{4,3,2,1,0:T(8,128)(2,1)}, u32[]{:S(2)}, u32[]{:S(2)}) collective-permute-start(bf16[2,2,4,32,1024]{4,3,2,1,0:T(8,128)(2,1)} %pad_maximum_fusion.6), channel_id=1, source_target_pairs={{0,12},{1,13},{2,14},{3,15},{4,8},{5,9},{6,10},{7,11},{8,4},{9,5},... | collective-permute-start | bytes 3145736 | tf_op jit(solution)/shard_map/ppermute | solution.py:224
  70.6 26.6 %collective-permute-start.11 = (bf16[2,16,32,1024]{3,2,1,0:T(8,128)(2,1)S(1)}, bf16[2,16,32,1024]{3,2,1,0:T(8,128)(2,1)S(1)}, u32[]{:S(2)}, u32[]{:S(2)}) collective-permute-start(bf16[2,16,32,1024]{3,2,1,0:T(8,128)(2,1)S(1)} %bitcast.481), channel_id=1, source_target_pairs={{0,16},{16,0},{32,48},{48,32},{64,112},{80,96},{96,80},{112,64},{1... | collective-permute-start | bytes 6291464 | tf_op jit(solution)/shard_map/ppermute | solution.py:224
  99.9 54.1 %collective-permute-start.12 = (bf16[2,2,16,32,1024]{4,3,2,1,0:T(8,128)(2,1)}, bf16[2,2,16,32,1024]{4,3,2,1,0:T(8,128)(2,1)}, u32[]{:S(2)}, u32[]{:S(2)}) collective-permute-start(bf16[2,2,16,32,1024]{4,3,2,1,0:T(8,128)(2,1)} %pad_maximum_fusion), channel_id=1, source_target_pairs={{0,48},{16,32},{32,16},{48,0},{64,80},{80,64},{96,112},{112,96},{1... | collective-permute-start | bytes 12582920 | tf_op jit(solution)/shard_map/ppermute | solution.py:224
  162.8 18.6 %collective-permute-start.14 = (bf16[512,512]{1,0:T(8,128)(2,1)S(1)}, bf16[512,512]{1,0:T(8,128)(2,1)S(1)}, u32[]{:S(2)}, u32[]{:S(2)}) collective-permute-start(bf16[512,512]{1,0:T(8,128)(2,1)S(1)} %broadcast_select_fusion.10), channel_id=1, source_target_pairs={{0,64},{64,0},{1,65},{65,1},{2,66},{66,2},{3,67},{67,3},{4,68},{68... | collective-permute-start | bytes 1572872 | tf_op jit(solution)/shard_map/ppermute | solution.py:17
  188.8 7.8 %collective-permute-start.5 = (bf16[256,1024]{1,0:T(8,128)(2,1)S(1)}, bf16[256,1024]{1,0:T(8,128)(2,1)S(1)}, u32[]{:S(2)}, u32[]{:S(2)}) collective-permute-start(bf16[256,1024]{1,0:T(8,128)(2,1)S(1)} %convolution_convert_fusion.8), channel_id=1, source_target_pairs={{0,64},{64,0},{1,65},{65,1},{2,66},{66,2},{3,67},{67,3},{4,68},{68... | collective-permute-start | bytes 1572872 | tf_op jit(solution)/shard_map/ppermute | solution.py:17
  244.7 33.4 %collective-permute-start.17 = (bf16[2,16,32,1024]{3,2,1,0:T(8,128)(2,1)}, bf16[2,16,32,1024]{3,2,1,0:T(8,128)(2,1)}, u32[]{:S(2)}, u32[]{:S(2)}) collective-permute-start(bf16[2,16,32,1024]{3,2,1,0:T(8,128)(2,1)} %pad_maximum_fusion.2), channel_id=1, source_target_pairs={{0,16},{16,0},{32,48},{48,32},{64,112},{80,96},{96,80},{112,64},{1... | collective-permute-start | bytes 6291464 | tf_op jit(solution)/shard_map/ppermute | solution.py:224
  288.6 16.5 %collective-permute-start.20 = (bf16[16,32,1024]{2,1,0:T(8,128)(2,1)}, bf16[16,32,1024]{2,1,0:T(8,128)(2,1)}, u32[]{:S(2)}, u32[]{:S(2)}) collective-permute-start(bf16[16,32,1024]{2,1,0:T(8,128)(2,1)} %fusion.55), channel_id=1, source_target_pairs={{0,48},{16,32},{32,16},{48,0},{64,80},{80,64},{96,112},{112,96},{1... | collective-permute-start | bytes 3145736 | tf_op jit(solution)/shard_map/ppermute | solution.py:224
  292.4 10.2 %collective-permute-start.21 = (bf16[256,1024]{1,0:T(8,128)(2,1)}, bf16[256,1024]{1,0:T(8,128)(2,1)}, u32[]{:S(2)}, u32[]{:S(2)}) collective-permute-start(bf16[256,1024]{1,0:T(8,128)(2,1)} %fusion.68), channel_id=1, source_target_pairs={{0,64},{64,0},{1,65},{65,1},{2,66},{66,2},{3,67},{67,3},{4,68},{68... | collective-permute-start | bytes 1572872 | tf_op jit(solution)/shard_map/ppermute | solution.py:17
  316.4 18.9 %collective-permute-start.22 = (bf16[256,1024]{1,0:T(8,128)(2,1)}, bf16[256,1024]{1,0:T(8,128)(2,1)}, u32[]{:S(2)}, u32[]{:S(2)}) collective-permute-start(bf16[256,1024]{1,0:T(8,128)(2,1)} %fusion.71), channel_id=1, source_target_pairs={{0,64},{64,0},{1,65},{65,1},{2,66},{66,2},{3,67},{67,3},{4,68},{68... | collective-permute-start | bytes 1572872 | tf_op jit(solution)/shard_map/ppermute | solution.py:17
  321.5 29.9 %collective-permute-start.23 = (bf16[2,16,32,1024]{3,2,1,0:T(8,128)(2,1)}, bf16[2,16,32,1024]{3,2,1,0:T(8,128)(2,1)}, u32[]{:S(2)}, u32[]{:S(2)}) collective-permute-start(bf16[2,16,32,1024]{3,2,1,0:T(8,128)(2,1)} %pad_maximum_fusion.3), channel_id=1, source_target_pairs={{0,16},{16,0},{32,48},{48,32},{64,112},{80,96},{96,80},{112,64},{1... | collective-permute-start | bytes 6291464 | tf_op jit(solution)/shard_map/ppermute | solution.py:224
  328.0 55.9 %collective-permute-start.24 = (bf16[2,4,64,2048]{3,2,1,0:T(8,128)(2,1)}, bf16[2,4,64,2048]{3,2,1,0:T(8,128)(2,1)}, u32[]{:S(2)}, u32[]{:S(2)}) collective-permute-start(bf16[2,4,64,2048]{3,2,1,0:T(8,128)(2,1)} %pad_maximum_fusion.4), channel_id=1, source_target_pairs={{0,1},{1,0},{2,3},{3,2},{4,5},{5,4},{6,7},{7,6},{8,9},{9,8},{10,11... | collective-permute-start | bytes 6291464 | tf_op jit(solution)/shard_map/ppermute | solution.py:224
  386.9 14.3 %collective-permute-start.27 = (bf16[16,32,1024]{2,1,0:T(8,128)(2,1)}, bf16[16,32,1024]{2,1,0:T(8,128)(2,1)}, u32[]{:S(2)}, u32[]{:S(2)}) collective-permute-start(bf16[16,32,1024]{2,1,0:T(8,128)(2,1)} %fusion.54), channel_id=1, source_target_pairs={{0,48},{16,32},{32,16},{48,0},{64,80},{80,64},{96,112},{112,96},{1... | collective-permute-start | bytes 3145736 | tf_op jit(solution)/shard_map/ppermute | solution.py:224
  390.3 20.2 %collective-permute-start.28 = (bf16[4,64,2048]{2,1,0:T(8,128)(2,1)}, bf16[4,64,2048]{2,1,0:T(8,128)(2,1)}, u32[]{:S(2)}, u32[]{:S(2)}) collective-permute-start(bf16[4,64,2048]{2,1,0:T(8,128)(2,1)} %fusion.53), channel_id=1, source_target_pairs={{0,3},{1,2},{2,1},{3,0},{4,7},{5,6},{6,5},{7,4},{8,11},{9,10},{10,... | collective-permute-start | bytes 3145736 | tf_op jit(solution)/shard_map/ppermute | solution.py:224
  410.9 27.6 %collective-permute-start.29 = (bf16[2,4,64,2176]{3,2,1,0:T(8,128)(2,1)S(1)}, bf16[2,4,64,2176]{3,2,1,0:T(8,128)(2,1)S(1)}, u32[]{:S(2)}, u32[]{:S(2)}) collective-permute-start(bf16[2,4,64,2176]{3,2,1,0:T(8,128)(2,1)S(1)} %pad_maximum_fusion.1), channel_id=1, source_target_pairs={{0,4},{1,5},{2,6},{3,7},{4,0},{5,1},{6,2},{7,3},{8,12},{9,13},{10,... | collective-permute-start | bytes 6684680 | tf_op jit(solution)/shard_map/ppermute | solution.py:224
  419.3 14.9 %collective-permute-start.31 = (bf16[2,2,4,32,1024]{4,3,2,1,0:T(8,128)(2,1)S(1)}, bf16[2,2,4,32,1024]{4,3,2,1,0:T(8,128)(2,1)S(1)}, u32[]{:S(2)}, u32[]{:S(2)}) collective-permute-start(bf16[2,2,4,32,1024]{4,3,2,1,0:T(8,128)(2,1)S(1)} %pad_maximum_fusion.8), channel_id=1, source_target_pairs={{0,1},{1,0},{2,3},{3,2},{4,5},{5,4},{6,7},{7,6},{8,9},{9,8},{10,11... | collective-permute-start | bytes 3145736 | tf_op jit(solution)/shard_map/ppermute | solution.py:224
  423.5 9.3 %collective-permute-start.30 = (bf16[2,4,16,2048]{3,2,1,0:T(8,128)(2,1)S(1)}, bf16[2,4,16,2048]{3,2,1,0:T(8,128)(2,1)S(1)}, u32[]{:S(2)}, u32[]{:S(2)}) collective-permute-start(bf16[2,4,16,2048]{3,2,1,0:T(8,128)(2,1)S(1)} %pad_maximum_fusion.18), channel_id=1, source_target_pairs={{0,16},{16,0},{32,48},{48,32},{64,112},{80,96},{96,80},{112,64},{1... | collective-permute-start | bytes 1572872 | tf_op jit(solution)/shard_map/ppermute | solution.py:224
  440.0 15.0 %collective-permute-start.32 = (bf16[4,64,2176]{2,1,0:T(8,128)(2,1)}, bf16[4,64,2176]{2,1,0:T(8,128)(2,1)}, u32[]{:S(2)}, u32[]{:S(2)}) collective-permute-start(bf16[4,64,2176]{2,1,0:T(8,128)(2,1)} %fusion.89), channel_id=1, source_target_pairs={{0,12},{1,13},{2,14},{3,15},{4,8},{5,9},{6,10},{7,11},{8,4},{9,5},... | collective-permute-start | bytes 3342344 | tf_op jit(solution)/shard_map/ppermute | solution.py:224
  441.7 8.5 %collective-permute-start.34 = (bf16[2,4,32,1024]{3,2,1,0:T(8,128)(2,1)S(1)}, bf16[2,4,32,1024]{3,2,1,0:T(8,128)(2,1)}, u32[]{:S(2)}, u32[]{:S(2)}) collective-permute-start(bf16[2,4,32,1024]{3,2,1,0:T(8,128)(2,1)S(1)} %fusion.96), channel_id=1, source_target_pairs={{0,3},{1,2},{2,1},{3,0},{4,7},{5,6},{6,5},{7,4},{8,11},{9,10},{10,... | collective-permute-start | bytes 1572872 | tf_op jit(solution)/shard_map/ppermute | solution.py:224
  457.5 14.2 %collective-permute-start.35 = (bf16[2,64,2176]{2,1,0:T(8,128)(2,1)S(1)}, bf16[2,64,2176]{2,1,0:T(8,128)(2,1)S(1)}, u32[]{:S(2)}, u32[]{:S(2)}) collective-permute-start(bf16[2,64,2176]{2,1,0:T(8,128)(2,1)S(1)} %pad_maximum_fusion.17), channel_id=1, source_target_pairs={{0,1},{1,0},{2,3},{3,2},{4,5},{5,4},{6,7},{7,6},{8,9},{9,8},{10,11... | collective-permute-start | bytes 1671176 | tf_op jit(solution)/shard_map/ppermute | solution.py:224
  460.9 10.4 %collective-permute-start.36 = (bf16[2,16,2048]{2,1,0:T(8,128)(2,1)S(1)}, bf16[2,16,2048]{2,1,0:T(8,128)(2,1)S(1)}, u32[]{:S(2)}, u32[]{:S(2)}) collective-permute-start(bf16[2,16,2048]{2,1,0:T(8,128)(2,1)S(1)} %pad_maximum_fusion.24), channel_id=1, source_target_pairs={{0,4},{1,5},{2,6},{3,7},{4,0},{5,1},{6,2},{7,3},{8,12},{9,13},{10,... | collective-permute-start | bytes 393224 | tf_op jit(solution)/shard_map/ppermute | solution.py:224
  464.2 7.1 %collective-permute-start.37 = (bf16[2,2,32,1024]{3,2,1,0:T(8,128)(2,1)S(1)}, bf16[2,2,32,1024]{3,2,1,0:T(8,128)(2,1)S(1)}, u32[]{:S(2)}, u32[]{:S(2)}) collective-permute-start(bf16[2,2,32,1024]{3,2,1,0:T(8,128)(2,1)S(1)} %pad_maximum_fusion.22), channel_id=1, source_target_pairs={{0,4},{1,5},{2,6},{3,7},{4,0},{5,1},{6,2},{7,3},{8,12},{9,13},{10,... | collective-permute-start | bytes 786440 | tf_op jit(solution)/shard_map/ppermute | solution.py:224
  471.8 7.4 %collective-permute-start.39 = (bf16[64,2176]{1,0:T(8,128)(2,1)S(1)}, bf16[64,2176]{1,0:T(8,128)(2,1)S(1)}, u32[]{:S(2)}, u32[]{:S(2)}) collective-permute-start(bf16[64,2176]{1,0:T(8,128)(2,1)S(1)} %fusion.121), channel_id=1, source_target_pairs={{0,3},{1,2},{2,1},{3,0},{4,7},{5,6},{6,5},{7,4},{8,11},{9,10},{10,... | collective-permute-start | bytes 835592 | tf_op jit(solution)/shard_map/ppermute | solution.py:224
  479.4 11.2 %collective-permute-start.44 = (bf16[64,2176]{1,0:T(8,128)(2,1)S(1)}, bf16[64,2176]{1,0:T(8,128)(2,1)}, u32[]{:S(2)}, u32[]{:S(2)}) collective-permute-start(bf16[64,2176]{1,0:T(8,128)(2,1)S(1)} %fusion.104), channel_id=1, source_target_pairs={{0,16},{16,32},{32,48},{48,0},{1,17},{17,33},{33,49},{49,1},{2,18}... | collective-permute-start | bytes 835592 | tf_op jit(solution)/shard_map/ppermute | solution.py:231
  479.9 10.7 %collective-permute-start.45 = (bf16[64,2176]{1,0:T(8,128)(2,1)S(1)}, bf16[64,2176]{1,0:T(8,128)(2,1)}, u32[]{:S(2)}, u32[]{:S(2)}) collective-permute-start(bf16[64,2176]{1,0:T(8,128)(2,1)S(1)} %fusion.104), channel_id=1, source_target_pairs={{0,32},{16,48},{32,0},{48,16},{1,33},{17,49},{33,1},{49,17},{2,34}... | collective-permute-start | bytes 835592 | tf_op jit(solution)/shard_map/ppermute | solution.py:231
  481.7 8.9 %collective-permute-start.46 = (bf16[64,2176]{1,0:T(8,128)(2,1)S(1)}, bf16[64,2176]{1,0:T(8,128)(2,1)}, u32[]{:S(2)}, u32[]{:S(2)}) collective-permute-start(bf16[64,2176]{1,0:T(8,128)(2,1)S(1)} %fusion.104), channel_id=1, source_target_pairs={{0,48},{16,0},{32,16},{48,32},{1,49},{17,1},{33,17},{49,33},{2,50}... | collective-permute-start | bytes 835592 | tf_op jit(solution)/shard_map/ppermute | solution.py:231
  483.9 10.1 %collective-permute-start.43 = (bf16[16,10368]{1,0:T(8,128)(2,1)S(1)}, bf16[16,10368]{1,0:T(8,128)(2,1)S(1)}, u32[]{:S(2)}, u32[]{:S(2)}) collective-permute-start(bf16[16,10368]{1,0:T(8,128)(2,1)S(1)} %get-tuple-element.228), channel_id=1, source_target_pairs={{0,16},{16,0},{32,48},{48,32},{64,112},{80,96},{96,80},{112,64},{1... | collective-permute-start | bytes 995336 | tf_op jit(solution)/shard_map/ppermute | solution.py:224
  494.1 17.1 %collective-permute-start.47 = (bf16[2,16,10368]{2,1,0:T(8,128)(2,1)S(1)}, bf16[2,16,10368]{2,1,0:T(8,128)(2,1)S(1)}, u32[]{:S(2)}, u32[]{:S(2)}) collective-permute-start(bf16[2,16,10368]{2,1,0:T(8,128)(2,1)S(1)} %pad_maximum_fusion.16), channel_id=1, source_target_pairs={{0,48},{16,32},{32,16},{48,0},{64,80},{80,64},{96,112},{112,96},{1... | collective-permute-start | bytes 1990664 | tf_op jit(solution)/shard_map/ppermute | solution.py:224
  511.3 15.2 %collective-permute-start.49 = (bf16[64,2048]{1,0:T(8,128)(2,1)S(1)}, bf16[64,2048]{1,0:T(8,128)(2,1)S(1)}, u32[]{:S(2)}, u32[]{:S(2)}) collective-permute-start(bf16[64,2048]{1,0:T(8,128)(2,1)S(1)} %broadcast_select_fusion.25), channel_id=1, source_target_pairs={{0,64},{64,0},{1,65},{65,1},{2,66},{66,2},{3,67},{67,3},{4,68},{68... | collective-permute-start | bytes 786440 | tf_op jit(solution)/shard_map/ppermute | solution.py:17
  532.5 6.6 %collective-permute-start.50 = (bf16[128,1024]{1,0:T(8,128)(2,1)S(1)}, bf16[128,1024]{1,0:T(8,128)(2,1)}, u32[]{:S(2)}, u32[]{:S(2)}) collective-permute-start(bf16[128,1024]{1,0:T(8,128)(2,1)S(1)} %select_n.711), channel_id=1, source_target_pairs={{0,64},{64,0},{1,65},{65,1},{2,66},{66,2},{3,67},{67,3},{4,68},{68... | collective-permute-start | bytes 786440 | tf_op jit(solution)/shard_map/ppermute | solution.py:17
  (145 other events, 646.0 us)
Sparse Core Ops, SparseCore 0:
  17.7 124.1 all-gather.1
  305.3 99.4 reduce-scatter.1

commit v6 on v5

--- a/solution.py
+++ b/solution.py
@@ -112,8 +112,8 @@
     grad_upward = (dot_transposed(grad_mixed, weights["down"]) * kept["slope"]).astype(BF)
     passed = dot_transposed(grad_upward, weights["up"])
     grads = dict(
-        down=transpose_dot(kept["activated"], grad_mixed).astype(BF),
-        up=transpose_dot(kept["hidden"], grad_upward).astype(BF),
+        mixed=grad_mixed,
+        upward=grad_upward,
         bias_up=jnp.sum(grad_upward.astype(F32), axis=0),
         bias_down=jnp.sum(grad_mixed.astype(F32), axis=0),
         gain_mlp=grad_gain,
@@ -251,16 +251,32 @@
     def chunk(value, at, dim):
         return lax.dynamic_index_in_dim(value, at, dim, keepdims=False)
 
-    def scatter_one(value, axis, dim):
-        sent = [chunk(value, near[axis], dim), chunk(value, place[axis] ^ 2, dim)]
-        return trade(jnp.stack(sent), axis, (1, 3))
-
-    def scatter_two(value, beside, axis, dim):
-        sent = chunk(value, far[axis], dim).astype(F32) + beside[1].astype(F32)
+    def slices(value, dim):
+        def two(at, other):
+            return jnp.stack([chunk(value, at, dim), chunk(value, other, dim)])
+
+        return (lambda at: chunk(value, at, dim).astype(F32), two)
+
+    def products(left, right, shape):
+        def one(at):
+            return transpose_dot(chunk(left, at, 0), right).reshape(shape)
+
+        def two(at, other):
+            pair = jnp.stack([chunk(left, at, 0), chunk(left, other, 0)])
+            both = lax.dot_general(pair, right, (((1,), (0,)), ((), ())), preferred_element_type=F32)
+            return both.astype(BF).reshape((2,) + shape)
+
+        return (one, two)
+
+    def scatter_one(parts, axis):
+        return trade(parts[1](near[axis], place[axis] ^ 2), axis, (1, 3))
+
+    def scatter_two(parts, beside, axis):
+        sent = parts[0](far[axis]) + beside[1].astype(F32)
         return trade(sent.astype(BF), axis, (3, 1))
 
-    def scatter_end(value, beside, across, axis, dim):
-        kept = chunk(value, place[axis], dim).astype(F32) + beside[0].astype(F32)
+    def scatter_end(parts, beside, across, axis):
+        kept = parts[0](place[axis]) + beside[0].astype(F32)
         return (kept + across.astype(F32)).astype(BF)
 
     def together(*values):
@@ -305,26 +321,27 @@
     blocks = [mine_of(own, got) for own, got in zip(kept_part, got_part)]
     edges = (LANES, LANES + 3 * half, LANES + 4 * half, LANES + 4 * half + shards * unit)
 
-    side = []
-    for layer in range(2):
-        side += [(layer * edges[3] + at, b[layer]) for at, b in zip((0,) + edges, blocks[:4])]
-    side = placed(2 * edges[3], side)
-
     quarter = unit // RING
 
     def quarter_of(block):
         return chunk(block.reshape(RING, quarter, model), place["x"], 0)
 
-    c = jnp.stack([quarter_of(block) for block in blocks[4]])
-    cn = gather_one(c, "y")
-    c = gather_end(c, cn, gather_two(c, cn, "y"), "y", 1)
-    cn = gather_one(c, "z")
-    c = gather_end(c, cn, gather_two(c, cn, "z"), "z", 1).reshape(2, shards, quarter, model)
-    cn = gather_one(c, "x")
-    c = gather_end(c, cn, gather_two(c, cn, "x"), "x", 2).reshape(2, -1, model)
-
-    side = lax.all_gather(side, "shard", axis=0, tiled=True)
-    sides = [side[:, layer * edges[3] : (layer + 1) * edges[3]] for layer in range(2)]
+    span = quarter * model // rows
+
+    def gathered(layer, extra):
+        pieces = list(zip((0,) + edges, [b[layer] for b in blocks[:4]]))
+        pieces += [(edges[3] + n * span, piece) for n, piece in enumerate(extra)]
+        return placed(edges[3] + len(extra) * span, pieces)
+
+    def whole(block):
+        return lax.all_gather(block, "shard", axis=0, tiled=True)
+
+    side0 = whole(gathered(0, [quarter_of(block).reshape(rows, span) for block in blocks[4]]))
+    side1 = whole(after(gathered(1, []), side0))
+    c0, c1 = (
+        side0[:, edges[3] + n * span : edges[3] + (n + 1) * span].reshape(shards, quarter, model)
+        for n in range(2)
+    )
 
     def arranged(attn, down):
         flat = attn[:, :LANES].reshape(shards, rows, LANES)[:, :vector_rows, :rows].astype(F32)
@@ -371,76 +388,96 @@
     count = tokens.shape[0]
     seq_lengths = lengths[:, 0]
 
-    first_weights = arranged(sides[0], c[0])
+    first_weights = arranged(side0[:, : edges[3]], None)
+    cn = gather_one(c0, "x")
     attended, kept0 = forward_attention(tokens.reshape(-1, model), first_weights, seq_lengths)
+    cn, attended = together(cn, attended)
+    cf = gather_two(c0, cn, "x")
     activated = forward_hidden(attended, kept0, first_weights)
+    cf, activated = together(cf, activated)
+    first_weights["down"] = gather_end(c0, cn, cf, "x", 1).reshape(-1, model)
+    cn = gather_one(after(c1, cf), "x")
     middle = forward_output(activated, kept0, first_weights)
-    second_weights = arranged(sides[1], c[1])
+    cn, middle, side1 = together(cn, middle, side1)
+    cf = gather_two(c1, cn, "x")
+    second_weights = arranged(side1, None)
     attended, kept1 = forward_attention(middle, second_weights, seq_lengths)
     activated = forward_hidden(attended, kept1, second_weights)
+    cf, activated = together(cf, activated)
+    second_weights["down"] = gather_end(c1, cn, cf, "x", 1).reshape(-1, model)
     last = forward_output(activated, kept1, second_weights)
 
-    def down_of(grads):
-        return grads["down"].reshape(shards, RING, quarter, model)
+    def down_of(grads, kept):
+        left = kept["activated"].reshape(-1, shards, RING, quarter).transpose(2, 0, 1, 3)
+        left = left.reshape(RING, -1, shards * quarter)
+        return products(left, grads["mixed"], (shards, quarter, model))
+
+    def up_of(grads, kept):
+        left = kept["hidden"].reshape(-1, RING, RING, rows).transpose(2, 0, 1, 3)
+        return products(left.reshape(RING, -1, RING * rows), grads["upward"], (RING, rows, shards * unit))
+
+    def side_of(grads):
+        pieces = list(zip((0,) + edges, side_by_side(grads)))
+        return placed(edges[2], pieces).reshape(RING, RING, rows, -1)
 
     grad_hidden, grads1 = backward_mlp(cotangent.reshape(-1, model), kept1, second_weights)
-    c1 = down_of(grads1)
-    cn = scatter_one(c1, "x", 1)
+    c1, b1 = (down_of(grads1, kept1), up_of(grads1, kept1))
+    cn, bn = (scatter_one(c1, "x"), scatter_one(b1, "y"))
     grad_resid, grad_packed = backward_attention(grad_hidden, grads1, kept1, second_weights)
-    cn, grad_packed = together(cn, grad_packed)
-    cf = scatter_two(c1, cn, "x", 1)
+    cn, bn, grad_packed = together(cn, bn, grad_packed)
+    cf, bf = (scatter_two(c1, cn, "x"), scatter_two(b1, bn, "y"))
     grad_middle = backward_inputs(grad_resid, grad_packed, grads1, kept1, second_weights)
-    pieces = side_by_side(grads1) + (grads1["up"],)
-    side1 = placed(edges[3], list(zip((0,) + edges, pieces)))
-    side1, cf, grad_middle = together(side1, cf, grad_middle)
-    side1 = lax.psum_scatter(side1, "shard", scatter_dimension=0, tiled=True)
-    c1 = scatter_end(c1, cn, cf, "x", 1)
+    a1 = side_of(grads1)
+    a1, cf, bf, grad_middle = together(a1, cf, bf, grad_middle)
+    c1, b1 = (scatter_end(c1, cn, cf, "x"), scatter_end(b1, bn, bf, "y"))
+    a1 = slices(a1, 0)
+    an1 = scatter_one(a1, "z")
 
     grad_hidden, grads0 = backward_mlp(grad_middle, kept0, first_weights)
-    c0, b0 = (down_of(grads0), grads0["up"].reshape(RING, RING, rows, -1))
-    cn, bn = (scatter_one(c0, "x", 1), scatter_one(b0, "y", 1))
+    c0, b0 = (down_of(grads0, kept0), up_of(grads0, kept0))
+    cn, bn = (scatter_one(c0, "x"), scatter_one(b0, "y"))
     grad_resid, grad_packed = backward_attention(grad_hidden, grads0, kept0, first_weights)
-    cn, bn, grad_packed = together(cn, bn, grad_packed)
-    cf, bf = (scatter_two(c0, cn, "x", 1), scatter_two(b0, bn, "y", 1))
+    an1, cn, bn, grad_packed = together(an1, cn, bn, grad_packed)
+    af1 = scatter_two(a1, an1, "z")
+    cf, bf = (scatter_two(c0, cn, "x"), scatter_two(b0, bn, "y"))
     grad_first = backward_inputs(grad_resid, grad_packed, grads0, kept0, first_weights)
-    a0 = placed(edges[2], list(zip((0,) + edges, side_by_side(grads0))))
-    a0 = a0.reshape(RING, RING, rows, -1)
-    a0, cf, bf = together(a0, cf, bf)
-    c0, b0 = (scatter_end(c0, cn, cf, "x", 1), scatter_end(b0, bn, bf, "y", 1))
-
-    b = b0.reshape(RING, RING, rows // RING, -1)
+    a0 = side_of(grads0)
+    a0, af1, cf, bf = together(a0, af1, cf, bf)
+    a1 = scatter_end(a1, an1, af1, "z")
+    c0, b0 = (scatter_end(c0, cn, cf, "x"), scatter_end(b0, bn, bf, "y"))
+
+    b = jnp.stack([b0, b1]).reshape(2, RING, RING, rows // RING, -1)
     c = jnp.stack([c0, c1]).reshape(2, RING, RING, quarter, model)
-    an, bn, cn = together(scatter_one(a0, "z", 0), scatter_one(b, "x", 1), scatter_one(c, "y", 2))
-    af, bf, cf, side1 = together(
-        scatter_two(a0, an, "z", 0), scatter_two(b, bn, "x", 1), scatter_two(c, cn, "y", 2), side1
-    )
-    side1 = side1.reshape(RING, rows // RING, -1)
-    a0 = scatter_end(a0, an, af, "z", 0)
-    b, c = (scatter_end(b, bn, bf, "x", 1), scatter_end(c, cn, cf, "y", 2))
+    a0, a1, b, c = (slices(a0, 0), slices(a1, 0), slices(b, 2), slices(c, 2))
     an, bn, cn, dn = together(
-        scatter_one(a0, "y", 0), scatter_one(b, "z", 0), scatter_one(c, "z", 1), scatter_one(side1, "x", 0)
+        scatter_one(a0, "z"), scatter_one(b, "x"), scatter_one(c, "y"), scatter_one(a1, "y")
     )
     af, bf, cf, df = together(
-        scatter_two(a0, an, "y", 0),
-        scatter_two(b, bn, "z", 0),
-        scatter_two(c, cn, "z", 1),
-        scatter_two(side1, dn, "x", 0),
-    )
-    a0 = scatter_end(a0, an, af, "y", 0)
-    b, c = (scatter_end(b, bn, bf, "z", 0), scatter_end(c, cn, cf, "z", 1))
-    side1 = scatter_end(side1, dn, df, "x", 0)
-    wide = b.shape[1]
-    bc = jnp.concatenate([b, c[0].reshape(b.shape), c[1].reshape(b.shape), side1], axis=1)
-    bn = gather_one(bc, "x")
+        scatter_two(a0, an, "z"), scatter_two(b, bn, "x"), scatter_two(c, cn, "y"), scatter_two(a1, dn, "y")
+    )
+    a0 = slices(scatter_end(a0, an, af, "z"), 0)
+    a1 = slices(scatter_end(a1, dn, df, "y").reshape(RING, rows // RING, -1), 0)
+    b, c = (slices(scatter_end(b, bn, bf, "x"), 1), slices(scatter_end(c, cn, cf, "y"), 1))
+    an, bn, cn, dn = together(
+        scatter_one(a0, "y"), scatter_one(b, "z"), scatter_one(c, "z"), scatter_one(a1, "x")
+    )
+    af, bf, cf, df = together(
+        scatter_two(a0, an, "y"), scatter_two(b, bn, "z"), scatter_two(c, cn, "z"), scatter_two(a1, dn, "x")
+    )
+    a0 = scatter_end(a0, an, af, "y")
+    a1 = scatter_end(a1, dn, df, "x")
+    b, c = (scatter_end(b, bn, bf, "z"), scatter_end(c, cn, cf, "z"))
+    wide = shards * unit
+    rest = [b[0], c[0].reshape(-1, wide), b[1], c[1].reshape(-1, wide), a1]
+    rest = placed(4 * wide + edges[2], [(n * wide, piece) for n, piece in enumerate(rest)])
+    bn = gather_one(rest, "x")
     others = [hop(a0, n) for n in range(1, RING)]
     bn, others = together(bn, others)
-    a0 = a0.astype(F32) + sum(other.astype(F32) for other in others)
-    bc = gather_end(bc, bn, gather_two(bc, bn, "x"), "x", 0).reshape(rows, -1)
-    b0, side1 = (bc[:, :wide], bc[:, 3 * wide :])
-    c0, c1 = (bc[:, n * wide : (n + 1) * wide].reshape(unit, model) for n in (1, 2))
-
-    summed_first = (a0.astype(BF), b0, c0)
-    summed_second = (side1[:, : edges[2]], side1[:, edges[2] :], c1)
+    a0 = (a0.astype(F32) + sum(other.astype(F32) for other in others)).astype(BF)
+    rest = gather_end(rest, bn, gather_two(rest, bn, "x"), "x", 0).reshape(rows, -1)
+    b0, c0, b1, c1 = (rest[:, n * wide : (n + 1) * wide] for n in range(4))
+    summed_first = (a0, b0, c0.reshape(unit, model))
+    summed_second = (rest[:, 4 * wide :], b1, c1.reshape(unit, model))
     mine, sent = zip(*(mine_of(a, b) for a, b in zip(summed_first, summed_second)))
     both = [mine_of(a, swap(b)) for a, b in zip(mine, sent)]
     both = [[v.astype(F32) for v in pair] for pair in both]

time: 559 us -> 574 us (1.027)
  matrix products: 66.6 us -> 95.3 us
  local copies, waits for them, and re-layouts: 84.5 us -> 110 us
  waiting for transfers between devices: 218 us -> 193 us
  starting transfers between devices: 80.2 us -> 60.3 us
    ppermute x28 -> x32, waiting for transfers between devices: 205 us -> 104 us  [trade(): return lax.ppermute(value, ('section', name), route)]
    all_gather x1 -> x2, waiting for transfers between devices: 0.01 us -> 83.9 us  [whole(): return lax.all_gather(block, 'shard', axis=0, tiled=True)]
    ppermute x20, starting transfers between devices: 36.8 us -> 22 us  [swap(): return lax.ppermute(value, 'section', [(0, 1), (1, 0)])]
    mul x12, local copies, waits for them, and re-layouts: 0.95 us -> 13.5 us  [side_by_side(): whole += [0.5 * grads[name] for name in names]]
    dot_general x8 -> x12, matrix products: 14.7 us -> 25.3 us  [transpose_dot(): lax.dot_general(left, right, (((0,), (0,)), ((), ())), preferred_element_...]
    select_n x18, local copies, waits for them, and re-layouts: 2.77 us -> 11.7 us  [choose(): return jnp.where(first, low, high)]
    dot_general x0 -> x4, matrix products: none -> 8.22 us  [two(): lax.dot_general(pair, right, (((1,), (0,)), ((), ())), preferred_element_...]
    another operation x27 -> x26, other arithmetic: 5.23 us -> 13.2 us  [the longest x11 5.15 us: scatter_one(): return trade(jnp.stack(sent), axis, (1, 3))]
  transfers between devices with their start and end apart: 53 -> 57, of which waited for: 27 -> 20; matrix products, arithmetic and copies ran while one was open for 29% -> 39% of each run, Pallas kernels for 0% -> 0%
where the time goes in v6:
time: 574 us; the launch traced here: 563 us
  waiting for transfers between devices  193 us (34%)
  local copies, waits for them, and re-layouts  110 us (19%)
  matrix products  95.3 us (17%)
  other arithmetic  87 us (15%)
  starting transfers between devices  60.3 us (11%)
  between operations  17.4 us (3%)
    ppermute x32, waiting for transfers between devices, trade(): return lax.ppermute(value, ('section', name), route)  104 us
    all_gather x2, waiting for transfers between devices, whole(): return lax.all_gather(block, 'shard', axis=0, tiled=True)  83.9 us
    ppermute x32, starting transfers between devices, trade(): return lax.ppermute(value, ('section', name), route)  35.4 us
    dot_general x12, matrix products, transpose_dot(): lax.dot_general(left, right, (((0,), (0,)), ((), ())), preferred_element_...  25.3 us
    dot_general x8, matrix products, dot_transposed(): lax.dot_general(left, right, (((1,), (1,)), ((), ())), preferred_element_...  24.8 us
    dot_general x8, matrix products, dot(): return jnp.dot(left, right, preferred_element_type=F32)  24.4 us
    ppermute x20, starting transfers between devices, swap(): return lax.ppermute(value, 'section', [(0, 1), (1, 0)])  22 us
    select_n x23, other arithmetic, choose(): return jnp.where(first, low, high)  20.5 us
  transfers between devices with their start and end apart: 57, of which 20 were waited for; matrix products, arithmetic and copies ran while one was open for 39% of the time, Pallas kernels for 0%

profile of v6, /device:TPU:1, one launch (start us, length us, event | category | flops | bytes accessed | tf_op | source)
XLA Modules:
  0.0 563.0 jit_solution(16806450386639857878)
XLA Ops:
  18.3 83.9 %all-gather.3.cloned.1.call-done = bf16[1024,5248]{1,0:T(8,128)(2,1)} async-done(((bf16[64,5248]{1,0:T(8,128)(2,1)}), bf16[1024,5248]{1,0:T(8,128)(2,1)}) %all-gather.3.cloned.1.call-update) | async-done | bytes 10747920 | tf_op jit(solution)/shard_map/all_gather | solution.py:337
  104.0 3.0 fusion.35
  133.3 5.2 multiply_convert_fusion.1
  138.5 16.6 %collective-permute-done.6 = bf16[2,16,32,1024]{3,2,1,0:T(8,128)(2,1)S(1)} collective-permute-done((bf16[2,16,32,1024]{3,2,1,0:T(8,128)(2,1)S(1)}, bf16[2,16,32,1024]{3,2,1,0:T(8,128)(2,1)S(1)}, u32[]{:S(2)}, u32[]{:S(2)}) %collective-permute-start.6) | collective-permute-done | bytes 2097184 | tf_op jit(solution)/shard_map/ppermute | solution.py:224
  174.1 9.4 %collective-permute-done.9 = bf16[16,32,1024]{2,1,0:T(8,128)(2,1)} collective-permute-done((bf16[16,32,1024]{2,1,0:T(8,128)(2,1)}, bf16[16,32,1024]{2,1,0:T(8,128)(2,1)}, u32[]{:S(2)}, u32[]{:S(2)}) %collective-permute-start.9) | collective-permute-done | bytes 1048608 | tf_op jit(solution)/shard_map/ppermute | solution.py:224
  185.9 2.9 fusion.28
  216.1 5.2 multiply_convert_fusion
  221.3 13.0 %collective-permute-done.13 = bf16[2,16,32,1024]{3,2,1,0:T(8,128)(2,1)} collective-permute-done((bf16[2,16,32,1024]{3,2,1,0:T(8,128)(2,1)}, bf16[2,16,32,1024]{3,2,1,0:T(8,128)(2,1)}, u32[]{:S(2)}, u32[]{:S(2)}) %collective-permute-start.13) | collective-permute-done | bytes 2097184 | tf_op jit(solution)/shard_map/ppermute | solution.py:224
  238.9 4.3 convolution_convert_fusion.10
  257.5 4.2 convert_reduce_fusion.1
  261.8 4.7 fusion.69
  284.0 3.5 multiply_reduce_fusion.3
  311.6 3.8 fusion.63
  329.5 2.9 concatenate.74
  343.2 4.7 fusion.72
  372.2 3.4 fusion.49
  375.6 3.2 add_convert_fusion.2
  378.8 2.9 multiply_reduce_fusion
  401.0 3.0 fusion.87
  410.4 4.9 collective-permute-done.30
  415.3 6.1 %collective-permute-done.29 = bf16[16,32,1024]{2,1,0:T(8,128)(2,1)} collective-permute-done((bf16[16,32,1024]{2,1,0:T(8,128)(2,1)}, bf16[16,32,1024]{2,1,0:T(8,128)(2,1)}, u32[]{:S(2)}, u32[]{:S(2)}) %collective-permute-start.29) | collective-permute-done | bytes 1048608 | tf_op jit(solution)/shard_map/ppermute | solution.py:224
  435.4 9.4 %collective-permute-done.34 = bf16[2,64,2176]{2,1,0:T(8,128)(2,1)S(1)} collective-permute-done((bf16[2,64,2176]{2,1,0:T(8,128)(2,1)S(1)}, bf16[2,64,2176]{2,1,0:T(8,128)(2,1)S(1)}, u32[]{:S(2)}, u32[]{:S(2)}) %collective-permute-start.34) | collective-permute-done | bytes 557088 | tf_op jit(solution)/shard_map/ppermute | solution.py:224
  445.3 11.7 %collective-permute-done.31 = bf16[2,4,64,2176]{3,2,1,0:T(8,128)(2,1)S(1)} collective-permute-done((bf16[2,4,64,2176]{3,2,1,0:T(8,128)(2,1)S(1)}, bf16[2,4,64,2176]{3,2,1,0:T(8,128)(2,1)S(1)}, u32[]{:S(2)}, u32[]{:S(2)}) %collective-permute-start.31) | collective-permute-done | bytes 2228256 | tf_op jit(solution)/shard_map/ppermute | solution.py:224
  464.4 5.4 collective-permute-done.38
  470.5 4.7 collective-permute-done.35
  486.2 2.9 fusion.66
  489.1 6.1 %collective-permute-start.26 = (bf16[256,1024]{1,0:T(8,128)(2,1)S(1)}, bf16[256,1024]{1,0:T(8,128)(2,1)S(1)}, u32[]{:S(2)}, u32[]{:S(2)}) collective-permute-start(bf16[256,1024]{1,0:T(8,128)(2,1)S(1)} %fusion.66), channel_id=1, source_target_pairs={{0,64},{64,0},{1,65},{65,1},{2,66},{66,2},{3,67},{67,3},{4,68},{68... | collective-permute-start | bytes 1572872 | tf_op jit(solution)/shard_map/ppermute | solution.py:17
  510.8 3.6 collective-permute-done.48
  515.1 8.5 %collective-permute-done.47 = bf16[16,10368]{1,0:T(8,128)(2,1)S(1)} collective-permute-done((bf16[16,10368]{1,0:T(8,128)(2,1)S(1)}, bf16[16,10368]{1,0:T(8,128)(2,1)S(1)}, u32[]{:S(2)}, u32[]{:S(2)}) %collective-permute-start.47) | collective-permute-done | bytes 331808 | tf_op jit(solution)/shard_map/ppermute | solution.py:224
  523.9 9.8 %collective-permute-done.51 = bf16[2,16,10368]{2,1,0:T(8,128)(2,1)S(1)} collective-permute-done((bf16[2,16,10368]{2,1,0:T(8,128)(2,1)S(1)}, bf16[2,16,10368]{2,1,0:T(8,128)(2,1)S(1)}, u32[]{:S(2)}, u32[]{:S(2)}) %collective-permute-start.51) | collective-permute-done | bytes 663584 | tf_op jit(solution)/shard_map/ppermute | solution.py:224
  533.8 5.4 collective-permute-start.53
  544.5 3.0 reshape.925
  (798 shorter events, 284.4 us)
Async XLA Ops:
  7.3 94.9 %all-gather.3.cloned.1.call-start = ((), (), s32[]{:S(2)}) async-start(), calls=%async_computation | async-start | bytes 11419648 | tf_op jit(solution)/shard_map/all_gather | solution.py:337
  18.2 165.3 %all-gather.5.cloned.1.call-start = ((), (), s32[]{:S(2)}) async-start(), calls=%async_computation.1 | async-start | bytes 9191424 | tf_op jit(solution)/shard_map/all_gather | solution.py:337
  111.6 15.5 %collective-permute-start.5 = (bf16[16,32,1024]{2,1,0:T(8,128)(2,1)}, bf16[16,32,1024]{2,1,0:T(8,128)(2,1)}, u32[]{:S(2)}, u32[]{:S(2)}) collective-permute-start(bf16[16,32,1024]{2,1,0:T(8,128)(2,1)} %reshape.856), channel_id=1, source_target_pairs={{0,16},{16,0},{32,48},{48,32},{64,112},{80,96},{96,80},{112,64},{1... | collective-permute-start | bytes 3145736 | tf_op jit(solution)/shard_map/ppermute | solution.py:224
  129.3 25.8 %collective-permute-start.6 = (bf16[2,16,32,1024]{3,2,1,0:T(8,128)(2,1)S(1)}, bf16[2,16,32,1024]{3,2,1,0:T(8,128)(2,1)S(1)}, u32[]{:S(2)}, u32[]{:S(2)}) collective-permute-start(bf16[2,16,32,1024]{3,2,1,0:T(8,128)(2,1)S(1)} %pad_maximum_fusion.2), channel_id=1, source_target_pairs={{0,48},{16,32},{32,16},{48,0},{64,80},{80,64},{96,112},{112,96},{1... | collective-permute-start | bytes 6291464 | tf_op jit(solution)/shard_map/ppermute | solution.py:224
  157.5 14.3 %collective-permute-start.10 = (bf16[256,1024]{1,0:T(8,128)(2,1)}, bf16[256,1024]{1,0:T(8,128)(2,1)}, u32[]{:S(2)}, u32[]{:S(2)}) collective-permute-start(bf16[256,1024]{1,0:T(8,128)(2,1)} %convolution_convert_fusion.11), channel_id=1, source_target_pairs={{0,64},{64,0},{1,65},{65,1},{2,66},{66,2},{3,67},{67,3},{4,68},{68... | collective-permute-start | bytes 1572872 | tf_op jit(solution)/shard_map/ppermute | solution.py:17
  168.3 15.3 %collective-permute-start.9 = (bf16[16,32,1024]{2,1,0:T(8,128)(2,1)}, bf16[16,32,1024]{2,1,0:T(8,128)(2,1)}, u32[]{:S(2)}, u32[]{:S(2)}) collective-permute-start(bf16[16,32,1024]{2,1,0:T(8,128)(2,1)} %reshape.855), channel_id=1, source_target_pairs={{0,16},{16,0},{32,48},{48,32},{64,112},{80,96},{96,80},{112,64},{1... | collective-permute-start | bytes 3145736 | tf_op jit(solution)/shard_map/ppermute | solution.py:224
  208.5 25.7 %collective-permute-start.13 = (bf16[2,16,32,1024]{3,2,1,0:T(8,128)(2,1)}, bf16[2,16,32,1024]{3,2,1,0:T(8,128)(2,1)}, u32[]{:S(2)}, u32[]{:S(2)}) collective-permute-start(bf16[2,16,32,1024]{3,2,1,0:T(8,128)(2,1)} %pad_maximum_fusion.3), channel_id=1, source_target_pairs={{0,48},{16,32},{32,16},{48,0},{64,80},{80,64},{96,112},{112,96},{1... | collective-permute-start | bytes 6291464 | tf_op jit(solution)/shard_map/ppermute | solution.py:224
  266.5 17.5 %collective-permute-start.17 = (bf16[256,1024]{1,0:T(8,128)(2,1)}, bf16[256,1024]{1,0:T(8,128)(2,1)}, u32[]{:S(2)}, u32[]{:S(2)}) collective-permute-start(bf16[256,1024]{1,0:T(8,128)(2,1)} %fusion.69), channel_id=1, source_target_pairs={{0,64},{64,0},{1,65},{65,1},{2,66},{66,2},{3,67},{67,3},{4,68},{68... | collective-permute-start | bytes 1572872 | tf_op jit(solution)/shard_map/ppermute | solution.py:17
  268.6 43.0 %collective-permute-start.16 = (bf16[2,4,64,2048]{3,2,1,0:T(8,128)(2,1)}, bf16[2,4,64,2048]{3,2,1,0:T(8,128)(2,1)}, u32[]{:S(2)}, u32[]{:S(2)}) collective-permute-start(bf16[2,4,64,2048]{3,2,1,0:T(8,128)(2,1)} %bitcast.49), channel_id=1, source_target_pairs={{0,1},{1,0},{2,3},{3,2},{4,5},{5,4},{6,7},{7,6},{8,9},{9,8},{10,11... | collective-permute-start | bytes 6291464 | tf_op jit(solution)/shard_map/ppermute | solution.py:224
  272.9 38.7 %collective-permute-start.15 = (bf16[2,16,32,1024]{3,2,1,0:T(8,128)(2,1)}, bf16[2,16,32,1024]{3,2,1,0:T(8,128)(2,1)}, u32[]{:S(2)}, u32[]{:S(2)}) collective-permute-start(bf16[2,16,32,1024]{3,2,1,0:T(8,128)(2,1)} %bitcast.44), channel_id=1, source_target_pairs={{0,16},{16,0},{32,48},{48,32},{64,112},{80,96},{96,80},{112,64},{1... | collective-permute-start | bytes 6291464 | tf_op jit(solution)/shard_map/ppermute | solution.py:224
  297.5 11.7 %collective-permute-start.18 = (bf16[512,512]{1,0:T(8,128)(2,1)}, bf16[512,512]{1,0:T(8,128)(2,1)}, u32[]{:S(2)}, u32[]{:S(2)}) collective-permute-start(bf16[512,512]{1,0:T(8,128)(2,1)} %broadcast_select_fusion.6), channel_id=1, source_target_pairs={{0,64},{64,0},{1,65},{65,1},{2,66},{66,2},{3,67},{67,3},{4,68},{68... | collective-permute-start | bytes 1572872 | tf_op jit(solution)/shard_map/ppermute | solution.py:17
  315.7 20.1 %collective-permute-start.21 = (bf16[256,1024]{1,0:T(8,128)(2,1)}, bf16[256,1024]{1,0:T(8,128)(2,1)}, u32[]{:S(2)}, u32[]{:S(2)}) collective-permute-start(bf16[256,1024]{1,0:T(8,128)(2,1)} %fusion.63), channel_id=1, source_target_pairs={{0,64},{64,0},{1,65},{65,1},{2,66},{66,2},{3,67},{67,3},{4,68},{68... | collective-permute-start | bytes 1572872 | tf_op jit(solution)/shard_map/ppermute | solution.py:17
  318.5 20.5 %collective-permute-start.20 = (bf16[4,64,2048]{2,1,0:T(8,128)(2,1)}, bf16[4,64,2048]{2,1,0:T(8,128)(2,1)}, u32[]{:S(2)}, u32[]{:S(2)}) collective-permute-start(bf16[4,64,2048]{2,1,0:T(8,128)(2,1)} %fusion.31), channel_id=1, source_target_pairs={{0,3},{1,2},{2,1},{3,0},{4,7},{5,6},{6,5},{7,4},{8,11},{9,10},{10,... | collective-permute-start | bytes 3145736 | tf_op jit(solution)/shard_map/ppermute | solution.py:224
  321.2 17.8 %collective-permute-start.19 = (bf16[16,32,1024]{2,1,0:T(8,128)(2,1)}, bf16[16,32,1024]{2,1,0:T(8,128)(2,1)}, u32[]{:S(2)}, u32[]{:S(2)}) collective-permute-start(bf16[16,32,1024]{2,1,0:T(8,128)(2,1)} %fusion.53), channel_id=1, source_target_pairs={{0,48},{16,32},{32,16},{48,0},{64,80},{80,64},{96,112},{112,96},{1... | collective-permute-start | bytes 3145736 | tf_op jit(solution)/shard_map/ppermute | solution.py:224
  347.9 30.9 %collective-permute-start.22 = (bf16[256,1024]{1,0:T(8,128)(2,1)}, bf16[256,1024]{1,0:T(8,128)(2,1)}, u32[]{:S(2)}, u32[]{:S(2)}) collective-permute-start(bf16[256,1024]{1,0:T(8,128)(2,1)} %fusion.72), channel_id=1, source_target_pairs={{0,64},{64,0},{1,65},{65,1},{2,66},{66,2},{3,67},{67,3},{4,68},{68... | collective-permute-start | bytes 1572872 | tf_op jit(solution)/shard_map/ppermute | solution.py:17
  351.8 46.5 %collective-permute-start.25 = (bf16[2,4,64,2048]{3,2,1,0:T(8,128)(2,1)}, bf16[2,4,64,2048]{3,2,1,0:T(8,128)(2,1)}, u32[]{:S(2)}, u32[]{:S(2)}) collective-permute-start(bf16[2,4,64,2048]{3,2,1,0:T(8,128)(2,1)} %bitcast.73), channel_id=1, source_target_pairs={{0,1},{1,0},{2,3},{3,2},{4,5},{5,4},{6,7},{7,6},{8,9},{9,8},{10,11... | collective-permute-start | bytes 6291464 | tf_op jit(solution)/shard_map/ppermute | solution.py:224
  356.0 42.3 %collective-permute-start.24 = (bf16[2,16,32,1024]{3,2,1,0:T(8,128)(2,1)}, bf16[2,16,32,1024]{3,2,1,0:T(8,128)(2,1)}, u32[]{:S(2)}, u32[]{:S(2)}) collective-permute-start(bf16[2,16,32,1024]{3,2,1,0:T(8,128)(2,1)} %bitcast.68), channel_id=1, source_target_pairs={{0,16},{16,0},{32,48},{48,32},{64,112},{80,96},{96,80},{112,64},{1... | collective-permute-start | bytes 6291464 | tf_op jit(solution)/shard_map/ppermute | solution.py:224
  360.2 38.2 %collective-permute-start.23 = (bf16[2,4,64,2176]{3,2,1,0:T(8,128)(2,1)}, bf16[2,4,64,2176]{3,2,1,0:T(8,128)(2,1)}, u32[]{:S(2)}, u32[]{:S(2)}) collective-permute-start(bf16[2,4,64,2176]{3,2,1,0:T(8,128)(2,1)} %pad_maximum_fusion), channel_id=1, source_target_pairs={{0,4},{1,5},{2,6},{3,7},{4,0},{5,1},{6,2},{7,3},{8,12},{9,13},{10,... | collective-permute-start | bytes 6684680 | tf_op jit(solution)/shard_map/ppermute | solution.py:224
  401.0 14.3 %collective-permute-start.30 = (bf16[4,64,2048]{2,1,0:T(8,128)(2,1)}, bf16[4,64,2048]{2,1,0:T(8,128)(2,1)}, u32[]{:S(2)}, u32[]{:S(2)}) collective-permute-start(bf16[4,64,2048]{2,1,0:T(8,128)(2,1)} %fusion.32), channel_id=1, source_target_pairs={{0,3},{1,2},{2,1},{3,0},{4,7},{5,6},{6,5},{7,4},{8,11},{9,10},{10,... | collective-permute-start | bytes 3145736 | tf_op jit(solution)/shard_map/ppermute | solution.py:224
  404.1 17.3 %collective-permute-start.28 = (bf16[4,64,2176]{2,1,0:T(8,128)(2,1)}, bf16[4,64,2176]{2,1,0:T(8,128)(2,1)}, u32[]{:S(2)}, u32[]{:S(2)}) collective-permute-start(bf16[4,64,2176]{2,1,0:T(8,128)(2,1)} %fusion.87), channel_id=1, source_target_pairs={{0,12},{1,13},{2,14},{3,15},{4,8},{5,9},{6,10},{7,11},{8,4},{9,5},... | collective-permute-start | bytes 3342344 | tf_op jit(solution)/shard_map/ppermute | solution.py:224
  407.1 14.3 %collective-permute-start.29 = (bf16[16,32,1024]{2,1,0:T(8,128)(2,1)}, bf16[16,32,1024]{2,1,0:T(8,128)(2,1)}, u32[]{:S(2)}, u32[]{:S(2)}) collective-permute-start(bf16[16,32,1024]{2,1,0:T(8,128)(2,1)} %fusion.52), channel_id=1, source_target_pairs={{0,48},{16,32},{32,16},{48,0},{64,80},{80,64},{96,112},{112,96},{1... | collective-permute-start | bytes 3145736 | tf_op jit(solution)/shard_map/ppermute | solution.py:224
  423.7 21.1 %collective-permute-start.33 = (bf16[2,2,4,32,1024]{4,3,2,1,0:T(8,128)(2,1)S(1)}, bf16[2,2,4,32,1024]{4,3,2,1,0:T(8,128)(2,1)S(1)}, u32[]{:S(2)}, u32[]{:S(2)}) collective-permute-start(bf16[2,2,4,32,1024]{4,3,2,1,0:T(8,128)(2,1)S(1)} %pad_maximum_fusion.7), channel_id=1, source_target_pairs={{0,1},{1,0},{2,3},{3,2},{4,5},{5,4},{6,7},{7,6},{8,9},{9,8},{10,11... | collective-permute-start | bytes 3145736 | tf_op jit(solution)/shard_map/ppermute | solution.py:224
  429.4 27.6 %collective-permute-start.31 = (bf16[2,4,64,2176]{3,2,1,0:T(8,128)(2,1)S(1)}, bf16[2,4,64,2176]{3,2,1,0:T(8,128)(2,1)S(1)}, u32[]{:S(2)}, u32[]{:S(2)}) collective-permute-start(bf16[2,4,64,2176]{3,2,1,0:T(8,128)(2,1)S(1)} %pad_maximum_fusion.1), channel_id=1, source_target_pairs={{0,4},{1,5},{2,6},{3,7},{4,0},{5,1},{6,2},{7,3},{8,12},{9,13},{10,... | collective-permute-start | bytes 6684680 | tf_op jit(solution)/shard_map/ppermute | solution.py:224
  430.3 14.9 %collective-permute-start.32 = (bf16[2,2,4,16,2048]{4,3,1,2,0:T(8,128)(2,1)S(1)}, bf16[2,2,4,16,2048]{4,3,1,2,0:T(8,128)(2,1)S(1)}, u32[]{:S(2)}, u32[]{:S(2)}) collective-permute-start(bf16[2,2,4,16,2048]{4,3,1,2,0:T(8,128)(2,1)S(1)} %pad_maximum_fusion.6), channel_id=1, source_target_pairs={{0,16},{16,0},{32,48},{48,32},{64,112},{80,96},{96,80},{112,64},{1... | collective-permute-start | bytes 3145736 | tf_op jit(solution)/shard_map/ppermute | solution.py:224
  433.5 11.3 %collective-permute-start.34 = (bf16[2,64,2176]{2,1,0:T(8,128)(2,1)S(1)}, bf16[2,64,2176]{2,1,0:T(8,128)(2,1)S(1)}, u32[]{:S(2)}, u32[]{:S(2)}) collective-permute-start(bf16[2,64,2176]{2,1,0:T(8,128)(2,1)S(1)} %pad_maximum_fusion.16), channel_id=1, source_target_pairs={{0,1},{1,0},{2,3},{3,2},{4,5},{5,4},{6,7},{7,6},{8,9},{9,8},{10,11... | collective-permute-start | bytes 1671176 | tf_op jit(solution)/shard_map/ppermute | solution.py:224
  458.2 11.6 %collective-permute-start.37 = (bf16[2,4,32,1024]{3,2,1,0:T(8,128)(2,1)}, bf16[2,4,32,1024]{3,2,1,0:T(8,128)(2,1)}, u32[]{:S(2)}, u32[]{:S(2)}) collective-permute-start(bf16[2,4,32,1024]{3,2,1,0:T(8,128)(2,1)} %fusion.97), channel_id=1, source_target_pairs={{0,3},{1,2},{2,1},{3,0},{4,7},{5,6},{6,5},{7,4},{8,11},{9,10},{10,... | collective-permute-start | bytes 1572872 | tf_op jit(solution)/shard_map/ppermute | solution.py:224
  460.3 15.0 %collective-permute-start.35 = (bf16[4,64,2176]{2,1,0:T(8,128)(2,1)}, bf16[4,64,2176]{2,1,0:T(8,128)(2,1)}, u32[]{:S(2)}, u32[]{:S(2)}) collective-permute-start(bf16[4,64,2176]{2,1,0:T(8,128)(2,1)} %fusion.88), channel_id=1, source_target_pairs={{0,12},{1,13},{2,14},{3,15},{4,8},{5,9},{6,10},{7,11},{8,4},{9,5},... | collective-permute-start | bytes 3342344 | tf_op jit(solution)/shard_map/ppermute | solution.py:224
  476.5 18.8 %collective-permute-start.42 = (bf16[2,16,2176]{2,1,0:T(8,128)(2,1)S(1)}, bf16[2,16,2176]{2,1,0:T(8,128)(2,1)S(1)}, u32[]{:S(2)}, u32[]{:S(2)}) collective-permute-start(bf16[2,16,2176]{2,1,0:T(8,128)(2,1)S(1)} %pad_maximum_fusion.20), channel_id=1, source_target_pairs={{0,16},{16,0},{32,48},{48,32},{64,112},{80,96},{96,80},{112,64},{1... | collective-permute-start | bytes 417800 | tf_op jit(solution)/shard_map/ppermute | solution.py:224
  478.3 17.0 %collective-permute-start.41 = (bf16[2,2,32,1024]{3,2,1,0:T(8,128)(2,1)S(1)}, bf16[2,2,32,1024]{3,2,1,0:T(8,128)(2,1)S(1)}, u32[]{:S(2)}, u32[]{:S(2)}) collective-permute-start(bf16[2,2,32,1024]{3,2,1,0:T(8,128)(2,1)S(1)} %pad_maximum_fusion.19), channel_id=1, source_target_pairs={{0,4},{1,5},{2,6},{3,7},{4,0},{5,1},{6,2},{7,3},{8,12},{9,13},{10,... | collective-permute-start | bytes 786440 | tf_op jit(solution)/shard_map/ppermute | solution.py:224
  483.4 11.9 %collective-permute-start.39 = (bf16[2,64,2176]{2,1,0:T(8,128)(2,1)S(1)}, bf16[2,64,2176]{2,1,0:T(8,128)(2,1)S(1)}, u32[]{:S(2)}, u32[]{:S(2)}) collective-permute-start(bf16[2,64,2176]{2,1,0:T(8,128)(2,1)S(1)} %pad_maximum_fusion.17), channel_id=1, source_target_pairs={{0,1},{1,0},{2,3},{3,2},{4,5},{5,4},{6,7},{7,6},{8,9},{9,8},{10,11... | collective-permute-start | bytes 1671176 | tf_op jit(solution)/shard_map/ppermute | solution.py:224
  509.6 14.0 %collective-permute-start.47 = (bf16[16,10368]{1,0:T(8,128)(2,1)S(1)}, bf16[16,10368]{1,0:T(8,128)(2,1)S(1)}, u32[]{:S(2)}, u32[]{:S(2)}) collective-permute-start(bf16[16,10368]{1,0:T(8,128)(2,1)S(1)} %fusion.203), channel_id=1, source_target_pairs={{0,16},{16,0},{32,48},{48,32},{64,112},{80,96},{96,80},{112,64},{1... | collective-permute-start | bytes 995336 | tf_op jit(solution)/shard_map/ppermute | solution.py:224
  542.0 11.6 %collective-permute-start.54 = (bf16[128,1024]{1,0:T(8,128)(2,1)}, bf16[128,1024]{1,0:T(8,128)(2,1)}, u32[]{:S(2)}, u32[]{:S(2)}) collective-permute-start(bf16[128,1024]{1,0:T(8,128)(2,1)} %select_n.719), channel_id=1, source_target_pairs={{0,64},{64,0},{1,65},{65,1},{2,66},{66,2},{3,67},{67,3},{4,68},{68... | collective-permute-start | bytes 786440 | tf_op jit(solution)/shard_map/ppermute | solution.py:17
  (208 other events, 1325.7 us)
Sparse Core Ops, SparseCore 0:
  18.4 83.7 all-gather.2
  104.3 71.7 all-gather.4

commit v7 on v6

--- a/solution.py
+++ b/solution.py
@@ -1,6 +1,8 @@
 import jax
 import jax.numpy as jnp
 from jax import lax
+from jax.experimental import pallas as pl
+from jax.experimental.pallas import tpu as pltpu
 from jax.sharding import PartitionSpec as P
 
 
@@ -49,37 +51,84 @@
     )
 
 
-def heads_of(packed, number, count):
-    width = packed.shape[1] // 3
-    piece = packed[:, number * width : (number + 1) * width]
-    return piece.reshape(count, -1, width // HEAD_DIM, HEAD_DIM).transpose(0, 2, 1, 3)
-
-
-def join_heads(parts):
-    count, heads, rows, size = parts.shape
-    return parts.transpose(0, 2, 1, 3).reshape(count * rows, heads * size)
-
-
-def masked_scores(queries, keys, seq_lengths):
-    scores = jnp.einsum("nhqd,nhkd->nhqk", queries, keys, preferred_element_type=F32)
-    scores = scores * HEAD_DIM ** (-0.5)
-    positions = lax.broadcasted_iota(jnp.int32, scores.shape, 3)
-    return jnp.where(positions < seq_lengths[:, None, None, None], scores, -1000000000.0)
+def head_masks(rows):
+    lane = lax.broadcasted_iota(jnp.int32, (rows, LANES), 1)
+    return [lane < HEAD_DIM, lane >= HEAD_DIM]
+
+
+def soft_weights_of(queries, keys, mask, seq_length):
+    queries = jnp.where(mask, queries, 0.0).astype(BF)
+    scores = dot_transposed(queries, keys) * HEAD_DIM ** (-0.5)
+    positions = lax.broadcasted_iota(jnp.int32, scores.shape, 1)
+    scores = jnp.where(positions < seq_length, scores, -1000000000.0)
+    exponent = jnp.exp(scores - jnp.max(scores, axis=-1, keepdims=True))
+    return exponent / jnp.sum(exponent, axis=-1, keepdims=True)
+
+
+def pairs_of(packed_ref, count):
+    rows, width = (packed_ref.shape[0] // count, packed_ref.shape[1] // 3)
+    for n in range(count):
+        for at in range(0, width, LANES):
+            yield (n, pl.ds(n * rows, rows), [pl.ds(k * width + at, LANES) for k in range(3)])
+
+
+def attention_kernel(lengths_ref, packed_ref, attended_ref):
+    count = lengths_ref.shape[0]
+    masks = head_masks(packed_ref.shape[0] // count)
+    for n, rows, columns in pairs_of(packed_ref, count):
+        queries, keys, values = (packed_ref[rows, at] for at in columns)
+        queries = queries.astype(F32)
+        parts = []
+        for mask in masks:
+            soft_weights = soft_weights_of(queries, keys, mask, lengths_ref[n])
+            parts.append(dot(soft_weights.astype(BF), values))
+        attended_ref[rows, columns[0]] = jnp.where(masks[0], *parts).astype(BF)
+
+
+def attention_back_kernel(lengths_ref, packed_ref, grad_ref, out_ref):
+    count = lengths_ref.shape[0]
+    scaling = HEAD_DIM ** (-0.5)
+    masks = head_masks(packed_ref.shape[0] // count)
+    for n, rows, columns in pairs_of(packed_ref, count):
+        queries, keys, values = (packed_ref[rows, at] for at in columns)
+        grads = grad_ref[rows, columns[0]]
+        wide_queries, wide_grads = (queries.astype(F32), grads.astype(F32))
+        parts = []
+        for mask in masks:
+            soft_weights = soft_weights_of(wide_queries, keys, mask, lengths_ref[n])
+            own = jnp.where(mask, wide_grads, 0.0).astype(BF)
+            grad_soft = dot_transposed(own, values)
+            mean = jnp.sum(grad_soft * soft_weights, axis=-1, keepdims=True)
+            grad_scores = (soft_weights * (grad_soft - mean)).astype(BF)
+            parts.append(
+                (
+                    dot(grad_scores, keys) * scaling,
+                    transpose_dot(grad_scores, queries) * scaling,
+                    transpose_dot(soft_weights.astype(BF), grads),
+                )
+            )
+        for at, low, high in zip(columns, *parts):
+            out_ref[rows, at] = jnp.where(masks[0], low, high).astype(BF)
+
+
+def attention_call(kernel, width, seq_lengths, *arrays):
+    rows = arrays[0].shape[0]
+    vmem = pl.BlockSpec(memory_space=pltpu.VMEM)
+    return pl.pallas_call(
+        kernel,
+        out_shape=jax.ShapeDtypeStruct((rows, width), BF),
+        in_specs=[pl.BlockSpec(memory_space=pltpu.SMEM)] + [vmem] * len(arrays),
+        out_specs=vmem,
+        cost_estimate=pl.CostEstimate(
+            flops=4 * rows * 128 * width, bytes_accessed=4 * rows * width, transcendentals=0
+        ),
+    )(seq_lengths, *arrays)
 
 
 def forward_attention(inputs, weights, seq_lengths):
-    count = seq_lengths.shape[0]
     packed = (dot(inputs, weights["qkv"]) + weights["bias_qkv"]).astype(BF)
-    queries, keys, values = (heads_of(packed, n, count) for n in range(3))
-    scores = masked_scores(queries, keys, seq_lengths)
-    row_max = jnp.max(scores, axis=-1, keepdims=True)
-    exponent = jnp.exp(scores - row_max)
-    soft_weights = exponent / jnp.sum(exponent, axis=-1, keepdims=True)
-    attended = jnp.einsum(
-        "nhqk,nhkd->nhqd", soft_weights.astype(BF), values, preferred_element_type=F32
-    )
-    attended = join_heads(attended.astype(BF))
-    return (attended, dict(inputs=inputs, qkv=(queries, keys, values), soft_weights=soft_weights))
+    attended = attention_call(attention_kernel, packed.shape[1] // 3, seq_lengths, packed)
+    return (attended, dict(inputs=inputs, packed=packed, seq_lengths=seq_lengths))
 
 
 def forward_hidden(attended, kept, weights):
@@ -123,7 +172,6 @@
 
 
 def backward_attention(grad_hidden, grads, kept, weights):
-    scaling = HEAD_DIM ** (-0.5)
     normed = kept["normed_attn"]
     grad_resid = norm_back(grad_hidden * weights["gain_attn"], normed, kept["inverse_attn"])
     grad_branch = grad_resid.astype(BF)
@@ -133,30 +181,10 @@
         bias_out=jnp.sum(grad_branch.astype(F32), axis=0),
         out=transpose_dot(kept["attended"], grad_branch).astype(BF),
     )
-    queries, keys, values = kept["qkv"]
-    count = queries.shape[0]
+    packed = kept["packed"]
     grad_attended = dot_transposed(grad_branch, weights["out"]).astype(BF)
-    grad_attended = grad_attended.reshape(count, -1, queries.shape[1], HEAD_DIM)
-    grad_attended = grad_attended.transpose(0, 2, 1, 3)
-    soft_weights = kept["soft_weights"]
-    grad_values = jnp.einsum(
-        "nhqk,nhqd->nhkd", soft_weights.astype(BF), grad_attended, preferred_element_type=F32
-    )
-    grad_soft = jnp.einsum(
-        "nhqd,nhkd->nhqk", grad_attended, values, preferred_element_type=F32
-    )
-    grad_scores = soft_weights * (
-        grad_soft - jnp.sum(grad_soft * soft_weights, axis=-1, keepdims=True)
-    )
-    grad_scores = grad_scores.astype(BF)
-    grad_queries = scaling * jnp.einsum(
-        "nhqk,nhkd->nhqd", grad_scores, keys, preferred_element_type=F32
-    )
-    grad_keys = scaling * jnp.einsum(
-        "nhqk,nhqd->nhkd", grad_scores, queries, preferred_element_type=F32
-    )
-    grad_packed = jnp.concatenate(
-        [join_heads(g.astype(BF)) for g in (grad_queries, grad_keys, grad_values)], axis=1
+    grad_packed = attention_call(
+        attention_back_kernel, packed.shape[1], kept["seq_lengths"], packed, grad_attended
     )
     return (grad_resid, grad_packed)
 

time: 574 us -> 570 us (level)
  Pallas kernels: 0 us -> 33.2 us
  local copies, waits for them, and re-layouts: 110 us -> 86.6 us
  matrix products: 95.3 us -> 82.5 us
  other arithmetic: 87 us -> 79.9 us
    pallas_call x0 -> x4, Pallas kernels: none -> 33.2 us  [attention_call(): pl.pallas_call(kernel, out_shape=jax.ShapeDtypeStruct((rows, width), BF),...]
    dot_general x10 -> x0, matrix products: 8.95 us -> none  [the longest x2 3.73 us: backward_attention(): jnp.einsum('nhqd,nhkd->nhqk', grad_attended, values, preferred_element_ty...]
    reshape x11 -> x0, local copies, waits for them, and re-layouts: 7.74 us -> none  [the longest x9 5.24 us: heads_of(): piece.reshape(count, -1, width // HEAD_DIM, HEAD_DIM).transpose(0, 2, 1, 3)]
    convert_element_type x10 -> x0, local copies, waits for them, and re-layouts: 5.94 us -> none  [the longest x2 3.06 us: backward_attention(): grad_attended = dot_transposed(grad_branch, weights['out']).astype(BF)]
    unnamed x378 -> x303, local copies, waits for them, and re-layouts: 15.3 us -> 11.3 us
  transfers between devices with their start and end apart: 57 -> 57, of which waited for: 20 -> 19; matrix products, arithmetic and copies ran while one was open for 39% -> 33% of each run, Pallas kernels for 0% -> 6%
where the time goes in v7:
time: 570 us; the launch traced here: 559 us
  waiting for transfers between devices  198 us (35%)
  local copies, waits for them, and re-layouts  86.6 us (15%)
  matrix products  82.5 us (14%)
  other arithmetic  79.9 us (14%)
  starting transfers between devices  62.5 us (11%)
  Pallas kernels  33.2 us (6%)
  between operations  16.7 us (3%)
    ppermute x32, waiting for transfers between devices, trade(): return lax.ppermute(value, ('section', name), route)  108 us
    all_gather x2, waiting for transfers between devices, whole(): return lax.all_gather(block, 'shard', axis=0, tiled=True)  84 us
    ppermute x32, starting transfers between devices, trade(): return lax.ppermute(value, ('section', name), route)  33.6 us
    pallas_call x4, Pallas kernels, attention_call(): pl.pallas_call(kernel, out_shape=jax.ShapeDtypeStruct((rows, width), BF),...  33.2 us
    dot_general x8, matrix products, dot_transposed(): lax.dot_general(left, right, (((1,), (1,)), ((), ())), preferred_element_...  26.2 us
    ppermute x20, starting transfers between devices, swap(): return lax.ppermute(value, 'section', [(0, 1), (1, 0)])  25.6 us
    dot_general x12, matrix products, transpose_dot(): lax.dot_general(left, right, (((0,), (0,)), ((), ())), preferred_element_...  24.3 us
    dot_general x8, matrix products, dot(): return jnp.dot(left, right, preferred_element_type=F32)  23.9 us
  transfers between devices with their start and end apart: 57, of which 19 were waited for; matrix products, arithmetic and copies ran while one was open for 33% of the time, Pallas kernels for 6%

profile of v7, /device:TPU:1, one launch (start us, length us, event | category | flops | bytes accessed | tf_op | source)
XLA Modules:
  0.0 559.3 jit_solution(7621026032090117014)
XLA Ops:
  17.8 84.0 %all-gather.3.cloned.1.call-done = bf16[1024,5248]{1,0:T(8,128)(2,1)} async-done(((bf16[64,5248]{1,0:T(8,128)(2,1)}), bf16[1024,5248]{1,0:T(8,128)(2,1)}) %all-gather.3.cloned.1.call-update) | async-done | bytes 10747920 | tf_op jit(solution)/shard_map/all_gather | solution.py:365
  112.0 4.2 fusion.33.packed_ref
  116.2 7.1 %shard_map.271 = bf16[256,512]{1,0:T(8,128)(2,1)} custom-call(s32[2]{0:T(128)} %bitcast.473, bf16[256,1536]{1,0:T(8,128)(2,1)} %fusion.33.packed_ref), custom_call_target="tpu_custom_call" | custom-call | flops 67108864 | bytes 524288 | tf_op jit(solution)/shard_map/pallas_call | solution.py:117
  134.3 20.3 %collective-permute-done.6 = bf16[2,16,32,1024]{3,2,1,0:T(8,128)(2,1)S(1)} collective-permute-done((bf16[2,16,32,1024]{3,2,1,0:T(8,128)(2,1)S(1)}, bf16[2,16,32,1024]{3,2,1,0:T(8,128)(2,1)S(1)}, u32[]{:S(2)}, u32[]{:S(2)}) %collective-permute-start.6) | collective-permute-done | bytes 2097184 | tf_op jit(solution)/shard_map/ppermute | solution.py:252
  172.3 10.5 %collective-permute-done.9 = bf16[16,32,1024]{2,1,0:T(8,128)(2,1)} collective-permute-done((bf16[16,32,1024]{2,1,0:T(8,128)(2,1)}, bf16[16,32,1024]{2,1,0:T(8,128)(2,1)}, u32[]{:S(2)}, u32[]{:S(2)}) %collective-permute-start.9) | collective-permute-done | bytes 1048608 | tf_op jit(solution)/shard_map/ppermute | solution.py:252
  185.2 3.8 fusion.23.packed_ref
  190.5 7.1 %shard_map.272 = bf16[256,512]{1,0:T(8,128)(2,1)} custom-call(s32[2]{0:T(128)} %bitcast.474, bf16[256,1536]{1,0:T(8,128)(2,1)} %fusion.23.packed_ref), custom_call_target="tpu_custom_call" | custom-call | flops 67108864 | bytes 524288 | tf_op jit(solution)/shard_map/pallas_call | solution.py:117
  215.1 5.2 multiply_convert_fusion
  220.3 13.0 %collective-permute-done.13 = bf16[2,16,32,1024]{3,2,1,0:T(8,128)(2,1)} collective-permute-done((bf16[2,16,32,1024]{3,2,1,0:T(8,128)(2,1)}, bf16[2,16,32,1024]{3,2,1,0:T(8,128)(2,1)}, u32[]{:S(2)}, u32[]{:S(2)}) %collective-permute-start.13) | collective-permute-done | bytes 2097184 | tf_op jit(solution)/shard_map/ppermute | solution.py:252
  237.9 4.3 convolution_convert_fusion.10
  256.5 4.2 convert_reduce_fusion.1
  260.8 4.7 fusion.61
  282.0 2.9 multiply_reduce_fusion.2
  297.1 9.5 %shard_map.273 = bf16[256,1536]{1,0:T(8,128)(2,1)} custom-call(s32[2]{0:T(128)} %bitcast.475, bf16[256,1536]{1,0:T(8,128)(2,1)} %fusion.23.packed_ref, bf16[256,512]{1,0:T(8,128)(2,1)} %convolution_convert_fusion.13.grad_ref), custom_call_target="tpu_custom_call" | custom-call | flops 201326592 | bytes 1572864 | tf_op jit(solution)/shard_map/pallas_call | solution.py:117
  309.1 3.8 fusion.55
  340.7 4.7 fusion.64
  368.9 3.4 fusion.47
  372.3 3.2 add_convert_fusion.2
  383.0 9.5 %shard_map.274 = bf16[256,1536]{1,0:T(8,128)(2,1)} custom-call(s32[2]{0:T(128)} %bitcast.476, bf16[256,1536]{1,0:T(8,128)(2,1)} %fusion.33.packed_ref, bf16[256,512]{1,0:T(8,128)(2,1)} %convolution_convert_fusion.12.grad_ref), custom_call_target="tpu_custom_call" | custom-call | flops 201326592 | bytes 1572864 | tf_op jit(solution)/shard_map/pallas_call | solution.py:117
  396.7 3.0 fusion.67
  406.2 4.7 collective-permute-done.30
  410.9 6.2 %collective-permute-done.29 = bf16[16,32,1024]{2,1,0:T(8,128)(2,1)} collective-permute-done((bf16[16,32,1024]{2,1,0:T(8,128)(2,1)}, bf16[16,32,1024]{2,1,0:T(8,128)(2,1)}, u32[]{:S(2)}, u32[]{:S(2)}) %collective-permute-start.29) | collective-permute-done | bytes 1048608 | tf_op jit(solution)/shard_map/ppermute | solution.py:252
  432.0 8.4 %collective-permute-done.34 = bf16[2,64,2176]{2,1,0:T(8,128)(2,1)S(1)} collective-permute-done((bf16[2,64,2176]{2,1,0:T(8,128)(2,1)S(1)}, bf16[2,64,2176]{2,1,0:T(8,128)(2,1)S(1)}, u32[]{:S(2)}, u32[]{:S(2)}) %collective-permute-start.34) | collective-permute-done | bytes 557088 | tf_op jit(solution)/shard_map/ppermute | solution.py:252
  441.2 11.6 %collective-permute-done.31 = bf16[2,4,64,2176]{3,2,1,0:T(8,128)(2,1)S(1)} collective-permute-done((bf16[2,4,64,2176]{3,2,1,0:T(8,128)(2,1)S(1)}, bf16[2,4,64,2176]{3,2,1,0:T(8,128)(2,1)S(1)}, u32[]{:S(2)}, u32[]{:S(2)}) %collective-permute-start.31) | collective-permute-done | bytes 2228256 | tf_op jit(solution)/shard_map/ppermute | solution.py:252
  460.9 4.7 collective-permute-done.38
  466.4 4.9 collective-permute-done.35
  483.2 2.9 fusion.58
  486.1 5.3 collective-permute-start.26
  505.7 4.8 collective-permute-done.48
  511.1 6.5 %collective-permute-done.47 = bf16[16,10368]{1,0:T(8,128)(2,1)S(1)} collective-permute-done((bf16[16,10368]{1,0:T(8,128)(2,1)S(1)}, bf16[16,10368]{1,0:T(8,128)(2,1)S(1)}, u32[]{:S(2)}, u32[]{:S(2)}) %collective-permute-start.47) | collective-permute-done | bytes 331808 | tf_op jit(solution)/shard_map/ppermute | solution.py:252
  517.8 12.6 %collective-permute-done.51 = bf16[2,16,10368]{2,1,0:T(8,128)(2,1)S(1)} collective-permute-done((bf16[2,16,10368]{2,1,0:T(8,128)(2,1)S(1)}, bf16[2,16,10368]{2,1,0:T(8,128)(2,1)S(1)}, u32[]{:S(2)}, u32[]{:S(2)}) %collective-permute-start.51) | collective-permute-done | bytes 663584 | tf_op jit(solution)/shard_map/ppermute | solution.py:252
  530.5 8.8 %collective-permute-start.53 = (bf16[64,2048]{1,0:T(8,128)(2,1)S(1)}, bf16[64,2048]{1,0:T(8,128)(2,1)S(1)}, u32[]{:S(2)}, u32[]{:S(2)}) collective-permute-start(bf16[64,2048]{1,0:T(8,128)(2,1)S(1)} %broadcast_select_fusion.25), channel_id=1, source_target_pairs={{0,64},{64,0},{1,65},{65,1},{2,66},{66,2},{3,67},{67,3},{4,68},{68... | collective-permute-start | bytes 786440 | tf_op jit(solution)/shard_map/ppermute | solution.py:19
  (690 shorter events, 252.9 us)
Async XLA Ops:
  7.3 94.5 %all-gather.3.cloned.1.call-start = ((), (), s32[]{:S(2)}) async-start(), calls=%async_computation | async-start | bytes 11419648 | tf_op jit(solution)/shard_map/all_gather | solution.py:365
  17.8 165.0 %all-gather.5.cloned.1.call-start = ((), (), s32[]{:S(2)}) async-start(), calls=%async_computation.1 | async-start | bytes 9191424 | tf_op jit(solution)/shard_map/all_gather | solution.py:365
  104.8 20.9 %collective-permute-start.5 = (bf16[16,32,1024]{2,1,0:T(8,128)(2,1)}, bf16[16,32,1024]{2,1,0:T(8,128)(2,1)}, u32[]{:S(2)}, u32[]{:S(2)}) collective-permute-start(bf16[16,32,1024]{2,1,0:T(8,128)(2,1)} %reshape.801), channel_id=1, source_target_pairs={{0,16},{16,0},{32,48},{48,32},{64,112},{80,96},{96,80},{112,64},{1... | collective-permute-start | bytes 3145736 | tf_op jit(solution)/shard_map/ppermute | solution.py:252
  111.7 12.3 %collective-permute-start.7 = (bf16[512,512]{1,0:T(8,128)(2,1)}, bf16[512,512]{1,0:T(8,128)(2,1)S(1)}, u32[]{:S(2)}, u32[]{:S(2)}) collective-permute-start(bf16[512,512]{1,0:T(8,128)(2,1)} %broadcast_select_fusion.14), channel_id=1, source_target_pairs={{0,64},{64,0},{1,65},{65,1},{2,66},{66,2},{3,67},{67,3},{4,68},{68... | collective-permute-start | bytes 1572872 | tf_op jit(solution)/shard_map/ppermute | solution.py:19
  129.1 25.6 %collective-permute-start.6 = (bf16[2,16,32,1024]{3,2,1,0:T(8,128)(2,1)S(1)}, bf16[2,16,32,1024]{3,2,1,0:T(8,128)(2,1)S(1)}, u32[]{:S(2)}, u32[]{:S(2)}) collective-permute-start(bf16[2,16,32,1024]{3,2,1,0:T(8,128)(2,1)S(1)} %pad_maximum_fusion.2), channel_id=1, source_target_pairs={{0,48},{16,32},{32,16},{48,0},{64,80},{80,64},{96,112},{112,96},{1... | collective-permute-start | bytes 6291464 | tf_op jit(solution)/shard_map/ppermute | solution.py:252
  157.0 13.0 %collective-permute-start.10 = (bf16[256,1024]{1,0:T(8,128)(2,1)}, bf16[256,1024]{1,0:T(8,128)(2,1)}, u32[]{:S(2)}, u32[]{:S(2)}) collective-permute-start(bf16[256,1024]{1,0:T(8,128)(2,1)} %convolution_convert_fusion.11), channel_id=1, source_target_pairs={{0,64},{64,0},{1,65},{65,1},{2,66},{66,2},{3,67},{67,3},{4,68},{68... | collective-permute-start | bytes 1572872 | tf_op jit(solution)/shard_map/ppermute | solution.py:19
  167.6 15.3 %collective-permute-start.9 = (bf16[16,32,1024]{2,1,0:T(8,128)(2,1)}, bf16[16,32,1024]{2,1,0:T(8,128)(2,1)}, u32[]{:S(2)}, u32[]{:S(2)}) collective-permute-start(bf16[16,32,1024]{2,1,0:T(8,128)(2,1)} %reshape.800), channel_id=1, source_target_pairs={{0,16},{16,0},{32,48},{48,32},{64,112},{80,96},{96,80},{112,64},{1... | collective-permute-start | bytes 3145736 | tf_op jit(solution)/shard_map/ppermute | solution.py:252
  184.9 14.0 %collective-permute-start.11 = (bf16[512,512]{1,0:T(8,128)(2,1)}, bf16[512,512]{1,0:T(8,128)(2,1)}, u32[]{:S(2)}, u32[]{:S(2)}) collective-permute-start(bf16[512,512]{1,0:T(8,128)(2,1)} %broadcast_select_fusion.10), channel_id=1, source_target_pairs={{0,64},{64,0},{1,65},{65,1},{2,66},{66,2},{3,67},{67,3},{4,68},{68... | collective-permute-start | bytes 1572872 | tf_op jit(solution)/shard_map/ppermute | solution.py:19
  207.3 26.0 %collective-permute-start.13 = (bf16[2,16,32,1024]{3,2,1,0:T(8,128)(2,1)}, bf16[2,16,32,1024]{3,2,1,0:T(8,128)(2,1)}, u32[]{:S(2)}, u32[]{:S(2)}) collective-permute-start(bf16[2,16,32,1024]{3,2,1,0:T(8,128)(2,1)} %pad_maximum_fusion.3), channel_id=1, source_target_pairs={{0,48},{16,32},{32,16},{48,0},{64,80},{80,64},{96,112},{112,96},{1... | collective-permute-start | bytes 6291464 | tf_op jit(solution)/shard_map/ppermute | solution.py:252
  265.5 16.6 %collective-permute-start.17 = (bf16[256,1024]{1,0:T(8,128)(2,1)}, bf16[256,1024]{1,0:T(8,128)(2,1)}, u32[]{:S(2)}, u32[]{:S(2)}) collective-permute-start(bf16[256,1024]{1,0:T(8,128)(2,1)} %fusion.61), channel_id=1, source_target_pairs={{0,64},{64,0},{1,65},{65,1},{2,66},{66,2},{3,67},{67,3},{4,68},{68... | collective-permute-start | bytes 1572872 | tf_op jit(solution)/shard_map/ppermute | solution.py:19
  267.5 41.5 %collective-permute-start.16 = (bf16[2,4,64,2048]{3,2,1,0:T(8,128)(2,1)}, bf16[2,4,64,2048]{3,2,1,0:T(8,128)(2,1)}, u32[]{:S(2)}, u32[]{:S(2)}) collective-permute-start(bf16[2,4,64,2048]{3,2,1,0:T(8,128)(2,1)} %bitcast.41), channel_id=1, source_target_pairs={{0,1},{1,0},{2,3},{3,2},{4,5},{5,4},{6,7},{7,6},{8,9},{9,8},{10,11... | collective-permute-start | bytes 6291464 | tf_op jit(solution)/shard_map/ppermute | solution.py:252
  272.0 37.0 %collective-permute-start.15 = (bf16[2,16,32,1024]{3,2,1,0:T(8,128)(2,1)}, bf16[2,16,32,1024]{3,2,1,0:T(8,128)(2,1)}, u32[]{:S(2)}, u32[]{:S(2)}) collective-permute-start(bf16[2,16,32,1024]{3,2,1,0:T(8,128)(2,1)} %bitcast.36), channel_id=1, source_target_pairs={{0,16},{16,0},{32,48},{48,32},{64,112},{80,96},{96,80},{112,64},{1... | collective-permute-start | bytes 6291464 | tf_op jit(solution)/shard_map/ppermute | solution.py:252
  289.2 17.4 %collective-permute-start.18 = (bf16[512,512]{1,0:T(8,128)(2,1)}, bf16[512,512]{1,0:T(8,128)(2,1)}, u32[]{:S(2)}, u32[]{:S(2)}) collective-permute-start(bf16[512,512]{1,0:T(8,128)(2,1)} %broadcast_select_fusion.6), channel_id=1, source_target_pairs={{0,64},{64,0},{1,65},{65,1},{2,66},{66,2},{3,67},{67,3},{4,68},{68... | collective-permute-start | bytes 1572872 | tf_op jit(solution)/shard_map/ppermute | solution.py:19
  313.0 20.3 %collective-permute-start.21 = (bf16[256,1024]{1,0:T(8,128)(2,1)}, bf16[256,1024]{1,0:T(8,128)(2,1)}, u32[]{:S(2)}, u32[]{:S(2)}) collective-permute-start(bf16[256,1024]{1,0:T(8,128)(2,1)} %fusion.55), channel_id=1, source_target_pairs={{0,64},{64,0},{1,65},{65,1},{2,66},{66,2},{3,67},{67,3},{4,68},{68... | collective-permute-start | bytes 1572872 | tf_op jit(solution)/shard_map/ppermute | solution.py:19
  316.3 20.2 %collective-permute-start.20 = (bf16[4,64,2048]{2,1,0:T(8,128)(2,1)}, bf16[4,64,2048]{2,1,0:T(8,128)(2,1)}, u32[]{:S(2)}, u32[]{:S(2)}) collective-permute-start(bf16[4,64,2048]{2,1,0:T(8,128)(2,1)} %fusion.29), channel_id=1, source_target_pairs={{0,3},{1,2},{2,1},{3,0},{4,7},{5,6},{6,5},{7,4},{8,11},{9,10},{10,... | collective-permute-start | bytes 3145736 | tf_op jit(solution)/shard_map/ppermute | solution.py:252
  318.9 17.6 %collective-permute-start.19 = (bf16[16,32,1024]{2,1,0:T(8,128)(2,1)}, bf16[16,32,1024]{2,1,0:T(8,128)(2,1)}, u32[]{:S(2)}, u32[]{:S(2)}) collective-permute-start(bf16[16,32,1024]{2,1,0:T(8,128)(2,1)} %fusion.51), channel_id=1, source_target_pairs={{0,48},{16,32},{32,16},{48,0},{64,80},{80,64},{96,112},{112,96},{1... | collective-permute-start | bytes 3145736 | tf_op jit(solution)/shard_map/ppermute | solution.py:252
  345.4 30.1 %collective-permute-start.22 = (bf16[256,1024]{1,0:T(8,128)(2,1)}, bf16[256,1024]{1,0:T(8,128)(2,1)}, u32[]{:S(2)}, u32[]{:S(2)}) collective-permute-start(bf16[256,1024]{1,0:T(8,128)(2,1)} %fusion.64), channel_id=1, source_target_pairs={{0,64},{64,0},{1,65},{65,1},{2,66},{66,2},{3,67},{67,3},{4,68},{68... | collective-permute-start | bytes 1572872 | tf_op jit(solution)/shard_map/ppermute | solution.py:19
  349.5 44.5 %collective-permute-start.25 = (bf16[2,4,64,2048]{3,2,1,0:T(8,128)(2,1)}, bf16[2,4,64,2048]{3,2,1,0:T(8,128)(2,1)}, u32[]{:S(2)}, u32[]{:S(2)}) collective-permute-start(bf16[2,4,64,2048]{3,2,1,0:T(8,128)(2,1)} %bitcast.61), channel_id=1, source_target_pairs={{0,1},{1,0},{2,3},{3,2},{4,5},{5,4},{6,7},{7,6},{8,9},{9,8},{10,11... | collective-permute-start | bytes 6291464 | tf_op jit(solution)/shard_map/ppermute | solution.py:252
  354.0 40.0 %collective-permute-start.24 = (bf16[2,16,32,1024]{3,2,1,0:T(8,128)(2,1)}, bf16[2,16,32,1024]{3,2,1,0:T(8,128)(2,1)}, u32[]{:S(2)}, u32[]{:S(2)}) collective-permute-start(bf16[2,16,32,1024]{3,2,1,0:T(8,128)(2,1)} %bitcast.56), channel_id=1, source_target_pairs={{0,16},{16,0},{32,48},{48,32},{64,112},{80,96},{96,80},{112,64},{1... | collective-permute-start | bytes 6291464 | tf_op jit(solution)/shard_map/ppermute | solution.py:252
  357.2 36.8 %collective-permute-start.23 = (bf16[2,4,64,2176]{3,2,1,0:T(8,128)(2,1)}, bf16[2,4,64,2176]{3,2,1,0:T(8,128)(2,1)}, u32[]{:S(2)}, u32[]{:S(2)}) collective-permute-start(bf16[2,4,64,2176]{3,2,1,0:T(8,128)(2,1)} %pad_maximum_fusion), channel_id=1, source_target_pairs={{0,4},{1,5},{2,6},{3,7},{4,0},{5,1},{6,2},{7,3},{8,12},{9,13},{10,... | collective-permute-start | bytes 6684680 | tf_op jit(solution)/shard_map/ppermute | solution.py:252
  396.7 14.3 %collective-permute-start.30 = (bf16[4,64,2048]{2,1,0:T(8,128)(2,1)}, bf16[4,64,2048]{2,1,0:T(8,128)(2,1)}, u32[]{:S(2)}, u32[]{:S(2)}) collective-permute-start(bf16[4,64,2048]{2,1,0:T(8,128)(2,1)} %fusion.30), channel_id=1, source_target_pairs={{0,3},{1,2},{2,1},{3,0},{4,7},{5,6},{6,5},{7,4},{8,11},{9,10},{10,... | collective-permute-start | bytes 3145736 | tf_op jit(solution)/shard_map/ppermute | solution.py:252
  399.8 17.4 %collective-permute-start.28 = (bf16[4,64,2176]{2,1,0:T(8,128)(2,1)}, bf16[4,64,2176]{2,1,0:T(8,128)(2,1)}, u32[]{:S(2)}, u32[]{:S(2)}) collective-permute-start(bf16[4,64,2176]{2,1,0:T(8,128)(2,1)} %fusion.67), channel_id=1, source_target_pairs={{0,12},{1,13},{2,14},{3,15},{4,8},{5,9},{6,10},{7,11},{8,4},{9,5},... | collective-permute-start | bytes 3342344 | tf_op jit(solution)/shard_map/ppermute | solution.py:252
  402.9 14.3 %collective-permute-start.29 = (bf16[16,32,1024]{2,1,0:T(8,128)(2,1)}, bf16[16,32,1024]{2,1,0:T(8,128)(2,1)}, u32[]{:S(2)}, u32[]{:S(2)}) collective-permute-start(bf16[16,32,1024]{2,1,0:T(8,128)(2,1)} %fusion.50), channel_id=1, source_target_pairs={{0,48},{16,32},{32,16},{48,0},{64,80},{80,64},{96,112},{112,96},{1... | collective-permute-start | bytes 3145736 | tf_op jit(solution)/shard_map/ppermute | solution.py:252
  419.5 20.9 %collective-permute-start.33 = (bf16[2,2,4,32,1024]{4,3,2,1,0:T(8,128)(2,1)S(1)}, bf16[2,2,4,32,1024]{4,3,2,1,0:T(8,128)(2,1)S(1)}, u32[]{:S(2)}, u32[]{:S(2)}) collective-permute-start(bf16[2,2,4,32,1024]{4,3,2,1,0:T(8,128)(2,1)S(1)} %pad_maximum_fusion.7), channel_id=1, source_target_pairs={{0,1},{1,0},{2,3},{3,2},{4,5},{5,4},{6,7},{7,6},{8,9},{9,8},{10,11... | collective-permute-start | bytes 3145736 | tf_op jit(solution)/shard_map/ppermute | solution.py:252
  425.2 27.6 %collective-permute-start.31 = (bf16[2,4,64,2176]{3,2,1,0:T(8,128)(2,1)S(1)}, bf16[2,4,64,2176]{3,2,1,0:T(8,128)(2,1)S(1)}, u32[]{:S(2)}, u32[]{:S(2)}) collective-permute-start(bf16[2,4,64,2176]{3,2,1,0:T(8,128)(2,1)S(1)} %pad_maximum_fusion.1), channel_id=1, source_target_pairs={{0,4},{1,5},{2,6},{3,7},{4,0},{5,1},{6,2},{7,3},{8,12},{9,13},{10,... | collective-permute-start | bytes 6684680 | tf_op jit(solution)/shard_map/ppermute | solution.py:252
  426.3 14.9 %collective-permute-start.32 = (bf16[2,2,4,16,2048]{4,3,1,2,0:T(8,128)(2,1)S(1)}, bf16[2,2,4,16,2048]{4,3,1,2,0:T(8,128)(2,1)S(1)}, u32[]{:S(2)}, u32[]{:S(2)}) collective-permute-start(bf16[2,2,4,16,2048]{4,3,1,2,0:T(8,128)(2,1)S(1)} %pad_maximum_fusion.6), channel_id=1, source_target_pairs={{0,16},{16,0},{32,48},{48,32},{64,112},{80,96},{96,80},{112,64},{1... | collective-permute-start | bytes 3145736 | tf_op jit(solution)/shard_map/ppermute | solution.py:252
  454.0 11.6 %collective-permute-start.37 = (bf16[2,4,32,1024]{3,2,1,0:T(8,128)(2,1)}, bf16[2,4,32,1024]{3,2,1,0:T(8,128)(2,1)}, u32[]{:S(2)}, u32[]{:S(2)}) collective-permute-start(bf16[2,4,32,1024]{3,2,1,0:T(8,128)(2,1)} %fusion.77), channel_id=1, source_target_pairs={{0,3},{1,2},{2,1},{3,0},{4,7},{5,6},{6,5},{7,4},{8,11},{9,10},{10,... | collective-permute-start | bytes 1572872 | tf_op jit(solution)/shard_map/ppermute | solution.py:252
  456.1 15.1 %collective-permute-start.35 = (bf16[4,64,2176]{2,1,0:T(8,128)(2,1)}, bf16[4,64,2176]{2,1,0:T(8,128)(2,1)}, u32[]{:S(2)}, u32[]{:S(2)}) collective-permute-start(bf16[4,64,2176]{2,1,0:T(8,128)(2,1)} %fusion.68), channel_id=1, source_target_pairs={{0,12},{1,13},{2,14},{3,15},{4,8},{5,9},{6,10},{7,11},{8,4},{9,5},... | collective-permute-start | bytes 3342344 | tf_op jit(solution)/shard_map/ppermute | solution.py:252
  472.5 18.9 %collective-permute-start.42 = (bf16[2,16,2176]{2,1,0:T(8,128)(2,1)S(1)}, bf16[2,16,2176]{2,1,0:T(8,128)(2,1)S(1)}, u32[]{:S(2)}, u32[]{:S(2)}) collective-permute-start(bf16[2,16,2176]{2,1,0:T(8,128)(2,1)S(1)} %pad_maximum_fusion.18), channel_id=1, source_target_pairs={{0,16},{16,0},{32,48},{48,32},{64,112},{80,96},{96,80},{112,64},{1... | collective-permute-start | bytes 417800 | tf_op jit(solution)/shard_map/ppermute | solution.py:252
  475.2 16.1 %collective-permute-start.41 = (bf16[2,2,32,1024]{3,2,1,0:T(8,128)(2,1)S(1)}, bf16[2,2,32,1024]{3,2,1,0:T(8,128)(2,1)S(1)}, u32[]{:S(2)}, u32[]{:S(2)}) collective-permute-start(bf16[2,2,32,1024]{3,2,1,0:T(8,128)(2,1)S(1)} %pad_maximum_fusion.17), channel_id=1, source_target_pairs={{0,4},{1,5},{2,6},{3,7},{4,0},{5,1},{6,2},{7,3},{8,12},{9,13},{10,... | collective-permute-start | bytes 786440 | tf_op jit(solution)/shard_map/ppermute | solution.py:252
  505.3 12.3 %collective-permute-start.47 = (bf16[16,10368]{1,0:T(8,128)(2,1)S(1)}, bf16[16,10368]{1,0:T(8,128)(2,1)S(1)}, u32[]{:S(2)}, u32[]{:S(2)}) collective-permute-start(bf16[16,10368]{1,0:T(8,128)(2,1)S(1)} %fusion.151), channel_id=1, source_target_pairs={{0,16},{16,0},{32,48},{48,32},{64,112},{80,96},{96,80},{112,64},{1... | collective-permute-start | bytes 995336 | tf_op jit(solution)/shard_map/ppermute | solution.py:252
  517.6 12.8 %collective-permute-start.51 = (bf16[2,16,10368]{2,1,0:T(8,128)(2,1)S(1)}, bf16[2,16,10368]{2,1,0:T(8,128)(2,1)S(1)}, u32[]{:S(2)}, u32[]{:S(2)}) collective-permute-start(bf16[2,16,10368]{2,1,0:T(8,128)(2,1)S(1)} %pad_maximum_fusion.13), channel_id=1, source_target_pairs={{0,48},{16,32},{32,16},{48,0},{64,80},{80,64},{96,112},{112,96},{1... | collective-permute-start | bytes 1990664 | tf_op jit(solution)/shard_map/ppermute | solution.py:252
  (175 other events, 1154.9 us)
Sparse Core Ops, SparseCore 0:
  17.9 83.8 all-gather.2
  104.0 71.7 all-gather.4

commit v8 on v7

--- a/solution.py
+++ b/solution.py
@@ -35,6 +35,10 @@
 
 def dot_transposed(left, right):
     return lax.dot_general(left, right, (((1,), (1,)), ((), ())), preferred_element_type=F32)
+
+
+def sum_rows(values):
+    return jnp.sum(values, axis=0, keepdims=True)
 
 
 def norm_rows(values):
@@ -125,8 +129,11 @@
     )(seq_lengths, *arrays)
 
 
-def forward_attention(inputs, weights, seq_lengths):
-    packed = (dot(inputs, weights["qkv"]) + weights["bias_qkv"]).astype(BF)
+def forward_packed(inputs, weights):
+    return (dot(inputs, weights["qkv"]) + weights["bias_qkv"]).astype(BF)
+
+
+def forward_attention(inputs, packed, seq_lengths):
     attended = attention_call(attention_kernel, packed.shape[1] // 3, seq_lengths, packed)
     return (attended, dict(inputs=inputs, packed=packed, seq_lengths=seq_lengths))
 
@@ -154,8 +161,8 @@
 def backward_mlp(grad_result, kept, weights):
     grad_result = grad_result.astype(F32)
     normed = kept["normed_mlp"]
-    grad_gain = jnp.sum(grad_result * normed, axis=0)
-    grad_shift = jnp.sum(grad_result, axis=0)
+    grad_gain = sum_rows(grad_result * normed)
+    grad_shift = sum_rows(grad_result)
     grad_resid = norm_back(grad_result * weights["gain_mlp"], normed, kept["inverse_mlp"])
     grad_mixed = grad_resid.astype(BF)
     grad_upward = (dot_transposed(grad_mixed, weights["down"]) * kept["slope"]).astype(BF)
@@ -163,8 +170,8 @@
     grads = dict(
         mixed=grad_mixed,
         upward=grad_upward,
-        bias_up=jnp.sum(grad_upward.astype(F32), axis=0),
-        bias_down=jnp.sum(grad_mixed.astype(F32), axis=0),
+        bias_up=sum_rows(grad_upward.astype(F32)),
+        bias_down=sum_rows(grad_mixed.astype(F32)),
         gain_mlp=grad_gain,
         shift_mlp=grad_shift,
     )
@@ -176,9 +183,9 @@
     grad_resid = norm_back(grad_hidden * weights["gain_attn"], normed, kept["inverse_attn"])
     grad_branch = grad_resid.astype(BF)
     grads.update(
-        gain_attn=jnp.sum(grad_hidden * normed, axis=0),
-        shift_attn=jnp.sum(grad_hidden, axis=0),
-        bias_out=jnp.sum(grad_branch.astype(F32), axis=0),
+        gain_attn=sum_rows(grad_hidden * normed),
+        shift_attn=sum_rows(grad_hidden),
+        bias_out=sum_rows(grad_branch.astype(F32)),
         out=transpose_dot(kept["attended"], grad_branch).astype(BF),
     )
     packed = kept["packed"]
@@ -190,11 +197,11 @@
 
 
 def backward_inputs(grad_resid, grad_packed, grads, kept, weights):
-    columns = jnp.sum(grad_packed.astype(F32), axis=0)
-    width = columns.shape[0] // 3
+    columns = sum_rows(grad_packed.astype(F32))
+    width = columns.shape[1] // 3
     grads.update(
-        bias_q=columns[:width],
-        bias_v=columns[2 * width :],
+        bias_q=columns[:, :width],
+        bias_v=columns[:, 2 * width :],
         qkv=transpose_dot(kept["inputs"], grad_packed).astype(BF),
     )
     passed = dot_transposed(grad_packed, weights["qkv"])
@@ -373,11 +380,12 @@
 
     def arranged(attn, down):
         flat = attn[:, :LANES].reshape(shards, rows, LANES)[:, :vector_rows, :rows].astype(F32)
-        whole = [flat[:, n].reshape(-1) for n in range(8)]
+        lines = flat[:, :8].transpose(1, 0, 2).reshape(8, model)
+        whole = [lines[n : n + 1] for n in range(8)]
         bias_up_part = flat[:, 8:].reshape(shards, 2, unit)
-        bias_up_part = choose(bias_up_part[:, 0], bias_up_part[:, 1]).reshape(-1)
-        bias_q_part = choose(whole[0][:half], whole[0][half:])
-        bias_v_part = choose(whole[1][:half], whole[1][half:])
+        bias_up_part = choose(bias_up_part[:, 0], bias_up_part[:, 1]).reshape(1, -1)
+        bias_q_part = choose(whole[0][:, :half], whole[0][:, half:])
+        bias_v_part = choose(whole[1][:, :half], whole[1][:, half:])
         out = attn[:, edges[1] : edges[2]]
         held, handed = mine_of(out[:half], out[half:])
         arrived = swap(handed)
@@ -386,7 +394,7 @@
             out=jnp.concatenate(mine_of(held, arrived), axis=1),
             up=attn[:, edges[2] :],
             down=down,
-            bias_qkv=jnp.concatenate([bias_q_part, jnp.zeros_like(bias_q_part), bias_v_part]),
+            bias_qkv=jnp.concatenate([bias_q_part, 0.0 * bias_q_part, bias_v_part], axis=1),
             bias_out=whole[2],
             gain_attn=whole[3],
             shift_attn=whole[4],
@@ -396,31 +404,30 @@
             bias_up=bias_up_part,
         )
 
-    def side_by_side(grads):
+    def vectors_of(grads):
+        def widened(part):
+            return jnp.concatenate([choose(part, 0.0), choose(0.0, part)], axis=1)
+
+        names = ("bias_out", "gain_attn", "shift_attn", "bias_down", "gain_mlp", "shift_mlp")
+        lines = [widened(grads["bias_q"]), widened(grads["bias_v"])]
+        lines = jnp.concatenate(lines + [0.5 * grads[name] for name in names], axis=0)
+        lines = lines.reshape(8, shards, rows).transpose(1, 0, 2)
+        spread = widened(grads["bias_up"].reshape(shards, unit)).reshape(shards, -1, rows)
+        return jnp.concatenate([lines, spread], axis=1)
+
+    def sides_of(grads):
         held, handed = mine_of(grads["out"][:, :half], grads["out"][:, half:])
-        out = jnp.concatenate(mine_of(held, swap(handed)), axis=0)
-
-        def widened(part):
-            return jnp.concatenate([choose(part, 0.0), choose(0.0, part)])
-
-        whole = [widened(grads["bias_q"]), widened(grads["bias_v"])]
-        names = ("bias_out", "gain_attn", "shift_attn", "bias_down", "gain_mlp", "shift_mlp")
-        whole += [0.5 * grads[name] for name in names]
-        part = grads["bias_up"].reshape(shards, unit)
-        spread = jnp.concatenate([choose(part, 0.0), choose(0.0, part)], axis=1)
-        flat = [v.reshape(shards, 1, rows) for v in whole] + [spread.reshape(shards, -1, rows)]
-        flat = jnp.concatenate(flat, axis=1).astype(BF)
-        flat = jnp.pad(flat, ((0, 0), (0, rows - vector_rows), (0, LANES - rows)))
-        return (flat.reshape(shards * rows, LANES), grads["qkv"], out)
+        return [grads["qkv"], jnp.concatenate(mine_of(held, swap(handed)), axis=0)]
 
     count = tokens.shape[0]
     seq_lengths = lengths[:, 0]
 
     first_weights = arranged(side0[:, : edges[3]], None)
     cn = gather_one(c0, "x")
-    attended, kept0 = forward_attention(tokens.reshape(-1, model), first_weights, seq_lengths)
-    cn, attended = together(cn, attended)
+    packed = forward_packed(tokens.reshape(-1, model), first_weights)
+    cn, packed = together(cn, packed)
     cf = gather_two(c0, cn, "x")
+    attended, kept0 = forward_attention(tokens.reshape(-1, model), packed, seq_lengths)
     activated = forward_hidden(attended, kept0, first_weights)
     cf, activated = together(cf, activated)
     first_weights["down"] = gather_end(c0, cn, cf, "x", 1).reshape(-1, model)
@@ -429,9 +436,10 @@
     cn, middle, side1 = together(cn, middle, side1)
     cf = gather_two(c1, cn, "x")
     second_weights = arranged(side1, None)
-    attended, kept1 = forward_attention(middle, second_weights, seq_lengths)
+    packed = forward_packed(middle, second_weights)
+    attended, kept1 = forward_attention(middle, packed, seq_lengths)
+    cf, attended = together(cf, attended)
     activated = forward_hidden(attended, kept1, second_weights)
-    cf, activated = together(cf, activated)
     second_weights["down"] = gather_end(c1, cn, cf, "x", 1).reshape(-1, model)
     last = forward_output(activated, kept1, second_weights)
 
@@ -444,9 +452,9 @@
         left = kept["hidden"].reshape(-1, RING, RING, rows).transpose(2, 0, 1, 3)
         return products(left.reshape(RING, -1, RING * rows), grads["upward"], (RING, rows, shards * unit))
 
-    def side_of(grads):
-        pieces = list(zip((0,) + edges, side_by_side(grads)))
-        return placed(edges[2], pieces).reshape(RING, RING, rows, -1)
+    def side_by_side(pieces, ends):
+        joined = placed(ends[-1], list(zip((0,) + ends, pieces)))
+        return joined.reshape(RING, RING, rows, -1)
 
     grad_hidden, grads1 = backward_mlp(cotangent.reshape(-1, model), kept1, second_weights)
     c1, b1 = (down_of(grads1, kept1), up_of(grads1, kept1))
@@ -455,7 +463,7 @@
     cn, bn, grad_packed = together(cn, bn, grad_packed)
     cf, bf = (scatter_two(c1, cn, "x"), scatter_two(b1, bn, "y"))
     grad_middle = backward_inputs(grad_resid, grad_packed, grads1, kept1, second_weights)
-    a1 = side_of(grads1)
+    a1 = side_by_side(sides_of(grads1), (3 * half, 4 * half))
     a1, cf, bf, grad_middle = together(a1, cf, bf, grad_middle)
     c1, b1 = (scatter_end(c1, cn, cf, "x"), scatter_end(b1, bn, bf, "y"))
     a1 = slices(a1, 0)
@@ -469,7 +477,9 @@
     af1 = scatter_two(a1, an1, "z")
     cf, bf = (scatter_two(c0, cn, "x"), scatter_two(b0, bn, "y"))
     grad_first = backward_inputs(grad_resid, grad_packed, grads0, kept0, first_weights)
-    a0 = side_of(grads0)
+    flat = jnp.concatenate([vectors_of(grads0), vectors_of(grads1)], axis=2).astype(BF)
+    flat = jnp.pad(flat, ((0, 0), (0, rows - vector_rows), (0, LANES - 2 * rows)))
+    a0 = side_by_side([flat.reshape(-1, LANES)] + sides_of(grads0), edges[:3])
     a0, af1, cf, bf = together(a0, af1, cf, bf)
     a1 = scatter_end(a1, an1, af1, "z")
     c0, b0 = (scatter_end(c0, cn, cf, "x"), scatter_end(b0, bn, bf, "y"))
@@ -497,27 +507,28 @@
     b, c = (scatter_end(b, bn, bf, "z"), scatter_end(c, cn, cf, "z"))
     wide = shards * unit
     rest = [b[0], c[0].reshape(-1, wide), b[1], c[1].reshape(-1, wide), a1]
-    rest = placed(4 * wide + edges[2], [(n * wide, piece) for n, piece in enumerate(rest)])
-    bn = gather_one(rest, "x")
+    rest = placed(4 * wide + 4 * half, [(n * wide, piece) for n, piece in enumerate(rest)])
     others = [hop(a0, n) for n in range(1, RING)]
-    bn, others = together(bn, others)
+    spread = [hop(rest, n) for n in range(1, RING)]
+    others, spread = together(others, spread)
     a0 = (a0.astype(F32) + sum(other.astype(F32) for other in others)).astype(BF)
-    rest = gather_end(rest, bn, gather_two(rest, bn, "x"), "x", 0).reshape(rows, -1)
+    whole = put(jnp.zeros((RING,) + rest.shape, BF), rest, place["x"], 0)
+    for n, piece in enumerate(spread):
+        whole = put(whole, piece, (place["x"] - n - 1) % RING, 0)
+    rest = whole.reshape(rows, -1)
     b0, c0, b1, c1 = (rest[:, n * wide : (n + 1) * wide] for n in range(4))
-    summed_first = (a0, b0, c0.reshape(unit, model))
+    summed_first = (a0[:, LANES:], b0, c0.reshape(unit, model))
     summed_second = (rest[:, 4 * wide :], b1, c1.reshape(unit, model))
     mine, sent = zip(*(mine_of(a, b) for a, b in zip(summed_first, summed_second)))
     both = [mine_of(a, swap(b)) for a, b in zip(mine, sent)]
     both = [[v.astype(F32) for v in pair] for pair in both]
     (side_a, side_b), (up_a, up_b), (down_a, down_b) = both
-
-    def cut(block):
-        flat = block[:vector_rows, :rows]
-        return (flat, block[:, LANES : edges[1]].reshape(rows, 3, half), block[:, edges[1] :])
-
-    (flat_a, qkv_a, out_a), (flat_b, qkv_b, out_b) = (cut(side_a), cut(side_b))
+    flat = a0[:vector_rows, :LANES]
+    flat = flat.astype(F32) + swap(flat).astype(F32)
+    flat = choose(flat[:, :rows], flat[:, rows : 2 * rows])
+    qkv_a, qkv_b = (side[:, : 3 * half].reshape(rows, 3, half) for side in (side_a, side_b))
+    out_a, out_b = (side[:, 3 * half :] for side in (side_a, side_b))
     up_a, up_b = (up_a.reshape(rows, shards, unit), up_b.reshape(rows, shards, unit))
-    flat = flat_a + flat_b
     whole = [flat[n] for n in range(8)]
     grads = (
         jnp.stack([qkv_a, qkv_b], axis=2).reshape(rows, -1),

time: 570 us -> 560 us (0.982)
  waiting for transfers between devices: 198 us -> 168 us
  matrix products: 82.5 us -> 89.7 us
  starting transfers between devices: 62.5 us -> 68.7 us
    ppermute x32 -> x30, waiting for transfers between devices: 108 us -> 66.9 us  [trade(): return lax.ppermute(value, ('section', name), route)]
    ppermute x3 -> x6, waiting for transfers between devices: 5.39 us -> 16.3 us  [hop(): return lax.ppermute(value, 'dp', route)]
    unnamed x303 -> x290, local copies, waits for them, and re-layouts: 11.3 us -> 16.1 us
    select_n x23 -> x22, other arithmetic: 18.7 us -> 16.7 us  [choose(): return jnp.where(first, low, high)]
    ppermute x32 -> x30, starting transfers between devices: 33.6 us -> 35.5 us  [trade(): return lax.ppermute(value, ('section', name), route)]
    select_n x18 -> x10, local copies, waits for them, and re-layouts: 11.6 us -> 10.8 us  [choose(): return jnp.where(first, low, high)]
    ppermute x20 -> x21, starting transfers between devices: 25.6 us -> 25.4 us  [swap(): return lax.ppermute(value, 'section', [(0, 1), (1, 0)])]
  transfers between devices with their start and end apart: 57 -> 59, of which waited for: 19 -> 21; matrix products, arithmetic and copies ran while one was open for 33% -> 36% of each run, Pallas kernels for 6% -> 6%
where the time goes in v8:
time: 560 us; the launch traced here: 550 us
  waiting for transfers between devices  168 us (30%)
  matrix products  89.7 us (16%)
  local copies, waits for them, and re-layouts  88.8 us (16%)
  other arithmetic  84.5 us (15%)
  starting transfers between devices  68.7 us (12%)
  Pallas kernels  33.2 us (6%)
  between operations  17.1 us (3%)
    all_gather x2, waiting for transfers between devices, whole(): return lax.all_gather(block, 'shard', axis=0, tiled=True)  84 us
    ppermute x30, waiting for transfers between devices, trade(): return lax.ppermute(value, ('section', name), route)  66.9 us
    ppermute x30, starting transfers between devices, trade(): return lax.ppermute(value, ('section', name), route)  35.5 us
    pallas_call x4, Pallas kernels, attention_call(): pl.pallas_call(kernel, out_shape=jax.ShapeDtypeStruct((rows, width), BF),...  33.2 us
    dot_general x8, matrix products, dot_transposed(): lax.dot_general(left, right, (((1,), (1,)), ((), ())), preferred_element_...  28.4 us
    dot_general x8, matrix products, dot(): return jnp.dot(left, right, preferred_element_type=F32)  27.2 us
    dot_general x12, matrix products, transpose_dot(): lax.dot_general(left, right, (((0,), (0,)), ((), ())), preferred_element_...  26 us
    ppermute x21, starting transfers between devices, swap(): return lax.ppermute(value, 'section', [(0, 1), (1, 0)])  25.4 us
  transfers between devices with their start and end apart: 59, of which 21 were waited for; matrix products, arithmetic and copies ran while one was open for 36% of the time, Pallas kernels for 6%

profile of v8, /device:TPU:1, one launch (start us, length us, event | category | flops | bytes accessed | tf_op | source)
XLA Modules:
  0.0 549.7 jit_solution(15388520674030262662)
XLA Ops:
  17.8 84.0 %all-gather.3.cloned.1.call-done = bf16[1024,5248]{1,0:T(8,128)(2,1)} async-done(((bf16[64,5248]{1,0:T(8,128)(2,1)}), bf16[1024,5248]{1,0:T(8,128)(2,1)}) %all-gather.3.cloned.1.call-update) | async-done | bytes 10747920 | tf_op jit(solution)/shard_map/all_gather | solution.py:372
  118.2 4.3 fusion.32.packed_ref
  125.8 7.1 %shard_map.271 = bf16[256,512]{1,0:T(8,128)(2,1)} custom-call(s32[2]{0:T(128)} %bitcast.478, bf16[256,1536]{1,0:T(8,128)(2,1)} %fusion.32.packed_ref), custom_call_target="tpu_custom_call" | custom-call | flops 67108864 | bytes 524288 | tf_op jit(solution)/shard_map/pallas_call | solution.py:121
  138.2 5.1 multiply_convert_fusion.1
  143.2 17.7 %collective-permute-done.6 = bf16[2,16,32,1024]{3,2,1,0:T(8,128)(2,1)S(1)} collective-permute-done((bf16[2,16,32,1024]{3,2,1,0:T(8,128)(2,1)S(1)}, bf16[2,16,32,1024]{3,2,1,0:T(8,128)(2,1)S(1)}, u32[]{:S(2)}, u32[]{:S(2)}) %collective-permute-start.6) | collective-permute-done | bytes 2097184 | tf_op jit(solution)/shard_map/ppermute | solution.py:259
  176.8 9.5 %collective-permute-done.9 = bf16[16,32,1024]{2,1,0:T(8,128)(2,1)} collective-permute-done((bf16[16,32,1024]{2,1,0:T(8,128)(2,1)}, bf16[16,32,1024]{2,1,0:T(8,128)(2,1)}, u32[]{:S(2)}, u32[]{:S(2)}) %collective-permute-start.9) | collective-permute-done | bytes 1048608 | tf_op jit(solution)/shard_map/ppermute | solution.py:259
  187.3 3.1 pad_maximum_fusion.2
  196.1 3.8 fusion.22.packed_ref
  205.2 7.1 %shard_map.272 = bf16[256,512]{1,0:T(8,128)(2,1)} custom-call(s32[2]{0:T(128)} %bitcast.479, bf16[256,1536]{1,0:T(8,128)(2,1)} %fusion.22.packed_ref), custom_call_target="tpu_custom_call" | custom-call | flops 67108864 | bytes 524288 | tf_op jit(solution)/shard_map/pallas_call | solution.py:121
  224.8 5.0 multiply_convert_fusion
  229.8 4.6 convolution_convert_fusion.10
  245.5 4.7 convert_reduce_fusion
  250.1 4.6 fusion.60
  275.2 3.5 multiply_reduce_fusion
  290.7 9.5 %shard_map.273 = bf16[256,1536]{1,0:T(8,128)(2,1)} custom-call(s32[2]{0:T(128)} %bitcast.480, bf16[256,1536]{1,0:T(8,128)(2,1)} %fusion.22.packed_ref, bf16[256,512]{1,0:T(8,128)(2,1)} %convolution_convert_fusion.13.grad_ref), custom_call_target="tpu_custom_call" | custom-call | flops 201326592 | bytes 1572864 | tf_op jit(solution)/shard_map/pallas_call | solution.py:121
  302.7 3.8 fusion.54
  326.3 4.4 maximum_maximum_fusion
  338.4 4.7 fusion.63
  369.5 3.2 fusion.45
  372.8 3.2 add_convert_fusion.1
  383.5 9.6 %shard_map.274 = bf16[256,1536]{1,0:T(8,128)(2,1)} custom-call(s32[2]{0:T(128)} %bitcast.481, bf16[256,1536]{1,0:T(8,128)(2,1)} %fusion.32.packed_ref, bf16[256,512]{1,0:T(8,128)(2,1)} %convolution_convert_fusion.12.grad_ref), custom_call_target="tpu_custom_call" | custom-call | flops 201326592 | bytes 1572864 | tf_op jit(solution)/shard_map/pallas_call | solution.py:121
  406.3 5.2 collective-permute-done.30
  414.3 3.1 collective-permute-done.28
  437.6 7.9 %collective-permute-done.34 = bf16[2,64,2048]{2,1,0:T(8,128)(2,1)} collective-permute-done((bf16[2,64,2048]{2,1,0:T(8,128)(2,1)}, bf16[2,64,2048]{2,1,0:T(8,128)(2,1)}, u32[]{:S(2)}, u32[]{:S(2)}) %collective-permute-start.34) | collective-permute-done | bytes 524320 | tf_op jit(solution)/shard_map/ppermute | solution.py:259
  445.5 6.7 %collective-permute-done.31 = bf16[2,4,64,2176]{3,2,1,0:T(8,128)(2,1)} collective-permute-done((bf16[2,4,64,2176]{3,2,1,0:T(8,128)(2,1)}, bf16[2,4,64,2176]{3,2,1,0:T(8,128)(2,1)}, u32[]{:S(2)}, u32[]{:S(2)}) %collective-permute-start.31) | collective-permute-done | bytes 2228256 | tf_op jit(solution)/shard_map/ppermute | solution.py:259
  462.1 3.8 collective-permute-done.38
  466.2 5.0 collective-permute-done.35
  484.9 4.6 collective-permute-start.26
  498.8 3.8 collective-permute-start.48
  509.7 5.8 %collective-permute-done.50 = bf16[16,10240]{1,0:T(8,128)(2,1)S(1)} collective-permute-done((bf16[16,10240]{1,0:T(8,128)(2,1)S(1)}, bf16[16,10240]{1,0:T(8,128)(2,1)S(1)}, u32[]{:S(2)}, u32[]{:S(2)}) %collective-permute-start.50) | collective-permute-done | bytes 327712 | tf_op jit(solution)/shard_map/ppermute | solution.py:266
  515.4 7.7 %collective-permute-done.51 = bf16[16,10240]{1,0:T(8,128)(2,1)S(1)} collective-permute-done((bf16[16,10240]{1,0:T(8,128)(2,1)S(1)}, bf16[16,10240]{1,0:T(8,128)(2,1)S(1)}, u32[]{:S(2)}, u32[]{:S(2)}) %collective-permute-start.51) | collective-permute-done | bytes 327712 | tf_op jit(solution)/shard_map/ppermute | solution.py:266
  523.3 7.3 %collective-permute-start.54 = (bf16[12,128]{1,0:T(8,128)(2,1)S(1)}, bf16[12,128]{1,0:T(8,128)(2,1)S(1)}, u32[]{:S(2)}, u32[]{:S(2)}) collective-permute-start(bf16[12,128]{1,0:T(8,128)(2,1)S(1)} %slice.576), channel_id=1, source_target_pairs={{0,64},{64,0},{1,65},{65,1},{2,66},{66,2},{3,67},{67,3},{4,68},{68... | collective-permute-start | bytes 9224 | tf_op jit(solution)/shard_map/ppermute | solution.py:19
  (682 shorter events, 269.2 us)
Async XLA Ops:
  7.3 94.5 %all-gather.3.cloned.1.call-start = ((), (), s32[]{:S(2)}) async-start(), calls=%async_computation | async-start | bytes 11419648 | tf_op jit(solution)/shard_map/all_gather | solution.py:372
  17.8 168.5 %all-gather.5.cloned.1.call-start = ((), (), s32[]{:S(2)}) async-start(), calls=%async_computation.1 | async-start | bytes 9191424 | tf_op jit(solution)/shard_map/all_gather | solution.py:372
  110.3 15.5 %collective-permute-start.5 = (bf16[16,32,1024]{2,1,0:T(8,128)(2,1)}, bf16[16,32,1024]{2,1,0:T(8,128)(2,1)S(1)}, u32[]{:S(2)}, u32[]{:S(2)}) collective-permute-start(bf16[16,32,1024]{2,1,0:T(8,128)(2,1)} %reshape.653), channel_id=1, source_target_pairs={{0,16},{16,0},{32,48},{48,32},{64,112},{80,96},{96,80},{112,64},{1... | collective-permute-start | bytes 3145736 | tf_op jit(solution)/shard_map/ppermute | solution.py:259
  135.1 25.8 %collective-permute-start.6 = (bf16[2,16,32,1024]{3,2,1,0:T(8,128)(2,1)S(1)}, bf16[2,16,32,1024]{3,2,1,0:T(8,128)(2,1)S(1)}, u32[]{:S(2)}, u32[]{:S(2)}) collective-permute-start(bf16[2,16,32,1024]{3,2,1,0:T(8,128)(2,1)S(1)} %pad_maximum_fusion.1), channel_id=1, source_target_pairs={{0,48},{16,32},{32,16},{48,0},{64,80},{80,64},{96,112},{112,96},{1... | collective-permute-start | bytes 6291464 | tf_op jit(solution)/shard_map/ppermute | solution.py:259
  171.0 15.3 %collective-permute-start.9 = (bf16[16,32,1024]{2,1,0:T(8,128)(2,1)}, bf16[16,32,1024]{2,1,0:T(8,128)(2,1)}, u32[]{:S(2)}, u32[]{:S(2)}) collective-permute-start(bf16[16,32,1024]{2,1,0:T(8,128)(2,1)} %reshape.652), channel_id=1, source_target_pairs={{0,16},{16,0},{32,48},{48,32},{64,112},{80,96},{96,80},{112,64},{1... | collective-permute-start | bytes 3145736 | tf_op jit(solution)/shard_map/ppermute | solution.py:259
  190.4 25.7 %collective-permute-start.11 = (bf16[2,16,32,1024]{3,2,1,0:T(8,128)(2,1)}, bf16[2,16,32,1024]{3,2,1,0:T(8,128)(2,1)}, u32[]{:S(2)}, u32[]{:S(2)}) collective-permute-start(bf16[2,16,32,1024]{3,2,1,0:T(8,128)(2,1)} %pad_maximum_fusion.2), channel_id=1, source_target_pairs={{0,48},{16,32},{32,16},{48,0},{64,80},{80,64},{96,112},{112,96},{1... | collective-permute-start | bytes 6291464 | tf_op jit(solution)/shard_map/ppermute | solution.py:259
  193.4 21.2 %collective-permute-start.12 = (bf16[512,512]{1,0:T(8,128)(2,1)}, bf16[512,512]{1,0:T(8,128)(2,1)}, u32[]{:S(2)}, u32[]{:S(2)}) collective-permute-start(bf16[512,512]{1,0:T(8,128)(2,1)} %broadcast_select_fusion.10), channel_id=1, source_target_pairs={{0,64},{64,0},{1,65},{65,1},{2,66},{66,2},{3,67},{67,3},{4,68},{68... | collective-permute-start | bytes 1572872 | tf_op jit(solution)/shard_map/ppermute | solution.py:19
  254.8 20.4 %collective-permute-start.17 = (bf16[256,1024]{1,0:T(8,128)(2,1)}, bf16[256,1024]{1,0:T(8,128)(2,1)}, u32[]{:S(2)}, u32[]{:S(2)}) collective-permute-start(bf16[256,1024]{1,0:T(8,128)(2,1)} %fusion.60), channel_id=1, source_target_pairs={{0,64},{64,0},{1,65},{65,1},{2,66},{66,2},{3,67},{67,3},{4,68},{68... | collective-permute-start | bytes 1572872 | tf_op jit(solution)/shard_map/ppermute | solution.py:19
  257.3 45.4 %collective-permute-start.16 = (bf16[2,4,64,2048]{3,2,1,0:T(8,128)(2,1)}, bf16[2,4,64,2048]{3,2,1,0:T(8,128)(2,1)}, u32[]{:S(2)}, u32[]{:S(2)}) collective-permute-start(bf16[2,4,64,2048]{3,2,1,0:T(8,128)(2,1)} %bitcast.43), channel_id=1, source_target_pairs={{0,1},{1,0},{2,3},{3,2},{4,5},{5,4},{6,7},{7,6},{8,9},{9,8},{10,11... | collective-permute-start | bytes 6291464 | tf_op jit(solution)/shard_map/ppermute | solution.py:259
  261.5 41.2 %collective-permute-start.15 = (bf16[2,16,32,1024]{3,2,1,0:T(8,128)(2,1)}, bf16[2,16,32,1024]{3,2,1,0:T(8,128)(2,1)}, u32[]{:S(2)}, u32[]{:S(2)}) collective-permute-start(bf16[2,16,32,1024]{3,2,1,0:T(8,128)(2,1)} %bitcast.38), channel_id=1, source_target_pairs={{0,16},{16,0},{32,48},{48,32},{64,112},{80,96},{96,80},{112,64},{1... | collective-permute-start | bytes 6291464 | tf_op jit(solution)/shard_map/ppermute | solution.py:259
  282.3 17.9 %collective-permute-start.18 = (bf16[512,512]{1,0:T(8,128)(2,1)}, bf16[512,512]{1,0:T(8,128)(2,1)}, u32[]{:S(2)}, u32[]{:S(2)}) collective-permute-start(bf16[512,512]{1,0:T(8,128)(2,1)} %broadcast_select_fusion.6), channel_id=1, source_target_pairs={{0,64},{64,0},{1,65},{65,1},{2,66},{66,2},{3,67},{67,3},{4,68},{68... | collective-permute-start | bytes 1572872 | tf_op jit(solution)/shard_map/ppermute | solution.py:19
  309.3 21.4 %collective-permute-start.21 = (bf16[256,1024]{1,0:T(8,128)(2,1)}, bf16[256,1024]{1,0:T(8,128)(2,1)}, u32[]{:S(2)}, u32[]{:S(2)}) collective-permute-start(bf16[256,1024]{1,0:T(8,128)(2,1)} %fusion.54), channel_id=1, source_target_pairs={{0,64},{64,0},{1,65},{65,1},{2,66},{66,2},{3,67},{67,3},{4,68},{68... | collective-permute-start | bytes 1572872 | tf_op jit(solution)/shard_map/ppermute | solution.py:19
  312.6 20.6 %collective-permute-start.20 = (bf16[4,64,2048]{2,1,0:T(8,128)(2,1)}, bf16[4,64,2048]{2,1,0:T(8,128)(2,1)}, u32[]{:S(2)}, u32[]{:S(2)}) collective-permute-start(bf16[4,64,2048]{2,1,0:T(8,128)(2,1)} %fusion.28), channel_id=1, source_target_pairs={{0,3},{1,2},{2,1},{3,0},{4,7},{5,6},{6,5},{7,4},{8,11},{9,10},{10,... | collective-permute-start | bytes 3145736 | tf_op jit(solution)/shard_map/ppermute | solution.py:259
  315.3 17.9 %collective-permute-start.19 = (bf16[16,32,1024]{2,1,0:T(8,128)(2,1)}, bf16[16,32,1024]{2,1,0:T(8,128)(2,1)}, u32[]{:S(2)}, u32[]{:S(2)}) collective-permute-start(bf16[16,32,1024]{2,1,0:T(8,128)(2,1)} %fusion.49), channel_id=1, source_target_pairs={{0,48},{16,32},{32,16},{48,0},{64,80},{80,64},{96,112},{112,96},{1... | collective-permute-start | bytes 3145736 | tf_op jit(solution)/shard_map/ppermute | solution.py:259
  343.1 32.8 %collective-permute-start.22 = (bf16[256,1024]{1,0:T(8,128)(2,1)}, bf16[256,1024]{1,0:T(8,128)(2,1)}, u32[]{:S(2)}, u32[]{:S(2)}) collective-permute-start(bf16[256,1024]{1,0:T(8,128)(2,1)} %fusion.63), channel_id=1, source_target_pairs={{0,64},{64,0},{1,65},{65,1},{2,66},{66,2},{3,67},{67,3},{4,68},{68... | collective-permute-start | bytes 1572872 | tf_op jit(solution)/shard_map/ppermute | solution.py:19
  346.5 48.0 %collective-permute-start.25 = (bf16[2,4,64,2048]{3,2,1,0:T(8,128)(2,1)}, bf16[2,4,64,2048]{3,2,1,0:T(8,128)(2,1)}, u32[]{:S(2)}, u32[]{:S(2)}) collective-permute-start(bf16[2,4,64,2048]{3,2,1,0:T(8,128)(2,1)} %bitcast.62), channel_id=1, source_target_pairs={{0,1},{1,0},{2,3},{3,2},{4,5},{5,4},{6,7},{7,6},{8,9},{9,8},{10,11... | collective-permute-start | bytes 6291464 | tf_op jit(solution)/shard_map/ppermute | solution.py:259
  350.8 43.8 %collective-permute-start.24 = (bf16[2,16,32,1024]{3,2,1,0:T(8,128)(2,1)}, bf16[2,16,32,1024]{3,2,1,0:T(8,128)(2,1)}, u32[]{:S(2)}, u32[]{:S(2)}) collective-permute-start(bf16[2,16,32,1024]{3,2,1,0:T(8,128)(2,1)} %bitcast.57), channel_id=1, source_target_pairs={{0,16},{16,0},{32,48},{48,32},{64,112},{80,96},{96,80},{112,64},{1... | collective-permute-start | bytes 6291464 | tf_op jit(solution)/shard_map/ppermute | solution.py:259
  354.8 39.7 %collective-permute-start.23 = (bf16[2,4,64,2048]{3,2,1,0:T(8,128)(2,1)}, bf16[2,4,64,2048]{3,2,1,0:T(8,128)(2,1)}, u32[]{:S(2)}, u32[]{:S(2)}) collective-permute-start(bf16[2,4,64,2048]{3,2,1,0:T(8,128)(2,1)} %pad_maximum_fusion.3), channel_id=1, source_target_pairs={{0,4},{1,5},{2,6},{3,7},{4,0},{5,1},{6,2},{7,3},{8,12},{9,13},{10,... | collective-permute-start | bytes 6291464 | tf_op jit(solution)/shard_map/ppermute | solution.py:259
  380.7 12.4 %collective-permute-start.27 = (bf16[512,512]{1,0:T(8,128)(2,1)}, bf16[512,512]{1,0:T(8,128)(2,1)}, u32[]{:S(2)}, u32[]{:S(2)}) collective-permute-start(bf16[512,512]{1,0:T(8,128)(2,1)} %broadcast_select_fusion.2), channel_id=1, source_target_pairs={{0,64},{64,0},{1,65},{65,1},{2,66},{66,2},{3,67},{67,3},{4,68},{68... | collective-permute-start | bytes 1572872 | tf_op jit(solution)/shard_map/ppermute | solution.py:19
  397.3 14.3 %collective-permute-start.30 = (bf16[4,64,2048]{2,1,0:T(8,128)(2,1)}, bf16[4,64,2048]{2,1,0:T(8,128)(2,1)}, u32[]{:S(2)}, u32[]{:S(2)}) collective-permute-start(bf16[4,64,2048]{2,1,0:T(8,128)(2,1)} %fusion.29), channel_id=1, source_target_pairs={{0,3},{1,2},{2,1},{3,0},{4,7},{5,6},{6,5},{7,4},{8,11},{9,10},{10,... | collective-permute-start | bytes 3145736 | tf_op jit(solution)/shard_map/ppermute | solution.py:259
  400.0 14.3 %collective-permute-start.29 = (bf16[16,32,1024]{2,1,0:T(8,128)(2,1)}, bf16[16,32,1024]{2,1,0:T(8,128)(2,1)}, u32[]{:S(2)}, u32[]{:S(2)}) collective-permute-start(bf16[16,32,1024]{2,1,0:T(8,128)(2,1)} %fusion.48), channel_id=1, source_target_pairs={{0,48},{16,32},{32,16},{48,0},{64,80},{80,64},{96,112},{112,96},{1... | collective-permute-start | bytes 3145736 | tf_op jit(solution)/shard_map/ppermute | solution.py:259
  403.1 14.3 %collective-permute-start.28 = (bf16[4,64,2048]{2,1,0:T(8,128)(2,1)}, bf16[4,64,2048]{2,1,0:T(8,128)(2,1)}, u32[]{:S(2)}, u32[]{:S(2)}) collective-permute-start(bf16[4,64,2048]{2,1,0:T(8,128)(2,1)} %fusion.71), channel_id=1, source_target_pairs={{0,12},{1,13},{2,14},{3,15},{4,8},{5,9},{6,10},{7,11},{8,4},{9,5},... | collective-permute-start | bytes 3145736 | tf_op jit(solution)/shard_map/ppermute | solution.py:259
  420.7 24.8 %collective-permute-start.33 = (bf16[2,2,4,32,1024]{4,3,2,1,0:T(8,128)(2,1)}, bf16[2,2,4,32,1024]{4,3,2,1,0:T(8,128)(2,1)}, u32[]{:S(2)}, u32[]{:S(2)}) collective-permute-start(bf16[2,2,4,32,1024]{4,3,2,1,0:T(8,128)(2,1)} %pad_maximum_fusion.7), channel_id=1, source_target_pairs={{0,1},{1,0},{2,3},{3,2},{4,5},{5,4},{6,7},{7,6},{8,9},{9,8},{10,11... | collective-permute-start | bytes 3145736 | tf_op jit(solution)/shard_map/ppermute | solution.py:259
  424.4 27.8 %collective-permute-start.31 = (bf16[2,4,64,2176]{3,2,1,0:T(8,128)(2,1)}, bf16[2,4,64,2176]{3,2,1,0:T(8,128)(2,1)}, u32[]{:S(2)}, u32[]{:S(2)}) collective-permute-start(bf16[2,4,64,2176]{3,2,1,0:T(8,128)(2,1)} %pad_maximum_fusion), channel_id=1, source_target_pairs={{0,4},{1,5},{2,6},{3,7},{4,0},{5,1},{6,2},{7,3},{8,12},{9,13},{10,... | collective-permute-start | bytes 6684680 | tf_op jit(solution)/shard_map/ppermute | solution.py:259
  429.4 16.1 %collective-permute-start.32 = (bf16[2,2,4,16,2048]{4,3,1,2,0:T(8,128)(2,1)}, bf16[2,2,4,16,2048]{4,3,1,2,0:T(8,128)(2,1)}, u32[]{:S(2)}, u32[]{:S(2)}) collective-permute-start(bf16[2,2,4,16,2048]{4,3,1,2,0:T(8,128)(2,1)} %pad_maximum_fusion.6), channel_id=1, source_target_pairs={{0,16},{16,0},{32,48},{48,32},{64,112},{80,96},{96,80},{112,64},{1... | collective-permute-start | bytes 3145736 | tf_op jit(solution)/shard_map/ppermute | solution.py:259
  453.5 12.4 %collective-permute-start.37 = (bf16[2,4,32,1024]{3,2,1,0:T(8,128)(2,1)S(1)}, bf16[2,4,32,1024]{3,2,1,0:T(8,128)(2,1)S(1)}, u32[]{:S(2)}, u32[]{:S(2)}) collective-permute-start(bf16[2,4,32,1024]{3,2,1,0:T(8,128)(2,1)S(1)} %fusion.76), channel_id=1, source_target_pairs={{0,3},{1,2},{2,1},{3,0},{4,7},{5,6},{6,5},{7,4},{8,11},{9,10},{10,... | collective-permute-start | bytes 1572872 | tf_op jit(solution)/shard_map/ppermute | solution.py:259
  456.5 14.7 %collective-permute-start.35 = (bf16[4,64,2176]{2,1,0:T(8,128)(2,1)S(1)}, bf16[4,64,2176]{2,1,0:T(8,128)(2,1)S(1)}, u32[]{:S(2)}, u32[]{:S(2)}) collective-permute-start(bf16[4,64,2176]{2,1,0:T(8,128)(2,1)S(1)} %fusion.66), channel_id=1, source_target_pairs={{0,12},{1,13},{2,14},{3,15},{4,8},{5,9},{6,10},{7,11},{8,4},{9,5},... | collective-permute-start | bytes 3342344 | tf_op jit(solution)/shard_map/ppermute | solution.py:259
  472.4 17.2 %collective-permute-start.42 = (bf16[2,16,2048]{2,1,0:T(8,128)(2,1)S(1)}, bf16[2,16,2048]{2,1,0:T(8,128)(2,1)S(1)}, u32[]{:S(2)}, u32[]{:S(2)}) collective-permute-start(bf16[2,16,2048]{2,1,0:T(8,128)(2,1)S(1)} %pad_maximum_fusion.17), channel_id=1, source_target_pairs={{0,16},{16,0},{32,48},{48,32},{64,112},{80,96},{96,80},{112,64},{1... | collective-permute-start | bytes 393224 | tf_op jit(solution)/shard_map/ppermute | solution.py:259
  474.2 15.3 %collective-permute-start.41 = (bf16[2,2,32,1024]{3,2,1,0:T(8,128)(2,1)S(1)}, bf16[2,2,32,1024]{3,2,1,0:T(8,128)(2,1)S(1)}, u32[]{:S(2)}, u32[]{:S(2)}) collective-permute-start(bf16[2,2,32,1024]{3,2,1,0:T(8,128)(2,1)S(1)} %pad_maximum_fusion.16), channel_id=1, source_target_pairs={{0,4},{1,5},{2,6},{3,7},{4,0},{5,1},{6,2},{7,3},{8,12},{9,13},{10,... | collective-permute-start | bytes 786440 | tf_op jit(solution)/shard_map/ppermute | solution.py:259
  503.6 11.8 %collective-permute-start.50 = (bf16[16,10240]{1,0:T(8,128)(2,1)S(1)}, bf16[16,10240]{1,0:T(8,128)(2,1)S(1)}, u32[]{:S(2)}, u32[]{:S(2)}) collective-permute-start(bf16[16,10240]{1,0:T(8,128)(2,1)S(1)} %fusion.150), channel_id=1, source_target_pairs={{0,16},{16,32},{32,48},{48,0},{1,17},{17,33},{33,49},{49,1},{2,18}... | collective-permute-start | bytes 983048 | tf_op jit(solution)/shard_map/ppermute | solution.py:266
  504.6 18.6 %collective-permute-start.51 = (bf16[16,10240]{1,0:T(8,128)(2,1)S(1)}, bf16[16,10240]{1,0:T(8,128)(2,1)S(1)}, u32[]{:S(2)}, u32[]{:S(2)}) collective-permute-start(bf16[16,10240]{1,0:T(8,128)(2,1)S(1)} %fusion.150), channel_id=1, source_target_pairs={{0,32},{16,48},{32,0},{48,16},{1,33},{17,49},{33,1},{49,17},{2,34}... | collective-permute-start | bytes 983048 | tf_op jit(solution)/shard_map/ppermute | solution.py:266
  505.7 17.4 %collective-permute-start.52 = (bf16[16,10240]{1,0:T(8,128)(2,1)S(1)}, bf16[16,10240]{1,0:T(8,128)(2,1)S(1)}, u32[]{:S(2)}, u32[]{:S(2)}) collective-permute-start(bf16[16,10240]{1,0:T(8,128)(2,1)S(1)} %fusion.150), channel_id=1, source_target_pairs={{0,48},{16,0},{32,16},{48,32},{1,49},{17,1},{33,17},{49,33},{2,50}... | collective-permute-start | bytes 983048 | tf_op jit(solution)/shard_map/ppermute | solution.py:266
  (162 other events, 947.0 us)
Sparse Core Ops, SparseCore 0:
  17.9 83.8 all-gather.2
  104.0 71.8 all-gather.4

commit v9 on v8

--- a/solution.py
+++ b/solution.py
@@ -380,7 +380,7 @@
 
     def arranged(attn, down):
         flat = attn[:, :LANES].reshape(shards, rows, LANES)[:, :vector_rows, :rows].astype(F32)
-        lines = flat[:, :8].transpose(1, 0, 2).reshape(8, model)
+        lines = lax.optimization_barrier(flat[:, :8].transpose(1, 0, 2).reshape(8, model))
         whole = [lines[n : n + 1] for n in range(8)]
         bias_up_part = flat[:, 8:].reshape(shards, 2, unit)
         bias_up_part = choose(bias_up_part[:, 0], bias_up_part[:, 1]).reshape(1, -1)
@@ -411,8 +411,9 @@
         names = ("bias_out", "gain_attn", "shift_attn", "bias_down", "gain_mlp", "shift_mlp")
         lines = [widened(grads["bias_q"]), widened(grads["bias_v"])]
         lines = jnp.concatenate(lines + [0.5 * grads[name] for name in names], axis=0)
+        lines, spread = lax.optimization_barrier((lines, grads["bias_up"]))
         lines = lines.reshape(8, shards, rows).transpose(1, 0, 2)
-        spread = widened(grads["bias_up"].reshape(shards, unit)).reshape(shards, -1, rows)
+        spread = widened(spread.reshape(shards, unit)).reshape(shards, -1, rows)
         return jnp.concatenate([lines, spread], axis=1)
 
     def sides_of(grads):
@@ -433,13 +434,14 @@
     first_weights["down"] = gather_end(c0, cn, cf, "x", 1).reshape(-1, model)
     cn = gather_one(after(c1, cf), "x")
     middle = forward_output(activated, kept0, first_weights)
-    cn, middle, side1 = together(cn, middle, side1)
-    cf = gather_two(c1, cn, "x")
+    middle, side1 = together(middle, side1)
     second_weights = arranged(side1, None)
     packed = forward_packed(middle, second_weights)
+    cn, packed = together(cn, packed)
+    cf = gather_two(c1, cn, "x")
     attended, kept1 = forward_attention(middle, packed, seq_lengths)
-    cf, attended = together(cf, attended)
     activated = forward_hidden(attended, kept1, second_weights)
+    cf, activated = together(cf, activated)
     second_weights["down"] = gather_end(c1, cn, cf, "x", 1).reshape(-1, model)
     last = forward_output(activated, kept1, second_weights)
 

time: 560 us -> 516 us (0.921)
  local copies, waits for them, and re-layouts: 88.8 us -> 56.1 us
  other arithmetic: 84.5 us -> 74.6 us
  waiting for transfers between devices: 168 us -> 174 us
    mul x16 -> x0, local copies, waits for them, and re-layouts: 12.6 us -> none  [the longest x12 11.6 us: vectors_of(): 0.5 * grads[name]]
    another operation x16 -> x2, other arithmetic: 9.92 us -> 0.1 us
    select_n x10, local copies, waits for them, and re-layouts: 10.8 us -> 1.72 us  [choose(): return jnp.where(first, low, high)]
    ppermute x30, waiting for transfers between devices: 66.9 us -> 72.8 us  [trade(): return lax.ppermute(value, ('section', name), route)]
    unnamed x290 -> x268, local copies, waits for them, and re-layouts: 16.1 us -> 12.9 us
    select_n x22 -> x23, other arithmetic: 16.7 us -> 17.9 us  [choose(): return jnp.where(first, low, high)]
  transfers between devices with their start and end apart: 59 -> 59, of which waited for: 21 -> 27; matrix products, arithmetic and copies ran while one was open for 36% -> 31% of each run, Pallas kernels for 6% -> 7%
where the time goes in v9:
time: 516 us; the launch traced here: 507 us
  waiting for transfers between devices  174 us (34%)
  matrix products  85 us (16%)
  other arithmetic  74.6 us (14%)
  starting transfers between devices  67.4 us (13%)
  local copies, waits for them, and re-layouts  56.1 us (11%)
  Pallas kernels  33.2 us (6%)
  between operations  17 us (3%)
    all_gather x2, waiting for transfers between devices, whole(): return lax.all_gather(block, 'shard', axis=0, tiled=True)  84 us
    ppermute x30, waiting for transfers between devices, trade(): return lax.ppermute(value, ('section', name), route)  72.8 us
    ppermute x30, starting transfers between devices, trade(): return lax.ppermute(value, ('section', name), route)  34.5 us
    pallas_call x4, Pallas kernels, attention_call(): pl.pallas_call(kernel, out_shape=jax.ShapeDtypeStruct((rows, width), BF),...  33.2 us
    ppermute x21, starting transfers between devices, swap(): return lax.ppermute(value, 'section', [(0, 1), (1, 0)])  27.3 us
    dot_general x8, matrix products, dot(): return jnp.dot(left, right, preferred_element_type=F32)  27.3 us
    dot_general x12, matrix products, transpose_dot(): lax.dot_general(left, right, (((0,), (0,)), ((), ())), preferred_element_...  25.6 us
    dot_general x8, matrix products, dot_transposed(): lax.dot_general(left, right, (((1,), (1,)), ((), ())), preferred_element_...  23.9 us
  transfers between devices with their start and end apart: 59, of which 27 were waited for; matrix products, arithmetic and copies ran while one was open for 31% of the time, Pallas kernels for 7%

profile of v9, /device:TPU:1, one launch (start us, length us, event | category | flops | bytes accessed | tf_op | source)
XLA Modules:
  0.0 507.1 jit_solution(5812857695111967266)
XLA Ops:
  17.9 84.0 %all-gather.3.cloned.1.call-done = bf16[1024,5248]{1,0:T(8,128)(2,1)} async-done(((bf16[64,5248]{1,0:T(8,128)(2,1)}), bf16[1024,5248]{1,0:T(8,128)(2,1)}) %all-gather.3.cloned.1.call-update) | async-done | bytes 10747920 | tf_op jit(solution)/shard_map/all_gather | solution.py:372
  112.7 4.6 fusion.32.packed_ref
  122.0 7.1 %shard_map.271 = bf16[256,512]{1,0:T(8,128)(2,1)} custom-call(s32[2]{0:T(128)} %bitcast.545, bf16[256,1536]{1,0:T(8,128)(2,1)} %fusion.32.packed_ref), custom_call_target="tpu_custom_call" | custom-call | flops 67108864 | bytes 524288 | tf_op jit(solution)/shard_map/pallas_call | solution.py:121
  134.4 5.2 %multiply_convert_fusion.1 = (bf16[256,2048]{1,0:T(8,128)(2,1)S(1)}, f32[256,2048]{1,0:T(8,128)}) fusion(f32[2048]{0:T(1024)S(1)} %bitcast.542, bf16[256,1024]{1,0:T(8,128)(2,1)S(1)} %add_convert_fusion.9, bf16[1024,5248]{1,0:T(8,128)(2,1)} %all-gather.3.cloned.1.call-done), kind=kOutput, calls=%fused_computation.90 | convolution fusion | flops 1076887552 | bytes 7872512 | tf_op jit(solution)/shard_map/dot_general | solution.py:29
  139.5 17.6 %collective-permute-done.8 = bf16[2,16,32,1024]{3,2,1,0:T(8,128)(2,1)S(1)} collective-permute-done((bf16[2,16,32,1024]{3,2,1,0:T(8,128)(2,1)S(1)}, bf16[2,16,32,1024]{3,2,1,0:T(8,128)(2,1)S(1)}, u32[]{:S(2)}, u32[]{:S(2)}) %collective-permute-start.8) | collective-permute-done | bytes 2097184 | tf_op jit(solution)/shard_map/ppermute | solution.py:259
  179.5 3.9 fusion.22.packed_ref
  188.5 7.1 %shard_map.272 = bf16[256,512]{1,0:T(8,128)(2,1)} custom-call(s32[2]{0:T(128)} %bitcast.546, bf16[256,1536]{1,0:T(8,128)(2,1)} %fusion.22.packed_ref), custom_call_target="tpu_custom_call" | custom-call | flops 67108864 | bytes 524288 | tf_op jit(solution)/shard_map/pallas_call | solution.py:121
  198.0 3.4 collective-permute-start.12
  206.1 5.0 multiply_convert_fusion
  218.6 4.3 convolution_convert_fusion.10
  237.2 4.6 convert_reduce_fusion
  241.8 3.9 fusion.60
  262.4 9.4 %shard_map.273 = bf16[256,1536]{1,0:T(8,128)(2,1)} custom-call(s32[2]{0:T(128)} %bitcast.547, bf16[256,1536]{1,0:T(8,128)(2,1)} %fusion.22.packed_ref, bf16[256,512]{1,0:T(8,128)(2,1)} %convolution_convert_fusion.13.grad_ref), custom_call_target="tpu_custom_call" | custom-call | flops 201326592 | bytes 1572864 | tf_op jit(solution)/shard_map/pallas_call | solution.py:121
  274.4 4.6 collective-permute-done.15
  279.0 3.7 fusion.54
  293.6 8.0 %maximum_maximum_fusion = bf16[1024,2048]{1,0:T(8,128)(2,1)S(1)} fusion(bf16[512,512]{1,0:T(8,128)(2,1)S(1)} %copy-done.49, bf16[512,512]{1,0:T(8,128)(2,1)S(1)} %copy-done.48, bf16[1024,1536]{1,0:T(8,128)(2,1)S(1)} %convolution_convert_fusion.1), kind=kLoop, calls=%fused_computation | loop fusion | flops 12582912 | bytes 8388608 | tf_op jit(solution)/shard_map/dynamic_update_slice | solution.py:323
  309.5 3.9 fusion.63
  313.4 4.0 collective-permute-start.22
  325.9 3.1 fusion.45
  329.1 3.1 add_convert_fusion.1
  336.9 9.6 %shard_map.274 = bf16[256,1536]{1,0:T(8,128)(2,1)} custom-call(s32[2]{0:T(128)} %bitcast.548, bf16[256,1536]{1,0:T(8,128)(2,1)} %fusion.32.packed_ref, bf16[256,512]{1,0:T(8,128)(2,1)} %convolution_convert_fusion.12.grad_ref), custom_call_target="tpu_custom_call" | custom-call | flops 201326592 | bytes 1572864 | tf_op jit(solution)/shard_map/pallas_call | solution.py:121
  357.5 3.0 fusion.71
  363.6 5.3 %collective-permute-done.30 = bf16[4,64,2048]{2,1,0:T(8,128)(2,1)} collective-permute-done((bf16[4,64,2048]{2,1,0:T(8,128)(2,1)}, bf16[4,64,2048]{2,1,0:T(8,128)(2,1)}, u32[]{:S(2)}, u32[]{:S(2)}) %collective-permute-start.30) | collective-permute-done | bytes 1048608 | tf_op jit(solution)/shard_map/ppermute | solution.py:259
  371.7 2.9 collective-permute-done.28
  395.2 9.1 %collective-permute-done.34 = bf16[2,64,2048]{2,1,0:T(8,128)(2,1)} collective-permute-done((bf16[2,64,2048]{2,1,0:T(8,128)(2,1)}, bf16[2,64,2048]{2,1,0:T(8,128)(2,1)}, u32[]{:S(2)}, u32[]{:S(2)}) %collective-permute-start.34) | collective-permute-done | bytes 524320 | tf_op jit(solution)/shard_map/ppermute | solution.py:259
  404.3 5.0 collective-permute-done.31
  418.9 3.9 collective-permute-done.38
  423.1 5.0 collective-permute-done.35
  462.8 3.8 collective-permute-done.47
  467.2 4.0 collective-permute-done.50
  471.2 7.2 %collective-permute-done.51 = bf16[16,10240]{1,0:T(8,128)(2,1)S(1)} collective-permute-done((bf16[16,10240]{1,0:T(8,128)(2,1)S(1)}, bf16[16,10240]{1,0:T(8,128)(2,1)S(1)}, u32[]{:S(2)}, u32[]{:S(2)}) %collective-permute-start.51) | collective-permute-done | bytes 327712 | tf_op jit(solution)/shard_map/ppermute | solution.py:266
  479.6 8.6 %collective-permute-start.54 = (bf16[12,128]{1,0:T(8,128)(2,1)S(1)}, bf16[12,128]{1,0:T(8,128)(2,1)S(1)}, u32[]{:S(2)}, u32[]{:S(2)}) collective-permute-start(bf16[12,128]{1,0:T(8,128)(2,1)S(1)} %slice.540), channel_id=1, source_target_pairs={{0,64},{64,0},{1,65},{65,1},{2,66},{66,2},{3,67},{67,3},{4,68},{68... | collective-permute-start | bytes 9224 | tf_op jit(solution)/shard_map/ppermute | solution.py:19
  (629 shorter events, 232.2 us)
Async XLA Ops:
  7.3 94.6 %all-gather.3.cloned.1.call-start = ((), (), s32[]{:S(2)}) async-start(), calls=%async_computation | async-start | bytes 11419648 | tf_op jit(solution)/shard_map/all_gather | solution.py:372
  17.8 158.3 %all-gather.5.cloned.1.call-start = ((), (), s32[]{:S(2)}) async-start(), calls=%async_computation.1 | async-start | bytes 9191424 | tf_op jit(solution)/shard_map/all_gather | solution.py:372
  106.5 15.5 %collective-permute-start.5 = (bf16[16,32,1024]{2,1,0:T(8,128)(2,1)}, bf16[16,32,1024]{2,1,0:T(8,128)(2,1)S(1)}, u32[]{:S(2)}, u32[]{:S(2)}) collective-permute-start(bf16[16,32,1024]{2,1,0:T(8,128)(2,1)} %reshape.557), channel_id=1, source_target_pairs={{0,16},{16,0},{32,48},{48,32},{64,112},{80,96},{96,80},{112,64},{1... | collective-permute-start | bytes 3145736 | tf_op jit(solution)/shard_map/ppermute | solution.py:259
  131.3 25.8 %collective-permute-start.8 = (bf16[2,16,32,1024]{3,2,1,0:T(8,128)(2,1)S(1)}, bf16[2,16,32,1024]{3,2,1,0:T(8,128)(2,1)S(1)}, u32[]{:S(2)}, u32[]{:S(2)}) collective-permute-start(bf16[2,16,32,1024]{3,2,1,0:T(8,128)(2,1)S(1)} %pad_maximum_fusion.1), channel_id=1, source_target_pairs={{0,48},{16,32},{32,16},{48,0},{64,80},{80,64},{96,112},{112,96},{1... | collective-permute-start | bytes 6291464 | tf_op jit(solution)/shard_map/ppermute | solution.py:259
  159.6 14.2 %collective-permute-start.9 = (bf16[256,1024]{1,0:T(8,128)(2,1)}, bf16[256,1024]{1,0:T(8,128)(2,1)}, u32[]{:S(2)}, u32[]{:S(2)}) collective-permute-start(bf16[256,1024]{1,0:T(8,128)(2,1)} %convolution_convert_fusion.11), channel_id=1, source_target_pairs={{0,64},{64,0},{1,65},{65,1},{2,66},{66,2},{3,67},{67,3},{4,68},{68... | collective-permute-start | bytes 1572872 | tf_op jit(solution)/shard_map/ppermute | solution.py:19
  170.2 15.3 %collective-permute-start.10 = (bf16[16,32,1024]{2,1,0:T(8,128)(2,1)}, bf16[16,32,1024]{2,1,0:T(8,128)(2,1)}, u32[]{:S(2)}, u32[]{:S(2)}) collective-permute-start(bf16[16,32,1024]{2,1,0:T(8,128)(2,1)} %reshape.562), channel_id=1, source_target_pairs={{0,16},{16,0},{32,48},{48,32},{64,112},{80,96},{96,80},{112,64},{1... | collective-permute-start | bytes 3145736 | tf_op jit(solution)/shard_map/ppermute | solution.py:259
  185.5 10.7 %collective-permute-start.11 = (bf16[512,512]{1,0:T(8,128)(2,1)}, bf16[512,512]{1,0:T(8,128)(2,1)S(1)}, u32[]{:S(2)}, u32[]{:S(2)}) collective-permute-start(bf16[512,512]{1,0:T(8,128)(2,1)} %broadcast_select_fusion.10), channel_id=1, source_target_pairs={{0,64},{64,0},{1,65},{65,1},{2,66},{66,2},{3,67},{67,3},{4,68},{68... | collective-permute-start | bytes 1572872 | tf_op jit(solution)/shard_map/ppermute | solution.py:19
  188.4 25.6 %collective-permute-start.13 = (bf16[2,16,32,1024]{3,2,1,0:T(8,128)(2,1)}, bf16[2,16,32,1024]{3,2,1,0:T(8,128)(2,1)}, u32[]{:S(2)}, u32[]{:S(2)}) collective-permute-start(bf16[2,16,32,1024]{3,2,1,0:T(8,128)(2,1)} %pad_maximum_fusion.2), channel_id=1, source_target_pairs={{0,48},{16,32},{32,16},{48,0},{64,80},{80,64},{96,112},{112,96},{1... | collective-permute-start | bytes 6291464 | tf_op jit(solution)/shard_map/ppermute | solution.py:259
  245.7 10.6 %collective-permute-start.17 = (bf16[256,1024]{1,0:T(8,128)(2,1)S(1)}, bf16[256,1024]{1,0:T(8,128)(2,1)S(1)}, u32[]{:S(2)}, u32[]{:S(2)}) collective-permute-start(bf16[256,1024]{1,0:T(8,128)(2,1)S(1)} %fusion.60), channel_id=1, source_target_pairs={{0,64},{64,0},{1,65},{65,1},{2,66},{66,2},{3,67},{67,3},{4,68},{68... | collective-permute-start | bytes 1572872 | tf_op jit(solution)/shard_map/ppermute | solution.py:19
  247.9 26.5 %collective-permute-start.16 = (bf16[2,4,64,2048]{3,2,1,0:T(8,128)(2,1)}, bf16[2,4,64,2048]{3,2,1,0:T(8,128)(2,1)}, u32[]{:S(2)}, u32[]{:S(2)}) collective-permute-start(bf16[2,4,64,2048]{3,2,1,0:T(8,128)(2,1)} %bitcast.55), channel_id=1, source_target_pairs={{0,1},{1,0},{2,3},{3,2},{4,5},{5,4},{6,7},{7,6},{8,9},{9,8},{10,11... | collective-permute-start | bytes 6291464 | tf_op jit(solution)/shard_map/ppermute | solution.py:259
  252.4 26.6 %collective-permute-start.15 = (bf16[2,16,32,1024]{3,2,1,0:T(8,128)(2,1)}, bf16[2,16,32,1024]{3,2,1,0:T(8,128)(2,1)}, u32[]{:S(2)}, u32[]{:S(2)}) collective-permute-start(bf16[2,16,32,1024]{3,2,1,0:T(8,128)(2,1)} %bitcast.50), channel_id=1, source_target_pairs={{0,16},{16,0},{32,48},{48,32},{64,112},{80,96},{96,80},{112,64},{1... | collective-permute-start | bytes 6291464 | tf_op jit(solution)/shard_map/ppermute | solution.py:259
  261.2 10.7 %collective-permute-start.18 = (bf16[512,512]{1,0:T(8,128)(2,1)}, bf16[512,512]{1,0:T(8,128)(2,1)}, u32[]{:S(2)}, u32[]{:S(2)}) collective-permute-start(bf16[512,512]{1,0:T(8,128)(2,1)} %broadcast_select_fusion.6), channel_id=1, source_target_pairs={{0,64},{64,0},{1,65},{65,1},{2,66},{66,2},{3,67},{67,3},{4,68},{68... | collective-permute-start | bytes 1572872 | tf_op jit(solution)/shard_map/ppermute | solution.py:19
  282.9 18.8 %collective-permute-start.21 = (bf16[256,1024]{1,0:T(8,128)(2,1)}, bf16[256,1024]{1,0:T(8,128)(2,1)}, u32[]{:S(2)}, u32[]{:S(2)}) collective-permute-start(bf16[256,1024]{1,0:T(8,128)(2,1)} %fusion.54), channel_id=1, source_target_pairs={{0,64},{64,0},{1,65},{65,1},{2,66},{66,2},{3,67},{67,3},{4,68},{68... | collective-permute-start | bytes 1572872 | tf_op jit(solution)/shard_map/ppermute | solution.py:19
  285.6 18.5 %collective-permute-start.20 = (bf16[4,64,2048]{2,1,0:T(8,128)(2,1)}, bf16[4,64,2048]{2,1,0:T(8,128)(2,1)}, u32[]{:S(2)}, u32[]{:S(2)}) collective-permute-start(bf16[4,64,2048]{2,1,0:T(8,128)(2,1)} %fusion.28), channel_id=1, source_target_pairs={{0,3},{1,2},{2,1},{3,0},{4,7},{5,6},{6,5},{7,4},{8,11},{9,10},{10,... | collective-permute-start | bytes 3145736 | tf_op jit(solution)/shard_map/ppermute | solution.py:259
  288.5 15.7 %collective-permute-start.19 = (bf16[16,32,1024]{2,1,0:T(8,128)(2,1)}, bf16[16,32,1024]{2,1,0:T(8,128)(2,1)}, u32[]{:S(2)}, u32[]{:S(2)}) collective-permute-start(bf16[16,32,1024]{2,1,0:T(8,128)(2,1)} %fusion.49), channel_id=1, source_target_pairs={{0,48},{16,32},{32,16},{48,0},{64,80},{80,64},{96,112},{112,96},{1... | collective-permute-start | bytes 3145736 | tf_op jit(solution)/shard_map/ppermute | solution.py:259
  313.4 18.8 %collective-permute-start.22 = (bf16[256,1024]{1,0:T(8,128)(2,1)S(1)}, bf16[256,1024]{1,0:T(8,128)(2,1)S(1)}, u32[]{:S(2)}, u32[]{:S(2)}) collective-permute-start(bf16[256,1024]{1,0:T(8,128)(2,1)S(1)} %fusion.63), channel_id=1, source_target_pairs={{0,64},{64,0},{1,65},{65,1},{2,66},{66,2},{3,67},{67,3},{4,68},{68... | collective-permute-start | bytes 1572872 | tf_op jit(solution)/shard_map/ppermute | solution.py:19
  319.5 29.1 %collective-permute-start.25 = (bf16[2,4,64,2048]{3,2,1,0:T(8,128)(2,1)}, bf16[2,4,64,2048]{3,2,1,0:T(8,128)(2,1)}, u32[]{:S(2)}, u32[]{:S(2)}) collective-permute-start(bf16[2,4,64,2048]{3,2,1,0:T(8,128)(2,1)} %bitcast.74), channel_id=1, source_target_pairs={{0,1},{1,0},{2,3},{3,2},{4,5},{5,4},{6,7},{7,6},{8,9},{9,8},{10,11... | collective-permute-start | bytes 6291464 | tf_op jit(solution)/shard_map/ppermute | solution.py:259
  323.7 26.4 %collective-permute-start.24 = (bf16[2,16,32,1024]{3,2,1,0:T(8,128)(2,1)}, bf16[2,16,32,1024]{3,2,1,0:T(8,128)(2,1)}, u32[]{:S(2)}, u32[]{:S(2)}) collective-permute-start(bf16[2,16,32,1024]{3,2,1,0:T(8,128)(2,1)} %bitcast.69), channel_id=1, source_target_pairs={{0,16},{16,0},{32,48},{48,32},{64,112},{80,96},{96,80},{112,64},{1... | collective-permute-start | bytes 6291464 | tf_op jit(solution)/shard_map/ppermute | solution.py:259
  325.5 26.6 %collective-permute-start.23 = (bf16[2,4,64,2048]{3,2,1,0:T(8,128)(2,1)}, bf16[2,4,64,2048]{3,2,1,0:T(8,128)(2,1)}, u32[]{:S(2)}, u32[]{:S(2)}) collective-permute-start(bf16[2,4,64,2048]{3,2,1,0:T(8,128)(2,1)} %pad_maximum_fusion.3), channel_id=1, source_target_pairs={{0,4},{1,5},{2,6},{3,7},{4,0},{5,1},{6,2},{7,3},{8,12},{9,13},{10,... | collective-permute-start | bytes 6291464 | tf_op jit(solution)/shard_map/ppermute | solution.py:259
  335.6 10.8 %collective-permute-start.27 = (bf16[512,512]{1,0:T(8,128)(2,1)}, bf16[512,512]{1,0:T(8,128)(2,1)}, u32[]{:S(2)}, u32[]{:S(2)}) collective-permute-start(bf16[512,512]{1,0:T(8,128)(2,1)} %broadcast_select_fusion.2), channel_id=1, source_target_pairs={{0,64},{64,0},{1,65},{65,1},{2,66},{66,2},{3,67},{67,3},{4,68},{68... | collective-permute-start | bytes 1572872 | tf_op jit(solution)/shard_map/ppermute | solution.py:19
  354.7 14.3 %collective-permute-start.30 = (bf16[4,64,2048]{2,1,0:T(8,128)(2,1)}, bf16[4,64,2048]{2,1,0:T(8,128)(2,1)}, u32[]{:S(2)}, u32[]{:S(2)}) collective-permute-start(bf16[4,64,2048]{2,1,0:T(8,128)(2,1)} %fusion.29), channel_id=1, source_target_pairs={{0,3},{1,2},{2,1},{3,0},{4,7},{5,6},{6,5},{7,4},{8,11},{9,10},{10,... | collective-permute-start | bytes 3145736 | tf_op jit(solution)/shard_map/ppermute | solution.py:259
  357.4 14.3 %collective-permute-start.29 = (bf16[16,32,1024]{2,1,0:T(8,128)(2,1)}, bf16[16,32,1024]{2,1,0:T(8,128)(2,1)}, u32[]{:S(2)}, u32[]{:S(2)}) collective-permute-start(bf16[16,32,1024]{2,1,0:T(8,128)(2,1)} %fusion.48), channel_id=1, source_target_pairs={{0,48},{16,32},{32,16},{48,0},{64,80},{80,64},{96,112},{112,96},{1... | collective-permute-start | bytes 3145736 | tf_op jit(solution)/shard_map/ppermute | solution.py:259
  360.5 14.2 %collective-permute-start.28 = (bf16[4,64,2048]{2,1,0:T(8,128)(2,1)}, bf16[4,64,2048]{2,1,0:T(8,128)(2,1)S(1)}, u32[]{:S(2)}, u32[]{:S(2)}) collective-permute-start(bf16[4,64,2048]{2,1,0:T(8,128)(2,1)} %fusion.71), channel_id=1, source_target_pairs={{0,12},{1,13},{2,14},{3,15},{4,8},{5,9},{6,10},{7,11},{8,4},{9,5},... | collective-permute-start | bytes 3145736 | tf_op jit(solution)/shard_map/ppermute | solution.py:259
  378.9 25.4 %collective-permute-start.33 = (bf16[2,2,4,32,1024]{4,3,2,1,0:T(8,128)(2,1)}, bf16[2,2,4,32,1024]{4,3,2,1,0:T(8,128)(2,1)}, u32[]{:S(2)}, u32[]{:S(2)}) collective-permute-start(bf16[2,2,4,32,1024]{4,3,2,1,0:T(8,128)(2,1)} %pad_maximum_fusion.7), channel_id=1, source_target_pairs={{0,1},{1,0},{2,3},{3,2},{4,5},{5,4},{6,7},{7,6},{8,9},{9,8},{10,11... | collective-permute-start | bytes 3145736 | tf_op jit(solution)/shard_map/ppermute | solution.py:259
  381.5 27.8 %collective-permute-start.31 = (bf16[2,4,64,2176]{3,2,1,0:T(8,128)(2,1)}, bf16[2,4,64,2176]{3,2,1,0:T(8,128)(2,1)}, u32[]{:S(2)}, u32[]{:S(2)}) collective-permute-start(bf16[2,4,64,2176]{3,2,1,0:T(8,128)(2,1)} %pad_maximum_fusion), channel_id=1, source_target_pairs={{0,4},{1,5},{2,6},{3,7},{4,0},{5,1},{6,2},{7,3},{8,12},{9,13},{10,... | collective-permute-start | bytes 6684680 | tf_op jit(solution)/shard_map/ppermute | solution.py:259
  388.1 16.2 %collective-permute-start.32 = (bf16[2,2,4,16,2048]{4,3,1,2,0:T(8,128)(2,1)}, bf16[2,2,4,16,2048]{4,3,1,2,0:T(8,128)(2,1)}, u32[]{:S(2)}, u32[]{:S(2)}) collective-permute-start(bf16[2,2,4,16,2048]{4,3,1,2,0:T(8,128)(2,1)} %pad_maximum_fusion.6), channel_id=1, source_target_pairs={{0,16},{16,0},{32,48},{48,32},{64,112},{80,96},{96,80},{112,64},{1... | collective-permute-start | bytes 3145736 | tf_op jit(solution)/shard_map/ppermute | solution.py:259
  410.6 12.2 %collective-permute-start.37 = (bf16[2,4,32,1024]{3,2,1,0:T(8,128)(2,1)S(1)}, bf16[2,4,32,1024]{3,2,1,0:T(8,128)(2,1)S(1)}, u32[]{:S(2)}, u32[]{:S(2)}) collective-permute-start(bf16[2,4,32,1024]{3,2,1,0:T(8,128)(2,1)S(1)} %fusion.76), channel_id=1, source_target_pairs={{0,3},{1,2},{2,1},{3,0},{4,7},{5,6},{6,5},{7,4},{8,11},{9,10},{10,... | collective-permute-start | bytes 1572872 | tf_op jit(solution)/shard_map/ppermute | solution.py:259
  413.4 14.7 %collective-permute-start.35 = (bf16[4,64,2176]{2,1,0:T(8,128)(2,1)S(1)}, bf16[4,64,2176]{2,1,0:T(8,128)(2,1)S(1)}, u32[]{:S(2)}, u32[]{:S(2)}) collective-permute-start(bf16[4,64,2176]{2,1,0:T(8,128)(2,1)S(1)} %fusion.66), channel_id=1, source_target_pairs={{0,12},{1,13},{2,14},{3,15},{4,8},{5,9},{6,10},{7,11},{8,4},{9,5},... | collective-permute-start | bytes 3342344 | tf_op jit(solution)/shard_map/ppermute | solution.py:259
  429.3 18.1 %collective-permute-start.42 = (bf16[2,16,2048]{2,1,0:T(8,128)(2,1)S(1)}, bf16[2,16,2048]{2,1,0:T(8,128)(2,1)S(1)}, u32[]{:S(2)}, u32[]{:S(2)}) collective-permute-start(bf16[2,16,2048]{2,1,0:T(8,128)(2,1)S(1)} %pad_maximum_fusion.17), channel_id=1, source_target_pairs={{0,16},{16,0},{32,48},{48,32},{64,112},{80,96},{96,80},{112,64},{1... | collective-permute-start | bytes 393224 | tf_op jit(solution)/shard_map/ppermute | solution.py:259
  433.4 14.0 %collective-permute-start.41 = (bf16[2,2,32,1024]{3,2,1,0:T(8,128)(2,1)S(1)}, bf16[2,2,32,1024]{3,2,1,0:T(8,128)(2,1)S(1)}, u32[]{:S(2)}, u32[]{:S(2)}) collective-permute-start(bf16[2,2,32,1024]{3,2,1,0:T(8,128)(2,1)S(1)} %pad_maximum_fusion.16), channel_id=1, source_target_pairs={{0,4},{1,5},{2,6},{3,7},{4,0},{5,1},{6,2},{7,3},{8,12},{9,13},{10,... | collective-permute-start | bytes 786440 | tf_op jit(solution)/shard_map/ppermute | solution.py:259
  461.3 17.1 %collective-permute-start.51 = (bf16[16,10240]{1,0:T(8,128)(2,1)S(1)}, bf16[16,10240]{1,0:T(8,128)(2,1)S(1)}, u32[]{:S(2)}, u32[]{:S(2)}) collective-permute-start(bf16[16,10240]{1,0:T(8,128)(2,1)S(1)} %fusion.150), channel_id=1, source_target_pairs={{0,32},{16,48},{32,0},{48,16},{1,33},{17,49},{33,1},{49,17},{2,34}... | collective-permute-start | bytes 983048 | tf_op jit(solution)/shard_map/ppermute | solution.py:266
  466.6 12.9 %collective-permute-start.52 = (bf16[16,10240]{1,0:T(8,128)(2,1)S(1)}, bf16[16,10240]{1,0:T(8,128)(2,1)S(1)}, u32[]{:S(2)}, u32[]{:S(2)}) collective-permute-start(bf16[16,10240]{1,0:T(8,128)(2,1)S(1)} %fusion.150), channel_id=1, source_target_pairs={{0,48},{16,0},{32,16},{48,32},{1,49},{17,1},{33,17},{49,33},{2,50}... | collective-permute-start | bytes 983048 | tf_op jit(solution)/shard_map/ppermute | solution.py:266
  (158 other events, 1051.2 us)
Sparse Core Ops, SparseCore 0:
  17.9 83.8 all-gather.2
  104.0 71.6 all-gather.4

commit v10 on v9

--- a/solution.py
+++ b/solution.py
@@ -455,7 +455,7 @@
         return products(left.reshape(RING, -1, RING * rows), grads["upward"], (RING, rows, shards * unit))
 
     def side_by_side(pieces, ends):
-        joined = placed(ends[-1], list(zip((0,) + ends, pieces)))
+        joined = placed(ends[-1], list(zip((0,) + ends, lax.optimization_barrier(pieces))))
         return joined.reshape(RING, RING, rows, -1)
 
     grad_hidden, grads1 = backward_mlp(cotangent.reshape(-1, model), kept1, second_weights)

time: 516 us -> 526 us (1.019)
  local copies, waits for them, and re-layouts: 56.1 us -> 70.9 us
  waiting for transfers between devices: 174 us -> 163 us
    ppermute x30, waiting for transfers between devices: 72.8 us -> 56.9 us  [trade(): return lax.ppermute(value, ('section', name), route)]
    unnamed x268 -> x256, local copies, waits for them, and re-layouts: 12.9 us -> 14.6 us
  transfers between devices with their start and end apart: 59 -> 59, of which waited for: 27 -> 18; matrix products, arithmetic and copies ran while one was open for 31% -> 35% of each run, Pallas kernels for 7% -> 6%
where the time goes in v10:
time: 526 us; the launch traced here: 517 us
  waiting for transfers between devices  163 us (31%)
  matrix products  86.9 us (17%)
  other arithmetic  78.2 us (15%)
  local copies, waits for them, and re-layouts  70.9 us (13%)
  starting transfers between devices  68.1 us (13%)
  Pallas kernels  33.1 us (6%)
  between operations  16.8 us (3%)
    all_gather x2, waiting for transfers between devices, whole(): return lax.all_gather(block, 'shard', axis=0, tiled=True)  84 us
    ppermute x30, waiting for transfers between devices, trade(): return lax.ppermute(value, ('section', name), route)  56.9 us
    ppermute x30, starting transfers between devices, trade(): return lax.ppermute(value, ('section', name), route)  34 us
    pallas_call x4, Pallas kernels, attention_call(): pl.pallas_call(kernel, out_shape=jax.ShapeDtypeStruct((rows, width), BF),...  33.1 us
    ppermute x21, starting transfers between devices, swap(): return lax.ppermute(value, 'section', [(0, 1), (1, 0)])  28.8 us
    dot_general x12, matrix products, transpose_dot(): lax.dot_general(left, right, (((0,), (0,)), ((), ())), preferred_element_...  27.4 us
    dot_general x8, matrix products, dot(): return jnp.dot(left, right, preferred_element_type=F32)  27.1 us
    dot_general x8, matrix products, dot_transposed(): lax.dot_general(left, right, (((1,), (1,)), ((), ())), preferred_element_...  24.1 us
  transfers between devices with their start and end apart: 59, of which 18 were waited for; matrix products, arithmetic and copies ran while one was open for 35% of the time, Pallas kernels for 6%

profile of v10, /device:TPU:1, one launch (start us, length us, event | category | flops | bytes accessed | tf_op | source)
XLA Modules:
  0.0 516.7 jit_solution(3600666371790131203)
XLA Ops:
  19.2 84.0 %all-gather.3.cloned.1.call-done = bf16[1024,5248]{1,0:T(8,128)(2,1)} async-done(((bf16[64,5248]{1,0:T(8,128)(2,1)}), bf16[1024,5248]{1,0:T(8,128)(2,1)}) %all-gather.3.cloned.1.call-update) | async-done | bytes 10747920 | tf_op jit(solution)/shard_map/all_gather | solution.py:372
  113.4 4.5 fusion.31.packed_ref
  120.2 3.2 collective-permute-done.5
  123.4 7.1 %shard_map.271 = bf16[256,512]{1,0:T(8,128)(2,1)} custom-call(s32[2]{0:T(128)} %bitcast.543, bf16[256,1536]{1,0:T(8,128)(2,1)} %fusion.31.packed_ref), custom_call_target="tpu_custom_call" | custom-call | flops 67108864 | bytes 524288 | tf_op jit(solution)/shard_map/pallas_call | solution.py:121
  135.7 5.2 %multiply_convert_fusion.1 = (bf16[256,2048]{1,0:T(8,128)(2,1)S(1)}, f32[256,2048]{1,0:T(8,128)}) fusion(f32[2048]{0:T(1024)S(1)} %bitcast.540, bf16[256,1024]{1,0:T(8,128)(2,1)S(1)} %add_convert_fusion.9, bf16[1024,5248]{1,0:T(8,128)(2,1)} %all-gather.3.cloned.1.call-done), kind=kOutput, calls=%fused_computation.89 | convolution fusion | flops 1076887552 | bytes 7872512 | tf_op jit(solution)/shard_map/dot_general | solution.py:29
  140.9 17.6 %collective-permute-done.8 = bf16[2,16,32,1024]{3,2,1,0:T(8,128)(2,1)S(1)} collective-permute-done((bf16[2,16,32,1024]{3,2,1,0:T(8,128)(2,1)S(1)}, bf16[2,16,32,1024]{3,2,1,0:T(8,128)(2,1)S(1)}, u32[]{:S(2)}, u32[]{:S(2)}) %collective-permute-start.8) | collective-permute-done | bytes 2097184 | tf_op jit(solution)/shard_map/ppermute | solution.py:259
  180.7 3.8 fusion.21.packed_ref
  189.6 7.1 %shard_map.272 = bf16[256,512]{1,0:T(8,128)(2,1)} custom-call(s32[2]{0:T(128)} %bitcast.544, bf16[256,1536]{1,0:T(8,128)(2,1)} %fusion.21.packed_ref), custom_call_target="tpu_custom_call" | custom-call | flops 67108864 | bytes 524288 | tf_op jit(solution)/shard_map/pallas_call | solution.py:121
  199.2 3.4 collective-permute-start.12
  207.3 5.0 multiply_convert_fusion
  219.6 4.3 convolution_convert_fusion.10
  242.0 4.6 convert_reduce_fusion
  246.6 3.9 fusion.59
  262.6 9.5 %shard_map.273 = bf16[256,1536]{1,0:T(8,128)(2,1)} custom-call(s32[2]{0:T(128)} %bitcast.545, bf16[256,1536]{1,0:T(8,128)(2,1)} %fusion.21.packed_ref, bf16[256,512]{1,0:T(8,128)(2,1)} %convolution_convert_fusion.13.grad_ref), custom_call_target="tpu_custom_call" | custom-call | flops 201326592 | bytes 1572864 | tf_op jit(solution)/shard_map/pallas_call | solution.py:121
  274.8 4.5 collective-permute-done.16
  282.0 3.8 fusion.53
  291.4 4.0 collective-permute-start.21
  309.3 3.8 fusion.62
  313.1 3.1 collective-permute-start.22
  328.4 3.0 fusion.44
  332.1 3.1 add_convert_fusion.1
  340.6 9.5 %shard_map.274 = bf16[256,1536]{1,0:T(8,128)(2,1)} custom-call(s32[2]{0:T(128)} %bitcast.546, bf16[256,1536]{1,0:T(8,128)(2,1)} %fusion.31.packed_ref, bf16[256,512]{1,0:T(8,128)(2,1)} %convolution_convert_fusion.12.grad_ref), custom_call_target="tpu_custom_call" | custom-call | flops 201326592 | bytes 1572864 | tf_op jit(solution)/shard_map/pallas_call | solution.py:121
  353.9 3.0 fusion.70
  377.0 4.7 copy.104
  407.7 13.7 %collective-permute-done.34 = bf16[2,64,2048]{2,1,0:T(8,128)(2,1)} collective-permute-done((bf16[2,64,2048]{2,1,0:T(8,128)(2,1)}, bf16[2,64,2048]{2,1,0:T(8,128)(2,1)}, u32[]{:S(2)}, u32[]{:S(2)}) %collective-permute-start.34) | collective-permute-done | bytes 524320 | tf_op jit(solution)/shard_map/ppermute | solution.py:259
  429.9 7.4 %collective-permute-done.38 = bf16[64,2048]{1,0:T(8,128)(2,1)S(1)} collective-permute-done((bf16[64,2048]{1,0:T(8,128)(2,1)S(1)}, bf16[64,2048]{1,0:T(8,128)(2,1)S(1)}, u32[]{:S(2)}, u32[]{:S(2)}) %collective-permute-start.38) | collective-permute-done | bytes 262176 | tf_op jit(solution)/shard_map/ppermute | solution.py:259
  449.0 2.9 fusion.56
  452.0 5.5 %collective-permute-start.26 = (bf16[256,1024]{1,0:T(8,128)(2,1)S(1)}, bf16[256,1024]{1,0:T(8,128)(2,1)S(1)}, u32[]{:S(2)}, u32[]{:S(2)}) collective-permute-start(bf16[256,1024]{1,0:T(8,128)(2,1)S(1)} %fusion.56), channel_id=1, source_target_pairs={{0,64},{64,0},{1,65},{65,1},{2,66},{66,2},{3,67},{67,3},{4,68},{68... | collective-permute-start | bytes 1572872 | tf_op jit(solution)/shard_map/ppermute | solution.py:19
  470.0 4.3 collective-permute-done.47
  474.9 4.9 collective-permute-done.49
  479.8 7.4 %collective-permute-done.50 = bf16[16,10240]{1,0:T(8,128)(2,1)S(1)} collective-permute-done((bf16[16,10240]{1,0:T(8,128)(2,1)S(1)}, bf16[16,10240]{1,0:T(8,128)(2,1)S(1)}, u32[]{:S(2)}, u32[]{:S(2)}) %collective-permute-start.50) | collective-permute-done | bytes 327712 | tf_op jit(solution)/shard_map/ppermute | solution.py:266
  491.9 3.7 collective-permute-start.54
  (621 shorter events, 244.6 us)
Async XLA Ops:
  7.2 96.0 %all-gather.3.cloned.1.call-start = ((), (), s32[]{:S(2)}) async-start(), calls=%async_computation | async-start | bytes 11419648 | tf_op jit(solution)/shard_map/all_gather | solution.py:372
  19.2 158.1 %all-gather.5.cloned.1.call-start = ((), (), s32[]{:S(2)}) async-start(), calls=%async_computation.1 | async-start | bytes 9191424 | tf_op jit(solution)/shard_map/all_gather | solution.py:372
  107.8 15.5 %collective-permute-start.5 = (bf16[16,32,1024]{2,1,0:T(8,128)(2,1)}, bf16[16,32,1024]{2,1,0:T(8,128)(2,1)S(1)}, u32[]{:S(2)}, u32[]{:S(2)}) collective-permute-start(bf16[16,32,1024]{2,1,0:T(8,128)(2,1)} %reshape.557), channel_id=1, source_target_pairs={{0,16},{16,0},{32,48},{48,32},{64,112},{80,96},{96,80},{112,64},{1... | collective-permute-start | bytes 3145736 | tf_op jit(solution)/shard_map/ppermute | solution.py:259
  132.7 25.8 %collective-permute-start.8 = (bf16[2,16,32,1024]{3,2,1,0:T(8,128)(2,1)S(1)}, bf16[2,16,32,1024]{3,2,1,0:T(8,128)(2,1)S(1)}, u32[]{:S(2)}, u32[]{:S(2)}) collective-permute-start(bf16[2,16,32,1024]{3,2,1,0:T(8,128)(2,1)S(1)} %pad_maximum_fusion.2), channel_id=1, source_target_pairs={{0,48},{16,32},{32,16},{48,0},{64,80},{80,64},{96,112},{112,96},{1... | collective-permute-start | bytes 6291464 | tf_op jit(solution)/shard_map/ppermute | solution.py:259
  161.0 14.1 %collective-permute-start.9 = (bf16[256,1024]{1,0:T(8,128)(2,1)}, bf16[256,1024]{1,0:T(8,128)(2,1)}, u32[]{:S(2)}, u32[]{:S(2)}) collective-permute-start(bf16[256,1024]{1,0:T(8,128)(2,1)} %convolution_convert_fusion.11), channel_id=1, source_target_pairs={{0,64},{64,0},{1,65},{65,1},{2,66},{66,2},{3,67},{67,3},{4,68},{68... | collective-permute-start | bytes 1572872 | tf_op jit(solution)/shard_map/ppermute | solution.py:19
  171.5 15.3 %collective-permute-start.10 = (bf16[16,32,1024]{2,1,0:T(8,128)(2,1)}, bf16[16,32,1024]{2,1,0:T(8,128)(2,1)}, u32[]{:S(2)}, u32[]{:S(2)}) collective-permute-start(bf16[16,32,1024]{2,1,0:T(8,128)(2,1)} %reshape.562), channel_id=1, source_target_pairs={{0,16},{16,0},{32,48},{48,32},{64,112},{80,96},{96,80},{112,64},{1... | collective-permute-start | bytes 3145736 | tf_op jit(solution)/shard_map/ppermute | solution.py:259
  189.5 25.5 %collective-permute-start.13 = (bf16[2,16,32,1024]{3,2,1,0:T(8,128)(2,1)}, bf16[2,16,32,1024]{3,2,1,0:T(8,128)(2,1)}, u32[]{:S(2)}, u32[]{:S(2)}) collective-permute-start(bf16[2,16,32,1024]{3,2,1,0:T(8,128)(2,1)} %pad_maximum_fusion.3), channel_id=1, source_target_pairs={{0,48},{16,32},{32,16},{48,0},{64,80},{80,64},{96,112},{112,96},{1... | collective-permute-start | bytes 6291464 | tf_op jit(solution)/shard_map/ppermute | solution.py:259
  239.6 35.2 %collective-permute-start.15 = (bf16[2,16,32,1024]{3,2,1,0:T(8,128)(2,1)}, bf16[2,16,32,1024]{3,2,1,0:T(8,128)(2,1)}, u32[]{:S(2)}, u32[]{:S(2)}) collective-permute-start(bf16[2,16,32,1024]{3,2,1,0:T(8,128)(2,1)} %bitcast.50), channel_id=1, source_target_pairs={{0,16},{16,0},{32,48},{48,32},{64,112},{80,96},{96,80},{112,64},{1... | collective-permute-start | bytes 6291464 | tf_op jit(solution)/shard_map/ppermute | solution.py:259
  252.7 26.6 %collective-permute-start.16 = (bf16[2,4,64,2048]{3,2,1,0:T(8,128)(2,1)}, bf16[2,4,64,2048]{3,2,1,0:T(8,128)(2,1)}, u32[]{:S(2)}, u32[]{:S(2)}) collective-permute-start(bf16[2,4,64,2048]{3,2,1,0:T(8,128)(2,1)} %bitcast.55), channel_id=1, source_target_pairs={{0,1},{1,0},{2,3},{3,2},{4,5},{5,4},{6,7},{7,6},{8,9},{9,8},{10,11... | collective-permute-start | bytes 6291464 | tf_op jit(solution)/shard_map/ppermute | solution.py:259
  288.6 14.4 %collective-permute-start.19 = (bf16[16,32,1024]{2,1,0:T(8,128)(2,1)}, bf16[16,32,1024]{2,1,0:T(8,128)(2,1)}, u32[]{:S(2)}, u32[]{:S(2)}) collective-permute-start(bf16[16,32,1024]{2,1,0:T(8,128)(2,1)} %fusion.48), channel_id=1, source_target_pairs={{0,48},{16,32},{32,16},{48,0},{64,80},{80,64},{96,112},{112,96},{1... | collective-permute-start | bytes 3145736 | tf_op jit(solution)/shard_map/ppermute | solution.py:259
  291.4 14.3 %collective-permute-start.20 = (bf16[4,64,2048]{2,1,0:T(8,128)(2,1)}, bf16[4,64,2048]{2,1,0:T(8,128)(2,1)}, u32[]{:S(2)}, u32[]{:S(2)}) collective-permute-start(bf16[4,64,2048]{2,1,0:T(8,128)(2,1)} %fusion.27), channel_id=1, source_target_pairs={{0,3},{1,2},{2,1},{3,0},{4,7},{5,6},{6,5},{7,4},{8,11},{9,10},{10,... | collective-permute-start | bytes 3145736 | tf_op jit(solution)/shard_map/ppermute | solution.py:259
  313.1 22.1 %collective-permute-start.22 = (bf16[256,1024]{1,0:T(8,128)(2,1)S(1)}, bf16[256,1024]{1,0:T(8,128)(2,1)S(1)}, u32[]{:S(2)}, u32[]{:S(2)}) collective-permute-start(bf16[256,1024]{1,0:T(8,128)(2,1)S(1)} %fusion.62), channel_id=1, source_target_pairs={{0,64},{64,0},{1,65},{65,1},{2,66},{66,2},{3,67},{67,3},{4,68},{68... | collective-permute-start | bytes 1572872 | tf_op jit(solution)/shard_map/ppermute | solution.py:19
  317.9 35.8 %collective-permute-start.23 = (bf16[2,4,64,2048]{3,2,1,0:T(8,128)(2,1)}, bf16[2,4,64,2048]{3,2,1,0:T(8,128)(2,1)}, u32[]{:S(2)}, u32[]{:S(2)}) collective-permute-start(bf16[2,4,64,2048]{3,2,1,0:T(8,128)(2,1)} %pad_maximum_fusion.4), channel_id=1, source_target_pairs={{0,4},{1,5},{2,6},{3,7},{4,0},{5,1},{6,2},{7,3},{8,12},{9,13},{10,... | collective-permute-start | bytes 6291464 | tf_op jit(solution)/shard_map/ppermute | solution.py:259
  322.4 31.2 %collective-permute-start.24 = (bf16[2,16,32,1024]{3,2,1,0:T(8,128)(2,1)}, bf16[2,16,32,1024]{3,2,1,0:T(8,128)(2,1)}, u32[]{:S(2)}, u32[]{:S(2)}) collective-permute-start(bf16[2,16,32,1024]{3,2,1,0:T(8,128)(2,1)} %bitcast.69), channel_id=1, source_target_pairs={{0,16},{16,0},{32,48},{48,32},{64,112},{80,96},{96,80},{112,64},{1... | collective-permute-start | bytes 6291464 | tf_op jit(solution)/shard_map/ppermute | solution.py:259
  327.0 26.7 %collective-permute-start.25 = (bf16[2,4,64,2048]{3,2,1,0:T(8,128)(2,1)}, bf16[2,4,64,2048]{3,2,1,0:T(8,128)(2,1)}, u32[]{:S(2)}, u32[]{:S(2)}) collective-permute-start(bf16[2,4,64,2048]{3,2,1,0:T(8,128)(2,1)} %bitcast.74), channel_id=1, source_target_pairs={{0,1},{1,0},{2,3},{3,2},{4,5},{5,4},{6,7},{7,6},{8,9},{9,8},{10,11... | collective-permute-start | bytes 6291464 | tf_op jit(solution)/shard_map/ppermute | solution.py:259
  338.4 12.9 %collective-permute-start.27 = (bf16[512,512]{1,0:T(8,128)(2,1)S(1)}, bf16[512,512]{1,0:T(8,128)(2,1)}, u32[]{:S(2)}, u32[]{:S(2)}) collective-permute-start(bf16[512,512]{1,0:T(8,128)(2,1)S(1)} %broadcast_select_fusion.2), channel_id=1, source_target_pairs={{0,64},{64,0},{1,65},{65,1},{2,66},{66,2},{3,67},{67,3},{4,68},{68... | collective-permute-start | bytes 1572872 | tf_op jit(solution)/shard_map/ppermute | solution.py:19
  356.8 28.0 %collective-permute-start.28 = (bf16[4,64,2048]{2,1,0:T(8,128)(2,1)}, bf16[4,64,2048]{2,1,0:T(8,128)(2,1)}, u32[]{:S(2)}, u32[]{:S(2)}) collective-permute-start(bf16[4,64,2048]{2,1,0:T(8,128)(2,1)} %fusion.70), channel_id=1, source_target_pairs={{0,12},{1,13},{2,14},{3,15},{4,8},{5,9},{6,10},{7,11},{8,4},{9,5},... | collective-permute-start | bytes 3145736 | tf_op jit(solution)/shard_map/ppermute | solution.py:259
  359.8 25.0 %collective-permute-start.29 = (bf16[16,32,1024]{2,1,0:T(8,128)(2,1)}, bf16[16,32,1024]{2,1,0:T(8,128)(2,1)}, u32[]{:S(2)}, u32[]{:S(2)}) collective-permute-start(bf16[16,32,1024]{2,1,0:T(8,128)(2,1)} %fusion.47), channel_id=1, source_target_pairs={{0,48},{16,32},{32,16},{48,0},{64,80},{80,64},{96,112},{112,96},{1... | collective-permute-start | bytes 3145736 | tf_op jit(solution)/shard_map/ppermute | solution.py:259
  362.6 22.3 %collective-permute-start.30 = (bf16[4,64,2048]{2,1,0:T(8,128)(2,1)}, bf16[4,64,2048]{2,1,0:T(8,128)(2,1)}, u32[]{:S(2)}, u32[]{:S(2)}) collective-permute-start(bf16[4,64,2048]{2,1,0:T(8,128)(2,1)} %fusion.28), channel_id=1, source_target_pairs={{0,3},{1,2},{2,1},{3,0},{4,7},{5,6},{6,5},{7,4},{8,11},{9,10},{10,... | collective-permute-start | bytes 3145736 | tf_op jit(solution)/shard_map/ppermute | solution.py:259
  388.5 32.9 %collective-permute-start.31 = (bf16[2,4,64,2176]{3,2,1,0:T(8,128)(2,1)}, bf16[2,4,64,2176]{3,2,1,0:T(8,128)(2,1)}, u32[]{:S(2)}, u32[]{:S(2)}) collective-permute-start(bf16[2,4,64,2176]{3,2,1,0:T(8,128)(2,1)} %pad_maximum_fusion.1), channel_id=1, source_target_pairs={{0,4},{1,5},{2,6},{3,7},{4,0},{5,1},{6,2},{7,3},{8,12},{9,13},{10,... | collective-permute-start | bytes 6684680 | tf_op jit(solution)/shard_map/ppermute | solution.py:259
  395.1 26.3 %collective-permute-start.32 = (bf16[2,2,4,16,2048]{4,3,1,2,0:T(8,128)(2,1)}, bf16[2,2,4,16,2048]{4,3,1,2,0:T(8,128)(2,1)}, u32[]{:S(2)}, u32[]{:S(2)}) collective-permute-start(bf16[2,2,4,16,2048]{4,3,1,2,0:T(8,128)(2,1)} %pad_maximum_fusion.9), channel_id=1, source_target_pairs={{0,16},{16,0},{32,48},{48,32},{64,112},{80,96},{96,80},{112,64},{1... | collective-permute-start | bytes 3145736 | tf_op jit(solution)/shard_map/ppermute | solution.py:259
  400.6 20.8 %collective-permute-start.33 = (bf16[2,2,4,32,1024]{4,3,2,1,0:T(8,128)(2,1)}, bf16[2,2,4,32,1024]{4,3,2,1,0:T(8,128)(2,1)}, u32[]{:S(2)}, u32[]{:S(2)}) collective-permute-start(bf16[2,2,4,32,1024]{4,3,2,1,0:T(8,128)(2,1)} %pad_maximum_fusion.10), channel_id=1, source_target_pairs={{0,1},{1,0},{2,3},{3,2},{4,5},{5,4},{6,7},{7,6},{8,9},{9,8},{10,11... | collective-permute-start | bytes 3145736 | tf_op jit(solution)/shard_map/ppermute | solution.py:259
  405.1 16.3 %collective-permute-start.34 = (bf16[2,64,2048]{2,1,0:T(8,128)(2,1)}, bf16[2,64,2048]{2,1,0:T(8,128)(2,1)}, u32[]{:S(2)}, u32[]{:S(2)}) collective-permute-start(bf16[2,64,2048]{2,1,0:T(8,128)(2,1)} %pad_maximum_fusion.17), channel_id=1, source_target_pairs={{0,1},{1,0},{2,3},{3,2},{4,5},{5,4},{6,7},{7,6},{8,9},{9,8},{10,11... | collective-permute-start | bytes 1572872 | tf_op jit(solution)/shard_map/ppermute | solution.py:259
  423.3 14.7 %collective-permute-start.35 = (bf16[4,64,2176]{2,1,0:T(8,128)(2,1)S(1)}, bf16[4,64,2176]{2,1,0:T(8,128)(2,1)S(1)}, u32[]{:S(2)}, u32[]{:S(2)}) collective-permute-start(bf16[4,64,2176]{2,1,0:T(8,128)(2,1)S(1)} %fusion.65), channel_id=1, source_target_pairs={{0,12},{1,13},{2,14},{3,15},{4,8},{5,9},{6,10},{7,11},{8,4},{9,5},... | collective-permute-start | bytes 3342344 | tf_op jit(solution)/shard_map/ppermute | solution.py:259
  424.7 12.6 %collective-permute-start.36 = (bf16[2,4,16,2048]{3,2,0,1:T(8,128)(2,1)S(1)}, bf16[2,4,16,2048]{3,2,0,1:T(8,128)(2,1)S(1)}, u32[]{:S(2)}, u32[]{:S(2)}) collective-permute-start(bf16[2,4,16,2048]{3,2,0,1:T(8,128)(2,1)S(1)} %fusion.76), channel_id=1, source_target_pairs={{0,48},{16,32},{32,16},{48,0},{64,80},{80,64},{96,112},{112,96},{1... | collective-permute-start | bytes 1572872 | tf_op jit(solution)/shard_map/ppermute | solution.py:259
  440.1 17.4 %collective-permute-start.39 = (bf16[2,64,2176]{2,1,0:T(8,128)(2,1)S(1)}, bf16[2,64,2176]{2,1,0:T(8,128)(2,1)S(1)}, u32[]{:S(2)}, u32[]{:S(2)}) collective-permute-start(bf16[2,64,2176]{2,1,0:T(8,128)(2,1)S(1)} %pad_maximum_fusion.16), channel_id=1, source_target_pairs={{0,1},{1,0},{2,3},{3,2},{4,5},{5,4},{6,7},{7,6},{8,9},{9,8},{10,11... | collective-permute-start | bytes 1671176 | tf_op jit(solution)/shard_map/ppermute | solution.py:259
  442.4 15.1 %collective-permute-start.40 = (bf16[2,2,16,2048]{3,2,1,0:T(8,128)(2,1)S(1)}, bf16[2,2,16,2048]{3,2,1,0:T(8,128)(2,1)S(1)}, u32[]{:S(2)}, u32[]{:S(2)}) collective-permute-start(bf16[2,2,16,2048]{3,2,1,0:T(8,128)(2,1)S(1)} %pad_maximum_fusion.18), channel_id=1, source_target_pairs={{0,4},{1,5},{2,6},{3,7},{4,0},{5,1},{6,2},{7,3},{8,12},{9,13},{10,... | collective-permute-start | bytes 786440 | tf_op jit(solution)/shard_map/ppermute | solution.py:259
  445.7 11.8 %collective-permute-start.41 = (bf16[2,2,32,1024]{3,2,1,0:T(8,128)(2,1)S(1)}, bf16[2,2,32,1024]{3,2,1,0:T(8,128)(2,1)S(1)}, u32[]{:S(2)}, u32[]{:S(2)}) collective-permute-start(bf16[2,2,32,1024]{3,2,1,0:T(8,128)(2,1)S(1)} %pad_maximum_fusion.19), channel_id=1, source_target_pairs={{0,4},{1,5},{2,6},{3,7},{4,0},{5,1},{6,2},{7,3},{8,12},{9,13},{10,... | collective-permute-start | bytes 786440 | tf_op jit(solution)/shard_map/ppermute | solution.py:259
  466.0 13.8 %collective-permute-start.49 = (bf16[64,2176]{1,0:T(8,128)(2,1)S(1)}, bf16[64,2176]{1,0:T(8,128)(2,1)S(1)}, u32[]{:S(2)}, u32[]{:S(2)}) collective-permute-start(bf16[64,2176]{1,0:T(8,128)(2,1)S(1)} %fusion.90), channel_id=1, source_target_pairs={{0,48},{16,0},{32,16},{48,32},{1,49},{17,1},{33,17},{49,33},{2,50}... | collective-permute-start | bytes 835592 | tf_op jit(solution)/shard_map/ppermute | solution.py:266
  467.7 19.5 %collective-permute-start.50 = (bf16[16,10240]{1,0:T(8,128)(2,1)S(1)}, bf16[16,10240]{1,0:T(8,128)(2,1)S(1)}, u32[]{:S(2)}, u32[]{:S(2)}) collective-permute-start(bf16[16,10240]{1,0:T(8,128)(2,1)S(1)} %fusion.149), channel_id=1, source_target_pairs={{0,16},{16,32},{32,48},{48,0},{1,17},{17,33},{33,49},{49,1},{2,18}... | collective-permute-start | bytes 983048 | tf_op jit(solution)/shard_map/ppermute | solution.py:266
  468.1 20.9 %collective-permute-start.51 = (bf16[16,10240]{1,0:T(8,128)(2,1)S(1)}, bf16[16,10240]{1,0:T(8,128)(2,1)S(1)}, u32[]{:S(2)}, u32[]{:S(2)}) collective-permute-start(bf16[16,10240]{1,0:T(8,128)(2,1)S(1)} %fusion.149), channel_id=1, source_target_pairs={{0,32},{16,48},{32,0},{48,16},{1,33},{17,49},{33,1},{49,17},{2,34}... | collective-permute-start | bytes 983048 | tf_op jit(solution)/shard_map/ppermute | solution.py:266
  474.2 17.5 %collective-permute-start.52 = (bf16[16,10240]{1,0:T(8,128)(2,1)S(1)}, bf16[16,10240]{1,0:T(8,128)(2,1)S(1)}, u32[]{:S(2)}, u32[]{:S(2)}) collective-permute-start(bf16[16,10240]{1,0:T(8,128)(2,1)S(1)} %fusion.149), channel_id=1, source_target_pairs={{0,48},{16,0},{32,16},{48,32},{1,49},{17,1},{33,17},{49,33},{2,50}... | collective-permute-start | bytes 983048 | tf_op jit(solution)/shard_map/ppermute | solution.py:266
  (152 other events, 982.2 us)
Sparse Core Ops, SparseCore 0:
  19.3 83.8 all-gather.2
  105.3 71.7 all-gather.4
